TPU v7x, 32 devices: a whole 2x2x4 slice. The times are simulated.
32 devices in a mesh: ctx: 4 (over y, x), head: 4 (over z), pipe: 2 (over core).
Axes of the slice: x: 2, y: 2, z: 4, core: 2. Of those that a mesh axis runs over, the one named last changes fastest.
Arguments:
- queries: bfloat16 [2, 512, 8192], P('pipe', 'ctx', 'head'), may hold values from -6 to 6
- keys: bfloat16 [2, 512, 8192], P('pipe', 'ctx', 'head'), may hold values from -6 to 6
- values: bfloat16 [2, 512, 8192], P('pipe', 'ctx', 'head'), may hold values from -6 to 6
- gates: bfloat16 [2, 512, 8192], P('pipe', 'ctx', 'head'), may hold values from -6 to 6
- log_decay: float32 [2, 512, 64], P('pipe', 'ctx', 'head'), may hold values from -1 to 0
- segment_ids: int32 [2, 512], P('pipe', 'ctx'), may hold values from 0 to 7, never falling along the last dimension, each value on 1 to 128 neighbouring positions
- norm_gain: float32 [2, 8192], P('pipe', 'head'), may hold values from 0.1 to 1.9
- out_weight: bfloat16 [2, 8192, 6144], P('pipe', 'head', 'ctx'), may hold values from -0.0625 to 0.0625
Outputs:
- handed: bfloat16 [2, 512, 6144], P('pipe', 'ctx', 'head')
Inputs may be any that keep to these rules, and one draw needn't show every extreme that they name: `segment_ids`: along each section's tokens the ids never fall; a document has at most a quarter of 512 tokens, and one has exactly that many.
All inputs are finite; a program needn't handle non-finite values.
Results may differ from a plain program's by a relative error of at most 0.02.
Values may be sent and summed in bfloat16 or wider, within the bound.
No kernel may reach another device: no remote copies, remote signals or barrier semaphores. Data moves between devices by JAX's collectives and lax.ppermute only.
A program may use at most 128 MiB of HBM per device.

v0:
```python
import jax
import jax.numpy as jnp
from jax import lax
from jax.sharding import PartitionSpec as P

DH = 128


highest = lax.Precision.HIGHEST


def entering(shard, axis, combine, identity):
    count, index = (lax.axis_size(axis), lax.axis_index(axis))
    everything = jax.tree.map(
        lambda part, kind: lax.all_gather(part.astype(kind), axis),
        shard,
        (jnp.bfloat16, jnp.bfloat16, jnp.bfloat16),
    )
    start = jax.tree.map(
        lambda part, zero: jnp.broadcast_to(jnp.asarray(zero, part.dtype), part.shape),
        shard,
        identity,
    )

    def hop(k, before):
        reached = k < index
        new = combine(
            before, jax.tree.map(lambda part, own: part[k].astype(own.dtype), everything, shard)
        )
        return jax.tree.map(lambda a, b: jnp.where(reached, a, b), new, before)

    return lax.fori_loop(0, count, hop, start)


def from_behind(shard, axis, by):
    count = lax.axis_size(axis)
    return lax.ppermute(shard, axis, [(i, (i + by) % count) for i in range(count)])


def block_step(carried, pieces):
    kv_state, doc_id = carried
    query_rows, key_rows, value_rows, rate_rows, doc_rows = pieces
    length = doc_rows.shape[0]
    running = jnp.cumsum(rate_rows, axis=0)
    running_t = running.T
    causal = lax.broadcasted_iota(jnp.int32, (length, length), 0) >= lax.broadcasted_iota(
        jnp.int32, (length, length), 1
    )
    allowed = causal & (doc_rows[:, None] == doc_rows[None, :])
    log_gaps = running_t[:, :, None] - running_t[:, None, :]
    weights = jnp.where(allowed[None], jnp.exp(jnp.where(allowed[None], log_gaps, 0.0)), 0.0)
    scores = jnp.einsum("ihd,jhd->hij", query_rows, key_rows, preferred_element_type=jnp.float32)
    mixed = (scores * weights).astype(jnp.bfloat16)
    inside = jnp.einsum("hij,jhd->ihd", mixed, value_rows, preferred_element_type=jnp.float32)
    value_full = value_rows.astype(jnp.float32)
    reaches = jnp.exp(running) * (doc_rows == doc_id).astype(jnp.float32)[:, None]
    carried_part = jnp.einsum(
        "ihd,hde->ihe",
        query_rows.astype(jnp.float32) * reaches[:, :, None],
        kv_state,
        precision=highest,
    )
    final_doc = doc_rows[-1]
    retain = (doc_id == final_doc).astype(jnp.float32)
    fading = (
        jnp.exp(running[-1][None, :] - running)
        * (doc_rows == final_doc).astype(jnp.float32)[:, None]
    )
    fresh_part = jnp.einsum(
        "jhd,jhe->hde",
        key_rows.astype(jnp.float32) * fading[:, :, None],
        value_full,
        precision=highest,
    )
    new_state = retain * jnp.exp(running[-1])[:, None, None] * kv_state + fresh_part
    return ((new_state, final_doc), inside + carried_part)


def sweep(query3, key3, value3, rate_rows, doc_rows, start_state, start_doc):
    rows_here = doc_rows.shape[0]
    heads_here = query3.shape[1]
    block_len = min(512, rows_here)
    block_count = rows_here // block_len
    pieces = (
        query3.reshape(block_count, block_len, heads_here, DH),
        key3.reshape(block_count, block_len, heads_here, DH),
        value3.reshape(block_count, block_len, heads_here, DH),
        rate_rows.reshape(block_count, block_len, heads_here),
        doc_rows.reshape(block_count, block_len),
    )
    final_carry, attended = lax.scan(block_step, (start_state, start_doc), pieces)
    return (final_carry[0], attended.reshape(rows_here, heads_here, DH))


def combine_pair(earlier, later):
    rate_early, state_early, doc_early = earlier
    rate_late, state_late, doc_late = later
    linked = ((doc_early == doc_late) | (doc_early < 0) | (doc_late < 0)).astype(jnp.float32)
    merged = linked[0] * rate_late[:, None, None] * state_early + state_late
    return (rate_early * rate_late, merged, jnp.where(doc_late < 0, doc_early, doc_late))


def carry_in(shard_rates, shard_state, shard_doc):
    heads_here = shard_rates.shape[0]
    neutral = (
        jnp.ones((heads_here,), jnp.float32),
        jnp.zeros((heads_here, DH, DH), jnp.float32),
        jnp.full((1,), -1.0, jnp.float32),
    )
    prefix = entering((shard_rates, shard_state, shard_doc), "ctx", combine_pair, neutral)
    return (prefix[1], prefix[2])


def on_device(queries, keys, values, gates, log_decay, segment_ids, norm_gain, out_weight):
    rows_here = queries.shape[1]
    width = queries.shape[2]
    heads_here = width // DH
    query3 = queries[0].reshape(rows_here, heads_here, DH)
    key3 = keys[0].reshape(rows_here, heads_here, DH)
    value3 = values[0].reshape(rows_here, heads_here, DH)
    rate_rows = log_decay[0]
    doc_rows = segment_ids[0].astype(jnp.float32)
    running = jnp.cumsum(rate_rows, axis=0)
    shard_rates = jnp.exp(running[-1])
    shard_doc = doc_rows[-1:]
    fading = (
        jnp.exp(running[-1][None, :] - running)
        * (doc_rows == shard_doc[0]).astype(jnp.float32)[:, None]
    )
    shard_state = jnp.einsum(
        "jhd,jhe->hde",
        key3.astype(jnp.float32) * fading[:, :, None],
        value3.astype(jnp.float32),
        precision=highest,
    )
    incoming, incoming_doc = carry_in(shard_rates, shard_state, shard_doc)
    ignored, attended = sweep(query3, key3, value3, rate_rows, doc_rows, incoming, incoming_doc[0])
    scaling = lax.rsqrt(jnp.mean(attended * attended, axis=-1, keepdims=True) + 1e-06)
    normed = (
        (attended * scaling).reshape(rows_here, width)
        * norm_gain[0][None, :]
        * jax.nn.sigmoid(gates[0].astype(jnp.float32))
    ).astype(jnp.bfloat16)
    weight_here = out_weight[0]
    partial_value = jnp.dot(
        normed,
        lax.all_gather(weight_here, "ctx", axis=1, tiled=True),
        preferred_element_type=jnp.float32,
    )
    summed = lax.psum_scatter(
        partial_value.astype(jnp.bfloat16), "head", scatter_dimension=1, tiled=True
    )
    handed = from_behind(summed, "pipe", 1)
    return handed[None]


def solution(mesh):
    return jax.shard_map(
        on_device,
        mesh=mesh,
        in_specs=(
            P("pipe", "ctx", "head"),
            P("pipe", "ctx", "head"),
            P("pipe", "ctx", "head"),
            P("pipe", "ctx", "head"),
            P("pipe", "ctx", "head"),
            P("pipe", "ctx"),
            P("pipe", "head"),
            P("pipe", "head", "ctx"),
        ),
        out_specs=P("pipe", "ctx", "head"),
        check_vma=False,
    )
```

profile of v0, /device:TPU:0, one launch (start us, length us, event | category | flops | bytes accessed | tf_op | source)
XLA Modules:
  0.0 339.8 jit_solution(6853338392075896185)
XLA Ops:
  6.5 0.9 copy.33
  8.8 1.3 compare_convert_fusion.1
  10.3 1.3 copy.46
  11.6 1.1 copy.48
  12.8 1.5 convolution_convert_fusion
  14.3 0.7 all-gather.8.cloned.1.call-update
  16.4 0.8 dynamic-update-slice
  17.1 11.4 %all-reduce = bf16[4]{0:T(256)(128)(2,1)S(1)} all-reduce(bf16[4]{0:T(256)(128)(2,1)S(1)} %dynamic-update-slice), channel_id=1, replica_groups=mesh['ctx'=4,'head'=4,'pipe'=2] {'ctx'}, use_global_device_ids=true, to_apply=%add | all-reduce | flops 4 | bytes 16
  28.5 7.0 %all-gather.2 = bf16[4,1,16]{2,1,0:T(2,128)(2,1)S(1)} all-gather(bf16[1,1,16]{2,1,0:T(2,128)(2,1)S(1)} %get-tuple-element.198), channel_id=1, replica_groups=mesh['ctx'=4,'head'=4,'pipe'=2] {'ctx'}, dimensions={0}, use_global_device_ids=true | all-gather | bytes 160 | tf_op jit(solution)/shard_map/all_gather | solution.py:15
  35.8 1.8 convolution_bitcast_fusion.1
  37.6 14.9 %all-gather.6.cloned.1.call-done = bf16[64,128,128]{2,1,0:T(8,128)(2,1)} async-done(((bf16[16,128,128]{2,1,0:T(8,128)(2,1)}), bf16[64,128,128]{2,1,0:T(8,128)(2,1)}) %all-gather.6.cloned.1.call-update) | async-done | bytes 2097168 | tf_op jit(solution)/shard_map/all_gather | solution.py:15
  52.5 16.7 %while.10 = (s32[]{:T(128)}, f32[16,128,128]{2,1,0:T(8,128)S(1)}, f32[1]{0:T(128)}, s32[]{:T(128)}, bf16[4,1]{0,1:T(2,128)(2,1)S(1)}, /*index=5*/bf16[4,16]{1,0:...) while((s32[]{:T(128)}, f32[16,128,128]{2,1,0:T(8,128)S(1)}, ...), condition=%wide.region_2.3_spmd.clone, body=%wide.region_1.2_spmd.clone.sunk | while | flops 1310764 | bytes 2621799 | solution.py:32
  54.6 1.3 fusion.43
  56.6 0.7 constant_dynamic-slice_fusion.3
  58.7 1.3 fusion.43
  60.7 0.7 constant_dynamic-slice_fusion.3
  62.8 1.5 fusion.43
  67.2 1.4 fusion.43
  69.4 2.3 multiply_reduce_fusion
  72.2 209.9 %all-gather.8.cloned.1.call-done = bf16[1,2048,6144]{2,1,0:T(8,128)(2,1)} async-done(((bf16[1,2048,1536]{2,1,0:T(8,128)(2,1)}), bf16[1,2048,6144]{2,1,0:T(8,128)(2,1)}) %all-gather.8.cloned.1.call-update) | async-done | bytes 25165840 | tf_op jit(solution)/shard_map/all_gather | solution.py:147
  282.1 13.1 %fusion.6 = bf16[128,6144]{1,0:T(8,128)(2,1)} fusion(bf16[1,2048,6144]{2,1,0:T(8,128)(2,1)} %all-gather.8.cloned.1.call-done, bf16[1,128,2048]{2,1,0:T(8,128)(2,1)} %param.13, f32[128,2048]{1,0:T(8,128)S(1)} %copy.43, f32[2048]{0:T(1024)S(1)} %bitcast.80), kind=kOutput, calls=%fused_computation.9 | convolution fusion | flops 3223846912 | bytes 28319744 | tf_op jit(solution)/shard_map/dot_general | solution.py:145
  295.2 35.4 %reduce-scatter.2.cloned.1.call-done = bf16[128,1536]{1,0:T(8,128)(2,1)} async-done(((bf16[128,6144]{1,0:T(8,128)(2,1)}), bf16[128,1536]{1,0:T(8,128)(2,1)}) %reduce-scatter.2.cloned.1.call-update) | async-done | bytes 393232 | tf_op jit(solution)/shard_map/reduce_scatter | solution.py:150
  330.6 1.9 collective-permute-done
  332.6 0.7 copy.77
  (41 shorter events, 4.5 us)
Async XLA Ops:
  6.5 9.2 %copy-start.4 = (u32[32]{0:T(128)S(1)}, u32[32]{0:T(128)}, u32[]{:S(2)}) copy-start(u32[32]{0:T(128)} %constant.78) | copy-start | bytes 388
  6.5 29.0 %copy-start.1 = (bf16[1,128,2048]{2,1,0:T(8,128)(2,1)S(1)}, bf16[1,128,2048]{2,1,0:T(8,128)(2,1)}, u32[]{:S(2)}) copy-start(bf16[1,128,2048]{2,1,0:T(8,128)(2,1)} %param.10) | copy-start | bytes 1572868
  6.5 46.0 %all-gather.6.cloned.1.call-start = ((), (), s32[]{:S(2)}) async-start(), calls=%async_computation.2 | async-start | bytes 2621440 | tf_op jit(solution)/shard_map/all_gather | solution.py:15
  14.3 267.8 %all-gather.8.cloned.1.call-start = ((), (), s32[]{:S(2)}) async-start(), calls=%async_computation.3 | async-start | bytes 31457280 | tf_op jit(solution)/shard_map/all_gather | solution.py:147
  15.0 315.6 %reduce-scatter.2.cloned.1.call-start = ((), (), s32[]{:S(2)}) async-start(), calls=%async_computation.1 | async-start | bytes 1966080 | tf_op jit(solution)/shard_map/reduce_scatter | solution.py:150
  52.5 16.8 %copy-start.3 = (s32[1,128]{1,0:T(1,128)S(1)}, s32[1,128]{1,0:T(1,128)}, u32[]{:S(2)}) copy-start(s32[1,128]{1,0:T(1,128)} %param.15) | copy-start | bytes 1540
  52.5 16.9 %copy-start = (f32[128,16,128]{0,2,1:T(8,128)S(1)}, f32[128,16,128]{0,2,1:T(8,128)}, u32[]{:S(2)}) copy-start(f32[128,16,128]{0,2,1:T(8,128)} %convolution_bitcast_fusion.1) | copy-start | bytes 3145732
  69.3 212.8 %copy-start.2 = (f32[1,2048]{1,0:T(1,128)S(1)}, f32[1,2048]{1,0:T(1,128)}, u32[]{:S(2)}) copy-start(f32[1,2048]{1,0:T(1,128)} %param.16) | copy-start | bytes 24580
  330.6 1.9 collective-permute-start
Sparse Core Ops, SparseCore 0:
  14.4 38.0 all-gather.5
  54.4 227.6 all-gather.7
  295.3 35.2 reduce-scatter.1
where the time goes:
time: 340 us
  waiting for transfers between devices  263 us (77%)
  matrix products  18.6 us (5%)
  blocking collectives  18.4 us (5%)
  between operations  13.9 us (4%)
  local copies, waits for them, and re-layouts  9.3 us (3%)
  loops' own time  8.57 us (3%)
  other arithmetic  8.05 us (2%)
    all_gather x1, waiting for transfers between devices, on_device(): lax.all_gather(weight_here, 'ctx', axis=1, tiled=True)  210 us
    reduce_scatter x1, waiting for transfers between devices, on_device(): lax.psum_scatter(partial_value.astype(jnp.bfloat16), 'head', scatter_dime...  35.4 us
    all_gather x1, waiting for transfers between devices, entering(): lax.all_gather(part.astype(kind), axis)  14.9 us
    dot_general x1, matrix products, on_device(): jnp.dot(normed, lax.all_gather(weight_here, 'ctx', axis=1, tiled=True), p...  13.1 us
    unnamed x1, blocking collectives  11.4 us
    another operation x1, loops' own time, entering(): return lax.fori_loop(0, count, hop, start)  8.57 us
    all_gather x1, blocking collectives, entering(): lax.all_gather(part.astype(kind), axis)  6.97 us
  transfers between devices with their start and end apart: 4, of which 4 were waited for; matrix products, arithmetic and copies ran while one was open for 4% of the time, Pallas kernels for 0%

commit v1 on v0

v1 whole, which is shorter than its diff:
```python
import functools
import math

import jax
import jax.numpy as jnp
from jax import lax
from jax.experimental import pallas as pl
from jax.experimental.pallas import tpu as pltpu
from jax.sharding import PartitionSpec as P

DH = 128
EXTRA = 16
VMEM = pl.BlockSpec(memory_space=pltpu.VMEM)
ANY = pl.BlockSpec(memory_space=pl.ANY)
HBM = pl.BlockSpec(memory_space=pltpu.HBM)


def dot(a, b, contract=((1,), (0,)), precision=None):
    return lax.dot_general(
        a, b, (contract, ((), ())), preferred_element_type=jnp.float32, precision=precision
    )


def running_sums(rate):
    rows = rate.shape[1]
    upper = (
        lax.broadcasted_iota(jnp.int32, (rows, rows), 0)
        <= lax.broadcasted_iota(jnp.int32, (rows, rows), 1)
    ).astype(jnp.float32)
    across = dot(rate, upper, precision=lax.Precision.HIGHEST)
    columns = dot(upper, rate, ((0,), (1,)), precision=lax.Precision.HIGHEST)
    return columns, across


def state_kernel(
    first,
    key_hbm,
    value_hbm,
    rate_hbm,
    doc_hbm,
    *refs,
):
    out_ref, key_ref, value_ref, rate_ref, doc_ref, sems, small = refs[-7:]
    rows = rate_ref.shape[1]
    wide = key_ref.shape[1]
    heads = wide // DH
    parts = sems.shape[0]
    piece = wide // parts
    copies = [
        pltpu.make_async_copy(rate_hbm.at[0], rate_ref, small.at[0]),
        pltpu.make_async_copy(doc_hbm, doc_ref, small.at[1]),
    ]
    pieces = []
    for part in range(parts):
        source = pl.ds(first * DH + part * piece, piece)
        span = pl.ds(part * piece, piece)
        pieces.append(
            [
                pltpu.make_async_copy(
                    key_hbm.at[0, :, source], key_ref.at[:, span], sems.at[part, 0]
                ),
                pltpu.make_async_copy(
                    value_hbm.at[0, :, source], value_ref.at[:, span], sems.at[part, 1]
                ),
            ]
        )
    for copy in copies + sum(pieces, []):
        copy.start()
    for copy in copies:
        copy.wait()
    columns, across = running_sums(rate_ref[...])
    doc = doc_ref[...]
    last_doc = doc[:, rows - 1 :]
    fading = jnp.where(doc == last_doc, jnp.exp(across[:, rows - 1 :] - across), 0.0)
    fading_columns = fading.T
    out_ref[wide:, :] = jnp.broadcast_to(
        (last_doc + 1).astype(jnp.float32), (EXTRA, DH)
    ).astype(jnp.bfloat16)
    for part in range(parts):
        for copy in pieces[part]:
            copy.wait()
        for k in range(part * heads // parts, (part + 1) * heads // parts):
            span = slice(k * DH, (k + 1) * DH)
            h = first + k
            faded = (key_ref[:, span].astype(jnp.float32) * fading_columns[:, h : h + 1]).astype(
                jnp.bfloat16
            )
            out_ref[span, :] = dot(faded, value_ref[:, span], ((0,), (0,))).astype(jnp.bfloat16)


def inside_kernel(
    query_hbm,
    key_hbm,
    value_hbm,
    gate_hbm,
    rate_hbm,
    doc_hbm,
    gain_hbm,
    weight_hbm,
    out_ref,
    factor_ref,
    reach_ref,
    doc_out_ref,
    query_ref,
    weight_ref,
    key_ref,
    value_ref,
    gate_ref,
    rate_ref,
    doc_ref,
    gain_ref,
    sems,
):
    sources = [rate_hbm.at[0], doc_hbm, gain_hbm, query_hbm.at[0], key_hbm.at[0], value_hbm.at[0]]
    sources += [gate_hbm.at[0], weight_hbm.at[0]]
    targets = [rate_ref, doc_ref, gain_ref, query_ref, key_ref, value_ref, gate_ref, weight_ref]
    copies = [
        pltpu.make_async_copy(source, target, sems.at[i])
        for i, (source, target) in enumerate(zip(sources, targets))
    ]
    for copy in copies:
        copy.start()
    for copy in copies[:3]:
        copy.wait()
    heads, rows = rate_ref.shape
    columns, across = running_sums(rate_ref[...])
    reach_ref[...] = jnp.exp(columns)
    doc_across = jnp.broadcast_to(doc_ref[...].astype(jnp.float32) + 1.0, (rows, rows))
    doc_out_ref[...] = doc_across.T
    allowed = (
        lax.broadcasted_iota(jnp.int32, (rows, rows), 0)
        >= lax.broadcasted_iota(jnp.int32, (rows, rows), 1)
    ) & (doc_across == doc_across.T)
    for copy in copies[3:6]:
        copy.wait()
    for h in range(heads):
        span = slice(h * DH, (h + 1) * DH)
        gaps = columns[:, h : h + 1] - across[h : h + 1, :]
        weights = jnp.where(allowed, jnp.exp(jnp.where(allowed, gaps, 0.0)), 0.0)
        scores = dot(query_ref[:, span], key_ref[:, span], ((1,), (1,)))
        mixed = (scores * weights).astype(jnp.bfloat16)
        out_ref[:, span] = dot(mixed, value_ref[:, span])
    copies[6].wait()
    for h in range(heads):
        span = slice(h * DH, (h + 1) * DH)
        gate = jax.nn.sigmoid(gate_ref[:, span].astype(jnp.float32))
        factor_ref[:, span] = gain_ref[:, span] * gate
    copies[7].wait()


def finish_kernel(
    first, inside_ref, factor_ref, reach_ref, doc_ref, query_ref, state_ref, *refs
):
    out_ref = refs[-1]
    wide = out_ref.shape[1]
    incoming = state_ref[wide:, :].astype(jnp.float32)[0:1, :]
    reached = (doc_ref[...] == incoming).astype(jnp.float32)
    for k in range(wide // DH):
        h = first + k
        span = slice(h * DH, (h + 1) * DH)
        own = slice(k * DH, (k + 1) * DH)
        reaches = reach_ref[:, h : h + 1] * reached
        attended = inside_ref[:, span] + reaches * dot(query_ref[:, span], state_ref[own, :])
        scaling = lax.rsqrt(jnp.mean(attended * attended, axis=-1, keepdims=True) + 1e-06)
        out_ref[:, own] = (attended * scaling * factor_ref[:, span]).astype(jnp.bfloat16)


def project_kernel(sides, other, *refs):
    out_ref = refs[-1]
    count = sides * out_ref.shape[0]
    pieces, weight_ref = refs[:count], refs[count]
    blocks, rows, columns = out_ref.shape
    half = (lax.axis_index("head") & 1) ^ other
    wide = math.gcd(columns, 256)
    depth = pieces[0].shape[1]
    everything = [
        jnp.concatenate([piece[...] for piece in pieces[i::sides]], axis=0) for i in range(sides)
    ]
    for start in range(0, columns, wide):
        span = pl.ds(pl.multiple_of(half * columns + start, wide), wide)
        result = sum(
            dot(everything[i], weight_ref[i * depth : (i + 1) * depth, span]) for i in range(sides)
        ).astype(jnp.bfloat16)
        for j in range(blocks):
            out_ref[j, :, start : start + wide] = result[j * rows : (j + 1) * rows]


def merge_kernel(keep_ref, arrived_ref, *refs):
    for i, out_ref in enumerate(refs[-keep_ref.shape[0] :]):
        total = keep_ref[i].astype(jnp.float32) + arrived_ref[i].astype(jnp.float32)
        out_ref[...] = total.astype(jnp.bfloat16)


def pick_kernel(*refs):
    block_refs, out_refs = refs[: len(refs) // 2], refs[len(refs) // 2 :]
    at = lax.axis_index("ctx") ^ lax.axis_index("head")
    for m, out_ref in enumerate(out_refs):
        for j, block_ref in enumerate(block_refs):

            @pl.when((at ^ m) == j)
            def _(out_ref=out_ref, block_ref=block_ref):
                out_ref[...] = block_ref[...]


def last_kernel(*refs):
    out_ref = refs[-1]
    wide = refs[0].shape[1]
    for m in range(2):
        total = refs[m][...].astype(jnp.float32) + refs[m + 2][...].astype(jnp.float32)
        half = (lax.axis_index("head") & 1) ^ m
        out_ref[0, :, pl.ds(pl.multiple_of(half * wide, wide), wide)] = total.astype(jnp.bfloat16)


def call(kernel, out_shape, name, limit=24, **more):
    return pl.pallas_call(
        kernel,
        out_shape=out_shape,
        compiler_params=pltpu.CompilerParams(vmem_limit_bytes=limit * 2**20),
        cost_estimate=pl.CostEstimate(flops=1, bytes_accessed=1, transcendentals=0),
        name=name,
        **more,
    )


def on_device(sizes, queries, keys, values, gates, log_decay, segment_ids, norm_gain, out_weight):
    n_ctx, n_head, n_pipe = sizes
    rows, width = queries.shape[1:]
    heads = width // DH
    tokens = rows * n_ctx
    hops = min(n_ctx - 1, -(-(tokens // 4 - 1) // rows))

    def stay(array):
        return pltpu.with_memory_space_constraint(array, pltpu.HBM)

    rates = stay(jnp.swapaxes(log_decay, 1, 2))
    queries, keys, values, gates = map(stay, (queries, keys, values, gates))
    segment_ids, norm_gain, out_weight = map(stay, (segment_ids, norm_gain, out_weight))
    columns = out_weight.shape[2]
    sides = 2
    side = heads // sides
    wide = side * DH

    def from_before(array, by):
        return lax.ppermute(array, "ctx", [(i, i + by) for i in range(n_ctx - by)])

    def state_of(first, after):
        parts = 2 if side % 2 == 0 else 1
        return call(
            functools.partial(state_kernel, first),
            jax.ShapeDtypeStruct((wide + EXTRA, DH), jnp.bfloat16),
            "shard_state",
            in_specs=[HBM] * 4 + [ANY] * len(after),
            scratch_shapes=[
                pltpu.VMEM((rows, wide), jnp.bfloat16),
                pltpu.VMEM((rows, wide), jnp.bfloat16),
                pltpu.VMEM((heads, rows), jnp.float32),
                pltpu.VMEM((1, rows), jnp.int32),
                pltpu.SemaphoreType.DMA((parts, 2)),
                pltpu.SemaphoreType.DMA((2,)),
            ],
        )(keys, values, rates, segment_ids, *after)

    def entering(state, first):
        incoming = from_before(state, 1)
        if hops > 1:
            decay = jnp.exp(jnp.sum(log_decay[0, :, first : first + side], axis=0))
            decay = decay.astype(jnp.bfloat16)
            total = incoming[:wide].reshape(side, DH, DH).astype(jnp.float32)
            through = jnp.ones((side,), jnp.float32)
            for by in range(2, hops + 1):
                through = through * from_before(decay, by - 1).astype(jnp.float32)
                far = from_before(state, by)
                same = jnp.where(far[wide, 0] == incoming[wide, 0], through, 0.0)
                far = far[:wide].reshape(side, DH, DH).astype(jnp.float32)
                total = total + same[:, None, None] * far
            total = total.reshape(wide, DH).astype(jnp.bfloat16)
            incoming = jnp.concatenate([total, incoming[wide:]], axis=0)
        return incoming

    states = []
    for i in range(sides):
        states.append(state_of(i * side, states))
    incoming = [entering(state, i * side) for i, state in enumerate(states)]

    inside, factor, reach, docs, query, weight = call(
        inside_kernel,
        (
            pltpu.VMEM((rows, width), jnp.float32),
            pltpu.VMEM((rows, width), jnp.float32),
            pltpu.VMEM((rows, heads), jnp.float32),
            pltpu.VMEM((rows, DH), jnp.float32),
            pltpu.VMEM((rows, width), jnp.bfloat16),
            pltpu.VMEM((width, columns), jnp.bfloat16),
        ),
        "inside",
        in_specs=[HBM] * 8,
        scratch_shapes=[
            pltpu.VMEM((rows, width), jnp.bfloat16),
            pltpu.VMEM((rows, width), jnp.bfloat16),
            pltpu.VMEM((rows, width), jnp.bfloat16),
            pltpu.VMEM((heads, rows), jnp.float32),
            pltpu.VMEM((1, rows), jnp.int32),
            pltpu.VMEM((1, width), jnp.float32),
            pltpu.SemaphoreType.DMA((8,)),
        ],
    )(queries, keys, values, gates, rates, segment_ids, norm_gain, out_weight)

    def finish(i, after):
        return call(
            functools.partial(finish_kernel, i * side),
            jax.ShapeDtypeStruct((rows, wide), jnp.bfloat16),
            "finish",
            in_specs=[VMEM] * 6 + [ANY] * len(after),
        )(inside, factor, reach, docs, query, incoming[i], *after)

    if n_ctx != 4 or n_head != 4 or n_pipe != 2:
        normed = jnp.concatenate([finish(i, ()) for i in range(sides)], axis=1)
        normed = lax.all_gather(normed, "ctx", axis=0, tiled=True)
        blocks = jnp.dot(normed, weight, preferred_element_type=jnp.float32).astype(jnp.bfloat16)
        blocks = lax.all_to_all(blocks.reshape(n_ctx, rows, columns), "ctx", 0, 0, tiled=True)
        blocks = blocks.reshape(n_head, n_ctx // n_head, rows, columns)
        blocks = lax.all_to_all(blocks, "head", 0, 0, tiled=True)
        total = jnp.sum(blocks.astype(jnp.float32), axis=0).astype(jnp.bfloat16)
        total = jnp.swapaxes(total, 0, 1).reshape(1, rows, -1)
        return lax.ppermute(total, "pipe", [(s, (s + 1) % n_pipe) for s in range(n_pipe)])

    def moved(array, target):
        names = ("ctx", "head", "pipe")
        spots = [(i, j, s) for i in range(n_ctx) for j in range(n_head) for s in range(n_pipe)]
        place = {spot: at for at, spot in enumerate(spots)}
        return lax.ppermute(array, names, [(place[spot], place[target(*spot)]) for spot in spots])

    def swapped(array, by):
        return moved(array, lambda i, j, s: (i ^ by, j, s))

    pieces = []
    for i in range(sides):
        own = finish(i, ())
        one, two = swapped(own, 1), swapped(own, 2)
        pieces.append([own, one, two, swapped(two, 1) if i % 2 else swapped(one, 2)])

    part = columns // 2
    single = jax.ShapeDtypeStruct((rows, part), jnp.bfloat16)

    def project(picked, other, after=()):
        shape = jax.ShapeDtypeStruct((len(picked), rows, part), jnp.bfloat16)
        kernel = functools.partial(project_kernel, sides, other)
        operands = [pieces[i][j] for j in picked for i in range(sides)]
        specs = [VMEM] * (len(operands) + 1) + [ANY] * len(after)
        return call(kernel, shape, "project", in_specs=specs)(*operands, weight, *after)

    blocks = [None] * n_ctx
    after, before = (pieces[0][2],), ()
    for picked in ((0,), (1, 2), (3,)):
        arrived = moved(project(picked, 1, after), lambda i, j, s: (i, j ^ 1, s))
        specs = [VMEM] * 2 + [ANY] * len(before)
        merged = call(merge_kernel, (single,) * len(picked), "merge", in_specs=specs)(
            project(picked, 0), arrived, *before
        )
        before = merged[:1]
        for k, block in zip(picked, merged):
            blocks[k] = swapped(block, k) if k else block
        after = (blocks[0],)
    picked = call(pick_kernel, (single,) * n_head, "pick")(*blocks)
    arrived = [
        moved(block, lambda i, j, s, m=m: (i, j ^ m, 1 - s)) for m, block in enumerate(picked)
    ]
    out = jax.ShapeDtypeStruct((1, rows, columns), jnp.bfloat16)
    return call(last_kernel, out, "last")(*arrived)


def solution(mesh):
    sizes = tuple(mesh.shape[axis] for axis in ("ctx", "head", "pipe"))
    return jax.shard_map(
        functools.partial(on_device, sizes),
        mesh=mesh,
        in_specs=(
            P("pipe", "ctx", "head"),
            P("pipe", "ctx", "head"),
            P("pipe", "ctx", "head"),
            P("pipe", "ctx", "head"),
            P("pipe", "ctx", "head"),
            P("pipe", "ctx"),
            P("pipe", "head"),
            P("pipe", "head", "ctx"),
        ),
        out_specs=P("pipe", "ctx", "head"),
        check_vma=False,
    )
```

time: 340 us -> 80.8 us (0.24)
  the two profiles are of different devices: /device:TPU:0 before, /device:TPU:11 now
where the time goes in v1:
time: 80.8 us; the launch traced here: 80.5 us
  waiting for transfers between devices  38.6 us (48%)
  starting transfers between devices  26.5 us (33%)
  Pallas kernels  15.3 us (19%)
    ppermute x16, waiting for transfers between devices, moved(): lax.ppermute(array, names, [(place[spot], place[target(*spot)]) for spot...  37.1 us
    ppermute x16, starting transfers between devices, moved(): lax.ppermute(array, names, [(place[spot], place[target(*spot)]) for spot...  20.3 us
    ppermute x2, starting transfers between devices, from_before(): return lax.ppermute(array, 'ctx', [(i, i + by) for i in range(n_ctx - by)])  6.24 us
    pallas_call x6, Pallas kernels, project(): call(kernel, shape, 'project', in_specs=specs)(*operands, weight, *after)  4.42 us
    pallas_call x1, Pallas kernels, on_device(): call(inside_kernel, (pltpu.VMEM((rows, width), jnp.float32), pltpu.VMEM((...  4.23 us
    pallas_call x2, Pallas kernels, state_of(): call(functools.partial(state_kernel, first), jax.ShapeDtypeStruct((wide +...  3.95 us
  transfers between devices with their start and end apart: 18, of which 12 were waited for; matrix products, arithmetic and copies ran while one was open for 0% of the time, Pallas kernels for 15%

profile of v1, /device:TPU:11, one launch (start us, length us, event | category | flops | bytes accessed | tf_op | source)
XLA Modules:
  0.0 80.5 jit_solution(12552780838572767447)
XLA Ops:
  0.0 2.0 %shard_state.2.refs_0_ = bf16[1040,128]{1,0:T(8,128)(2,1)S(1)} custom-call(bf16[1,128,2048]{2,1,0:T(8,128)(2,1)} %key_hbm.5, bf16[1,128,2048]{2,1,0:T(8,128)(2,1)} %value_hbm.5, f32[1,16,128]{2,1,0:T(8,128)} %bitcast.1, s32[1,128]{1,0:T(1,128)} %doc_hbm.5), custom_call_target="tpu_custom_call" | custom-call | flops 1 | bytes 1 | tf_op jit(solution)/shard_map/shard_state/pallas_call | solution.py:248
  2.0 3.1 %collective-permute-start = (bf16[1040,128]{1,0:T(8,128)(2,1)S(1)}, bf16[1040,128]{1,0:T(8,128)(2,1)S(1)}, u32[]{:S(2)}, u32[]{:S(2)}) collective-permute-start(bf16[1040,128]{1,0:T(8,128)(2,1)S(1)} %shard_state.2.refs_0_), channel_id=1, source_target_pairs={{0,8},{8,16},{16,24},{1,9},{9,17},{17,25},{2,10},{10,18},{18,26},{... | collective-permute-start | bytes 798728 | tf_op jit(solution)/shard_map/ppermute | solution.py:244
  5.1 2.0 %shard_state.3 = bf16[1040,128]{1,0:T(8,128)(2,1)S(1)} custom-call(bf16[1,128,2048]{2,1,0:T(8,128)(2,1)} %key_hbm.5, bf16[1,128,2048]{2,1,0:T(8,128)(2,1)} %value_hbm.5, f32[1,16,128]{2,1,0:T(8,128)} %bitcast.2, s32[1,128]{1,0:T(1,128)} %doc_hbm.5, bf16[1040,128]{1,0:T(8,128)(2,1)S(1)} %shard_state.2.refs_0_), custom_call_target="tpu_custom_call" | custom-call | flops 1 | bytes 1 | tf_op jit(solution)/shard_map/shard_state/pallas_call | solution.py:248
  7.1 3.1 %collective-permute-start.1 = (bf16[1040,128]{1,0:T(8,128)(2,1)S(1)}, bf16[1040,128]{1,0:T(8,128)(2,1)S(1)}, u32[]{:S(2)}, u32[]{:S(2)}) collective-permute-start(bf16[1040,128]{1,0:T(8,128)(2,1)S(1)} %shard_state.3), channel_id=1, source_target_pairs={{0,8},{8,16},{16,24},{1,9},{9,17},{17,25},{2,10},{10,18},{18,26},{... | collective-permute-start | bytes 798728 | tf_op jit(solution)/shard_map/ppermute | solution.py:244
  10.2 4.2 %inside.1 = (f32[128,2048]{1,0:T(8,128)S(1)}, f32[128,2048]{1,0:T(8,128)S(1)}, f32[128,16]{1,0:T(8,128)S(1)}, f32[128,128]{1,0:T(8,128)S(1)}, bf16[128,2048]{1,0...) custom-call(bf16[1,128,2048]{2,1,0:T(8,128)(2,1)} %query_hbm.1, bf16[1,128,2048]{2,1,0:T(8,128)(2,1)} %key_hbm.5, ...), custom_call_target="tpu_custom_call" | custom-call | flops 1 | bytes 1 | tf_op jit(solution)/shard_map/inside/pallas_call | solution.py:285
  15.7 1.5 %collective-permute-done.1.state_ref = bf16[1040,128]{1,0:T(8,128)(2,1)S(1)} collective-permute-done((bf16[1040,128]{1,0:T(8,128)(2,1)S(1)}, bf16[1040,128]{1,0:T(8,128)(2,1)S(1)}, u32[]{:S(2)}, u32[]{:S(2)}) %collective-permute-start.1) | collective-permute-done | bytes 266272 | tf_op jit(solution)/shard_map/ppermute | solution.py:244
  17.9 1.0 %collective-permute-start.6 = (bf16[128,1024]{1,0:T(8,128)(2,1)S(1)}, bf16[128,1024]{1,0:T(8,128)(2,1)S(1)}, u32[]{:S(2)}, u32[]{:S(2)}) collective-permute-start(bf16[128,1024]{1,0:T(8,128)(2,1)S(1)} %finish.3.refs_1_), channel_id=1, source_target_pairs={{0,16},{1,17},{2,18},{3,19},{4,20},{5,21},{6,22},{7,23},{8,24},{9,... | collective-permute-start | bytes 786440 | tf_op jit(solution)/shard_map/ppermute | solution.py:331
  18.9 1.4 %collective-permute-start.5 = (bf16[128,1024]{1,0:T(8,128)(2,1)S(1)}, bf16[128,1024]{1,0:T(8,128)(2,1)S(1)}, u32[]{:S(2)}, u32[]{:S(2)}) collective-permute-start(bf16[128,1024]{1,0:T(8,128)(2,1)S(1)} %finish.3.refs_1_), channel_id=1, source_target_pairs={{0,8},{1,9},{2,10},{3,11},{4,12},{5,13},{6,14},{7,15},{8,0},{9,1},... | collective-permute-start | bytes 786440 | tf_op jit(solution)/shard_map/ppermute | solution.py:331
  20.3 1.5 %collective-permute-done.2.refs_3_.refs_2_ = bf16[128,1024]{1,0:T(8,128)(2,1)S(1)} collective-permute-done((bf16[128,1024]{1,0:T(8,128)(2,1)S(1)}, bf16[128,1024]{1,0:T(8,128)(2,1)S(1)}, u32[]{:S(2)}, u32[]{:S(2)}) %collective-permute-start.2) | collective-permute-done | bytes 262176 | tf_op jit(solution)/shard_map/ppermute | solution.py:331
  23.1 4.4 %collective-permute-done.6.refs_3_ = bf16[128,1024]{1,0:T(8,128)(2,1)S(1)} collective-permute-done((bf16[128,1024]{1,0:T(8,128)(2,1)S(1)}, bf16[128,1024]{1,0:T(8,128)(2,1)S(1)}, u32[]{:S(2)}, u32[]{:S(2)}) %collective-permute-start.6) | collective-permute-done | bytes 262176 | tf_op jit(solution)/shard_map/ppermute | solution.py:331
  27.5 1.8 %collective-permute-start.11 = (bf16[128,1024]{1,0:T(8,128)(2,1)S(1)}, bf16[128,1024]{1,0:T(8,128)(2,1)S(1)}, u32[]{:S(2)}, u32[]{:S(2)}) collective-permute-start(bf16[128,1024]{1,0:T(8,128)(2,1)S(1)} %collective-permute-done.6.refs_3_), channel_id=1, source_target_pairs={{0,8},{1,9},{2,10},{3,11},{4,12},{5,13},{6,14},{7,15},{8,0},{9,1},... | collective-permute-start | bytes 786440 | tf_op jit(solution)/shard_map/ppermute | solution.py:331
  30.0 1.0 %project.9 = bf16[2,128,768]{2,1,0:T(8,128)(2,1)S(1)} custom-call(bf16[128,1024]{1,0:T(8,128)(2,1)S(1)} %collective-permute-done.4.refs_0_, bf16[128,1024]{1,0:T(8,128)(2,1)S(1)} %collective-permute-done.5.refs_1_, bf16[128,1024]{1,0:T(8,128)(2,1)S(1)} %collective-permute-done.2.refs_3_.refs_2_, bf16[128,1024]{1,0:T(8,128)(2,1)S(1)} %collective-permute-done.6.refs_3_, ...), custom_call_target="tpu_custom_call" | custom-call | flops 1 | bytes 1 | tf_op jit(solution)/shard_map/project/pallas_call | solution.py:350
  31.3 1.9 %collective-permute-done.10.refs_0_ = bf16[128,1024]{1,0:T(8,128)(2,1)S(1)} collective-permute-done((bf16[128,1024]{1,0:T(8,128)(2,1)S(1)}, bf16[128,1024]{1,0:T(8,128)(2,1)S(1)}, u32[]{:S(2)}, u32[]{:S(2)}) %collective-permute-start.10) | collective-permute-done | bytes 262176 | tf_op jit(solution)/shard_map/ppermute | solution.py:331
  35.9 3.5 %collective-permute-done.7.arrived_ref = bf16[2,128,768]{2,1,0:T(8,128)(2,1)S(1)} collective-permute-done((bf16[2,128,768]{2,1,0:T(8,128)(2,1)S(1)}, bf16[2,128,768]{2,1,0:T(8,128)(2,1)S(1)}, u32[]{:S(2)}, u32[]{:S(2)}) %collective-permute-start.7) | collective-permute-done | bytes 393248 | tf_op jit(solution)/shard_map/ppermute | solution.py:331
  39.5 3.7 %collective-permute-start.9 = (bf16[128,768]{1,0:T(8,128)(2,1)S(1)}, bf16[128,768]{1,0:T(8,128)(2,1)S(1)}, u32[]{:S(2)}, u32[]{:S(2)}) collective-permute-start(bf16[128,768]{1,0:T(8,128)(2,1)S(1)} %get-tuple-element.24), channel_id=1, source_target_pairs={{0,16},{1,17},{2,18},{3,19},{4,20},{5,21},{6,22},{7,23},{8,24},{9,... | collective-permute-start | bytes 589832 | tf_op jit(solution)/shard_map/ppermute | solution.py:331
  43.7 3.1 %collective-permute-start.13 = (bf16[128,768]{1,0:T(8,128)(2,1)S(1)}, bf16[128,768]{1,0:T(8,128)(2,1)S(1)}, u32[]{:S(2)}, u32[]{:S(2)}) collective-permute-start(bf16[128,768]{1,0:T(8,128)(2,1)S(1)} %merge.5), channel_id=1, source_target_pairs={{0,24},{1,25},{2,26},{3,27},{4,28},{5,29},{6,30},{7,31},{8,16},{9,... | collective-permute-start | bytes 589832 | tf_op jit(solution)/shard_map/ppermute | solution.py:331
  46.8 1.8 %collective-permute-start.8 = (bf16[128,768]{1,0:T(8,128)(2,1)S(1)}, bf16[128,768]{1,0:T(8,128)(2,1)S(1)}, u32[]{:S(2)}, u32[]{:S(2)}) collective-permute-start(bf16[128,768]{1,0:T(8,128)(2,1)S(1)} %get-tuple-element.23.refs_0_), channel_id=1, source_target_pairs={{0,8},{1,9},{2,10},{3,11},{4,12},{5,13},{6,14},{7,15},{8,0},{9,1},... | collective-permute-start | bytes 589832 | tf_op jit(solution)/shard_map/ppermute | solution.py:331
  48.6 1.4 %collective-permute-done.13.refs_3_ = bf16[128,768]{1,0:T(8,128)(2,1)S(1)} collective-permute-done((bf16[128,768]{1,0:T(8,128)(2,1)S(1)}, bf16[128,768]{1,0:T(8,128)(2,1)S(1)}, u32[]{:S(2)}, u32[]{:S(2)}) %collective-permute-start.13) | collective-permute-done | bytes 196640 | tf_op jit(solution)/shard_map/ppermute | solution.py:331
  50.0 5.8 %collective-permute-done.8.refs_1_ = bf16[128,768]{1,0:T(8,128)(2,1)S(1)} collective-permute-done((bf16[128,768]{1,0:T(8,128)(2,1)S(1)}, bf16[128,768]{1,0:T(8,128)(2,1)S(1)}, u32[]{:S(2)}, u32[]{:S(2)}) %collective-permute-start.8) | collective-permute-done | bytes 196640 | tf_op jit(solution)/shard_map/ppermute | solution.py:331
  55.8 3.0 %collective-permute-start.14 = (bf16[128,768]{1,0:T(8,128)(2,1)S(1)}, bf16[128,768]{1,0:T(8,128)(2,1)S(1)}, u32[]{:S(2)}, u32[]{:S(2)}) collective-permute-start(bf16[128,768]{1,0:T(8,128)(2,1)S(1)} %get-tuple-element.25), channel_id=1, source_target_pairs={{0,1},{1,0},{2,3},{3,2},{4,5},{5,4},{6,7},{7,6},{8,9},{9,8},{10,11... | collective-permute-start | bytes 589832 | tf_op jit(solution)/shard_map/ppermute | solution.py:331
  59.0 2.6 %collective-permute-start.16 = (bf16[128,768]{1,0:T(8,128)(2,1)S(1)}, bf16[128,768]{1,0:T(8,128)(2,1)S(1)}, u32[]{:S(2)}, u32[]{:S(2)}) collective-permute-start(bf16[128,768]{1,0:T(8,128)(2,1)S(1)} %get-tuple-element.27), channel_id=1, source_target_pairs={{0,5},{1,4},{2,7},{3,6},{4,1},{5,0},{6,3},{7,2},{8,13},{9,12},{10,... | collective-permute-start | bytes 589832 | tf_op jit(solution)/shard_map/ppermute | solution.py:331
  61.8 5.0 %collective-permute-done.15.refs_1_ = bf16[128,768]{1,0:T(8,128)(2,1)S(1)} collective-permute-done((bf16[128,768]{1,0:T(8,128)(2,1)S(1)}, bf16[128,768]{1,0:T(8,128)(2,1)S(1)}, u32[]{:S(2)}, u32[]{:S(2)}) %collective-permute-start.15) | collective-permute-done | bytes 196640 | tf_op jit(solution)/shard_map/ppermute | solution.py:331
  66.7 7.8 %collective-permute-done.16.refs_2_ = bf16[128,768]{1,0:T(8,128)(2,1)S(1)} collective-permute-done((bf16[128,768]{1,0:T(8,128)(2,1)S(1)}, bf16[128,768]{1,0:T(8,128)(2,1)S(1)}, u32[]{:S(2)}, u32[]{:S(2)}) %collective-permute-start.16) | collective-permute-done | bytes 196640 | tf_op jit(solution)/shard_map/ppermute | solution.py:331
  74.6 5.1 %collective-permute-done.17.refs_3_ = bf16[128,768]{1,0:T(8,128)(2,1)S(1)} collective-permute-done((bf16[128,768]{1,0:T(8,128)(2,1)S(1)}, bf16[128,768]{1,0:T(8,128)(2,1)S(1)}, u32[]{:S(2)}, u32[]{:S(2)}) %collective-permute-start.17) | collective-permute-done | bytes 196640 | tf_op jit(solution)/shard_map/ppermute | solution.py:331
  (28 shorter events, 8.4 us)
Async XLA Ops:
  2.0 12.5 %collective-permute-start = (bf16[1040,128]{1,0:T(8,128)(2,1)S(1)}, bf16[1040,128]{1,0:T(8,128)(2,1)S(1)}, u32[]{:S(2)}, u32[]{:S(2)}) collective-permute-start(bf16[1040,128]{1,0:T(8,128)(2,1)S(1)} %shard_state.2.refs_0_), channel_id=1, source_target_pairs={{0,8},{8,16},{16,24},{1,9},{9,17},{17,25},{2,10},{10,18},{18,26},{... | collective-permute-start | bytes 798728 | tf_op jit(solution)/shard_map/ppermute | solution.py:244
  7.1 10.0 %collective-permute-start.1 = (bf16[1040,128]{1,0:T(8,128)(2,1)S(1)}, bf16[1040,128]{1,0:T(8,128)(2,1)S(1)}, u32[]{:S(2)}, u32[]{:S(2)}) collective-permute-start(bf16[1040,128]{1,0:T(8,128)(2,1)S(1)} %shard_state.3), channel_id=1, source_target_pairs={{0,8},{8,16},{16,24},{1,9},{9,17},{17,25},{2,10},{10,18},{18,26},{... | collective-permute-start | bytes 798728 | tf_op jit(solution)/shard_map/ppermute | solution.py:244
  15.2 6.6 %collective-permute-start.2 = (bf16[128,1024]{1,0:T(8,128)(2,1)S(1)}, bf16[128,1024]{1,0:T(8,128)(2,1)S(1)}, u32[]{:S(2)}, u32[]{:S(2)}) collective-permute-start(bf16[128,1024]{1,0:T(8,128)(2,1)S(1)} %finish.2.refs_0_), channel_id=1, source_target_pairs={{0,16},{1,17},{2,18},{3,19},{4,20},{5,21},{6,22},{7,23},{8,24},{9,... | collective-permute-start | bytes 786440 | tf_op jit(solution)/shard_map/ppermute | solution.py:331
  15.3 7.4 %collective-permute-start.4 = (bf16[128,1024]{1,0:T(8,128)(2,1)S(1)}, bf16[128,1024]{1,0:T(8,128)(2,1)S(1)}, u32[]{:S(2)}, u32[]{:S(2)}) collective-permute-start(bf16[128,1024]{1,0:T(8,128)(2,1)S(1)} %finish.2.refs_0_), channel_id=1, source_target_pairs={{0,8},{1,9},{2,10},{3,11},{4,12},{5,13},{6,14},{7,15},{8,0},{9,1},... | collective-permute-start | bytes 786440 | tf_op jit(solution)/shard_map/ppermute | solution.py:331
  17.9 9.6 %collective-permute-start.6 = (bf16[128,1024]{1,0:T(8,128)(2,1)S(1)}, bf16[128,1024]{1,0:T(8,128)(2,1)S(1)}, u32[]{:S(2)}, u32[]{:S(2)}) collective-permute-start(bf16[128,1024]{1,0:T(8,128)(2,1)S(1)} %finish.3.refs_1_), channel_id=1, source_target_pairs={{0,16},{1,17},{2,18},{3,19},{4,20},{5,21},{6,22},{7,23},{8,24},{9,... | collective-permute-start | bytes 786440 | tf_op jit(solution)/shard_map/ppermute | solution.py:331
  18.9 11.1 %collective-permute-start.5 = (bf16[128,1024]{1,0:T(8,128)(2,1)S(1)}, bf16[128,1024]{1,0:T(8,128)(2,1)S(1)}, u32[]{:S(2)}, u32[]{:S(2)}) collective-permute-start(bf16[128,1024]{1,0:T(8,128)(2,1)S(1)} %finish.3.refs_1_), channel_id=1, source_target_pairs={{0,8},{1,9},{2,10},{3,11},{4,12},{5,13},{6,14},{7,15},{8,0},{9,1},... | collective-permute-start | bytes 786440 | tf_op jit(solution)/shard_map/ppermute | solution.py:331
  22.5 7.5 %collective-permute-start.3 = (bf16[1,128,768]{2,1,0:T(8,128)(2,1)S(1)}, bf16[1,128,768]{2,1,0:T(8,128)(2,1)S(1)}, u32[]{:S(2)}, u32[]{:S(2)}) collective-permute-start(bf16[1,128,768]{2,1,0:T(8,128)(2,1)S(1)} %project.7), channel_id=1, source_target_pairs={{0,2},{1,3},{2,0},{3,1},{4,6},{5,7},{6,4},{7,5},{8,10},{9,11},{10,... | collective-permute-start | bytes 589832 | tf_op jit(solution)/shard_map/ppermute | solution.py:331
  22.7 10.4 %collective-permute-start.10 = (bf16[128,1024]{1,0:T(8,128)(2,1)S(1)}, bf16[128,1024]{1,0:T(8,128)(2,1)S(1)}, u32[]{:S(2)}, u32[]{:S(2)}) collective-permute-start(bf16[128,1024]{1,0:T(8,128)(2,1)S(1)} %collective-permute-done.4.refs_0_), channel_id=1, source_target_pairs={{0,16},{1,17},{2,18},{3,19},{4,20},{5,21},{6,22},{7,23},{8,24},{9,... | collective-permute-start | bytes 786440 | tf_op jit(solution)/shard_map/ppermute | solution.py:331
  27.5 5.9 %collective-permute-start.11 = (bf16[128,1024]{1,0:T(8,128)(2,1)S(1)}, bf16[128,1024]{1,0:T(8,128)(2,1)S(1)}, u32[]{:S(2)}, u32[]{:S(2)}) collective-permute-start(bf16[128,1024]{1,0:T(8,128)(2,1)S(1)} %collective-permute-done.6.refs_3_), channel_id=1, source_target_pairs={{0,8},{1,9},{2,10},{3,11},{4,12},{5,13},{6,14},{7,15},{8,0},{9,1},... | collective-permute-start | bytes 786440 | tf_op jit(solution)/shard_map/ppermute | solution.py:331
  31.0 8.4 %collective-permute-start.7 = (bf16[2,128,768]{2,1,0:T(8,128)(2,1)S(1)}, bf16[2,128,768]{2,1,0:T(8,128)(2,1)S(1)}, u32[]{:S(2)}, u32[]{:S(2)}) collective-permute-start(bf16[2,128,768]{2,1,0:T(8,128)(2,1)S(1)} %project.9), channel_id=1, source_target_pairs={{0,2},{1,3},{2,0},{3,1},{4,6},{5,7},{6,4},{7,5},{8,10},{9,11},{10,... | collective-permute-start | bytes 1179656 | tf_op jit(solution)/shard_map/ppermute | solution.py:331
  34.0 9.6 %collective-permute-start.12 = (bf16[1,128,768]{2,1,0:T(8,128)(2,1)S(1)}, bf16[1,128,768]{2,1,0:T(8,128)(2,1)S(1)}, u32[]{:S(2)}, u32[]{:S(2)}) collective-permute-start(bf16[1,128,768]{2,1,0:T(8,128)(2,1)S(1)} %project.11), channel_id=1, source_target_pairs={{0,2},{1,3},{2,0},{3,1},{4,6},{5,7},{6,4},{7,5},{8,10},{9,11},{10,... | collective-permute-start | bytes 589832 | tf_op jit(solution)/shard_map/ppermute | solution.py:331
  39.5 9.1 %collective-permute-start.9 = (bf16[128,768]{1,0:T(8,128)(2,1)S(1)}, bf16[128,768]{1,0:T(8,128)(2,1)S(1)}, u32[]{:S(2)}, u32[]{:S(2)}) collective-permute-start(bf16[128,768]{1,0:T(8,128)(2,1)S(1)} %get-tuple-element.24), channel_id=1, source_target_pairs={{0,16},{1,17},{2,18},{3,19},{4,20},{5,21},{6,22},{7,23},{8,24},{9,... | collective-permute-start | bytes 589832 | tf_op jit(solution)/shard_map/ppermute | solution.py:331
  43.7 6.3 %collective-permute-start.13 = (bf16[128,768]{1,0:T(8,128)(2,1)S(1)}, bf16[128,768]{1,0:T(8,128)(2,1)S(1)}, u32[]{:S(2)}, u32[]{:S(2)}) collective-permute-start(bf16[128,768]{1,0:T(8,128)(2,1)S(1)} %merge.5), channel_id=1, source_target_pairs={{0,24},{1,25},{2,26},{3,27},{4,28},{5,29},{6,30},{7,31},{8,16},{9,... | collective-permute-start | bytes 589832 | tf_op jit(solution)/shard_map/ppermute | solution.py:331
  46.8 8.9 %collective-permute-start.8 = (bf16[128,768]{1,0:T(8,128)(2,1)S(1)}, bf16[128,768]{1,0:T(8,128)(2,1)S(1)}, u32[]{:S(2)}, u32[]{:S(2)}) collective-permute-start(bf16[128,768]{1,0:T(8,128)(2,1)S(1)} %get-tuple-element.23.refs_0_), channel_id=1, source_target_pairs={{0,8},{1,9},{2,10},{3,11},{4,12},{5,13},{6,14},{7,15},{8,0},{9,1},... | collective-permute-start | bytes 589832 | tf_op jit(solution)/shard_map/ppermute | solution.py:331
  55.8 5.9 %collective-permute-start.14 = (bf16[128,768]{1,0:T(8,128)(2,1)S(1)}, bf16[128,768]{1,0:T(8,128)(2,1)S(1)}, u32[]{:S(2)}, u32[]{:S(2)}) collective-permute-start(bf16[128,768]{1,0:T(8,128)(2,1)S(1)} %get-tuple-element.25), channel_id=1, source_target_pairs={{0,1},{1,0},{2,3},{3,2},{4,5},{5,4},{6,7},{7,6},{8,9},{9,8},{10,11... | collective-permute-start | bytes 589832 | tf_op jit(solution)/shard_map/ppermute | solution.py:331
  58.9 7.9 %collective-permute-start.15 = (bf16[128,768]{1,0:T(8,128)(2,1)S(1)}, bf16[128,768]{1,0:T(8,128)(2,1)S(1)}, u32[]{:S(2)}, u32[]{:S(2)}) collective-permute-start(bf16[128,768]{1,0:T(8,128)(2,1)S(1)} %get-tuple-element.26), channel_id=1, source_target_pairs={{0,3},{1,2},{2,1},{3,0},{4,7},{5,6},{6,5},{7,4},{8,11},{9,10},{10,... | collective-permute-start | bytes 589832 | tf_op jit(solution)/shard_map/ppermute | solution.py:331
  59.0 15.6 %collective-permute-start.16 = (bf16[128,768]{1,0:T(8,128)(2,1)S(1)}, bf16[128,768]{1,0:T(8,128)(2,1)S(1)}, u32[]{:S(2)}, u32[]{:S(2)}) collective-permute-start(bf16[128,768]{1,0:T(8,128)(2,1)S(1)} %get-tuple-element.27), channel_id=1, source_target_pairs={{0,5},{1,4},{2,7},{3,6},{4,1},{5,0},{6,3},{7,2},{8,13},{9,12},{10,... | collective-permute-start | bytes 589832 | tf_op jit(solution)/shard_map/ppermute | solution.py:331
  61.6 18.1 %collective-permute-start.17 = (bf16[128,768]{1,0:T(8,128)(2,1)S(1)}, bf16[128,768]{1,0:T(8,128)(2,1)S(1)}, u32[]{:S(2)}, u32[]{:S(2)}) collective-permute-start(bf16[128,768]{1,0:T(8,128)(2,1)S(1)} %get-tuple-element.28), channel_id=1, source_target_pairs={{0,7},{1,6},{2,5},{3,4},{4,3},{5,2},{6,1},{7,0},{8,15},{9,14},{10,... | collective-permute-start | bytes 589832 | tf_op jit(solution)/shard_map/ppermute | solution.py:331

commit v2 on v1

--- a/solution.py
+++ b/solution.py
@@ -185,6 +185,10 @@
             out_ref[j, :, start : start + wide] = result[j * rows : (j + 1) * rows]
 
 
+def hold_kernel(source_ref, after_ref, out_ref):
+    out_ref[...] = source_ref[...]
+
+
 def merge_kernel(keep_ref, arrived_ref, *refs):
     for i, out_ref in enumerate(refs[-keep_ref.shape[0] :]):
         total = keep_ref[i].astype(jnp.float32) + arrived_ref[i].astype(jnp.float32)
@@ -207,7 +211,7 @@
     wide = refs[0].shape[1]
     for m in range(2):
         total = refs[m][...].astype(jnp.float32) + refs[m + 2][...].astype(jnp.float32)
-        half = (lax.axis_index("head") & 1) ^ m
+        half = (lax.axis_index("head") & 1) ^ 1 ^ m
         out_ref[0, :, pl.ds(pl.multiple_of(half * wide, wide), wide)] = total.astype(jnp.bfloat16)
 
 
@@ -336,8 +340,11 @@
     pieces = []
     for i in range(sides):
         own = finish(i, ())
-        one, two = swapped(own, 1), swapped(own, 2)
-        pieces.append([own, one, two, swapped(two, 1) if i % 2 else swapped(one, 2)])
+        pieces.append([own, swapped(own, 1), swapped(own, 2)])
+    block = jax.ShapeDtypeStruct((rows, wide), jnp.bfloat16)
+    held = call(hold_kernel, block, "hold", in_specs=[VMEM, ANY])(pieces[0][1], pieces[1][2])
+    pieces[1].append(swapped(pieces[1][2], 1))
+    pieces[0].append(swapped(held, 2))
 
     part = columns // 2
     single = jax.ShapeDtypeStruct((rows, part), jnp.bfloat16)
@@ -363,7 +370,7 @@
         after = (blocks[0],)
     picked = call(pick_kernel, (single,) * n_head, "pick")(*blocks)
     arrived = [
-        moved(block, lambda i, j, s, m=m: (i, j ^ m, 1 - s)) for m, block in enumerate(picked)
+        moved(picked[m], lambda i, j, s, m=m: (i, j ^ m, 1 - s)) for m in reversed(range(n_head))
     ]
     out = jax.ShapeDtypeStruct((1, rows, columns), jnp.bfloat16)
     return call(last_kernel, out, "last")(*arrived)

time: 80.8 us -> 81.4 us (level)
  the two profiles are of different devices: /device:TPU:11 before, /device:TPU:0 now
where the time goes in v2:
time: 81.4 us; the launch traced here: 81.1 us
  waiting for transfers between devices  37.3 us (46%)
  starting transfers between devices  28.3 us (35%)
  Pallas kernels  15.3 us (19%)
    ppermute x16, waiting for transfers between devices, moved(): lax.ppermute(array, names, [(place[spot], place[target(*spot)]) for spot...  37.3 us
    ppermute x16, starting transfers between devices, moved(): lax.ppermute(array, names, [(place[spot], place[target(*spot)]) for spot...  20.1 us
    ppermute x2, starting transfers between devices, from_before(): return lax.ppermute(array, 'ctx', [(i, i + by) for i in range(n_ctx - by)])  8.26 us
    pallas_call x6, Pallas kernels, project(): call(kernel, shape, 'project', in_specs=specs)(*operands, weight, *after)  4.41 us
    pallas_call x1, Pallas kernels, on_device(): call(inside_kernel, (pltpu.VMEM((rows, width), jnp.float32), pltpu.VMEM((...  4.23 us
    pallas_call x2, Pallas kernels, state_of(): call(functools.partial(state_kernel, first), jax.ShapeDtypeStruct((wide +...  3.95 us
  transfers between devices with their start and end apart: 18, of which 11 were waited for; matrix products, arithmetic and copies ran while one was open for 0% of the time, Pallas kernels for 15%

profile of v2, /device:TPU:0, one launch (start us, length us, event | category | flops | bytes accessed | tf_op | source)
XLA Modules:
  0.0 81.1 jit_solution(8514089448340640687)
XLA Ops:
  0.0 2.0 %shard_state.2.refs_0_ = bf16[1040,128]{1,0:T(8,128)(2,1)S(1)} custom-call(bf16[1,128,2048]{2,1,0:T(8,128)(2,1)} %key_hbm.5, bf16[1,128,2048]{2,1,0:T(8,128)(2,1)} %value_hbm.5, f32[1,16,128]{2,1,0:T(8,128)} %bitcast.1, s32[1,128]{1,0:T(1,128)} %doc_hbm.5), custom_call_target="tpu_custom_call" | custom-call | flops 1 | bytes 1 | tf_op jit(solution)/shard_map/shard_state/pallas_call | solution.py:252
  2.0 4.9 %collective-permute-start = (bf16[1040,128]{1,0:T(8,128)(2,1)S(1)}, bf16[1040,128]{1,0:T(8,128)(2,1)S(1)}, u32[]{:S(2)}, u32[]{:S(2)}) collective-permute-start(bf16[1040,128]{1,0:T(8,128)(2,1)S(1)} %shard_state.2.refs_0_), channel_id=1, source_target_pairs={{0,8},{8,16},{16,24},{1,9},{9,17},{17,25},{2,10},{10,18},{18,26},{... | collective-permute-start | bytes 798728 | tf_op jit(solution)/shard_map/ppermute | solution.py:248
  6.8 2.0 %shard_state.3 = bf16[1040,128]{1,0:T(8,128)(2,1)S(1)} custom-call(bf16[1,128,2048]{2,1,0:T(8,128)(2,1)} %key_hbm.5, bf16[1,128,2048]{2,1,0:T(8,128)(2,1)} %value_hbm.5, f32[1,16,128]{2,1,0:T(8,128)} %bitcast.2, s32[1,128]{1,0:T(1,128)} %doc_hbm.5, bf16[1040,128]{1,0:T(8,128)(2,1)S(1)} %shard_state.2.refs_0_), custom_call_target="tpu_custom_call" | custom-call | flops 1 | bytes 1 | tf_op jit(solution)/shard_map/shard_state/pallas_call | solution.py:252
  8.8 3.4 %collective-permute-start.1 = (bf16[1040,128]{1,0:T(8,128)(2,1)S(1)}, bf16[1040,128]{1,0:T(8,128)(2,1)S(1)}, u32[]{:S(2)}, u32[]{:S(2)}) collective-permute-start(bf16[1040,128]{1,0:T(8,128)(2,1)S(1)} %shard_state.3), channel_id=1, source_target_pairs={{0,8},{8,16},{16,24},{1,9},{9,17},{17,25},{2,10},{10,18},{18,26},{... | collective-permute-start | bytes 798728 | tf_op jit(solution)/shard_map/ppermute | solution.py:248
  12.2 4.2 %inside.1 = (f32[128,2048]{1,0:T(8,128)S(1)}, f32[128,2048]{1,0:T(8,128)S(1)}, f32[128,16]{1,0:T(8,128)S(1)}, f32[128,128]{1,0:T(8,128)S(1)}, bf16[128,2048]{1,0...) custom-call(bf16[1,128,2048]{2,1,0:T(8,128)(2,1)} %query_hbm.1, bf16[1,128,2048]{2,1,0:T(8,128)(2,1)} %key_hbm.5, ...), custom_call_target="tpu_custom_call" | custom-call | flops 1 | bytes 1 | tf_op jit(solution)/shard_map/inside/pallas_call | solution.py:289
  17.4 1.5 %collective-permute-start.4 = (bf16[128,1024]{1,0:T(8,128)(2,1)S(1)}, bf16[128,1024]{1,0:T(8,128)(2,1)S(1)}, u32[]{:S(2)}, u32[]{:S(2)}) collective-permute-start(bf16[128,1024]{1,0:T(8,128)(2,1)S(1)} %finish.2.refs_0_), channel_id=1, source_target_pairs={{0,8},{1,9},{2,10},{3,11},{4,12},{5,13},{6,14},{7,15},{8,0},{9,1},... | collective-permute-start | bytes 786440 | tf_op jit(solution)/shard_map/ppermute | solution.py:335
  19.7 3.5 %collective-permute-start.6 = (bf16[128,1024]{1,0:T(8,128)(2,1)S(1)}, bf16[128,1024]{1,0:T(8,128)(2,1)S(1)}, u32[]{:S(2)}, u32[]{:S(2)}) collective-permute-start(bf16[128,1024]{1,0:T(8,128)(2,1)S(1)} %finish.3.refs_1_), channel_id=1, source_target_pairs={{0,16},{1,17},{2,18},{3,19},{4,20},{5,21},{6,22},{7,23},{8,24},{9,... | collective-permute-start | bytes 786440 | tf_op jit(solution)/shard_map/ppermute | solution.py:335
  23.2 3.4 %collective-permute-done.2.refs_3_.refs_2_ = bf16[128,1024]{1,0:T(8,128)(2,1)S(1)} collective-permute-done((bf16[128,1024]{1,0:T(8,128)(2,1)S(1)}, bf16[128,1024]{1,0:T(8,128)(2,1)S(1)}, u32[]{:S(2)}, u32[]{:S(2)}) %collective-permute-start.2) | collective-permute-done | bytes 262176 | tf_op jit(solution)/shard_map/ppermute | solution.py:335
  27.2 1.6 %collective-permute-start.3 = (bf16[1,128,768]{2,1,0:T(8,128)(2,1)S(1)}, bf16[1,128,768]{2,1,0:T(8,128)(2,1)S(1)}, u32[]{:S(2)}, u32[]{:S(2)}) collective-permute-start(bf16[1,128,768]{2,1,0:T(8,128)(2,1)S(1)} %project.7), channel_id=1, source_target_pairs={{0,2},{1,3},{2,0},{3,1},{4,6},{5,7},{6,4},{7,5},{8,10},{9,11},{10,... | collective-permute-start | bytes 589832 | tf_op jit(solution)/shard_map/ppermute | solution.py:335
  28.8 1.6 %collective-permute-done.6.refs_3_.after_ref = bf16[128,1024]{1,0:T(8,128)(2,1)S(1)} collective-permute-done((bf16[128,1024]{1,0:T(8,128)(2,1)S(1)}, bf16[128,1024]{1,0:T(8,128)(2,1)S(1)}, u32[]{:S(2)}, u32[]{:S(2)}) %collective-permute-start.6) | collective-permute-done | bytes 262176 | tf_op jit(solution)/shard_map/ppermute | solution.py:335
  30.5 2.4 %collective-permute-start.10 = (bf16[128,1024]{1,0:T(8,128)(2,1)S(1)}, bf16[128,1024]{1,0:T(8,128)(2,1)S(1)}, u32[]{:S(2)}, u32[]{:S(2)}) collective-permute-start(bf16[128,1024]{1,0:T(8,128)(2,1)S(1)} %hold.1), channel_id=1, source_target_pairs={{0,16},{1,17},{2,18},{3,19},{4,20},{5,21},{6,22},{7,23},{8,24},{9,... | collective-permute-start | bytes 786440 | tf_op jit(solution)/shard_map/ppermute | solution.py:335
  34.6 1.6 %collective-permute-start.7 = (bf16[2,128,768]{2,1,0:T(8,128)(2,1)S(1)}, bf16[2,128,768]{2,1,0:T(8,128)(2,1)S(1)}, u32[]{:S(2)}, u32[]{:S(2)}) collective-permute-start(bf16[2,128,768]{2,1,0:T(8,128)(2,1)S(1)} %project.9), channel_id=1, source_target_pairs={{0,2},{1,3},{2,0},{3,1},{4,6},{5,7},{6,4},{7,5},{8,10},{9,11},{10,... | collective-permute-start | bytes 1179656 | tf_op jit(solution)/shard_map/ppermute | solution.py:335
  36.2 3.1 %collective-permute-done.10.refs_0_ = bf16[128,1024]{1,0:T(8,128)(2,1)S(1)} collective-permute-done((bf16[128,1024]{1,0:T(8,128)(2,1)S(1)}, bf16[128,1024]{1,0:T(8,128)(2,1)S(1)}, u32[]{:S(2)}, u32[]{:S(2)}) %collective-permute-start.10) | collective-permute-done | bytes 262176 | tf_op jit(solution)/shard_map/ppermute | solution.py:335
  39.4 1.5 %collective-permute-done.11.refs_1_ = bf16[128,1024]{1,0:T(8,128)(2,1)S(1)} collective-permute-done((bf16[128,1024]{1,0:T(8,128)(2,1)S(1)}, bf16[128,1024]{1,0:T(8,128)(2,1)S(1)}, u32[]{:S(2)}, u32[]{:S(2)}) %collective-permute-start.11) | collective-permute-done | bytes 262176 | tf_op jit(solution)/shard_map/ppermute | solution.py:335
  41.5 1.6 %collective-permute-start.12 = (bf16[1,128,768]{2,1,0:T(8,128)(2,1)S(1)}, bf16[1,128,768]{2,1,0:T(8,128)(2,1)S(1)}, u32[]{:S(2)}, u32[]{:S(2)}) collective-permute-start(bf16[1,128,768]{2,1,0:T(8,128)(2,1)S(1)} %project.11), channel_id=1, source_target_pairs={{0,2},{1,3},{2,0},{3,1},{4,6},{5,7},{6,4},{7,5},{8,10},{9,11},{10,... | collective-permute-start | bytes 589832 | tf_op jit(solution)/shard_map/ppermute | solution.py:335
  44.7 2.0 %collective-permute-done.7.arrived_ref = bf16[2,128,768]{2,1,0:T(8,128)(2,1)S(1)} collective-permute-done((bf16[2,128,768]{2,1,0:T(8,128)(2,1)S(1)}, bf16[2,128,768]{2,1,0:T(8,128)(2,1)S(1)}, u32[]{:S(2)}, u32[]{:S(2)}) %collective-permute-start.7) | collective-permute-done | bytes 393248 | tf_op jit(solution)/shard_map/ppermute | solution.py:335
  46.8 1.3 %collective-permute-start.9 = (bf16[128,768]{1,0:T(8,128)(2,1)S(1)}, bf16[128,768]{1,0:T(8,128)(2,1)S(1)}, u32[]{:S(2)}, u32[]{:S(2)}) collective-permute-start(bf16[128,768]{1,0:T(8,128)(2,1)S(1)} %get-tuple-element.24), channel_id=1, source_target_pairs={{0,16},{1,17},{2,18},{3,19},{4,20},{5,21},{6,22},{7,23},{8,24},{9,... | collective-permute-start | bytes 589832 | tf_op jit(solution)/shard_map/ppermute | solution.py:335
  48.1 1.6 %collective-permute-done.12.arrived_ref = bf16[1,128,768]{2,1,0:T(8,128)(2,1)S(1)} collective-permute-done((bf16[1,128,768]{2,1,0:T(8,128)(2,1)S(1)}, bf16[1,128,768]{2,1,0:T(8,128)(2,1)S(1)}, u32[]{:S(2)}, u32[]{:S(2)}) %collective-permute-start.12) | collective-permute-done | bytes 196640 | tf_op jit(solution)/shard_map/ppermute | solution.py:335
  49.7 1.6 %collective-permute-start.13 = (bf16[128,768]{1,0:T(8,128)(2,1)S(1)}, bf16[128,768]{1,0:T(8,128)(2,1)S(1)}, u32[]{:S(2)}, u32[]{:S(2)}) collective-permute-start(bf16[128,768]{1,0:T(8,128)(2,1)S(1)} %merge.5), channel_id=1, source_target_pairs={{0,24},{1,25},{2,26},{3,27},{4,28},{5,29},{6,30},{7,31},{8,16},{9,... | collective-permute-start | bytes 589832 | tf_op jit(solution)/shard_map/ppermute | solution.py:335
  51.7 3.2 %collective-permute-done.9.refs_2_ = bf16[128,768]{1,0:T(8,128)(2,1)S(1)} collective-permute-done((bf16[128,768]{1,0:T(8,128)(2,1)S(1)}, bf16[128,768]{1,0:T(8,128)(2,1)S(1)}, u32[]{:S(2)}, u32[]{:S(2)}) %collective-permute-start.9) | collective-permute-done | bytes 196640 | tf_op jit(solution)/shard_map/ppermute | solution.py:335
  55.0 3.5 %collective-permute-done.13.refs_3_ = bf16[128,768]{1,0:T(8,128)(2,1)S(1)} collective-permute-done((bf16[128,768]{1,0:T(8,128)(2,1)S(1)}, bf16[128,768]{1,0:T(8,128)(2,1)S(1)}, u32[]{:S(2)}, u32[]{:S(2)}) %collective-permute-start.13) | collective-permute-done | bytes 196640 | tf_op jit(solution)/shard_map/ppermute | solution.py:335
  60.5 1.8 %collective-permute-start.15 = (bf16[128,768]{1,0:T(8,128)(2,1)S(1)}, bf16[128,768]{1,0:T(8,128)(2,1)S(1)}, u32[]{:S(2)}, u32[]{:S(2)}) collective-permute-start(bf16[128,768]{1,0:T(8,128)(2,1)S(1)} %get-tuple-element.26), channel_id=1, source_target_pairs={{0,5},{1,4},{2,7},{3,6},{4,1},{5,0},{6,3},{7,2},{8,13},{9,12},{10,... | collective-permute-start | bytes 589832 | tf_op jit(solution)/shard_map/ppermute | solution.py:335
  63.8 4.6 %collective-permute-done.14.refs_0_ = bf16[128,768]{1,0:T(8,128)(2,1)S(1)} collective-permute-done((bf16[128,768]{1,0:T(8,128)(2,1)S(1)}, bf16[128,768]{1,0:T(8,128)(2,1)S(1)}, u32[]{:S(2)}, u32[]{:S(2)}) %collective-permute-start.14) | collective-permute-done | bytes 196640 | tf_op jit(solution)/shard_map/ppermute | solution.py:335
  68.4 11.9 %collective-permute-done.15.refs_1_ = bf16[128,768]{1,0:T(8,128)(2,1)S(1)} collective-permute-done((bf16[128,768]{1,0:T(8,128)(2,1)S(1)}, bf16[128,768]{1,0:T(8,128)(2,1)S(1)}, u32[]{:S(2)}, u32[]{:S(2)}) %collective-permute-start.15) | collective-permute-done | bytes 196640 | tf_op jit(solution)/shard_map/ppermute | solution.py:335
  (29 shorter events, 11.0 us)
Async XLA Ops:
  2.0 14.5 %collective-permute-start = (bf16[1040,128]{1,0:T(8,128)(2,1)S(1)}, bf16[1040,128]{1,0:T(8,128)(2,1)S(1)}, u32[]{:S(2)}, u32[]{:S(2)}) collective-permute-start(bf16[1040,128]{1,0:T(8,128)(2,1)S(1)} %shard_state.2.refs_0_), channel_id=1, source_target_pairs={{0,8},{8,16},{16,24},{1,9},{9,17},{17,25},{2,10},{10,18},{18,26},{... | collective-permute-start | bytes 798728 | tf_op jit(solution)/shard_map/ppermute | solution.py:248
  8.8 10.1 %collective-permute-start.1 = (bf16[1040,128]{1,0:T(8,128)(2,1)S(1)}, bf16[1040,128]{1,0:T(8,128)(2,1)S(1)}, u32[]{:S(2)}, u32[]{:S(2)}) collective-permute-start(bf16[1040,128]{1,0:T(8,128)(2,1)S(1)} %shard_state.3), channel_id=1, source_target_pairs={{0,8},{8,16},{16,24},{1,9},{9,17},{17,25},{2,10},{10,18},{18,26},{... | collective-permute-start | bytes 798728 | tf_op jit(solution)/shard_map/ppermute | solution.py:248
  17.3 9.3 %collective-permute-start.2 = (bf16[128,1024]{1,0:T(8,128)(2,1)S(1)}, bf16[128,1024]{1,0:T(8,128)(2,1)S(1)}, u32[]{:S(2)}, u32[]{:S(2)}) collective-permute-start(bf16[128,1024]{1,0:T(8,128)(2,1)S(1)} %finish.2.refs_0_), channel_id=1, source_target_pairs={{0,16},{1,17},{2,18},{3,19},{4,20},{5,21},{6,22},{7,23},{8,24},{9,... | collective-permute-start | bytes 786440 | tf_op jit(solution)/shard_map/ppermute | solution.py:335
  17.4 11.5 %collective-permute-start.4 = (bf16[128,1024]{1,0:T(8,128)(2,1)S(1)}, bf16[128,1024]{1,0:T(8,128)(2,1)S(1)}, u32[]{:S(2)}, u32[]{:S(2)}) collective-permute-start(bf16[128,1024]{1,0:T(8,128)(2,1)S(1)} %finish.2.refs_0_), channel_id=1, source_target_pairs={{0,8},{1,9},{2,10},{3,11},{4,12},{5,13},{6,14},{7,15},{8,0},{9,1},... | collective-permute-start | bytes 786440 | tf_op jit(solution)/shard_map/ppermute | solution.py:335
  19.7 10.8 %collective-permute-start.6 = (bf16[128,1024]{1,0:T(8,128)(2,1)S(1)}, bf16[128,1024]{1,0:T(8,128)(2,1)S(1)}, u32[]{:S(2)}, u32[]{:S(2)}) collective-permute-start(bf16[128,1024]{1,0:T(8,128)(2,1)S(1)} %finish.3.refs_1_), channel_id=1, source_target_pairs={{0,16},{1,17},{2,18},{3,19},{4,20},{5,21},{6,22},{7,23},{8,24},{9,... | collective-permute-start | bytes 786440 | tf_op jit(solution)/shard_map/ppermute | solution.py:335
  23.2 10.4 %collective-permute-start.5 = (bf16[128,1024]{1,0:T(8,128)(2,1)S(1)}, bf16[128,1024]{1,0:T(8,128)(2,1)S(1)}, u32[]{:S(2)}, u32[]{:S(2)}) collective-permute-start(bf16[128,1024]{1,0:T(8,128)(2,1)S(1)} %finish.3.refs_1_), channel_id=1, source_target_pairs={{0,8},{1,9},{2,10},{3,11},{4,12},{5,13},{6,14},{7,15},{8,0},{9,1},... | collective-permute-start | bytes 786440 | tf_op jit(solution)/shard_map/ppermute | solution.py:335
  27.2 6.3 %collective-permute-start.3 = (bf16[1,128,768]{2,1,0:T(8,128)(2,1)S(1)}, bf16[1,128,768]{2,1,0:T(8,128)(2,1)S(1)}, u32[]{:S(2)}, u32[]{:S(2)}) collective-permute-start(bf16[1,128,768]{2,1,0:T(8,128)(2,1)S(1)} %project.7), channel_id=1, source_target_pairs={{0,2},{1,3},{2,0},{3,1},{4,6},{5,7},{6,4},{7,5},{8,10},{9,11},{10,... | collective-permute-start | bytes 589832 | tf_op jit(solution)/shard_map/ppermute | solution.py:335
  30.5 8.9 %collective-permute-start.10 = (bf16[128,1024]{1,0:T(8,128)(2,1)S(1)}, bf16[128,1024]{1,0:T(8,128)(2,1)S(1)}, u32[]{:S(2)}, u32[]{:S(2)}) collective-permute-start(bf16[128,1024]{1,0:T(8,128)(2,1)S(1)} %hold.1), channel_id=1, source_target_pairs={{0,16},{1,17},{2,18},{3,19},{4,20},{5,21},{6,22},{7,23},{8,24},{9,... | collective-permute-start | bytes 786440 | tf_op jit(solution)/shard_map/ppermute | solution.py:335
  32.9 7.9 %collective-permute-start.11 = (bf16[128,1024]{1,0:T(8,128)(2,1)S(1)}, bf16[128,1024]{1,0:T(8,128)(2,1)S(1)}, u32[]{:S(2)}, u32[]{:S(2)}) collective-permute-start(bf16[128,1024]{1,0:T(8,128)(2,1)S(1)} %collective-permute-done.6.refs_3_.after_ref), channel_id=1, source_target_pairs={{0,8},{1,9},{2,10},{3,11},{4,12},{5,13},{6,14},{7,15},{8,0},{9,1},... | collective-permute-start | bytes 786440 | tf_op jit(solution)/shard_map/ppermute | solution.py:335
  34.6 12.1 %collective-permute-start.7 = (bf16[2,128,768]{2,1,0:T(8,128)(2,1)S(1)}, bf16[2,128,768]{2,1,0:T(8,128)(2,1)S(1)}, u32[]{:S(2)}, u32[]{:S(2)}) collective-permute-start(bf16[2,128,768]{2,1,0:T(8,128)(2,1)S(1)} %project.9), channel_id=1, source_target_pairs={{0,2},{1,3},{2,0},{3,1},{4,6},{5,7},{6,4},{7,5},{8,10},{9,11},{10,... | collective-permute-start | bytes 1179656 | tf_op jit(solution)/shard_map/ppermute | solution.py:335
  41.5 8.2 %collective-permute-start.12 = (bf16[1,128,768]{2,1,0:T(8,128)(2,1)S(1)}, bf16[1,128,768]{2,1,0:T(8,128)(2,1)S(1)}, u32[]{:S(2)}, u32[]{:S(2)}) collective-permute-start(bf16[1,128,768]{2,1,0:T(8,128)(2,1)S(1)} %project.11), channel_id=1, source_target_pairs={{0,2},{1,3},{2,0},{3,1},{4,6},{5,7},{6,4},{7,5},{8,10},{9,11},{10,... | collective-permute-start | bytes 589832 | tf_op jit(solution)/shard_map/ppermute | solution.py:335
  46.8 8.2 %collective-permute-start.9 = (bf16[128,768]{1,0:T(8,128)(2,1)S(1)}, bf16[128,768]{1,0:T(8,128)(2,1)S(1)}, u32[]{:S(2)}, u32[]{:S(2)}) collective-permute-start(bf16[128,768]{1,0:T(8,128)(2,1)S(1)} %get-tuple-element.24), channel_id=1, source_target_pairs={{0,16},{1,17},{2,18},{3,19},{4,20},{5,21},{6,22},{7,23},{8,24},{9,... | collective-permute-start | bytes 589832 | tf_op jit(solution)/shard_map/ppermute | solution.py:335
  49.7 8.8 %collective-permute-start.13 = (bf16[128,768]{1,0:T(8,128)(2,1)S(1)}, bf16[128,768]{1,0:T(8,128)(2,1)S(1)}, u32[]{:S(2)}, u32[]{:S(2)}) collective-permute-start(bf16[128,768]{1,0:T(8,128)(2,1)S(1)} %merge.5), channel_id=1, source_target_pairs={{0,24},{1,25},{2,26},{3,27},{4,28},{5,29},{6,30},{7,31},{8,16},{9,... | collective-permute-start | bytes 589832 | tf_op jit(solution)/shard_map/ppermute | solution.py:335
  51.3 8.1 %collective-permute-start.8 = (bf16[128,768]{1,0:T(8,128)(2,1)S(1)}, bf16[128,768]{1,0:T(8,128)(2,1)S(1)}, u32[]{:S(2)}, u32[]{:S(2)}) collective-permute-start(bf16[128,768]{1,0:T(8,128)(2,1)S(1)} %get-tuple-element.23.refs_0_), channel_id=1, source_target_pairs={{0,8},{1,9},{2,10},{3,11},{4,12},{5,13},{6,14},{7,15},{8,0},{9,1},... | collective-permute-start | bytes 589832 | tf_op jit(solution)/shard_map/ppermute | solution.py:335
  59.5 8.9 %collective-permute-start.14 = (bf16[128,768]{1,0:T(8,128)(2,1)S(1)}, bf16[128,768]{1,0:T(8,128)(2,1)S(1)}, u32[]{:S(2)}, u32[]{:S(2)}) collective-permute-start(bf16[128,768]{1,0:T(8,128)(2,1)S(1)} %get-tuple-element.25), channel_id=1, source_target_pairs={{0,7},{1,6},{2,5},{3,4},{4,3},{5,2},{6,1},{7,0},{8,15},{9,14},{10,... | collective-permute-start | bytes 589832 | tf_op jit(solution)/shard_map/ppermute | solution.py:335
  60.5 19.8 %collective-permute-start.15 = (bf16[128,768]{1,0:T(8,128)(2,1)S(1)}, bf16[128,768]{1,0:T(8,128)(2,1)S(1)}, u32[]{:S(2)}, u32[]{:S(2)}) collective-permute-start(bf16[128,768]{1,0:T(8,128)(2,1)S(1)} %get-tuple-element.26), channel_id=1, source_target_pairs={{0,5},{1,4},{2,7},{3,6},{4,1},{5,0},{6,3},{7,2},{8,13},{9,12},{10,... | collective-permute-start | bytes 589832 | tf_op jit(solution)/shard_map/ppermute | solution.py:335
  62.3 18.0 %collective-permute-start.16 = (bf16[128,768]{1,0:T(8,128)(2,1)S(1)}, bf16[128,768]{1,0:T(8,128)(2,1)S(1)}, u32[]{:S(2)}, u32[]{:S(2)}) collective-permute-start(bf16[128,768]{1,0:T(8,128)(2,1)S(1)} %get-tuple-element.27), channel_id=1, source_target_pairs={{0,3},{1,2},{2,1},{3,0},{4,7},{5,6},{6,5},{7,4},{8,11},{9,10},{10,... | collective-permute-start | bytes 589832 | tf_op jit(solution)/shard_map/ppermute | solution.py:335
  63.5 16.8 %collective-permute-start.17 = (bf16[128,768]{1,0:T(8,128)(2,1)S(1)}, bf16[128,768]{1,0:T(8,128)(2,1)S(1)}, u32[]{:S(2)}, u32[]{:S(2)}) collective-permute-start(bf16[128,768]{1,0:T(8,128)(2,1)S(1)} %get-tuple-element.28), channel_id=1, source_target_pairs={{0,1},{1,0},{2,3},{3,2},{4,5},{5,4},{6,7},{7,6},{8,9},{9,8},{10,11... | collective-permute-start | bytes 589832 | tf_op jit(solution)/shard_map/ppermute | solution.py:335

commit v3 on v1

--- a/solution.py
+++ b/solution.py
@@ -32,8 +32,27 @@
     return columns, across
 
 
+def own_fading(doc, across, key_ref, value_ref, first, out_ref):
+    rows = doc.shape[1]
+    wide = out_ref.shape[0] - EXTRA
+    last_doc = doc[:, rows - 1 :]
+    fading = jnp.where(doc == last_doc, jnp.exp(across[:, rows - 1 :] - across), 0.0)
+    fading_columns = fading.T
+    out_ref[wide:, :] = jnp.broadcast_to(
+        (last_doc + 1).astype(jnp.float32), (EXTRA, DH)
+    ).astype(jnp.bfloat16)
+    for k in range(wide // DH):
+        h = first + k
+        span = slice(h * DH, (h + 1) * DH)
+        faded = (key_ref[:, span].astype(jnp.float32) * fading_columns[:, h : h + 1]).astype(
+            jnp.bfloat16
+        )
+        out_ref[k * DH : (k + 1) * DH, :] = dot(faded, value_ref[:, span], ((0,), (0,))).astype(
+            jnp.bfloat16
+        )
+
+
 def state_kernel(
-    first,
     key_hbm,
     value_hbm,
     rate_hbm,
@@ -43,7 +62,6 @@
     out_ref, key_ref, value_ref, rate_ref, doc_ref, sems, small = refs[-7:]
     rows = rate_ref.shape[1]
     wide = key_ref.shape[1]
-    heads = wide // DH
     parts = sems.shape[0]
     piece = wide // parts
     copies = [
@@ -52,15 +70,14 @@
     ]
     pieces = []
     for part in range(parts):
-        source = pl.ds(first * DH + part * piece, piece)
         span = pl.ds(part * piece, piece)
         pieces.append(
             [
                 pltpu.make_async_copy(
-                    key_hbm.at[0, :, source], key_ref.at[:, span], sems.at[part, 0]
+                    key_hbm.at[0, :, span], key_ref.at[:, span], sems.at[part, 0]
                 ),
                 pltpu.make_async_copy(
-                    value_hbm.at[0, :, source], value_ref.at[:, span], sems.at[part, 1]
+                    value_hbm.at[0, :, span], value_ref.at[:, span], sems.at[part, 1]
                 ),
             ]
         )
@@ -69,23 +86,10 @@
     for copy in copies:
         copy.wait()
     columns, across = running_sums(rate_ref[...])
-    doc = doc_ref[...]
-    last_doc = doc[:, rows - 1 :]
-    fading = jnp.where(doc == last_doc, jnp.exp(across[:, rows - 1 :] - across), 0.0)
-    fading_columns = fading.T
-    out_ref[wide:, :] = jnp.broadcast_to(
-        (last_doc + 1).astype(jnp.float32), (EXTRA, DH)
-    ).astype(jnp.bfloat16)
     for part in range(parts):
         for copy in pieces[part]:
             copy.wait()
-        for k in range(part * heads // parts, (part + 1) * heads // parts):
-            span = slice(k * DH, (k + 1) * DH)
-            h = first + k
-            faded = (key_ref[:, span].astype(jnp.float32) * fading_columns[:, h : h + 1]).astype(
-                jnp.bfloat16
-            )
-            out_ref[span, :] = dot(faded, value_ref[:, span], ((0,), (0,))).astype(jnp.bfloat16)
+    own_fading(doc_ref[...], across, key_ref, value_ref, 0, out_ref)
 
 
 def inside_kernel(
@@ -149,46 +153,49 @@
 
 
 def finish_kernel(
-    first, inside_ref, factor_ref, reach_ref, doc_ref, query_ref, state_ref, *refs
+    inside_ref, factor_ref, reach_ref, doc_ref, query_ref, state_ref, *out_refs
 ):
+    heads = reach_ref.shape[1]
+    part = out_refs[0].shape[0]
+    incoming = state_ref[heads * DH :, :].astype(jnp.float32)[0:1, :]
+    reached = (doc_ref[...] == incoming).astype(jnp.float32)
+    for h in range(heads):
+        span = slice(h * DH, (h + 1) * DH)
+        reaches = reach_ref[:, h : h + 1] * reached
+        attended = inside_ref[:, span] + reaches * dot(query_ref[:, span], state_ref[span, :])
+        scaling = lax.rsqrt(jnp.mean(attended * attended, axis=-1, keepdims=True) + 1e-06)
+        normed = (attended * scaling * factor_ref[:, span]).astype(jnp.bfloat16)
+        for i, out_ref in enumerate(out_refs):
+            out_ref[:, span] = normed[i * part : (i + 1) * part]
+
+
+def project_kernel(other, *refs):
     out_ref = refs[-1]
-    wide = out_ref.shape[1]
-    incoming = state_ref[wide:, :].astype(jnp.float32)[0:1, :]
-    reached = (doc_ref[...] == incoming).astype(jnp.float32)
-    for k in range(wide // DH):
-        h = first + k
-        span = slice(h * DH, (h + 1) * DH)
-        own = slice(k * DH, (k + 1) * DH)
-        reaches = reach_ref[:, h : h + 1] * reached
-        attended = inside_ref[:, span] + reaches * dot(query_ref[:, span], state_ref[own, :])
-        scaling = lax.rsqrt(jnp.mean(attended * attended, axis=-1, keepdims=True) + 1e-06)
-        out_ref[:, own] = (attended * scaling * factor_ref[:, span]).astype(jnp.bfloat16)
-
-
-def project_kernel(sides, other, *refs):
-    out_ref = refs[-1]
-    count = sides * out_ref.shape[0]
-    pieces, weight_ref = refs[:count], refs[count]
     blocks, rows, columns = out_ref.shape
+    pieces, weight_ref = refs[:blocks], refs[blocks]
     half = (lax.axis_index("head") & 1) ^ other
     wide = math.gcd(columns, 256)
-    depth = pieces[0].shape[1]
-    everything = [
-        jnp.concatenate([piece[...] for piece in pieces[i::sides]], axis=0) for i in range(sides)
-    ]
+    everything = jnp.concatenate([piece[...] for piece in pieces], axis=0)
     for start in range(0, columns, wide):
         span = pl.ds(pl.multiple_of(half * columns + start, wide), wide)
-        result = sum(
-            dot(everything[i], weight_ref[i * depth : (i + 1) * depth, span]) for i in range(sides)
-        ).astype(jnp.bfloat16)
+        result = dot(everything, weight_ref[:, span]).astype(jnp.bfloat16)
         for j in range(blocks):
             out_ref[j, :, start : start + wide] = result[j * rows : (j + 1) * rows]
 
 
-def merge_kernel(keep_ref, arrived_ref, *refs):
-    for i, out_ref in enumerate(refs[-keep_ref.shape[0] :]):
-        total = keep_ref[i].astype(jnp.float32) + arrived_ref[i].astype(jnp.float32)
-        out_ref[...] = total.astype(jnp.bfloat16)
+def hold_kernel(upper_ref, lower_ref, *refs):
+    for source_ref, out_ref in zip((upper_ref, lower_ref), refs[-2:]):
+        out_ref[...] = source_ref[...]
+
+
+def merge_kernel(layout, *refs):
+    out_refs = refs[-len(layout) :]
+    rows = refs[0].shape[1]
+    for out_ref, places in zip(out_refs, layout):
+        for i, (source, block) in enumerate(places):
+            keep_ref, arrived_ref = refs[2 * source], refs[2 * source + 1]
+            total = keep_ref[block].astype(jnp.float32) + arrived_ref[block].astype(jnp.float32)
+            out_ref[i * rows : (i + 1) * rows, :] = total.astype(jnp.bfloat16)
 
 
 def pick_kernel(*refs):
@@ -207,7 +214,7 @@
     wide = refs[0].shape[1]
     for m in range(2):
         total = refs[m][...].astype(jnp.float32) + refs[m + 2][...].astype(jnp.float32)
-        half = (lax.axis_index("head") & 1) ^ m
+        half = (lax.axis_index("head") & 1) ^ 1 ^ m
         out_ref[0, :, pl.ds(pl.multiple_of(half * wide, wide), wide)] = total.astype(jnp.bfloat16)
 
 
@@ -236,29 +243,28 @@
     queries, keys, values, gates = map(stay, (queries, keys, values, gates))
     segment_ids, norm_gain, out_weight = map(stay, (segment_ids, norm_gain, out_weight))
     columns = out_weight.shape[2]
-    sides = 2
-    side = heads // sides
-    wide = side * DH
+    side = heads
+    wide = width
 
     def from_before(array, by):
         return lax.ppermute(array, "ctx", [(i, i + by) for i in range(n_ctx - by)])
 
-    def state_of(first, after):
-        parts = 2 if side % 2 == 0 else 1
-        return call(
-            functools.partial(state_kernel, first),
-            jax.ShapeDtypeStruct((wide + EXTRA, DH), jnp.bfloat16),
-            "shard_state",
-            in_specs=[HBM] * 4 + [ANY] * len(after),
-            scratch_shapes=[
-                pltpu.VMEM((rows, wide), jnp.bfloat16),
-                pltpu.VMEM((rows, wide), jnp.bfloat16),
-                pltpu.VMEM((heads, rows), jnp.float32),
-                pltpu.VMEM((1, rows), jnp.int32),
-                pltpu.SemaphoreType.DMA((parts, 2)),
-                pltpu.SemaphoreType.DMA((2,)),
-            ],
-        )(keys, values, rates, segment_ids, *after)
+    parts = 4 if side % 4 == 0 else 1
+    state_shape = jax.ShapeDtypeStruct((wide + EXTRA, DH), jnp.bfloat16)
+    state = call(
+        state_kernel,
+        state_shape,
+        "shard_state",
+        in_specs=[HBM] * 4,
+        scratch_shapes=[
+            pltpu.VMEM((rows, wide), jnp.bfloat16),
+            pltpu.VMEM((rows, wide), jnp.bfloat16),
+            pltpu.VMEM((heads, rows), jnp.float32),
+            pltpu.VMEM((1, rows), jnp.int32),
+            pltpu.SemaphoreType.DMA((parts, 2)),
+            pltpu.SemaphoreType.DMA((2,)),
+        ],
+    )(keys, values, rates, segment_ids)
 
     def entering(state, first):
         incoming = from_before(state, 1)
@@ -276,11 +282,6 @@
             total = total.reshape(wide, DH).astype(jnp.bfloat16)
             incoming = jnp.concatenate([total, incoming[wide:]], axis=0)
         return incoming
-
-    states = []
-    for i in range(sides):
-        states.append(state_of(i * side, states))
-    incoming = [entering(state, i * side) for i, state in enumerate(states)]
 
     inside, factor, reach, docs, query, weight = call(
         inside_kernel,
@@ -304,18 +305,17 @@
             pltpu.SemaphoreType.DMA((8,)),
         ],
     )(queries, keys, values, gates, rates, segment_ids, norm_gain, out_weight)
-
-    def finish(i, after):
-        return call(
-            functools.partial(finish_kernel, i * side),
-            jax.ShapeDtypeStruct((rows, wide), jnp.bfloat16),
-            "finish",
-            in_specs=[VMEM] * 6 + [ANY] * len(after),
-        )(inside, factor, reach, docs, query, incoming[i], *after)
+    incoming = entering(state, 0)
+
+    part = rows // 2
+    normed = call(
+        finish_kernel,
+        (jax.ShapeDtypeStruct((part, width), jnp.bfloat16),) * 2,
+        "finish",
+    )(inside, factor, reach, docs, query, incoming)
 
     if n_ctx != 4 or n_head != 4 or n_pipe != 2:
-        normed = jnp.concatenate([finish(i, ()) for i in range(sides)], axis=1)
-        normed = lax.all_gather(normed, "ctx", axis=0, tiled=True)
+        normed = lax.all_gather(jnp.concatenate(normed, axis=0), "ctx", axis=0, tiled=True)
         blocks = jnp.dot(normed, weight, preferred_element_type=jnp.float32).astype(jnp.bfloat16)
         blocks = lax.all_to_all(blocks.reshape(n_ctx, rows, columns), "ctx", 0, 0, tiled=True)
         blocks = blocks.reshape(n_head, n_ctx // n_head, rows, columns)
@@ -333,37 +333,49 @@
     def swapped(array, by):
         return moved(array, lambda i, j, s: (i ^ by, j, s))
 
-    pieces = []
-    for i in range(sides):
-        own = finish(i, ())
-        one, two = swapped(own, 1), swapped(own, 2)
-        pieces.append([own, one, two, swapped(two, 1) if i % 2 else swapped(one, 2)])
-
-    part = columns // 2
-    single = jax.ShapeDtypeStruct((rows, part), jnp.bfloat16)
+    single = jax.ShapeDtypeStruct((rows, columns // 2), jnp.bfloat16)
 
     def project(picked, other, after=()):
-        shape = jax.ShapeDtypeStruct((len(picked), rows, part), jnp.bfloat16)
-        kernel = functools.partial(project_kernel, sides, other)
-        operands = [pieces[i][j] for j in picked for i in range(sides)]
-        specs = [VMEM] * (len(operands) + 1) + [ANY] * len(after)
-        return call(kernel, shape, "project", in_specs=specs)(*operands, weight, *after)
-
-    blocks = [None] * n_ctx
-    after, before = (pieces[0][2],), ()
-    for picked in ((0,), (1, 2), (3,)):
-        arrived = moved(project(picked, 1, after), lambda i, j, s: (i, j ^ 1, s))
-        specs = [VMEM] * 2 + [ANY] * len(before)
-        merged = call(merge_kernel, (single,) * len(picked), "merge", in_specs=specs)(
-            project(picked, 0), arrived, *before
-        )
-        before = merged[:1]
-        for k, block in zip(picked, merged):
-            blocks[k] = swapped(block, k) if k else block
-        after = (blocks[0],)
+        shape = jax.ShapeDtypeStruct((len(picked), part, columns // 2), jnp.bfloat16)
+        specs = [VMEM] * (len(picked) + 1) + [ANY] * len(after)
+        kernel = functools.partial(project_kernel, other)
+        return call(kernel, shape, "project", in_specs=specs)(*picked, weight, *after)
+
+    def partner(send):
+        return moved(send, lambda i, j, s: (i, j ^ 1, s))
+
+    def merge(layout, sums, after=()):
+        specs = [VMEM] * len(sums) + [ANY] * len(after)
+        kernel = functools.partial(merge_kernel, layout)
+        return call(kernel, (single,) * len(layout), "merge", in_specs=specs)(*sums, *after)
+
+    upper, lower = normed
+    upper_1, lower_2 = swapped(upper, 1), swapped(lower, 2)
+    whole = (((0, 0), (0, 1)),)
+
+    def hold(pair, after):
+        shape = jax.ShapeDtypeStruct((part, width), jnp.bfloat16)
+        specs = [VMEM] * 2 + [ANY] * len(after)
+        return call(hold_kernel, (shape,) * 2, "hold", in_specs=specs)(*pair, *after)
+
+    own_send = project((upper, lower), 1)
+    own = merge(whole, (project((upper, lower), 0), partner(own_send)))
+    upper, lower = hold((upper, lower), (own_send,))
+    lower_1, upper_2 = swapped(lower, 1), swapped(upper, 2)
+    held = hold((upper_1, lower_2), (lower_1, upper_2))
+    beside = (upper_1, lower_1, upper_2, lower_2)
+    beside = merge(
+        (((0, 0), (0, 1)), ((0, 2), (0, 3))),
+        (project(beside, 0), partner(project(beside, 1, own))),
+    )
+    across = (swapped(held[0], 2), swapped(held[1], 1))
+    across = merge(whole, (project(across, 0), partner(project(across, 1))), beside[:1])
+    blocks = [
+        swapped(block, k) if k else block for k, block in enumerate((*own, *beside, *across))
+    ]
     picked = call(pick_kernel, (single,) * n_head, "pick")(*blocks)
     arrived = [
-        moved(block, lambda i, j, s, m=m: (i, j ^ m, 1 - s)) for m, block in enumerate(picked)
+        moved(picked[m], lambda i, j, s, m=m: (i, j ^ m, 1 - s)) for m in reversed(range(n_head))
     ]
     out = jax.ShapeDtypeStruct((1, rows, columns), jnp.bfloat16)
     return call(last_kernel, out, "last")(*arrived)

time: 80.8 us -> 82.5 us (1.021)
  the two profiles are of different devices: /device:TPU:11 before, /device:TPU:0 now
where the time goes in v3:
time: 82.5 us; the launch traced here: 82.3 us
  waiting for transfers between devices  42.7 us (52%)
  starting transfers between devices  25.4 us (31%)
  Pallas kernels  14 us (17%)
    ppermute x16, waiting for transfers between devices, moved(): lax.ppermute(array, names, [(place[spot], place[target(*spot)]) for spot...  35.7 us
    ppermute x16, starting transfers between devices, moved(): lax.ppermute(array, names, [(place[spot], place[target(*spot)]) for spot...  20.6 us
    ppermute x1, waiting for transfers between devices, from_before(): return lax.ppermute(array, 'ctx', [(i, i + by) for i in range(n_ctx - by)])  6.98 us
    ppermute x1, starting transfers between devices, from_before(): return lax.ppermute(array, 'ctx', [(i, i + by) for i in range(n_ctx - by)])  4.87 us
    pallas_call x6, Pallas kernels, project(): call(kernel, shape, 'project', in_specs=specs)(*picked, weight, *after)  4.42 us
    pallas_call x1, Pallas kernels, on_device(): call(inside_kernel, (pltpu.VMEM((rows, width), jnp.float32), pltpu.VMEM((...  4.23 us
    pallas_call x1, Pallas kernels, on_device(): call(state_kernel, state_shape, 'shard_state', in_specs=[HBM] * 4, scratc...  2.58 us
  transfers between devices with their start and end apart: 17, of which 14 were waited for; matrix products, arithmetic and copies ran while one was open for 0% of the time, Pallas kernels for 11%

profile of v3, /device:TPU:0, one launch (start us, length us, event | category | flops | bytes accessed | tf_op | source)
XLA Modules:
  0.0 82.3 jit_solution(17585331254244734647)
XLA Ops:
  0.0 2.6 %shard_state.1 = bf16[2064,128]{1,0:T(8,128)(2,1)S(1)} custom-call(bf16[1,128,2048]{2,1,0:T(8,128)(2,1)} %key_hbm.3, bf16[1,128,2048]{2,1,0:T(8,128)(2,1)} %value_hbm.3, f32[1,16,128]{2,1,0:T(8,128)} %bitcast.1, s32[1,128]{1,0:T(1,128)} %doc_hbm.3), custom_call_target="tpu_custom_call" | custom-call | flops 1 | bytes 1 | tf_op jit(solution)/shard_map/shard_state/pallas_call | solution.py:254
  2.6 4.9 %collective-permute-start = (bf16[2064,128]{1,0:T(8,128)(2,1)S(1)}, bf16[2064,128]{1,0:T(8,128)(2,1)S(1)}, u32[]{:S(2)}, u32[]{:S(2)}) collective-permute-start(bf16[2064,128]{1,0:T(8,128)(2,1)S(1)} %shard_state.1), channel_id=1, source_target_pairs={{0,8},{8,16},{16,24},{1,9},{9,17},{17,25},{2,10},{10,18},{18,26},{... | collective-permute-start | bytes 1585160 | tf_op jit(solution)/shard_map/ppermute | solution.py:250
  7.5 4.2 %inside.1 = (f32[128,2048]{1,0:T(8,128)S(1)}, f32[128,2048]{1,0:T(8,128)S(1)}, f32[128,16]{1,0:T(8,128)S(1)}, f32[128,128]{1,0:T(8,128)S(1)}, bf16[128,2048]{1,0...) custom-call(bf16[1,128,2048]{2,1,0:T(8,128)(2,1)} %query_hbm.1, bf16[1,128,2048]{2,1,0:T(8,128)(2,1)} %key_hbm.3, ...), custom_call_target="tpu_custom_call" | custom-call | flops 1 | bytes 1 | tf_op jit(solution)/shard_map/inside/pallas_call | solution.py:286
  11.7 7.0 %collective-permute-done.state_ref = bf16[2064,128]{1,0:T(8,128)(2,1)S(1)} collective-permute-done((bf16[2064,128]{1,0:T(8,128)(2,1)S(1)}, bf16[2064,128]{1,0:T(8,128)(2,1)S(1)}, u32[]{:S(2)}, u32[]{:S(2)}) %collective-permute-start) | collective-permute-done | bytes 528416 | tf_op jit(solution)/shard_map/ppermute | solution.py:250
  18.7 1.6 %finish.1 = (bf16[64,2048]{1,0:T(8,128)(2,1)S(1)}, bf16[64,2048]{1,0:T(8,128)(2,1)S(1)}) custom-call(f32[128,2048]{1,0:T(8,128)S(1)} %get-tuple-element.23.inside_ref, f32[128,2048]{1,0:T(8,128)S(1)} %get-tuple-element.24.factor_ref, f32[128,16]{1,0:T(8,128)S(1)} %get-tuple-element.25.reach_ref, f32[128,128]{1,0:T(8,128)S(1)} %get-tuple-element.26.doc_ref, ...), custom_call_target="tpu_custom_call" | custom-call | flops 1 | bytes 1 | tf_op jit(solution)/shard_map/finish/pallas_call | solution.py:311
  20.3 2.5 %collective-permute-start.2 = (bf16[64,2048]{1,0:T(8,128)(2,1)S(1)}, bf16[64,2048]{1,0:T(8,128)(2,1)S(1)}, u32[]{:S(2)}, u32[]{:S(2)}) collective-permute-start(bf16[64,2048]{1,0:T(8,128)(2,1)S(1)} %get-tuple-element.28.refs_0_.upper_ref), channel_id=1, source_target_pairs={{0,8},{1,9},{2,10},{3,11},{4,12},{5,13},{6,14},{7,15},{8,0},{9,1},... | collective-permute-start | bytes 786440 | tf_op jit(solution)/shard_map/ppermute | solution.py:331
  23.5 1.6 %collective-permute-start.5 = (bf16[64,2048]{1,0:T(8,128)(2,1)S(1)}, bf16[64,2048]{1,0:T(8,128)(2,1)S(1)}, u32[]{:S(2)}, u32[]{:S(2)}) collective-permute-start(bf16[64,2048]{1,0:T(8,128)(2,1)S(1)} %get-tuple-element.29.refs_1_.lower_ref), channel_id=1, source_target_pairs={{0,16},{1,17},{2,18},{3,19},{4,20},{5,21},{6,22},{7,23},{8,24},{9,... | collective-permute-start | bytes 786440 | tf_op jit(solution)/shard_map/ppermute | solution.py:331
  25.1 1.5 %collective-permute-start.3 = (bf16[64,2048]{1,0:T(8,128)(2,1)S(1)}, bf16[64,2048]{1,0:T(8,128)(2,1)S(1)}, u32[]{:S(2)}, u32[]{:S(2)}) collective-permute-start(bf16[64,2048]{1,0:T(8,128)(2,1)S(1)} %get-tuple-element.31), channel_id=1, source_target_pairs={{0,8},{1,9},{2,10},{3,11},{4,12},{5,13},{6,14},{7,15},{8,0},{9,1},... | collective-permute-start | bytes 786440 | tf_op jit(solution)/shard_map/ppermute | solution.py:331
  26.6 1.6 %collective-permute-start.1 = (bf16[2,64,768]{2,1,0:T(8,128)(2,1)S(1)}, bf16[2,64,768]{2,1,0:T(8,128)(2,1)S(1)}, u32[]{:S(2)}, u32[]{:S(2)}) collective-permute-start(bf16[2,64,768]{2,1,0:T(8,128)(2,1)S(1)} %project.7.refs_0_), channel_id=1, source_target_pairs={{0,2},{1,3},{2,0},{3,1},{4,6},{5,7},{6,4},{7,5},{8,10},{9,11},{10,... | collective-permute-start | bytes 589832 | tf_op jit(solution)/shard_map/ppermute | solution.py:331
  28.2 1.9 %collective-permute-done.2.refs_0_.upper_ref = bf16[64,2048]{1,0:T(8,128)(2,1)S(1)} collective-permute-done((bf16[64,2048]{1,0:T(8,128)(2,1)S(1)}, bf16[64,2048]{1,0:T(8,128)(2,1)S(1)}, u32[]{:S(2)}, u32[]{:S(2)}) %collective-permute-start.2) | collective-permute-done | bytes 262176 | tf_op jit(solution)/shard_map/ppermute | solution.py:331
  30.1 2.7 %collective-permute-done.5.refs_3_.lower_ref = bf16[64,2048]{1,0:T(8,128)(2,1)S(1)} collective-permute-done((bf16[64,2048]{1,0:T(8,128)(2,1)S(1)}, bf16[64,2048]{1,0:T(8,128)(2,1)S(1)}, u32[]{:S(2)}, u32[]{:S(2)}) %collective-permute-start.5) | collective-permute-done | bytes 262176 | tf_op jit(solution)/shard_map/ppermute | solution.py:331
  33.9 2.1 %collective-permute-done.4.refs_2_.refs_1_ = bf16[64,2048]{1,0:T(8,128)(2,1)S(1)} collective-permute-done((bf16[64,2048]{1,0:T(8,128)(2,1)S(1)}, bf16[64,2048]{1,0:T(8,128)(2,1)S(1)}, u32[]{:S(2)}, u32[]{:S(2)}) %collective-permute-start.4) | collective-permute-done | bytes 262176 | tf_op jit(solution)/shard_map/ppermute | solution.py:331
  36.1 1.6 %collective-permute-start.9 = (bf16[64,2048]{1,0:T(8,128)(2,1)S(1)}, bf16[64,2048]{1,0:T(8,128)(2,1)S(1)}, u32[]{:S(2)}, u32[]{:S(2)}) collective-permute-start(bf16[64,2048]{1,0:T(8,128)(2,1)S(1)} %get-tuple-element.35), channel_id=1, source_target_pairs={{0,16},{1,17},{2,18},{3,19},{4,20},{5,21},{6,22},{7,23},{8,24},{9,... | collective-permute-start | bytes 786440 | tf_op jit(solution)/shard_map/ppermute | solution.py:331
  37.7 1.4 %collective-permute-start.10 = (bf16[64,2048]{1,0:T(8,128)(2,1)S(1)}, bf16[64,2048]{1,0:T(8,128)(2,1)S(1)}, u32[]{:S(2)}, u32[]{:S(2)}) collective-permute-start(bf16[64,2048]{1,0:T(8,128)(2,1)S(1)} %get-tuple-element.36), channel_id=1, source_target_pairs={{0,8},{1,9},{2,10},{3,11},{4,12},{5,13},{6,14},{7,15},{8,0},{9,1},... | collective-permute-start | bytes 786440 | tf_op jit(solution)/shard_map/ppermute | solution.py:331
  40.8 1.6 %collective-permute-start.6 = (bf16[4,64,768]{2,1,0:T(8,128)(2,1)S(1)}, bf16[4,64,768]{2,1,0:T(8,128)(2,1)S(1)}, u32[]{:S(2)}, u32[]{:S(2)}) collective-permute-start(bf16[4,64,768]{2,1,0:T(8,128)(2,1)S(1)} %project.9), channel_id=1, source_target_pairs={{0,2},{1,3},{2,0},{3,1},{4,6},{5,7},{6,4},{7,5},{8,10},{9,11},{10,... | collective-permute-start | bytes 1179656 | tf_op jit(solution)/shard_map/ppermute | solution.py:331
  42.5 1.5 %collective-permute-done.10.refs_1_ = bf16[64,2048]{1,0:T(8,128)(2,1)S(1)} collective-permute-done((bf16[64,2048]{1,0:T(8,128)(2,1)S(1)}, bf16[64,2048]{1,0:T(8,128)(2,1)S(1)}, u32[]{:S(2)}, u32[]{:S(2)}) %collective-permute-start.10) | collective-permute-done | bytes 262176 | tf_op jit(solution)/shard_map/ppermute | solution.py:331
  44.6 1.6 %collective-permute-start.11 = (bf16[2,64,768]{2,1,0:T(8,128)(2,1)S(1)}, bf16[2,64,768]{2,1,0:T(8,128)(2,1)S(1)}, u32[]{:S(2)}, u32[]{:S(2)}) collective-permute-start(bf16[2,64,768]{2,1,0:T(8,128)(2,1)S(1)} %project.11), channel_id=1, source_target_pairs={{0,2},{1,3},{2,0},{3,1},{4,6},{5,7},{6,4},{7,5},{8,10},{9,11},{10,... | collective-permute-start | bytes 589832 | tf_op jit(solution)/shard_map/ppermute | solution.py:331
  47.9 3.3 %collective-permute-done.6.refs_1_ = bf16[4,64,768]{2,1,0:T(8,128)(2,1)S(1)} collective-permute-done((bf16[4,64,768]{2,1,0:T(8,128)(2,1)S(1)}, bf16[4,64,768]{2,1,0:T(8,128)(2,1)S(1)}, u32[]{:S(2)}, u32[]{:S(2)}) %collective-permute-start.6) | collective-permute-done | bytes 393248 | tf_op jit(solution)/shard_map/ppermute | solution.py:331
  53.3 1.6 %collective-permute-start.12 = (bf16[128,768]{1,0:T(8,128)(2,1)S(1)}, bf16[128,768]{1,0:T(8,128)(2,1)S(1)}, u32[]{:S(2)}, u32[]{:S(2)}) collective-permute-start(bf16[128,768]{1,0:T(8,128)(2,1)S(1)} %merge.5), channel_id=1, source_target_pairs={{0,24},{1,25},{2,26},{3,27},{4,28},{5,29},{6,30},{7,31},{8,16},{9,... | collective-permute-start | bytes 589832 | tf_op jit(solution)/shard_map/ppermute | solution.py:331
  55.0 2.4 %collective-permute-done.8.refs_2_ = bf16[128,768]{1,0:T(8,128)(2,1)S(1)} collective-permute-done((bf16[128,768]{1,0:T(8,128)(2,1)S(1)}, bf16[128,768]{1,0:T(8,128)(2,1)S(1)}, u32[]{:S(2)}, u32[]{:S(2)}) %collective-permute-start.8) | collective-permute-done | bytes 196640 | tf_op jit(solution)/shard_map/ppermute | solution.py:331
  57.6 3.0 %collective-permute-done.12.refs_3_ = bf16[128,768]{1,0:T(8,128)(2,1)S(1)} collective-permute-done((bf16[128,768]{1,0:T(8,128)(2,1)S(1)}, bf16[128,768]{1,0:T(8,128)(2,1)S(1)}, u32[]{:S(2)}, u32[]{:S(2)}) %collective-permute-start.12) | collective-permute-done | bytes 196640 | tf_op jit(solution)/shard_map/ppermute | solution.py:331
  60.8 2.7 %collective-permute-start.14 = (bf16[128,768]{1,0:T(8,128)(2,1)S(1)}, bf16[128,768]{1,0:T(8,128)(2,1)S(1)}, u32[]{:S(2)}, u32[]{:S(2)}) collective-permute-start(bf16[128,768]{1,0:T(8,128)(2,1)S(1)} %get-tuple-element.38), channel_id=1, source_target_pairs={{0,5},{1,4},{2,7},{3,6},{4,1},{5,0},{6,3},{7,2},{8,13},{9,12},{10,... | collective-permute-start | bytes 589832 | tf_op jit(solution)/shard_map/ppermute | solution.py:331
  65.0 4.7 %collective-permute-done.13.refs_0_ = bf16[128,768]{1,0:T(8,128)(2,1)S(1)} collective-permute-done((bf16[128,768]{1,0:T(8,128)(2,1)S(1)}, bf16[128,768]{1,0:T(8,128)(2,1)S(1)}, u32[]{:S(2)}, u32[]{:S(2)}) %collective-permute-start.13) | collective-permute-done | bytes 196640 | tf_op jit(solution)/shard_map/ppermute | solution.py:331
  69.6 11.8 %collective-permute-done.14.refs_1_ = bf16[128,768]{1,0:T(8,128)(2,1)S(1)} collective-permute-done((bf16[128,768]{1,0:T(8,128)(2,1)S(1)}, bf16[128,768]{1,0:T(8,128)(2,1)S(1)}, u32[]{:S(2)}, u32[]{:S(2)}) %collective-permute-start.14) | collective-permute-done | bytes 196640 | tf_op jit(solution)/shard_map/ppermute | solution.py:331
  (26 shorter events, 10.6 us)
Async XLA Ops:
  2.6 16.1 %collective-permute-start = (bf16[2064,128]{1,0:T(8,128)(2,1)S(1)}, bf16[2064,128]{1,0:T(8,128)(2,1)S(1)}, u32[]{:S(2)}, u32[]{:S(2)}) collective-permute-start(bf16[2064,128]{1,0:T(8,128)(2,1)S(1)} %shard_state.1), channel_id=1, source_target_pairs={{0,8},{8,16},{16,24},{1,9},{9,17},{17,25},{2,10},{10,18},{18,26},{... | collective-permute-start | bytes 1585160 | tf_op jit(solution)/shard_map/ppermute | solution.py:250
  20.3 9.8 %collective-permute-start.2 = (bf16[64,2048]{1,0:T(8,128)(2,1)S(1)}, bf16[64,2048]{1,0:T(8,128)(2,1)S(1)}, u32[]{:S(2)}, u32[]{:S(2)}) collective-permute-start(bf16[64,2048]{1,0:T(8,128)(2,1)S(1)} %get-tuple-element.28.refs_0_.upper_ref), channel_id=1, source_target_pairs={{0,8},{1,9},{2,10},{3,11},{4,12},{5,13},{6,14},{7,15},{8,0},{9,1},... | collective-permute-start | bytes 786440 | tf_op jit(solution)/shard_map/ppermute | solution.py:331
  23.5 9.3 %collective-permute-start.5 = (bf16[64,2048]{1,0:T(8,128)(2,1)S(1)}, bf16[64,2048]{1,0:T(8,128)(2,1)S(1)}, u32[]{:S(2)}, u32[]{:S(2)}) collective-permute-start(bf16[64,2048]{1,0:T(8,128)(2,1)S(1)} %get-tuple-element.29.refs_1_.lower_ref), channel_id=1, source_target_pairs={{0,16},{1,17},{2,18},{3,19},{4,20},{5,21},{6,22},{7,23},{8,24},{9,... | collective-permute-start | bytes 786440 | tf_op jit(solution)/shard_map/ppermute | solution.py:331
  25.1 8.8 %collective-permute-start.3 = (bf16[64,2048]{1,0:T(8,128)(2,1)S(1)}, bf16[64,2048]{1,0:T(8,128)(2,1)S(1)}, u32[]{:S(2)}, u32[]{:S(2)}) collective-permute-start(bf16[64,2048]{1,0:T(8,128)(2,1)S(1)} %get-tuple-element.31), channel_id=1, source_target_pairs={{0,8},{1,9},{2,10},{3,11},{4,12},{5,13},{6,14},{7,15},{8,0},{9,1},... | collective-permute-start | bytes 786440 | tf_op jit(solution)/shard_map/ppermute | solution.py:331
  26.6 9.5 %collective-permute-start.4 = (bf16[64,2048]{1,0:T(8,128)(2,1)S(1)}, bf16[64,2048]{1,0:T(8,128)(2,1)S(1)}, u32[]{:S(2)}, u32[]{:S(2)}) collective-permute-start(bf16[64,2048]{1,0:T(8,128)(2,1)S(1)} %get-tuple-element.32), channel_id=1, source_target_pairs={{0,16},{1,17},{2,18},{3,19},{4,20},{5,21},{6,22},{7,23},{8,24},{9,... | collective-permute-start | bytes 786440 | tf_op jit(solution)/shard_map/ppermute | solution.py:331
  26.6 13.1 %collective-permute-start.1 = (bf16[2,64,768]{2,1,0:T(8,128)(2,1)S(1)}, bf16[2,64,768]{2,1,0:T(8,128)(2,1)S(1)}, u32[]{:S(2)}, u32[]{:S(2)}) collective-permute-start(bf16[2,64,768]{2,1,0:T(8,128)(2,1)S(1)} %project.7.refs_0_), channel_id=1, source_target_pairs={{0,2},{1,3},{2,0},{3,1},{4,6},{5,7},{6,4},{7,5},{8,10},{9,11},{10,... | collective-permute-start | bytes 589832 | tf_op jit(solution)/shard_map/ppermute | solution.py:331
  36.1 6.4 %collective-permute-start.9 = (bf16[64,2048]{1,0:T(8,128)(2,1)S(1)}, bf16[64,2048]{1,0:T(8,128)(2,1)S(1)}, u32[]{:S(2)}, u32[]{:S(2)}) collective-permute-start(bf16[64,2048]{1,0:T(8,128)(2,1)S(1)} %get-tuple-element.35), channel_id=1, source_target_pairs={{0,16},{1,17},{2,18},{3,19},{4,20},{5,21},{6,22},{7,23},{8,24},{9,... | collective-permute-start | bytes 786440 | tf_op jit(solution)/shard_map/ppermute | solution.py:331
  37.7 6.4 %collective-permute-start.10 = (bf16[64,2048]{1,0:T(8,128)(2,1)S(1)}, bf16[64,2048]{1,0:T(8,128)(2,1)S(1)}, u32[]{:S(2)}, u32[]{:S(2)}) collective-permute-start(bf16[64,2048]{1,0:T(8,128)(2,1)S(1)} %get-tuple-element.36), channel_id=1, source_target_pairs={{0,8},{1,9},{2,10},{3,11},{4,12},{5,13},{6,14},{7,15},{8,0},{9,1},... | collective-permute-start | bytes 786440 | tf_op jit(solution)/shard_map/ppermute | solution.py:331
  40.8 10.4 %collective-permute-start.6 = (bf16[4,64,768]{2,1,0:T(8,128)(2,1)S(1)}, bf16[4,64,768]{2,1,0:T(8,128)(2,1)S(1)}, u32[]{:S(2)}, u32[]{:S(2)}) collective-permute-start(bf16[4,64,768]{2,1,0:T(8,128)(2,1)S(1)} %project.9), channel_id=1, source_target_pairs={{0,2},{1,3},{2,0},{3,1},{4,6},{5,7},{6,4},{7,5},{8,10},{9,11},{10,... | collective-permute-start | bytes 1179656 | tf_op jit(solution)/shard_map/ppermute | solution.py:331
  44.6 8.6 %collective-permute-start.11 = (bf16[2,64,768]{2,1,0:T(8,128)(2,1)S(1)}, bf16[2,64,768]{2,1,0:T(8,128)(2,1)S(1)}, u32[]{:S(2)}, u32[]{:S(2)}) collective-permute-start(bf16[2,64,768]{2,1,0:T(8,128)(2,1)S(1)} %project.11), channel_id=1, source_target_pairs={{0,2},{1,3},{2,0},{3,1},{4,6},{5,7},{6,4},{7,5},{8,10},{9,11},{10,... | collective-permute-start | bytes 589832 | tf_op jit(solution)/shard_map/ppermute | solution.py:331
  51.3 6.1 %collective-permute-start.8 = (bf16[128,768]{1,0:T(8,128)(2,1)S(1)}, bf16[128,768]{1,0:T(8,128)(2,1)S(1)}, u32[]{:S(2)}, u32[]{:S(2)}) collective-permute-start(bf16[128,768]{1,0:T(8,128)(2,1)S(1)} %get-tuple-element.34), channel_id=1, source_target_pairs={{0,16},{1,17},{2,18},{3,19},{4,20},{5,21},{6,22},{7,23},{8,24},{9,... | collective-permute-start | bytes 589832 | tf_op jit(solution)/shard_map/ppermute | solution.py:331
  51.9 5.7 %collective-permute-start.7 = (bf16[128,768]{1,0:T(8,128)(2,1)S(1)}, bf16[128,768]{1,0:T(8,128)(2,1)S(1)}, u32[]{:S(2)}, u32[]{:S(2)}) collective-permute-start(bf16[128,768]{1,0:T(8,128)(2,1)S(1)} %get-tuple-element.33.refs_2_), channel_id=1, source_target_pairs={{0,8},{1,9},{2,10},{3,11},{4,12},{5,13},{6,14},{7,15},{8,0},{9,1},... | collective-permute-start | bytes 589832 | tf_op jit(solution)/shard_map/ppermute | solution.py:331
  53.3 7.2 %collective-permute-start.12 = (bf16[128,768]{1,0:T(8,128)(2,1)S(1)}, bf16[128,768]{1,0:T(8,128)(2,1)S(1)}, u32[]{:S(2)}, u32[]{:S(2)}) collective-permute-start(bf16[128,768]{1,0:T(8,128)(2,1)S(1)} %merge.5), channel_id=1, source_target_pairs={{0,24},{1,25},{2,26},{3,27},{4,28},{5,29},{6,30},{7,31},{8,16},{9,... | collective-permute-start | bytes 589832 | tf_op jit(solution)/shard_map/ppermute | solution.py:331
  60.7 8.9 %collective-permute-start.13 = (bf16[128,768]{1,0:T(8,128)(2,1)S(1)}, bf16[128,768]{1,0:T(8,128)(2,1)S(1)}, u32[]{:S(2)}, u32[]{:S(2)}) collective-permute-start(bf16[128,768]{1,0:T(8,128)(2,1)S(1)} %get-tuple-element.37), channel_id=1, source_target_pairs={{0,7},{1,6},{2,5},{3,4},{4,3},{5,2},{6,1},{7,0},{8,15},{9,14},{10,... | collective-permute-start | bytes 589832 | tf_op jit(solution)/shard_map/ppermute | solution.py:331
  60.8 20.7 %collective-permute-start.14 = (bf16[128,768]{1,0:T(8,128)(2,1)S(1)}, bf16[128,768]{1,0:T(8,128)(2,1)S(1)}, u32[]{:S(2)}, u32[]{:S(2)}) collective-permute-start(bf16[128,768]{1,0:T(8,128)(2,1)S(1)} %get-tuple-element.38), channel_id=1, source_target_pairs={{0,5},{1,4},{2,7},{3,6},{4,1},{5,0},{6,3},{7,2},{8,13},{9,12},{10,... | collective-permute-start | bytes 589832 | tf_op jit(solution)/shard_map/ppermute | solution.py:331
  63.5 17.9 %collective-permute-start.15 = (bf16[128,768]{1,0:T(8,128)(2,1)S(1)}, bf16[128,768]{1,0:T(8,128)(2,1)S(1)}, u32[]{:S(2)}, u32[]{:S(2)}) collective-permute-start(bf16[128,768]{1,0:T(8,128)(2,1)S(1)} %get-tuple-element.39), channel_id=1, source_target_pairs={{0,3},{1,2},{2,1},{3,0},{4,7},{5,6},{6,5},{7,4},{8,11},{9,10},{10,... | collective-permute-start | bytes 589832 | tf_op jit(solution)/shard_map/ppermute | solution.py:331
  64.7 16.7 %collective-permute-start.16 = (bf16[128,768]{1,0:T(8,128)(2,1)S(1)}, bf16[128,768]{1,0:T(8,128)(2,1)S(1)}, u32[]{:S(2)}, u32[]{:S(2)}) collective-permute-start(bf16[128,768]{1,0:T(8,128)(2,1)S(1)} %get-tuple-element.40), channel_id=1, source_target_pairs={{0,1},{1,0},{2,3},{3,2},{4,5},{5,4},{6,7},{7,6},{8,9},{9,8},{10,11... | collective-permute-start | bytes 589832 | tf_op jit(solution)/shard_map/ppermute | solution.py:331

commit v4 on v3

--- a/solution.py
+++ b/solution.py
@@ -374,11 +374,10 @@
         swapped(block, k) if k else block for k, block in enumerate((*own, *beside, *across))
     ]
     picked = call(pick_kernel, (single,) * n_head, "pick")(*blocks)
-    arrived = [
-        moved(picked[m], lambda i, j, s, m=m: (i, j ^ m, 1 - s)) for m in reversed(range(n_head))
-    ]
+    arrived = [moved(picked[m], lambda i, j, s, m=m: (i, j ^ m, s)) for m in (3, 2, 1)]
     out = jax.ShapeDtypeStruct((1, rows, columns), jnp.bfloat16)
-    return call(last_kernel, out, "last")(*arrived)
+    out = call(last_kernel, out, "last")(*arrived, picked[0])
+    return moved(out, lambda i, j, s: (i, j, 1 - s))
 
 
 def solution(mesh):

time: 82.5 us -> 78.6 us (0.953)
  waiting for transfers between devices: 42.7 us -> 38.5 us
    ppermute x16, waiting for transfers between devices: 35.7 us -> 31.5 us  [moved(): lax.ppermute(array, names, [(place[spot], place[target(*spot)]) for spot...]
  transfers between devices with their start and end apart: 17 -> 17, of which waited for: 14 -> 15; matrix products, arithmetic and copies ran while one was open for 0% -> 0% of each run, Pallas kernels for 11% -> 11%
where the time goes in v4:
time: 78.6 us; the launch traced here: 78.4 us
  waiting for transfers between devices  38.5 us (49%)
  starting transfers between devices  25.7 us (33%)
  Pallas kernels  13.3 us (17%)
    ppermute x16, waiting for transfers between devices, moved(): lax.ppermute(array, names, [(place[spot], place[target(*spot)]) for spot...  31.5 us
    ppermute x16, starting transfers between devices, moved(): lax.ppermute(array, names, [(place[spot], place[target(*spot)]) for spot...  20.8 us
    ppermute x1, waiting for transfers between devices, from_before(): return lax.ppermute(array, 'ctx', [(i, i + by) for i in range(n_ctx - by)])  6.98 us
    ppermute x1, starting transfers between devices, from_before(): return lax.ppermute(array, 'ctx', [(i, i + by) for i in range(n_ctx - by)])  4.87 us
    pallas_call x6, Pallas kernels, project(): call(kernel, shape, 'project', in_specs=specs)(*picked, weight, *after)  4.42 us
    pallas_call x1, Pallas kernels, on_device(): call(inside_kernel, (pltpu.VMEM((rows, width), jnp.float32), pltpu.VMEM((...  4.23 us
    pallas_call x1, Pallas kernels, on_device(): call(state_kernel, state_shape, 'shard_state', in_specs=[HBM] * 4, scratc...  2.58 us
    pallas_call x1, Pallas kernels, on_device(): call(finish_kernel, (jax.ShapeDtypeStruct((part, width), jnp.bfloat16),)...  1.59 us
  transfers between devices with their start and end apart: 17, of which 15 were waited for; matrix products, arithmetic and copies ran while one was open for 0% of the time, Pallas kernels for 11%

profile of v4, /device:TPU:0, one launch (start us, length us, event | category | flops | bytes accessed | tf_op | source)
XLA Modules:
  0.0 78.4 jit_solution(10474431957880287102)
XLA Ops:
  0.0 2.6 %shard_state.1 = bf16[2064,128]{1,0:T(8,128)(2,1)S(1)} custom-call(bf16[1,128,2048]{2,1,0:T(8,128)(2,1)} %key_hbm.3, bf16[1,128,2048]{2,1,0:T(8,128)(2,1)} %value_hbm.3, f32[1,16,128]{2,1,0:T(8,128)} %bitcast.1, s32[1,128]{1,0:T(1,128)} %doc_hbm.3), custom_call_target="tpu_custom_call" | custom-call | flops 1 | bytes 1 | tf_op jit(solution)/shard_map/shard_state/pallas_call | solution.py:254
  2.6 4.9 %collective-permute-start = (bf16[2064,128]{1,0:T(8,128)(2,1)S(1)}, bf16[2064,128]{1,0:T(8,128)(2,1)S(1)}, u32[]{:S(2)}, u32[]{:S(2)}) collective-permute-start(bf16[2064,128]{1,0:T(8,128)(2,1)S(1)} %shard_state.1), channel_id=1, source_target_pairs={{0,8},{8,16},{16,24},{1,9},{9,17},{17,25},{2,10},{10,18},{18,26},{... | collective-permute-start | bytes 1585160 | tf_op jit(solution)/shard_map/ppermute | solution.py:250
  7.5 4.2 %inside.1 = (f32[128,2048]{1,0:T(8,128)S(1)}, f32[128,2048]{1,0:T(8,128)S(1)}, f32[128,16]{1,0:T(8,128)S(1)}, f32[128,128]{1,0:T(8,128)S(1)}, bf16[128,2048]{1,0...) custom-call(bf16[1,128,2048]{2,1,0:T(8,128)(2,1)} %query_hbm.1, bf16[1,128,2048]{2,1,0:T(8,128)(2,1)} %key_hbm.3, ...), custom_call_target="tpu_custom_call" | custom-call | flops 1 | bytes 1 | tf_op jit(solution)/shard_map/inside/pallas_call | solution.py:286
  11.7 7.0 %collective-permute-done.state_ref = bf16[2064,128]{1,0:T(8,128)(2,1)S(1)} collective-permute-done((bf16[2064,128]{1,0:T(8,128)(2,1)S(1)}, bf16[2064,128]{1,0:T(8,128)(2,1)S(1)}, u32[]{:S(2)}, u32[]{:S(2)}) %collective-permute-start) | collective-permute-done | bytes 528416 | tf_op jit(solution)/shard_map/ppermute | solution.py:250
  18.7 1.6 %finish.1 = (bf16[64,2048]{1,0:T(8,128)(2,1)S(1)}, bf16[64,2048]{1,0:T(8,128)(2,1)S(1)}) custom-call(f32[128,2048]{1,0:T(8,128)S(1)} %get-tuple-element.23.inside_ref, f32[128,2048]{1,0:T(8,128)S(1)} %get-tuple-element.24.factor_ref, f32[128,16]{1,0:T(8,128)S(1)} %get-tuple-element.25.reach_ref, f32[128,128]{1,0:T(8,128)S(1)} %get-tuple-element.26.doc_ref, ...), custom_call_target="tpu_custom_call" | custom-call | flops 1 | bytes 1 | tf_op jit(solution)/shard_map/finish/pallas_call | solution.py:311
  20.3 2.5 %collective-permute-start.2 = (bf16[64,2048]{1,0:T(8,128)(2,1)S(1)}, bf16[64,2048]{1,0:T(8,128)(2,1)S(1)}, u32[]{:S(2)}, u32[]{:S(2)}) collective-permute-start(bf16[64,2048]{1,0:T(8,128)(2,1)S(1)} %get-tuple-element.28.refs_0_.upper_ref), channel_id=1, source_target_pairs={{0,8},{1,9},{2,10},{3,11},{4,12},{5,13},{6,14},{7,15},{8,0},{9,1},... | collective-permute-start | bytes 786440 | tf_op jit(solution)/shard_map/ppermute | solution.py:331
  23.5 1.6 %collective-permute-start.5 = (bf16[64,2048]{1,0:T(8,128)(2,1)S(1)}, bf16[64,2048]{1,0:T(8,128)(2,1)S(1)}, u32[]{:S(2)}, u32[]{:S(2)}) collective-permute-start(bf16[64,2048]{1,0:T(8,128)(2,1)S(1)} %get-tuple-element.29.refs_1_.lower_ref), channel_id=1, source_target_pairs={{0,16},{1,17},{2,18},{3,19},{4,20},{5,21},{6,22},{7,23},{8,24},{9,... | collective-permute-start | bytes 786440 | tf_op jit(solution)/shard_map/ppermute | solution.py:331
  25.1 1.5 %collective-permute-start.3 = (bf16[64,2048]{1,0:T(8,128)(2,1)S(1)}, bf16[64,2048]{1,0:T(8,128)(2,1)S(1)}, u32[]{:S(2)}, u32[]{:S(2)}) collective-permute-start(bf16[64,2048]{1,0:T(8,128)(2,1)S(1)} %get-tuple-element.31), channel_id=1, source_target_pairs={{0,8},{1,9},{2,10},{3,11},{4,12},{5,13},{6,14},{7,15},{8,0},{9,1},... | collective-permute-start | bytes 786440 | tf_op jit(solution)/shard_map/ppermute | solution.py:331
  26.6 1.6 %collective-permute-start.1 = (bf16[2,64,768]{2,1,0:T(8,128)(2,1)S(1)}, bf16[2,64,768]{2,1,0:T(8,128)(2,1)S(1)}, u32[]{:S(2)}, u32[]{:S(2)}) collective-permute-start(bf16[2,64,768]{2,1,0:T(8,128)(2,1)S(1)} %project.7.refs_0_), channel_id=1, source_target_pairs={{0,2},{1,3},{2,0},{3,1},{4,6},{5,7},{6,4},{7,5},{8,10},{9,11},{10,... | collective-permute-start | bytes 589832 | tf_op jit(solution)/shard_map/ppermute | solution.py:331
  28.2 1.9 %collective-permute-done.2.refs_0_.upper_ref = bf16[64,2048]{1,0:T(8,128)(2,1)S(1)} collective-permute-done((bf16[64,2048]{1,0:T(8,128)(2,1)S(1)}, bf16[64,2048]{1,0:T(8,128)(2,1)S(1)}, u32[]{:S(2)}, u32[]{:S(2)}) %collective-permute-start.2) | collective-permute-done | bytes 262176 | tf_op jit(solution)/shard_map/ppermute | solution.py:331
  30.1 2.7 %collective-permute-done.5.refs_3_.lower_ref = bf16[64,2048]{1,0:T(8,128)(2,1)S(1)} collective-permute-done((bf16[64,2048]{1,0:T(8,128)(2,1)S(1)}, bf16[64,2048]{1,0:T(8,128)(2,1)S(1)}, u32[]{:S(2)}, u32[]{:S(2)}) %collective-permute-start.5) | collective-permute-done | bytes 262176 | tf_op jit(solution)/shard_map/ppermute | solution.py:331
  33.9 2.1 %collective-permute-done.4.refs_2_.refs_1_ = bf16[64,2048]{1,0:T(8,128)(2,1)S(1)} collective-permute-done((bf16[64,2048]{1,0:T(8,128)(2,1)S(1)}, bf16[64,2048]{1,0:T(8,128)(2,1)S(1)}, u32[]{:S(2)}, u32[]{:S(2)}) %collective-permute-start.4) | collective-permute-done | bytes 262176 | tf_op jit(solution)/shard_map/ppermute | solution.py:331
  36.1 1.6 %collective-permute-start.9 = (bf16[64,2048]{1,0:T(8,128)(2,1)S(1)}, bf16[64,2048]{1,0:T(8,128)(2,1)S(1)}, u32[]{:S(2)}, u32[]{:S(2)}) collective-permute-start(bf16[64,2048]{1,0:T(8,128)(2,1)S(1)} %get-tuple-element.35), channel_id=1, source_target_pairs={{0,16},{1,17},{2,18},{3,19},{4,20},{5,21},{6,22},{7,23},{8,24},{9,... | collective-permute-start | bytes 786440 | tf_op jit(solution)/shard_map/ppermute | solution.py:331
  40.8 1.6 %collective-permute-start.6 = (bf16[4,64,768]{2,1,0:T(8,128)(2,1)S(1)}, bf16[4,64,768]{2,1,0:T(8,128)(2,1)S(1)}, u32[]{:S(2)}, u32[]{:S(2)}) collective-permute-start(bf16[4,64,768]{2,1,0:T(8,128)(2,1)S(1)} %project.9), channel_id=1, source_target_pairs={{0,2},{1,3},{2,0},{3,1},{4,6},{5,7},{6,4},{7,5},{8,10},{9,11},{10,... | collective-permute-start | bytes 1179656 | tf_op jit(solution)/shard_map/ppermute | solution.py:331
  42.5 1.5 %collective-permute-done.10.refs_1_ = bf16[64,2048]{1,0:T(8,128)(2,1)S(1)} collective-permute-done((bf16[64,2048]{1,0:T(8,128)(2,1)S(1)}, bf16[64,2048]{1,0:T(8,128)(2,1)S(1)}, u32[]{:S(2)}, u32[]{:S(2)}) %collective-permute-start.10) | collective-permute-done | bytes 262176 | tf_op jit(solution)/shard_map/ppermute | solution.py:331
  44.6 1.6 %collective-permute-start.11 = (bf16[2,64,768]{2,1,0:T(8,128)(2,1)S(1)}, bf16[2,64,768]{2,1,0:T(8,128)(2,1)S(1)}, u32[]{:S(2)}, u32[]{:S(2)}) collective-permute-start(bf16[2,64,768]{2,1,0:T(8,128)(2,1)S(1)} %project.11), channel_id=1, source_target_pairs={{0,2},{1,3},{2,0},{3,1},{4,6},{5,7},{6,4},{7,5},{8,10},{9,11},{10,... | collective-permute-start | bytes 589832 | tf_op jit(solution)/shard_map/ppermute | solution.py:331
  47.9 3.3 %collective-permute-done.6.refs_1_ = bf16[4,64,768]{2,1,0:T(8,128)(2,1)S(1)} collective-permute-done((bf16[4,64,768]{2,1,0:T(8,128)(2,1)S(1)}, bf16[4,64,768]{2,1,0:T(8,128)(2,1)S(1)}, u32[]{:S(2)}, u32[]{:S(2)}) %collective-permute-start.6) | collective-permute-done | bytes 393248 | tf_op jit(solution)/shard_map/ppermute | solution.py:331
  53.3 1.6 %collective-permute-start.12 = (bf16[128,768]{1,0:T(8,128)(2,1)S(1)}, bf16[128,768]{1,0:T(8,128)(2,1)S(1)}, u32[]{:S(2)}, u32[]{:S(2)}) collective-permute-start(bf16[128,768]{1,0:T(8,128)(2,1)S(1)} %merge.5), channel_id=1, source_target_pairs={{0,24},{1,25},{2,26},{3,27},{4,28},{5,29},{6,30},{7,31},{8,16},{9,... | collective-permute-start | bytes 589832 | tf_op jit(solution)/shard_map/ppermute | solution.py:331
  55.0 2.4 %collective-permute-done.8.refs_2_ = bf16[128,768]{1,0:T(8,128)(2,1)S(1)} collective-permute-done((bf16[128,768]{1,0:T(8,128)(2,1)S(1)}, bf16[128,768]{1,0:T(8,128)(2,1)S(1)}, u32[]{:S(2)}, u32[]{:S(2)}) %collective-permute-start.8) | collective-permute-done | bytes 196640 | tf_op jit(solution)/shard_map/ppermute | solution.py:331
  57.6 3.0 %collective-permute-done.12.refs_3_ = bf16[128,768]{1,0:T(8,128)(2,1)S(1)} collective-permute-done((bf16[128,768]{1,0:T(8,128)(2,1)S(1)}, bf16[128,768]{1,0:T(8,128)(2,1)S(1)}, u32[]{:S(2)}, u32[]{:S(2)}) %collective-permute-start.12) | collective-permute-done | bytes 196640 | tf_op jit(solution)/shard_map/ppermute | solution.py:331
  60.7 3.6 %collective-permute-start.13 = (bf16[128,768]{1,0:T(8,128)(2,1)S(1)}, bf16[128,768]{1,0:T(8,128)(2,1)S(1)}, u32[]{:S(2)}, u32[]{:S(2)}) collective-permute-start(bf16[128,768]{1,0:T(8,128)(2,1)S(1)} %get-tuple-element.37), channel_id=1, source_target_pairs={{0,6},{1,7},{2,4},{3,5},{4,2},{5,3},{6,0},{7,1},{8,14},{9,15},{10,... | collective-permute-start | bytes 589832 | tf_op jit(solution)/shard_map/ppermute | solution.py:331
  65.2 3.2 %collective-permute-done.13.refs_0_ = bf16[128,768]{1,0:T(8,128)(2,1)S(1)} collective-permute-done((bf16[128,768]{1,0:T(8,128)(2,1)S(1)}, bf16[128,768]{1,0:T(8,128)(2,1)S(1)}, u32[]{:S(2)}, u32[]{:S(2)}) %collective-permute-start.13) | collective-permute-done | bytes 196640 | tf_op jit(solution)/shard_map/ppermute | solution.py:331
  68.4 7.4 %collective-permute-done.14.refs_1_ = bf16[128,768]{1,0:T(8,128)(2,1)S(1)} collective-permute-done((bf16[128,768]{1,0:T(8,128)(2,1)S(1)}, bf16[128,768]{1,0:T(8,128)(2,1)S(1)}, u32[]{:S(2)}, u32[]{:S(2)}) %collective-permute-start.14) | collective-permute-done | bytes 196640 | tf_op jit(solution)/shard_map/ppermute | solution.py:331
  75.9 1.7 %collective-permute-done.16 = bf16[1,128,1536]{2,1,0:T(8,128)(2,1)S(1)} collective-permute-done((bf16[1,128,1536]{2,1,0:T(8,128)(2,1)S(1)}, bf16[1,128,1536]{2,1,0:T(8,128)(2,1)S(1)}, u32[]{:S(2)}, u32[]{:S(2)}) %collective-permute-start.16) | collective-permute-done | bytes 393248 | tf_op jit(solution)/shard_map/ppermute | solution.py:331
  (27 shorter events, 11.4 us)
Async XLA Ops:
  2.6 16.1 %collective-permute-start = (bf16[2064,128]{1,0:T(8,128)(2,1)S(1)}, bf16[2064,128]{1,0:T(8,128)(2,1)S(1)}, u32[]{:S(2)}, u32[]{:S(2)}) collective-permute-start(bf16[2064,128]{1,0:T(8,128)(2,1)S(1)} %shard_state.1), channel_id=1, source_target_pairs={{0,8},{8,16},{16,24},{1,9},{9,17},{17,25},{2,10},{10,18},{18,26},{... | collective-permute-start | bytes 1585160 | tf_op jit(solution)/shard_map/ppermute | solution.py:250
  20.3 9.8 %collective-permute-start.2 = (bf16[64,2048]{1,0:T(8,128)(2,1)S(1)}, bf16[64,2048]{1,0:T(8,128)(2,1)S(1)}, u32[]{:S(2)}, u32[]{:S(2)}) collective-permute-start(bf16[64,2048]{1,0:T(8,128)(2,1)S(1)} %get-tuple-element.28.refs_0_.upper_ref), channel_id=1, source_target_pairs={{0,8},{1,9},{2,10},{3,11},{4,12},{5,13},{6,14},{7,15},{8,0},{9,1},... | collective-permute-start | bytes 786440 | tf_op jit(solution)/shard_map/ppermute | solution.py:331
  23.5 9.3 %collective-permute-start.5 = (bf16[64,2048]{1,0:T(8,128)(2,1)S(1)}, bf16[64,2048]{1,0:T(8,128)(2,1)S(1)}, u32[]{:S(2)}, u32[]{:S(2)}) collective-permute-start(bf16[64,2048]{1,0:T(8,128)(2,1)S(1)} %get-tuple-element.29.refs_1_.lower_ref), channel_id=1, source_target_pairs={{0,16},{1,17},{2,18},{3,19},{4,20},{5,21},{6,22},{7,23},{8,24},{9,... | collective-permute-start | bytes 786440 | tf_op jit(solution)/shard_map/ppermute | solution.py:331
  25.1 8.8 %collective-permute-start.3 = (bf16[64,2048]{1,0:T(8,128)(2,1)S(1)}, bf16[64,2048]{1,0:T(8,128)(2,1)S(1)}, u32[]{:S(2)}, u32[]{:S(2)}) collective-permute-start(bf16[64,2048]{1,0:T(8,128)(2,1)S(1)} %get-tuple-element.31), channel_id=1, source_target_pairs={{0,8},{1,9},{2,10},{3,11},{4,12},{5,13},{6,14},{7,15},{8,0},{9,1},... | collective-permute-start | bytes 786440 | tf_op jit(solution)/shard_map/ppermute | solution.py:331
  26.6 9.5 %collective-permute-start.4 = (bf16[64,2048]{1,0:T(8,128)(2,1)S(1)}, bf16[64,2048]{1,0:T(8,128)(2,1)S(1)}, u32[]{:S(2)}, u32[]{:S(2)}) collective-permute-start(bf16[64,2048]{1,0:T(8,128)(2,1)S(1)} %get-tuple-element.32), channel_id=1, source_target_pairs={{0,16},{1,17},{2,18},{3,19},{4,20},{5,21},{6,22},{7,23},{8,24},{9,... | collective-permute-start | bytes 786440 | tf_op jit(solution)/shard_map/ppermute | solution.py:331
  26.6 13.1 %collective-permute-start.1 = (bf16[2,64,768]{2,1,0:T(8,128)(2,1)S(1)}, bf16[2,64,768]{2,1,0:T(8,128)(2,1)S(1)}, u32[]{:S(2)}, u32[]{:S(2)}) collective-permute-start(bf16[2,64,768]{2,1,0:T(8,128)(2,1)S(1)} %project.7.refs_0_), channel_id=1, source_target_pairs={{0,2},{1,3},{2,0},{3,1},{4,6},{5,7},{6,4},{7,5},{8,10},{9,11},{10,... | collective-permute-start | bytes 589832 | tf_op jit(solution)/shard_map/ppermute | solution.py:331
  36.1 6.4 %collective-permute-start.9 = (bf16[64,2048]{1,0:T(8,128)(2,1)S(1)}, bf16[64,2048]{1,0:T(8,128)(2,1)S(1)}, u32[]{:S(2)}, u32[]{:S(2)}) collective-permute-start(bf16[64,2048]{1,0:T(8,128)(2,1)S(1)} %get-tuple-element.35), channel_id=1, source_target_pairs={{0,16},{1,17},{2,18},{3,19},{4,20},{5,21},{6,22},{7,23},{8,24},{9,... | collective-permute-start | bytes 786440 | tf_op jit(solution)/shard_map/ppermute | solution.py:331
  37.7 6.4 %collective-permute-start.10 = (bf16[64,2048]{1,0:T(8,128)(2,1)S(1)}, bf16[64,2048]{1,0:T(8,128)(2,1)S(1)}, u32[]{:S(2)}, u32[]{:S(2)}) collective-permute-start(bf16[64,2048]{1,0:T(8,128)(2,1)S(1)} %get-tuple-element.36), channel_id=1, source_target_pairs={{0,8},{1,9},{2,10},{3,11},{4,12},{5,13},{6,14},{7,15},{8,0},{9,1},... | collective-permute-start | bytes 786440 | tf_op jit(solution)/shard_map/ppermute | solution.py:331
  40.8 10.4 %collective-permute-start.6 = (bf16[4,64,768]{2,1,0:T(8,128)(2,1)S(1)}, bf16[4,64,768]{2,1,0:T(8,128)(2,1)S(1)}, u32[]{:S(2)}, u32[]{:S(2)}) collective-permute-start(bf16[4,64,768]{2,1,0:T(8,128)(2,1)S(1)} %project.9), channel_id=1, source_target_pairs={{0,2},{1,3},{2,0},{3,1},{4,6},{5,7},{6,4},{7,5},{8,10},{9,11},{10,... | collective-permute-start | bytes 1179656 | tf_op jit(solution)/shard_map/ppermute | solution.py:331
  44.6 8.6 %collective-permute-start.11 = (bf16[2,64,768]{2,1,0:T(8,128)(2,1)S(1)}, bf16[2,64,768]{2,1,0:T(8,128)(2,1)S(1)}, u32[]{:S(2)}, u32[]{:S(2)}) collective-permute-start(bf16[2,64,768]{2,1,0:T(8,128)(2,1)S(1)} %project.11), channel_id=1, source_target_pairs={{0,2},{1,3},{2,0},{3,1},{4,6},{5,7},{6,4},{7,5},{8,10},{9,11},{10,... | collective-permute-start | bytes 589832 | tf_op jit(solution)/shard_map/ppermute | solution.py:331
  51.3 6.1 %collective-permute-start.8 = (bf16[128,768]{1,0:T(8,128)(2,1)S(1)}, bf16[128,768]{1,0:T(8,128)(2,1)S(1)}, u32[]{:S(2)}, u32[]{:S(2)}) collective-permute-start(bf16[128,768]{1,0:T(8,128)(2,1)S(1)} %get-tuple-element.34), channel_id=1, source_target_pairs={{0,16},{1,17},{2,18},{3,19},{4,20},{5,21},{6,22},{7,23},{8,24},{9,... | collective-permute-start | bytes 589832 | tf_op jit(solution)/shard_map/ppermute | solution.py:331
  51.9 5.7 %collective-permute-start.7 = (bf16[128,768]{1,0:T(8,128)(2,1)S(1)}, bf16[128,768]{1,0:T(8,128)(2,1)S(1)}, u32[]{:S(2)}, u32[]{:S(2)}) collective-permute-start(bf16[128,768]{1,0:T(8,128)(2,1)S(1)} %get-tuple-element.33.refs_2_), channel_id=1, source_target_pairs={{0,8},{1,9},{2,10},{3,11},{4,12},{5,13},{6,14},{7,15},{8,0},{9,1},... | collective-permute-start | bytes 589832 | tf_op jit(solution)/shard_map/ppermute | solution.py:331
  53.3 7.2 %collective-permute-start.12 = (bf16[128,768]{1,0:T(8,128)(2,1)S(1)}, bf16[128,768]{1,0:T(8,128)(2,1)S(1)}, u32[]{:S(2)}, u32[]{:S(2)}) collective-permute-start(bf16[128,768]{1,0:T(8,128)(2,1)S(1)} %merge.5), channel_id=1, source_target_pairs={{0,24},{1,25},{2,26},{3,27},{4,28},{5,29},{6,30},{7,31},{8,16},{9,... | collective-permute-start | bytes 589832 | tf_op jit(solution)/shard_map/ppermute | solution.py:331
  60.7 7.7 %collective-permute-start.13 = (bf16[128,768]{1,0:T(8,128)(2,1)S(1)}, bf16[128,768]{1,0:T(8,128)(2,1)S(1)}, u32[]{:S(2)}, u32[]{:S(2)}) collective-permute-start(bf16[128,768]{1,0:T(8,128)(2,1)S(1)} %get-tuple-element.37), channel_id=1, source_target_pairs={{0,6},{1,7},{2,4},{3,5},{4,2},{5,3},{6,0},{7,1},{8,14},{9,15},{10,... | collective-permute-start | bytes 589832 | tf_op jit(solution)/shard_map/ppermute | solution.py:331
  64.3 11.4 %collective-permute-start.14 = (bf16[128,768]{1,0:T(8,128)(2,1)S(1)}, bf16[128,768]{1,0:T(8,128)(2,1)S(1)}, u32[]{:S(2)}, u32[]{:S(2)}) collective-permute-start(bf16[128,768]{1,0:T(8,128)(2,1)S(1)} %get-tuple-element.38), channel_id=1, source_target_pairs={{0,4},{1,5},{2,6},{3,7},{4,0},{5,1},{6,2},{7,3},{8,12},{9,13},{10,... | collective-permute-start | bytes 589832 | tf_op jit(solution)/shard_map/ppermute | solution.py:331
  64.3 11.4 %collective-permute-start.15 = (bf16[128,768]{1,0:T(8,128)(2,1)S(1)}, bf16[128,768]{1,0:T(8,128)(2,1)S(1)}, u32[]{:S(2)}, u32[]{:S(2)}) collective-permute-start(bf16[128,768]{1,0:T(8,128)(2,1)S(1)} %get-tuple-element.39), channel_id=1, source_target_pairs={{0,2},{1,3},{2,0},{3,1},{4,6},{5,7},{6,4},{7,5},{8,10},{9,11},{10,... | collective-permute-start | bytes 589832 | tf_op jit(solution)/shard_map/ppermute | solution.py:331
  75.8 1.8 %collective-permute-start.16 = (bf16[1,128,1536]{2,1,0:T(8,128)(2,1)S(1)}, bf16[1,128,1536]{2,1,0:T(8,128)(2,1)S(1)}, u32[]{:S(2)}, u32[]{:S(2)}) collective-permute-start(bf16[1,128,1536]{2,1,0:T(8,128)(2,1)S(1)} %last.1), channel_id=1, source_target_pairs={{0,1},{1,0},{2,3},{3,2},{4,5},{5,4},{6,7},{7,6},{8,9},{9,8},{10,11... | collective-permute-start | bytes 1179656 | tf_op jit(solution)/shard_map/ppermute | solution.py:331

commit v5 on v4

--- a/solution.py
+++ b/solution.py
@@ -153,20 +153,18 @@
 
 
 def finish_kernel(
-    inside_ref, factor_ref, reach_ref, doc_ref, query_ref, state_ref, *out_refs
+    first_row, inside_ref, factor_ref, reach_ref, doc_ref, query_ref, state_ref, out_ref
 ):
     heads = reach_ref.shape[1]
-    part = out_refs[0].shape[0]
+    here = slice(first_row, first_row + out_ref.shape[0])
     incoming = state_ref[heads * DH :, :].astype(jnp.float32)[0:1, :]
-    reached = (doc_ref[...] == incoming).astype(jnp.float32)
+    reached = (doc_ref[here, :] == incoming).astype(jnp.float32)
     for h in range(heads):
         span = slice(h * DH, (h + 1) * DH)
-        reaches = reach_ref[:, h : h + 1] * reached
-        attended = inside_ref[:, span] + reaches * dot(query_ref[:, span], state_ref[span, :])
+        reaches = reach_ref[here, h : h + 1] * reached
+        attended = inside_ref[here, span] + reaches * dot(query_ref[here, span], state_ref[span, :])
         scaling = lax.rsqrt(jnp.mean(attended * attended, axis=-1, keepdims=True) + 1e-06)
-        normed = (attended * scaling * factor_ref[:, span]).astype(jnp.bfloat16)
-        for i, out_ref in enumerate(out_refs):
-            out_ref[:, span] = normed[i * part : (i + 1) * part]
+        out_ref[:, span] = (attended * scaling * factor_ref[here, span]).astype(jnp.bfloat16)
 
 
 def project_kernel(other, *refs):
@@ -183,9 +181,8 @@
             out_ref[j, :, start : start + wide] = result[j * rows : (j + 1) * rows]
 
 
-def hold_kernel(upper_ref, lower_ref, *refs):
-    for source_ref, out_ref in zip((upper_ref, lower_ref), refs[-2:]):
-        out_ref[...] = source_ref[...]
+def hold_kernel(source_ref, *refs):
+    refs[-1][...] = source_ref[...]
 
 
 def merge_kernel(layout, *refs):
@@ -308,11 +305,13 @@
     incoming = entering(state, 0)
 
     part = rows // 2
-    normed = call(
-        finish_kernel,
-        (jax.ShapeDtypeStruct((part, width), jnp.bfloat16),) * 2,
-        "finish",
-    )(inside, factor, reach, docs, query, incoming)
+    piece = jax.ShapeDtypeStruct((part, width), jnp.bfloat16)
+
+    def finish(first_row):
+        kernel = functools.partial(finish_kernel, first_row)
+        return call(kernel, piece, "finish")(inside, factor, reach, docs, query, incoming)
+
+    normed = [finish(0), finish(part)]
 
     if n_ctx != 4 or n_head != 4 or n_pipe != 2:
         normed = lax.all_gather(jnp.concatenate(normed, axis=0), "ctx", axis=0, tiled=True)
@@ -349,27 +348,25 @@
         kernel = functools.partial(merge_kernel, layout)
         return call(kernel, (single,) * len(layout), "merge", in_specs=specs)(*sums, *after)
 
+    def hold(array, *after):
+        specs = [VMEM] + [ANY] * len(after)
+        return call(hold_kernel, piece, "hold", in_specs=specs)(array, *after)
+
     upper, lower = normed
-    upper_1, lower_2 = swapped(upper, 1), swapped(lower, 2)
     whole = (((0, 0), (0, 1)),)
-
-    def hold(pair, after):
-        shape = jax.ShapeDtypeStruct((part, width), jnp.bfloat16)
-        specs = [VMEM] * 2 + [ANY] * len(after)
-        return call(hold_kernel, (shape,) * 2, "hold", in_specs=specs)(*pair, *after)
-
+    upper_1, upper_2 = swapped(upper, 1), swapped(upper, 2)
     own_send = project((upper, lower), 1)
     own = merge(whole, (project((upper, lower), 0), partner(own_send)))
-    upper, lower = hold((upper, lower), (own_send,))
-    lower_1, upper_2 = swapped(lower, 1), swapped(upper, 2)
-    held = hold((upper_1, lower_2), (lower_1, upper_2))
-    beside = (upper_1, lower_1, upper_2, lower_2)
-    beside = merge(
-        (((0, 0), (0, 1)), ((0, 2), (0, 3))),
-        (project(beside, 0), partner(project(beside, 1, own))),
-    )
-    across = (swapped(held[0], 2), swapped(held[1], 1))
-    across = merge(whole, (project(across, 0), partner(project(across, 1))), beside[:1])
+    lower = hold(lower, own_send)
+    lower_1, lower_2 = swapped(lower, 1), swapped(lower, 2)
+    near = (upper_1, upper_2)
+    near_sum = (project(near, 0), partner(project(near, 1, own)))
+    later = (lower_1, lower_2)
+    later_sum = (project(later, 0), partner(project(later, 1, near_sum[1:])))
+    beside = merge((((0, 0), (1, 0)), ((0, 1), (1, 1))), near_sum + later_sum)
+    across = (swapped(hold(upper_1, lower_1, lower_2), 2), swapped(lower_2, 1))
+    across_sum = (project(across, 0), partner(project(across, 1, beside[:1])))
+    across = merge(whole, across_sum, beside[:1])
     blocks = [
         swapped(block, k) if k else block for k, block in enumerate((*own, *beside, *across))
     ]

time: 78.6 us -> 78.5 us (level)
  Pallas kernels: 13.3 us -> 14.7 us
  waiting for transfers between devices: 38.5 us -> 37.1 us
    ppermute x16 -> x17, waiting for transfers between devices: 31.5 us -> 30.1 us  [moved(): lax.ppermute(array, names, [(place[spot], place[target(*spot)]) for spot...]
    pallas_call x3 -> x4, Pallas kernels: 1.66 us -> 2.63 us  [the longest x2 2.59 us: finish(): call(kernel, piece, 'finish')(inside, factor, reach, docs, query, incoming)]
    pallas_call x6 -> x8, Pallas kernels: 4.42 us -> 4.82 us  [project(): call(kernel, shape, 'project', in_specs=specs)(*picked, weight, *after)]
    ppermute x16 -> x17, starting transfers between devices: 20.8 us -> 20.7 us  [moved(): lax.ppermute(array, names, [(place[spot], place[target(*spot)]) for spot...]
  transfers between devices with their start and end apart: 17 -> 18, of which waited for: 15 -> 12; matrix products, arithmetic and copies ran while one was open for 0% -> 0% of each run, Pallas kernels for 11% -> 13%
where the time goes in v5:
time: 78.5 us; the launch traced here: 78.3 us
  waiting for transfers between devices  37.1 us (47%)
  starting transfers between devices  25.6 us (33%)
  Pallas kernels  14.7 us (19%)
    ppermute x17, waiting for transfers between devices, moved(): lax.ppermute(array, names, [(place[spot], place[target(*spot)]) for spot...  30.1 us
    ppermute x17, starting transfers between devices, moved(): lax.ppermute(array, names, [(place[spot], place[target(*spot)]) for spot...  20.7 us
    ppermute x1, waiting for transfers between devices, from_before(): return lax.ppermute(array, 'ctx', [(i, i + by) for i in range(n_ctx - by)])  6.98 us
    ppermute x1, starting transfers between devices, from_before(): return lax.ppermute(array, 'ctx', [(i, i + by) for i in range(n_ctx - by)])  4.87 us
    pallas_call x8, Pallas kernels, project(): call(kernel, shape, 'project', in_specs=specs)(*picked, weight, *after)  4.82 us
    pallas_call x1, Pallas kernels, on_device(): call(inside_kernel, (pltpu.VMEM((rows, width), jnp.float32), pltpu.VMEM((...  4.23 us
    pallas_call x2, Pallas kernels, finish(): call(kernel, piece, 'finish')(inside, factor, reach, docs, query, incoming)  2.59 us
    pallas_call x1, Pallas kernels, on_device(): call(state_kernel, state_shape, 'shard_state', in_specs=[HBM] * 4, scratc...  2.58 us
  transfers between devices with their start and end apart: 18, of which 12 were waited for; matrix products, arithmetic and copies ran while one was open for 0% of the time, Pallas kernels for 13%

profile of v5, /device:TPU:0, one launch (start us, length us, event | category | flops | bytes accessed | tf_op | source)
XLA Modules:
  0.0 78.3 jit_solution(8762650177067753187)
XLA Ops:
  0.0 2.6 %shard_state.1 = bf16[2064,128]{1,0:T(8,128)(2,1)S(1)} custom-call(bf16[1,128,2048]{2,1,0:T(8,128)(2,1)} %key_hbm.3, bf16[1,128,2048]{2,1,0:T(8,128)(2,1)} %value_hbm.3, f32[1,16,128]{2,1,0:T(8,128)} %bitcast.1, s32[1,128]{1,0:T(1,128)} %doc_hbm.3), custom_call_target="tpu_custom_call" | custom-call | flops 1 | bytes 1 | tf_op jit(solution)/shard_map/shard_state/pallas_call | solution.py:251
  2.6 4.9 %collective-permute-start = (bf16[2064,128]{1,0:T(8,128)(2,1)S(1)}, bf16[2064,128]{1,0:T(8,128)(2,1)S(1)}, u32[]{:S(2)}, u32[]{:S(2)}) collective-permute-start(bf16[2064,128]{1,0:T(8,128)(2,1)S(1)} %shard_state.1), channel_id=1, source_target_pairs={{0,8},{8,16},{16,24},{1,9},{9,17},{17,25},{2,10},{10,18},{18,26},{... | collective-permute-start | bytes 1585160 | tf_op jit(solution)/shard_map/ppermute | solution.py:247
  7.5 4.2 %inside.1 = (f32[128,2048]{1,0:T(8,128)S(1)}, f32[128,2048]{1,0:T(8,128)S(1)}, f32[128,16]{1,0:T(8,128)S(1)}, f32[128,128]{1,0:T(8,128)S(1)}, bf16[128,2048]{1,0...) custom-call(bf16[1,128,2048]{2,1,0:T(8,128)(2,1)} %query_hbm.1, bf16[1,128,2048]{2,1,0:T(8,128)(2,1)} %key_hbm.3, ...), custom_call_target="tpu_custom_call" | custom-call | flops 1 | bytes 1 | tf_op jit(solution)/shard_map/inside/pallas_call | solution.py:283
  11.7 7.0 %collective-permute-done.state_ref = bf16[2064,128]{1,0:T(8,128)(2,1)S(1)} collective-permute-done((bf16[2064,128]{1,0:T(8,128)(2,1)S(1)}, bf16[2064,128]{1,0:T(8,128)(2,1)S(1)}, u32[]{:S(2)}, u32[]{:S(2)}) %collective-permute-start) | collective-permute-done | bytes 528416 | tf_op jit(solution)/shard_map/ppermute | solution.py:247
  18.7 1.3 %finish.2.refs_0_ = bf16[64,2048]{1,0:T(8,128)(2,1)S(1)} custom-call(f32[128,2048]{1,0:T(8,128)S(1)} %get-tuple-element.17.inside_ref, f32[128,2048]{1,0:T(8,128)S(1)} %get-tuple-element.18.factor_ref, f32[128,16]{1,0:T(8,128)S(1)} %get-tuple-element.19.reach_ref, f32[128,128]{1,0:T(8,128)S(1)} %get-tuple-element.20.doc_ref, ...), custom_call_target="tpu_custom_call" | custom-call | flops 1 | bytes 1 | tf_op jit(solution)/shard_map/finish/pallas_call | solution.py:312
  20.0 3.5 %collective-permute-start.3 = (bf16[64,2048]{1,0:T(8,128)(2,1)S(1)}, bf16[64,2048]{1,0:T(8,128)(2,1)S(1)}, u32[]{:S(2)}, u32[]{:S(2)}) collective-permute-start(bf16[64,2048]{1,0:T(8,128)(2,1)S(1)} %finish.2.refs_0_), channel_id=1, source_target_pairs={{0,16},{1,17},{2,18},{3,19},{4,20},{5,21},{6,22},{7,23},{8,24},{9,... | collective-permute-start | bytes 786440 | tf_op jit(solution)/shard_map/ppermute | solution.py:330
  24.1 1.3 %finish.3.refs_1_.source_ref = bf16[64,2048]{1,0:T(8,128)(2,1)S(1)} custom-call(f32[128,2048]{1,0:T(8,128)S(1)} %get-tuple-element.17.inside_ref, f32[128,2048]{1,0:T(8,128)S(1)} %get-tuple-element.18.factor_ref, f32[128,16]{1,0:T(8,128)S(1)} %get-tuple-element.19.reach_ref, f32[128,128]{1,0:T(8,128)S(1)} %get-tuple-element.20.doc_ref, ...), custom_call_target="tpu_custom_call" | custom-call | flops 1 | bytes 1 | tf_op jit(solution)/shard_map/finish/pallas_call | solution.py:312
  26.0 1.6 %collective-permute-start.1 = (bf16[2,64,768]{2,1,0:T(8,128)(2,1)S(1)}, bf16[2,64,768]{2,1,0:T(8,128)(2,1)S(1)}, u32[]{:S(2)}, u32[]{:S(2)}) collective-permute-start(bf16[2,64,768]{2,1,0:T(8,128)(2,1)S(1)} %project.9.refs_0_), channel_id=1, source_target_pairs={{0,2},{1,3},{2,0},{3,1},{4,6},{5,7},{6,4},{7,5},{8,10},{9,11},{10,... | collective-permute-start | bytes 589832 | tf_op jit(solution)/shard_map/ppermute | solution.py:330
  28.2 1.0 %collective-permute-start.5 = (bf16[64,2048]{1,0:T(8,128)(2,1)S(1)}, bf16[64,2048]{1,0:T(8,128)(2,1)S(1)}, u32[]{:S(2)}, u32[]{:S(2)}) collective-permute-start(bf16[64,2048]{1,0:T(8,128)(2,1)S(1)} %hold.2), channel_id=1, source_target_pairs={{0,8},{1,9},{2,10},{3,11},{4,12},{5,13},{6,14},{7,15},{8,0},{9,1},... | collective-permute-start | bytes 786440 | tf_op jit(solution)/shard_map/ppermute | solution.py:330
  29.8 1.9 %collective-permute-done.1.refs_1_ = bf16[2,64,768]{2,1,0:T(8,128)(2,1)S(1)} collective-permute-done((bf16[2,64,768]{2,1,0:T(8,128)(2,1)S(1)}, bf16[2,64,768]{2,1,0:T(8,128)(2,1)S(1)}, u32[]{:S(2)}, u32[]{:S(2)}) %collective-permute-start.1) | collective-permute-done | bytes 196640 | tf_op jit(solution)/shard_map/ppermute | solution.py:330
  32.6 2.4 %collective-permute-start.4 = (bf16[2,64,768]{2,1,0:T(8,128)(2,1)S(1)}, bf16[2,64,768]{2,1,0:T(8,128)(2,1)S(1)}, u32[]{:S(2)}, u32[]{:S(2)}) collective-permute-start(bf16[2,64,768]{2,1,0:T(8,128)(2,1)S(1)} %project.11), channel_id=1, source_target_pairs={{0,2},{1,3},{2,0},{3,1},{4,6},{5,7},{6,4},{7,5},{8,10},{9,11},{10,... | collective-permute-start | bytes 589832 | tf_op jit(solution)/shard_map/ppermute | solution.py:330
  35.5 1.5 %collective-permute-done.5.refs_0_ = bf16[64,2048]{1,0:T(8,128)(2,1)S(1)} collective-permute-done((bf16[64,2048]{1,0:T(8,128)(2,1)S(1)}, bf16[64,2048]{1,0:T(8,128)(2,1)S(1)}, u32[]{:S(2)}, u32[]{:S(2)}) %collective-permute-start.5) | collective-permute-done | bytes 262176 | tf_op jit(solution)/shard_map/ppermute | solution.py:330
  37.2 1.9 %collective-permute-done.4.refs_3_.refs_1_ = bf16[2,64,768]{2,1,0:T(8,128)(2,1)S(1)} collective-permute-done((bf16[2,64,768]{2,1,0:T(8,128)(2,1)S(1)}, bf16[2,64,768]{2,1,0:T(8,128)(2,1)S(1)}, u32[]{:S(2)}, u32[]{:S(2)}) %collective-permute-start.4) | collective-permute-done | bytes 196640 | tf_op jit(solution)/shard_map/ppermute | solution.py:330
  39.7 2.5 %collective-permute-start.7 = (bf16[2,64,768]{2,1,0:T(8,128)(2,1)S(1)}, bf16[2,64,768]{2,1,0:T(8,128)(2,1)S(1)}, u32[]{:S(2)}, u32[]{:S(2)}) collective-permute-start(bf16[2,64,768]{2,1,0:T(8,128)(2,1)S(1)} %project.13), channel_id=1, source_target_pairs={{0,2},{1,3},{2,0},{3,1},{4,6},{5,7},{6,4},{7,5},{8,10},{9,11},{10,... | collective-permute-start | bytes 589832 | tf_op jit(solution)/shard_map/ppermute | solution.py:330
  43.5 3.9 %collective-permute-done.7.refs_3_ = bf16[2,64,768]{2,1,0:T(8,128)(2,1)S(1)} collective-permute-done((bf16[2,64,768]{2,1,0:T(8,128)(2,1)S(1)}, bf16[2,64,768]{2,1,0:T(8,128)(2,1)S(1)}, u32[]{:S(2)}, u32[]{:S(2)}) %collective-permute-start.7) | collective-permute-done | bytes 196640 | tf_op jit(solution)/shard_map/ppermute | solution.py:330
  48.1 2.4 %collective-permute-start.12 = (bf16[2,64,768]{2,1,0:T(8,128)(2,1)S(1)}, bf16[2,64,768]{2,1,0:T(8,128)(2,1)S(1)}, u32[]{:S(2)}, u32[]{:S(2)}) collective-permute-start(bf16[2,64,768]{2,1,0:T(8,128)(2,1)S(1)} %project.15), channel_id=1, source_target_pairs={{0,2},{1,3},{2,0},{3,1},{4,6},{5,7},{6,4},{7,5},{8,10},{9,11},{10,... | collective-permute-start | bytes 589832 | tf_op jit(solution)/shard_map/ppermute | solution.py:330
  51.2 2.9 %collective-permute-done.12.refs_1_ = bf16[2,64,768]{2,1,0:T(8,128)(2,1)S(1)} collective-permute-done((bf16[2,64,768]{2,1,0:T(8,128)(2,1)S(1)}, bf16[2,64,768]{2,1,0:T(8,128)(2,1)S(1)}, u32[]{:S(2)}, u32[]{:S(2)}) %collective-permute-start.12) | collective-permute-done | bytes 196640 | tf_op jit(solution)/shard_map/ppermute | solution.py:330
  54.7 2.1 %collective-permute-done.9.refs_2_ = bf16[128,768]{1,0:T(8,128)(2,1)S(1)} collective-permute-done((bf16[128,768]{1,0:T(8,128)(2,1)S(1)}, bf16[128,768]{1,0:T(8,128)(2,1)S(1)}, u32[]{:S(2)}, u32[]{:S(2)}) %collective-permute-start.9) | collective-permute-done | bytes 196640 | tf_op jit(solution)/shard_map/ppermute | solution.py:330
  56.9 3.9 %collective-permute-done.13.refs_3_ = bf16[128,768]{1,0:T(8,128)(2,1)S(1)} collective-permute-done((bf16[128,768]{1,0:T(8,128)(2,1)S(1)}, bf16[128,768]{1,0:T(8,128)(2,1)S(1)}, u32[]{:S(2)}, u32[]{:S(2)}) %collective-permute-start.13) | collective-permute-done | bytes 196640 | tf_op jit(solution)/shard_map/ppermute | solution.py:330
  60.9 4.1 %collective-permute-start.14 = (bf16[128,768]{1,0:T(8,128)(2,1)S(1)}, bf16[128,768]{1,0:T(8,128)(2,1)S(1)}, u32[]{:S(2)}, u32[]{:S(2)}) collective-permute-start(bf16[128,768]{1,0:T(8,128)(2,1)S(1)} %get-tuple-element.25), channel_id=1, source_target_pairs={{0,6},{1,7},{2,4},{3,5},{4,2},{5,3},{6,0},{7,1},{8,14},{9,15},{10,... | collective-permute-start | bytes 589832 | tf_op jit(solution)/shard_map/ppermute | solution.py:330
  65.7 3.1 %collective-permute-done.14.refs_0_ = bf16[128,768]{1,0:T(8,128)(2,1)S(1)} collective-permute-done((bf16[128,768]{1,0:T(8,128)(2,1)S(1)}, bf16[128,768]{1,0:T(8,128)(2,1)S(1)}, u32[]{:S(2)}, u32[]{:S(2)}) %collective-permute-start.14) | collective-permute-done | bytes 196640 | tf_op jit(solution)/shard_map/ppermute | solution.py:330
  68.8 6.9 %collective-permute-done.15.refs_1_ = bf16[128,768]{1,0:T(8,128)(2,1)S(1)} collective-permute-done((bf16[128,768]{1,0:T(8,128)(2,1)S(1)}, bf16[128,768]{1,0:T(8,128)(2,1)S(1)}, u32[]{:S(2)}, u32[]{:S(2)}) %collective-permute-start.15) | collective-permute-done | bytes 196640 | tf_op jit(solution)/shard_map/ppermute | solution.py:330
  75.8 1.7 %collective-permute-done.17 = bf16[1,128,1536]{2,1,0:T(8,128)(2,1)S(1)} collective-permute-done((bf16[1,128,1536]{2,1,0:T(8,128)(2,1)S(1)}, bf16[1,128,1536]{2,1,0:T(8,128)(2,1)S(1)}, u32[]{:S(2)}, u32[]{:S(2)}) %collective-permute-start.17) | collective-permute-done | bytes 393248 | tf_op jit(solution)/shard_map/ppermute | solution.py:330
  77.6 0.7 copy.10
  (32 shorter events, 8.7 us)
Async XLA Ops:
  2.6 16.1 %collective-permute-start = (bf16[2064,128]{1,0:T(8,128)(2,1)S(1)}, bf16[2064,128]{1,0:T(8,128)(2,1)S(1)}, u32[]{:S(2)}, u32[]{:S(2)}) collective-permute-start(bf16[2064,128]{1,0:T(8,128)(2,1)S(1)} %shard_state.1), channel_id=1, source_target_pairs={{0,8},{8,16},{16,24},{1,9},{9,17},{17,25},{2,10},{10,18},{18,26},{... | collective-permute-start | bytes 1585160 | tf_op jit(solution)/shard_map/ppermute | solution.py:247
  20.0 11.8 %collective-permute-start.3 = (bf16[64,2048]{1,0:T(8,128)(2,1)S(1)}, bf16[64,2048]{1,0:T(8,128)(2,1)S(1)}, u32[]{:S(2)}, u32[]{:S(2)}) collective-permute-start(bf16[64,2048]{1,0:T(8,128)(2,1)S(1)} %finish.2.refs_0_), channel_id=1, source_target_pairs={{0,16},{1,17},{2,18},{3,19},{4,20},{5,21},{6,22},{7,23},{8,24},{9,... | collective-permute-start | bytes 786440 | tf_op jit(solution)/shard_map/ppermute | solution.py:330
  23.5 8.5 %collective-permute-start.2 = (bf16[64,2048]{1,0:T(8,128)(2,1)S(1)}, bf16[64,2048]{1,0:T(8,128)(2,1)S(1)}, u32[]{:S(2)}, u32[]{:S(2)}) collective-permute-start(bf16[64,2048]{1,0:T(8,128)(2,1)S(1)} %finish.2.refs_0_), channel_id=1, source_target_pairs={{0,8},{1,9},{2,10},{3,11},{4,12},{5,13},{6,14},{7,15},{8,0},{9,1},... | collective-permute-start | bytes 786440 | tf_op jit(solution)/shard_map/ppermute | solution.py:330
  26.0 5.7 %collective-permute-start.1 = (bf16[2,64,768]{2,1,0:T(8,128)(2,1)S(1)}, bf16[2,64,768]{2,1,0:T(8,128)(2,1)S(1)}, u32[]{:S(2)}, u32[]{:S(2)}) collective-permute-start(bf16[2,64,768]{2,1,0:T(8,128)(2,1)S(1)} %project.9.refs_0_), channel_id=1, source_target_pairs={{0,2},{1,3},{2,0},{3,1},{4,6},{5,7},{6,4},{7,5},{8,10},{9,11},{10,... | collective-permute-start | bytes 589832 | tf_op jit(solution)/shard_map/ppermute | solution.py:330
  27.6 7.3 %collective-permute-start.6 = (bf16[64,2048]{1,0:T(8,128)(2,1)S(1)}, bf16[64,2048]{1,0:T(8,128)(2,1)S(1)}, u32[]{:S(2)}, u32[]{:S(2)}) collective-permute-start(bf16[64,2048]{1,0:T(8,128)(2,1)S(1)} %hold.2), channel_id=1, source_target_pairs={{0,16},{1,17},{2,18},{3,19},{4,20},{5,21},{6,22},{7,23},{8,24},{9,... | collective-permute-start | bytes 786440 | tf_op jit(solution)/shard_map/ppermute | solution.py:330
  28.2 8.8 %collective-permute-start.5 = (bf16[64,2048]{1,0:T(8,128)(2,1)S(1)}, bf16[64,2048]{1,0:T(8,128)(2,1)S(1)}, u32[]{:S(2)}, u32[]{:S(2)}) collective-permute-start(bf16[64,2048]{1,0:T(8,128)(2,1)S(1)} %hold.2), channel_id=1, source_target_pairs={{0,8},{1,9},{2,10},{3,11},{4,12},{5,13},{6,14},{7,15},{8,0},{9,1},... | collective-permute-start | bytes 786440 | tf_op jit(solution)/shard_map/ppermute | solution.py:330
  32.6 6.5 %collective-permute-start.4 = (bf16[2,64,768]{2,1,0:T(8,128)(2,1)S(1)}, bf16[2,64,768]{2,1,0:T(8,128)(2,1)S(1)}, u32[]{:S(2)}, u32[]{:S(2)}) collective-permute-start(bf16[2,64,768]{2,1,0:T(8,128)(2,1)S(1)} %project.11), channel_id=1, source_target_pairs={{0,2},{1,3},{2,0},{3,1},{4,6},{5,7},{6,4},{7,5},{8,10},{9,11},{10,... | collective-permute-start | bytes 589832 | tf_op jit(solution)/shard_map/ppermute | solution.py:330
  35.0 12.4 %collective-permute-start.11 = (bf16[64,2048]{1,0:T(8,128)(2,1)S(1)}, bf16[64,2048]{1,0:T(8,128)(2,1)S(1)}, u32[]{:S(2)}, u32[]{:S(2)}) collective-permute-start(bf16[64,2048]{1,0:T(8,128)(2,1)S(1)} %collective-permute-done.6.refs_1_), channel_id=1, source_target_pairs={{0,8},{1,9},{2,10},{3,11},{4,12},{5,13},{6,14},{7,15},{8,0},{9,1},... | collective-permute-start | bytes 786440 | tf_op jit(solution)/shard_map/ppermute | solution.py:330
  37.1 10.4 %collective-permute-start.10 = (bf16[64,2048]{1,0:T(8,128)(2,1)S(1)}, bf16[64,2048]{1,0:T(8,128)(2,1)S(1)}, u32[]{:S(2)}, u32[]{:S(2)}) collective-permute-start(bf16[64,2048]{1,0:T(8,128)(2,1)S(1)} %hold.3), channel_id=1, source_target_pairs={{0,16},{1,17},{2,18},{3,19},{4,20},{5,21},{6,22},{7,23},{8,24},{9,... | collective-permute-start | bytes 786440 | tf_op jit(solution)/shard_map/ppermute | solution.py:330
  39.7 7.6 %collective-permute-start.7 = (bf16[2,64,768]{2,1,0:T(8,128)(2,1)S(1)}, bf16[2,64,768]{2,1,0:T(8,128)(2,1)S(1)}, u32[]{:S(2)}, u32[]{:S(2)}) collective-permute-start(bf16[2,64,768]{2,1,0:T(8,128)(2,1)S(1)} %project.13), channel_id=1, source_target_pairs={{0,2},{1,3},{2,0},{3,1},{4,6},{5,7},{6,4},{7,5},{8,10},{9,11},{10,... | collective-permute-start | bytes 589832 | tf_op jit(solution)/shard_map/ppermute | solution.py:330
  48.1 6.0 %collective-permute-start.12 = (bf16[2,64,768]{2,1,0:T(8,128)(2,1)S(1)}, bf16[2,64,768]{2,1,0:T(8,128)(2,1)S(1)}, u32[]{:S(2)}, u32[]{:S(2)}) collective-permute-start(bf16[2,64,768]{2,1,0:T(8,128)(2,1)S(1)} %project.15), channel_id=1, source_target_pairs={{0,2},{1,3},{2,0},{3,1},{4,6},{5,7},{6,4},{7,5},{8,10},{9,11},{10,... | collective-permute-start | bytes 589832 | tf_op jit(solution)/shard_map/ppermute | solution.py:330
  51.1 5.8 %collective-permute-start.8 = (bf16[128,768]{1,0:T(8,128)(2,1)S(1)}, bf16[128,768]{1,0:T(8,128)(2,1)S(1)}, u32[]{:S(2)}, u32[]{:S(2)}) collective-permute-start(bf16[128,768]{1,0:T(8,128)(2,1)S(1)} %get-tuple-element.23.refs_3_.refs_2_), channel_id=1, source_target_pairs={{0,8},{1,9},{2,10},{3,11},{4,12},{5,13},{6,14},{7,15},{8,0},{9,1},... | collective-permute-start | bytes 589832 | tf_op jit(solution)/shard_map/ppermute | solution.py:330
  51.1 5.7 %collective-permute-start.9 = (bf16[128,768]{1,0:T(8,128)(2,1)S(1)}, bf16[128,768]{1,0:T(8,128)(2,1)S(1)}, u32[]{:S(2)}, u32[]{:S(2)}) collective-permute-start(bf16[128,768]{1,0:T(8,128)(2,1)S(1)} %get-tuple-element.24), channel_id=1, source_target_pairs={{0,16},{1,17},{2,18},{3,19},{4,20},{5,21},{6,22},{7,23},{8,24},{9,... | collective-permute-start | bytes 589832 | tf_op jit(solution)/shard_map/ppermute | solution.py:330
  54.2 6.6 %collective-permute-start.13 = (bf16[128,768]{1,0:T(8,128)(2,1)S(1)}, bf16[128,768]{1,0:T(8,128)(2,1)S(1)}, u32[]{:S(2)}, u32[]{:S(2)}) collective-permute-start(bf16[128,768]{1,0:T(8,128)(2,1)S(1)} %merge.5), channel_id=1, source_target_pairs={{0,24},{1,25},{2,26},{3,27},{4,28},{5,29},{6,30},{7,31},{8,16},{9,... | collective-permute-start | bytes 589832 | tf_op jit(solution)/shard_map/ppermute | solution.py:330
  60.9 7.9 %collective-permute-start.14 = (bf16[128,768]{1,0:T(8,128)(2,1)S(1)}, bf16[128,768]{1,0:T(8,128)(2,1)S(1)}, u32[]{:S(2)}, u32[]{:S(2)}) collective-permute-start(bf16[128,768]{1,0:T(8,128)(2,1)S(1)} %get-tuple-element.25), channel_id=1, source_target_pairs={{0,6},{1,7},{2,4},{3,5},{4,2},{5,3},{6,0},{7,1},{8,14},{9,15},{10,... | collective-permute-start | bytes 589832 | tf_op jit(solution)/shard_map/ppermute | solution.py:330
  65.0 10.6 %collective-permute-start.15 = (bf16[128,768]{1,0:T(8,128)(2,1)S(1)}, bf16[128,768]{1,0:T(8,128)(2,1)S(1)}, u32[]{:S(2)}, u32[]{:S(2)}) collective-permute-start(bf16[128,768]{1,0:T(8,128)(2,1)S(1)} %get-tuple-element.26), channel_id=1, source_target_pairs={{0,4},{1,5},{2,6},{3,7},{4,0},{5,1},{6,2},{7,3},{8,12},{9,13},{10,... | collective-permute-start | bytes 589832 | tf_op jit(solution)/shard_map/ppermute | solution.py:330
  65.0 10.6 %collective-permute-start.16 = (bf16[128,768]{1,0:T(8,128)(2,1)S(1)}, bf16[128,768]{1,0:T(8,128)(2,1)S(1)}, u32[]{:S(2)}, u32[]{:S(2)}) collective-permute-start(bf16[128,768]{1,0:T(8,128)(2,1)S(1)} %get-tuple-element.27), channel_id=1, source_target_pairs={{0,2},{1,3},{2,0},{3,1},{4,6},{5,7},{6,4},{7,5},{8,10},{9,11},{10,... | collective-permute-start | bytes 589832 | tf_op jit(solution)/shard_map/ppermute | solution.py:330
  75.8 1.8 %collective-permute-start.17 = (bf16[1,128,1536]{2,1,0:T(8,128)(2,1)S(1)}, bf16[1,128,1536]{2,1,0:T(8,128)(2,1)S(1)}, u32[]{:S(2)}, u32[]{:S(2)}) collective-permute-start(bf16[1,128,1536]{2,1,0:T(8,128)(2,1)S(1)} %last.1), channel_id=1, source_target_pairs={{0,1},{1,0},{2,3},{3,2},{4,5},{5,4},{6,7},{7,6},{8,9},{9,8},{10,11... | collective-permute-start | bytes 1179656 | tf_op jit(solution)/shard_map/ppermute | solution.py:330

commit v6 on v4

--- a/solution.py
+++ b/solution.py
@@ -103,7 +103,6 @@
     weight_hbm,
     out_ref,
     factor_ref,
-    reach_ref,
     doc_out_ref,
     query_ref,
     weight_ref,
@@ -128,7 +127,7 @@
         copy.wait()
     heads, rows = rate_ref.shape
     columns, across = running_sums(rate_ref[...])
-    reach_ref[...] = jnp.exp(columns)
+    reach = jnp.exp(columns)
     doc_across = jnp.broadcast_to(doc_ref[...].astype(jnp.float32) + 1.0, (rows, rows))
     doc_out_ref[...] = doc_across.T
     allowed = (
@@ -144,6 +143,8 @@
         scores = dot(query_ref[:, span], key_ref[:, span], ((1,), (1,)))
         mixed = (scores * weights).astype(jnp.bfloat16)
         out_ref[:, span] = dot(mixed, value_ref[:, span])
+        reached = query_ref[:, span].astype(jnp.float32) * reach[:, h : h + 1]
+        query_ref[:, span] = reached.astype(jnp.bfloat16)
     copies[6].wait()
     for h in range(heads):
         span = slice(h * DH, (h + 1) * DH)
@@ -152,19 +153,18 @@
     copies[7].wait()
 
 
-def finish_kernel(
-    inside_ref, factor_ref, reach_ref, doc_ref, query_ref, state_ref, *out_refs
-):
-    heads = reach_ref.shape[1]
+def finish_kernel(inside_ref, factor_ref, doc_ref, query_ref, state_ref, *out_refs):
+    width = inside_ref.shape[1]
     part = out_refs[0].shape[0]
-    incoming = state_ref[heads * DH :, :].astype(jnp.float32)[0:1, :]
+    incoming = state_ref[width:, :].astype(jnp.float32)[0:1, :]
     reached = (doc_ref[...] == incoming).astype(jnp.float32)
-    for h in range(heads):
-        span = slice(h * DH, (h + 1) * DH)
-        reaches = reach_ref[:, h : h + 1] * reached
-        attended = inside_ref[:, span] + reaches * dot(query_ref[:, span], state_ref[span, :])
-        scaling = lax.rsqrt(jnp.mean(attended * attended, axis=-1, keepdims=True) + 1e-06)
-        normed = (attended * scaling * factor_ref[:, span]).astype(jnp.bfloat16)
+    average = jnp.full((DH, DH), 1.0 / DH, jnp.bfloat16)
+    for start in range(0, width, DH):
+        span = slice(start, start + DH)
+        attended = inside_ref[:, span] + reached * dot(query_ref[:, span], state_ref[span, :])
+        mean = dot((attended * attended).astype(jnp.bfloat16), average)
+        scaling = lax.rsqrt(mean + 1e-06) * factor_ref[:, span]
+        normed = (attended * scaling).astype(jnp.bfloat16)
         for i, out_ref in enumerate(out_refs):
             out_ref[:, span] = normed[i * part : (i + 1) * part]
 
@@ -199,14 +199,18 @@
 
 
 def pick_kernel(*refs):
-    block_refs, out_refs = refs[: len(refs) // 2], refs[len(refs) // 2 :]
+    count = lax.axis_size("head")
+    block_refs, out_refs = refs[: -count], refs[-count:]
     at = lax.axis_index("ctx") ^ lax.axis_index("head")
     for m, out_ref in enumerate(out_refs):
-        for j, block_ref in enumerate(block_refs):
+        for j in range(count):
 
             @pl.when((at ^ m) == j)
-            def _(out_ref=out_ref, block_ref=block_ref):
-                out_ref[...] = block_ref[...]
+            def _(out_ref=out_ref, j=j):
+                if j < count - 1:
+                    out_ref[...] = block_refs[j][...]
+                else:
+                    out_ref[...] = jnp.concatenate([ref[...] for ref in block_refs[j:]], axis=0)
 
 
 def last_kernel(*refs):
@@ -283,12 +287,11 @@
             incoming = jnp.concatenate([total, incoming[wide:]], axis=0)
         return incoming
 
-    inside, factor, reach, docs, query, weight = call(
+    inside, factor, docs, query, weight = call(
         inside_kernel,
         (
             pltpu.VMEM((rows, width), jnp.float32),
             pltpu.VMEM((rows, width), jnp.float32),
-            pltpu.VMEM((rows, heads), jnp.float32),
             pltpu.VMEM((rows, DH), jnp.float32),
             pltpu.VMEM((rows, width), jnp.bfloat16),
             pltpu.VMEM((width, columns), jnp.bfloat16),
@@ -312,7 +315,7 @@
         finish_kernel,
         (jax.ShapeDtypeStruct((part, width), jnp.bfloat16),) * 2,
         "finish",
-    )(inside, factor, reach, docs, query, incoming)
+    )(inside, factor, docs, query, incoming)
 
     if n_ctx != 4 or n_head != 4 or n_pipe != 2:
         normed = lax.all_gather(jnp.concatenate(normed, axis=0), "ctx", axis=0, tiled=True)
@@ -347,7 +350,8 @@
     def merge(layout, sums, after=()):
         specs = [VMEM] * len(sums) + [ANY] * len(after)
         kernel = functools.partial(merge_kernel, layout)
-        return call(kernel, (single,) * len(layout), "merge", in_specs=specs)(*sums, *after)
+        shapes = [jax.ShapeDtypeStruct((part * len(x), columns // 2), jnp.bfloat16) for x in layout]
+        return call(kernel, tuple(shapes), "merge", in_specs=specs)(*sums, *after)
 
     upper, lower = normed
     upper_1, lower_2 = swapped(upper, 1), swapped(lower, 2)
@@ -362,17 +366,18 @@
     own = merge(whole, (project((upper, lower), 0), partner(own_send)))
     upper, lower = hold((upper, lower), (own_send,))
     lower_1, upper_2 = swapped(lower, 1), swapped(upper, 2)
-    held = hold((upper_1, lower_2), (lower_1, upper_2))
+    held = hold((upper_1, lower_2), (lower_1, upper_2, *own))
     beside = (upper_1, lower_1, upper_2, lower_2)
+    beside_send, beside_keep = project(beside, 1, own), project(beside, 0)
     beside = merge(
         (((0, 0), (0, 1)), ((0, 2), (0, 3))),
-        (project(beside, 0), partner(project(beside, 1, own))),
+        (beside_keep, partner(beside_send)),
     )
     across = (swapped(held[0], 2), swapped(held[1], 1))
-    across = merge(whole, (project(across, 0), partner(project(across, 1))), beside[:1])
-    blocks = [
-        swapped(block, k) if k else block for k, block in enumerate((*own, *beside, *across))
-    ]
+    across_sum = (project(across, 0), partner(project(across, 1, (beside_keep,))))
+    across = merge((((0, 0),), ((0, 1),)), across_sum, beside[:1])
+    blocks = [*own, *(swapped(block, k + 1) for k, block in enumerate(beside))]
+    blocks += [swapped(block, 3) for block in across]
     picked = call(pick_kernel, (single,) * n_head, "pick")(*blocks)
     arrived = [moved(picked[m], lambda i, j, s, m=m: (i, j ^ m, s)) for m in (3, 2, 1)]
     out = jax.ShapeDtypeStruct((1, rows, columns), jnp.bfloat16)

time: 78.6 us -> 77.8 us (0.990)
  Pallas kernels: 13.3 us -> 12.2 us
  starting transfers between devices: 25.7 us -> 26.6 us
    pallas_call x1, Pallas kernels: 1.59 us -> 0.56 us  [on_device(): call(finish_kernel, (jax.ShapeDtypeStruct((part, width), jnp.bfloat16),)...]
    ppermute x16 -> x17, starting transfers between devices: 20.8 us -> 21.7 us  [moved(): lax.ppermute(array, names, [(place[spot], place[target(*spot)]) for spot...]
    ppermute x16 -> x17, waiting for transfers between devices: 31.5 us -> 31 us  [moved(): lax.ppermute(array, names, [(place[spot], place[target(*spot)]) for spot...]
  transfers between devices with their start and end apart: 17 -> 18, of which waited for: 15 -> 13; matrix products, arithmetic and copies ran while one was open for 0% -> 0% of each run, Pallas kernels for 11% -> 10%
where the time goes in v6:
time: 77.8 us; the launch traced here: 77.6 us
  waiting for transfers between devices  37.9 us (49%)
  starting transfers between devices  26.6 us (34%)
  Pallas kernels  12.2 us (16%)
    ppermute x17, waiting for transfers between devices, moved(): lax.ppermute(array, names, [(place[spot], place[target(*spot)]) for spot...  31 us
    ppermute x17, starting transfers between devices, moved(): lax.ppermute(array, names, [(place[spot], place[target(*spot)]) for spot...  21.7 us
    ppermute x1, waiting for transfers between devices, from_before(): return lax.ppermute(array, 'ctx', [(i, i + by) for i in range(n_ctx - by)])  6.98 us
    ppermute x1, starting transfers between devices, from_before(): return lax.ppermute(array, 'ctx', [(i, i + by) for i in range(n_ctx - by)])  4.87 us
    pallas_call x6, Pallas kernels, project(): call(kernel, shape, 'project', in_specs=specs)(*picked, weight, *after)  4.4 us
    pallas_call x1, Pallas kernels, on_device(): call(inside_kernel, (pltpu.VMEM((rows, width), jnp.float32), pltpu.VMEM((...  4.24 us
    pallas_call x1, Pallas kernels, on_device(): call(state_kernel, state_shape, 'shard_state', in_specs=[HBM] * 4, scratc...  2.58 us
  transfers between devices with their start and end apart: 18, of which 13 were waited for; matrix products, arithmetic and copies ran while one was open for 0% of the time, Pallas kernels for 10%

profile of v6, /device:TPU:0, one launch (start us, length us, event | category | flops | bytes accessed | tf_op | source)
XLA Modules:
  0.0 77.6 jit_solution(3102510443237112291)
XLA Ops:
  0.0 2.6 %shard_state.1 = bf16[2064,128]{1,0:T(8,128)(2,1)S(1)} custom-call(bf16[1,128,2048]{2,1,0:T(8,128)(2,1)} %key_hbm.3, bf16[1,128,2048]{2,1,0:T(8,128)(2,1)} %value_hbm.3, f32[1,16,128]{2,1,0:T(8,128)} %bitcast.1, s32[1,128]{1,0:T(1,128)} %doc_hbm.3), custom_call_target="tpu_custom_call" | custom-call | flops 1 | bytes 1 | tf_op jit(solution)/shard_map/shard_state/pallas_call | solution.py:258
  2.6 4.9 %collective-permute-start = (bf16[2064,128]{1,0:T(8,128)(2,1)S(1)}, bf16[2064,128]{1,0:T(8,128)(2,1)S(1)}, u32[]{:S(2)}, u32[]{:S(2)}) collective-permute-start(bf16[2064,128]{1,0:T(8,128)(2,1)S(1)} %shard_state.1), channel_id=1, source_target_pairs={{0,8},{8,16},{16,24},{1,9},{9,17},{17,25},{2,10},{10,18},{18,26},{... | collective-permute-start | bytes 1585160 | tf_op jit(solution)/shard_map/ppermute | solution.py:254
  7.5 4.2 %inside.1 = (f32[128,2048]{1,0:T(8,128)S(1)}, f32[128,2048]{1,0:T(8,128)S(1)}, f32[128,128]{1,0:T(8,128)S(1)}, bf16[128,2048]{1,0:T(8,128)(2,1)S(1)}, bf16[2048,1536]{1,0:T(8,128)(2,1)S(1)}) custom-call(bf16[1,128,2048]{2,1,0:T(8,128)(2,1)} %query_hbm.1, bf16[1,128,2048]{2,1,0:T(8,128)(2,1)} %key_hbm.3, bf16[1,128,2048]{2,1,0:T(8,128)(2,1)} %value_hbm.3, ...), custom_call_target="tpu_custom_call" | custom-call | flops 1 | bytes 1 | tf_op jit(solution)/shard_map/inside/pallas_call | solution.py:290
  11.7 7.0 %collective-permute-done.state_ref = bf16[2064,128]{1,0:T(8,128)(2,1)S(1)} collective-permute-done((bf16[2064,128]{1,0:T(8,128)(2,1)S(1)}, bf16[2064,128]{1,0:T(8,128)(2,1)S(1)}, u32[]{:S(2)}, u32[]{:S(2)}) %collective-permute-start) | collective-permute-done | bytes 528416 | tf_op jit(solution)/shard_map/ppermute | solution.py:254
  19.3 2.5 %collective-permute-start.2 = (bf16[64,2048]{1,0:T(8,128)(2,1)S(1)}, bf16[64,2048]{1,0:T(8,128)(2,1)S(1)}, u32[]{:S(2)}, u32[]{:S(2)}) collective-permute-start(bf16[64,2048]{1,0:T(8,128)(2,1)S(1)} %get-tuple-element.28.refs_0_.upper_ref), channel_id=1, source_target_pairs={{0,8},{1,9},{2,10},{3,11},{4,12},{5,13},{6,14},{7,15},{8,0},{9,1},... | collective-permute-start | bytes 786440 | tf_op jit(solution)/shard_map/ppermute | solution.py:334
  22.4 1.6 %collective-permute-start.5 = (bf16[64,2048]{1,0:T(8,128)(2,1)S(1)}, bf16[64,2048]{1,0:T(8,128)(2,1)S(1)}, u32[]{:S(2)}, u32[]{:S(2)}) collective-permute-start(bf16[64,2048]{1,0:T(8,128)(2,1)S(1)} %get-tuple-element.29.refs_1_.lower_ref), channel_id=1, source_target_pairs={{0,16},{1,17},{2,18},{3,19},{4,20},{5,21},{6,22},{7,23},{8,24},{9,... | collective-permute-start | bytes 786440 | tf_op jit(solution)/shard_map/ppermute | solution.py:334
  24.0 1.5 %collective-permute-start.3 = (bf16[64,2048]{1,0:T(8,128)(2,1)S(1)}, bf16[64,2048]{1,0:T(8,128)(2,1)S(1)}, u32[]{:S(2)}, u32[]{:S(2)}) collective-permute-start(bf16[64,2048]{1,0:T(8,128)(2,1)S(1)} %get-tuple-element.31), channel_id=1, source_target_pairs={{0,8},{1,9},{2,10},{3,11},{4,12},{5,13},{6,14},{7,15},{8,0},{9,1},... | collective-permute-start | bytes 786440 | tf_op jit(solution)/shard_map/ppermute | solution.py:334
  25.6 1.6 %collective-permute-start.1 = (bf16[2,64,768]{2,1,0:T(8,128)(2,1)S(1)}, bf16[2,64,768]{2,1,0:T(8,128)(2,1)S(1)}, u32[]{:S(2)}, u32[]{:S(2)}) collective-permute-start(bf16[2,64,768]{2,1,0:T(8,128)(2,1)S(1)} %project.7.refs_0_), channel_id=1, source_target_pairs={{0,2},{1,3},{2,0},{3,1},{4,6},{5,7},{6,4},{7,5},{8,10},{9,11},{10,... | collective-permute-start | bytes 589832 | tf_op jit(solution)/shard_map/ppermute | solution.py:334
  27.7 3.5 %collective-permute-done.1.refs_1_ = bf16[2,64,768]{2,1,0:T(8,128)(2,1)S(1)} collective-permute-done((bf16[2,64,768]{2,1,0:T(8,128)(2,1)S(1)}, bf16[2,64,768]{2,1,0:T(8,128)(2,1)S(1)}, u32[]{:S(2)}, u32[]{:S(2)}) %collective-permute-start.1) | collective-permute-done | bytes 196640 | tf_op jit(solution)/shard_map/ppermute | solution.py:334
  32.9 2.1 %collective-permute-done.4.refs_2_.refs_1_ = bf16[64,2048]{1,0:T(8,128)(2,1)S(1)} collective-permute-done((bf16[64,2048]{1,0:T(8,128)(2,1)S(1)}, bf16[64,2048]{1,0:T(8,128)(2,1)S(1)}, u32[]{:S(2)}, u32[]{:S(2)}) %collective-permute-start.4) | collective-permute-done | bytes 262176 | tf_op jit(solution)/shard_map/ppermute | solution.py:334
  36.0 1.6 %collective-permute-start.6 = (bf16[4,64,768]{2,1,0:T(8,128)(2,1)S(1)}, bf16[4,64,768]{2,1,0:T(8,128)(2,1)S(1)}, u32[]{:S(2)}, u32[]{:S(2)}) collective-permute-start(bf16[4,64,768]{2,1,0:T(8,128)(2,1)S(1)} %project.9), channel_id=1, source_target_pairs={{0,2},{1,3},{2,0},{3,1},{4,6},{5,7},{6,4},{7,5},{8,10},{9,11},{10,... | collective-permute-start | bytes 1179656 | tf_op jit(solution)/shard_map/ppermute | solution.py:334
  37.7 1.6 %collective-permute-start.9 = (bf16[64,2048]{1,0:T(8,128)(2,1)S(1)}, bf16[64,2048]{1,0:T(8,128)(2,1)S(1)}, u32[]{:S(2)}, u32[]{:S(2)}) collective-permute-start(bf16[64,2048]{1,0:T(8,128)(2,1)S(1)} %get-tuple-element.35), channel_id=1, source_target_pairs={{0,16},{1,17},{2,18},{3,19},{4,20},{5,21},{6,22},{7,23},{8,24},{9,... | collective-permute-start | bytes 786440 | tf_op jit(solution)/shard_map/ppermute | solution.py:334
  39.3 1.4 %collective-permute-start.10 = (bf16[64,2048]{1,0:T(8,128)(2,1)S(1)}, bf16[64,2048]{1,0:T(8,128)(2,1)S(1)}, u32[]{:S(2)}, u32[]{:S(2)}) collective-permute-start(bf16[64,2048]{1,0:T(8,128)(2,1)S(1)} %get-tuple-element.36), channel_id=1, source_target_pairs={{0,8},{1,9},{2,10},{3,11},{4,12},{5,13},{6,14},{7,15},{8,0},{9,1},... | collective-permute-start | bytes 786440 | tf_op jit(solution)/shard_map/ppermute | solution.py:334
  41.7 2.4 %collective-permute-done.9.refs_0_ = bf16[64,2048]{1,0:T(8,128)(2,1)S(1)} collective-permute-done((bf16[64,2048]{1,0:T(8,128)(2,1)S(1)}, bf16[64,2048]{1,0:T(8,128)(2,1)S(1)}, u32[]{:S(2)}, u32[]{:S(2)}) %collective-permute-start.9) | collective-permute-done | bytes 262176 | tf_op jit(solution)/shard_map/ppermute | solution.py:334
  44.1 1.5 %collective-permute-done.10.refs_1_ = bf16[64,2048]{1,0:T(8,128)(2,1)S(1)} collective-permute-done((bf16[64,2048]{1,0:T(8,128)(2,1)S(1)}, bf16[64,2048]{1,0:T(8,128)(2,1)S(1)}, u32[]{:S(2)}, u32[]{:S(2)}) %collective-permute-start.10) | collective-permute-done | bytes 262176 | tf_op jit(solution)/shard_map/ppermute | solution.py:334
  49.2 2.7 %collective-permute-done.11.refs_1_ = bf16[2,64,768]{2,1,0:T(8,128)(2,1)S(1)} collective-permute-done((bf16[2,64,768]{2,1,0:T(8,128)(2,1)S(1)}, bf16[2,64,768]{2,1,0:T(8,128)(2,1)S(1)}, u32[]{:S(2)}, u32[]{:S(2)}) %collective-permute-start.11) | collective-permute-done | bytes 196640 | tf_op jit(solution)/shard_map/ppermute | solution.py:334
  52.0 1.2 %collective-permute-start.12 = (bf16[64,768]{1,0:T(8,128)(2,1)S(1)}, bf16[64,768]{1,0:T(8,128)(2,1)S(1)}, u32[]{:S(2)}, u32[]{:S(2)}) collective-permute-start(bf16[64,768]{1,0:T(8,128)(2,1)S(1)} %get-tuple-element.37), channel_id=1, source_target_pairs={{0,24},{1,25},{2,26},{3,27},{4,28},{5,29},{6,30},{7,31},{8,16},{9,... | collective-permute-start | bytes 294920 | tf_op jit(solution)/shard_map/ppermute | solution.py:334
  53.2 1.8 %collective-permute-start.13 = (bf16[64,768]{1,0:T(8,128)(2,1)S(1)}, bf16[64,768]{1,0:T(8,128)(2,1)S(1)}, u32[]{:S(2)}, u32[]{:S(2)}) collective-permute-start(bf16[64,768]{1,0:T(8,128)(2,1)S(1)} %get-tuple-element.38), channel_id=1, source_target_pairs={{0,24},{1,25},{2,26},{3,27},{4,28},{5,29},{6,30},{7,31},{8,16},{9,... | collective-permute-start | bytes 294920 | tf_op jit(solution)/shard_map/ppermute | solution.py:334
  55.0 2.6 %collective-permute-done.12.refs_3_ = bf16[64,768]{1,0:T(8,128)(2,1)S(1)} collective-permute-done((bf16[64,768]{1,0:T(8,128)(2,1)S(1)}, bf16[64,768]{1,0:T(8,128)(2,1)S(1)}, u32[]{:S(2)}, u32[]{:S(2)}) %collective-permute-start.12) | collective-permute-done | bytes 98336 | tf_op jit(solution)/shard_map/ppermute | solution.py:334
  58.9 2.5 %collective-permute-start.14 = (bf16[128,768]{1,0:T(8,128)(2,1)S(1)}, bf16[128,768]{1,0:T(8,128)(2,1)S(1)}, u32[]{:S(2)}, u32[]{:S(2)}) collective-permute-start(bf16[128,768]{1,0:T(8,128)(2,1)S(1)} %get-tuple-element.39), channel_id=1, source_target_pairs={{0,6},{1,7},{2,4},{3,5},{4,2},{5,3},{6,0},{7,1},{8,14},{9,15},{10,... | collective-permute-start | bytes 589832 | tf_op jit(solution)/shard_map/ppermute | solution.py:334
  61.6 1.7 %collective-permute-start.16 = (bf16[128,768]{1,0:T(8,128)(2,1)S(1)}, bf16[128,768]{1,0:T(8,128)(2,1)S(1)}, u32[]{:S(2)}, u32[]{:S(2)}) collective-permute-start(bf16[128,768]{1,0:T(8,128)(2,1)S(1)} %get-tuple-element.41), channel_id=1, source_target_pairs={{0,2},{1,3},{2,0},{3,1},{4,6},{5,7},{6,4},{7,5},{8,10},{9,11},{10,... | collective-permute-start | bytes 589832 | tf_op jit(solution)/shard_map/ppermute | solution.py:334
  63.3 4.3 %collective-permute-done.14.refs_0_ = bf16[128,768]{1,0:T(8,128)(2,1)S(1)} collective-permute-done((bf16[128,768]{1,0:T(8,128)(2,1)S(1)}, bf16[128,768]{1,0:T(8,128)(2,1)S(1)}, u32[]{:S(2)}, u32[]{:S(2)}) %collective-permute-start.14) | collective-permute-done | bytes 196640 | tf_op jit(solution)/shard_map/ppermute | solution.py:334
  67.6 7.4 %collective-permute-done.15.refs_1_ = bf16[128,768]{1,0:T(8,128)(2,1)S(1)} collective-permute-done((bf16[128,768]{1,0:T(8,128)(2,1)S(1)}, bf16[128,768]{1,0:T(8,128)(2,1)S(1)}, u32[]{:S(2)}, u32[]{:S(2)}) %collective-permute-start.15) | collective-permute-done | bytes 196640 | tf_op jit(solution)/shard_map/ppermute | solution.py:334
  75.2 1.7 %collective-permute-done.17 = bf16[1,128,1536]{2,1,0:T(8,128)(2,1)S(1)} collective-permute-done((bf16[1,128,1536]{2,1,0:T(8,128)(2,1)S(1)}, bf16[1,128,1536]{2,1,0:T(8,128)(2,1)S(1)}, u32[]{:S(2)}, u32[]{:S(2)}) %collective-permute-start.17) | collective-permute-done | bytes 393248 | tf_op jit(solution)/shard_map/ppermute | solution.py:334
  (29 shorter events, 11.5 us)
Async XLA Ops:
  2.6 16.1 %collective-permute-start = (bf16[2064,128]{1,0:T(8,128)(2,1)S(1)}, bf16[2064,128]{1,0:T(8,128)(2,1)S(1)}, u32[]{:S(2)}, u32[]{:S(2)}) collective-permute-start(bf16[2064,128]{1,0:T(8,128)(2,1)S(1)} %shard_state.1), channel_id=1, source_target_pairs={{0,8},{8,16},{16,24},{1,9},{9,17},{17,25},{2,10},{10,18},{18,26},{... | collective-permute-start | bytes 1585160 | tf_op jit(solution)/shard_map/ppermute | solution.py:254
  19.3 12.0 %collective-permute-start.2 = (bf16[64,2048]{1,0:T(8,128)(2,1)S(1)}, bf16[64,2048]{1,0:T(8,128)(2,1)S(1)}, u32[]{:S(2)}, u32[]{:S(2)}) collective-permute-start(bf16[64,2048]{1,0:T(8,128)(2,1)S(1)} %get-tuple-element.28.refs_0_.upper_ref), channel_id=1, source_target_pairs={{0,8},{1,9},{2,10},{3,11},{4,12},{5,13},{6,14},{7,15},{8,0},{9,1},... | collective-permute-start | bytes 786440 | tf_op jit(solution)/shard_map/ppermute | solution.py:334
  22.4 9.3 %collective-permute-start.5 = (bf16[64,2048]{1,0:T(8,128)(2,1)S(1)}, bf16[64,2048]{1,0:T(8,128)(2,1)S(1)}, u32[]{:S(2)}, u32[]{:S(2)}) collective-permute-start(bf16[64,2048]{1,0:T(8,128)(2,1)S(1)} %get-tuple-element.29.refs_1_.lower_ref), channel_id=1, source_target_pairs={{0,16},{1,17},{2,18},{3,19},{4,20},{5,21},{6,22},{7,23},{8,24},{9,... | collective-permute-start | bytes 786440 | tf_op jit(solution)/shard_map/ppermute | solution.py:334
  24.0 8.8 %collective-permute-start.3 = (bf16[64,2048]{1,0:T(8,128)(2,1)S(1)}, bf16[64,2048]{1,0:T(8,128)(2,1)S(1)}, u32[]{:S(2)}, u32[]{:S(2)}) collective-permute-start(bf16[64,2048]{1,0:T(8,128)(2,1)S(1)} %get-tuple-element.31), channel_id=1, source_target_pairs={{0,8},{1,9},{2,10},{3,11},{4,12},{5,13},{6,14},{7,15},{8,0},{9,1},... | collective-permute-start | bytes 786440 | tf_op jit(solution)/shard_map/ppermute | solution.py:334
  25.5 9.5 %collective-permute-start.4 = (bf16[64,2048]{1,0:T(8,128)(2,1)S(1)}, bf16[64,2048]{1,0:T(8,128)(2,1)S(1)}, u32[]{:S(2)}, u32[]{:S(2)}) collective-permute-start(bf16[64,2048]{1,0:T(8,128)(2,1)S(1)} %get-tuple-element.32), channel_id=1, source_target_pairs={{0,16},{1,17},{2,18},{3,19},{4,20},{5,21},{6,22},{7,23},{8,24},{9,... | collective-permute-start | bytes 786440 | tf_op jit(solution)/shard_map/ppermute | solution.py:334
  25.6 5.7 %collective-permute-start.1 = (bf16[2,64,768]{2,1,0:T(8,128)(2,1)S(1)}, bf16[2,64,768]{2,1,0:T(8,128)(2,1)S(1)}, u32[]{:S(2)}, u32[]{:S(2)}) collective-permute-start(bf16[2,64,768]{2,1,0:T(8,128)(2,1)S(1)} %project.7.refs_0_), channel_id=1, source_target_pairs={{0,2},{1,3},{2,0},{3,1},{4,6},{5,7},{6,4},{7,5},{8,10},{9,11},{10,... | collective-permute-start | bytes 589832 | tf_op jit(solution)/shard_map/ppermute | solution.py:334
  36.0 10.8 %collective-permute-start.6 = (bf16[4,64,768]{2,1,0:T(8,128)(2,1)S(1)}, bf16[4,64,768]{2,1,0:T(8,128)(2,1)S(1)}, u32[]{:S(2)}, u32[]{:S(2)}) collective-permute-start(bf16[4,64,768]{2,1,0:T(8,128)(2,1)S(1)} %project.9), channel_id=1, source_target_pairs={{0,2},{1,3},{2,0},{3,1},{4,6},{5,7},{6,4},{7,5},{8,10},{9,11},{10,... | collective-permute-start | bytes 1179656 | tf_op jit(solution)/shard_map/ppermute | solution.py:334
  37.7 6.4 %collective-permute-start.9 = (bf16[64,2048]{1,0:T(8,128)(2,1)S(1)}, bf16[64,2048]{1,0:T(8,128)(2,1)S(1)}, u32[]{:S(2)}, u32[]{:S(2)}) collective-permute-start(bf16[64,2048]{1,0:T(8,128)(2,1)S(1)} %get-tuple-element.35), channel_id=1, source_target_pairs={{0,16},{1,17},{2,18},{3,19},{4,20},{5,21},{6,22},{7,23},{8,24},{9,... | collective-permute-start | bytes 786440 | tf_op jit(solution)/shard_map/ppermute | solution.py:334
  39.3 6.4 %collective-permute-start.10 = (bf16[64,2048]{1,0:T(8,128)(2,1)S(1)}, bf16[64,2048]{1,0:T(8,128)(2,1)S(1)}, u32[]{:S(2)}, u32[]{:S(2)}) collective-permute-start(bf16[64,2048]{1,0:T(8,128)(2,1)S(1)} %get-tuple-element.36), channel_id=1, source_target_pairs={{0,8},{1,9},{2,10},{3,11},{4,12},{5,13},{6,14},{7,15},{8,0},{9,1},... | collective-permute-start | bytes 786440 | tf_op jit(solution)/shard_map/ppermute | solution.py:334
  46.2 5.7 %collective-permute-start.11 = (bf16[2,64,768]{2,1,0:T(8,128)(2,1)S(1)}, bf16[2,64,768]{2,1,0:T(8,128)(2,1)S(1)}, u32[]{:S(2)}, u32[]{:S(2)}) collective-permute-start(bf16[2,64,768]{2,1,0:T(8,128)(2,1)S(1)} %project.11), channel_id=1, source_target_pairs={{0,2},{1,3},{2,0},{3,1},{4,6},{5,7},{6,4},{7,5},{8,10},{9,11},{10,... | collective-permute-start | bytes 589832 | tf_op jit(solution)/shard_map/ppermute | solution.py:334
  46.9 11.9 %collective-permute-start.8 = (bf16[128,768]{1,0:T(8,128)(2,1)S(1)}, bf16[128,768]{1,0:T(8,128)(2,1)S(1)}, u32[]{:S(2)}, u32[]{:S(2)}) collective-permute-start(bf16[128,768]{1,0:T(8,128)(2,1)S(1)} %get-tuple-element.34), channel_id=1, source_target_pairs={{0,16},{1,17},{2,18},{3,19},{4,20},{5,21},{6,22},{7,23},{8,24},{9,... | collective-permute-start | bytes 589832 | tf_op jit(solution)/shard_map/ppermute | solution.py:334
  47.4 11.3 %collective-permute-start.7 = (bf16[128,768]{1,0:T(8,128)(2,1)S(1)}, bf16[128,768]{1,0:T(8,128)(2,1)S(1)}, u32[]{:S(2)}, u32[]{:S(2)}) collective-permute-start(bf16[128,768]{1,0:T(8,128)(2,1)S(1)} %get-tuple-element.33.refs_2_), channel_id=1, source_target_pairs={{0,8},{1,9},{2,10},{3,11},{4,12},{5,13},{6,14},{7,15},{8,0},{9,1},... | collective-permute-start | bytes 589832 | tf_op jit(solution)/shard_map/ppermute | solution.py:334
  52.0 5.6 %collective-permute-start.12 = (bf16[64,768]{1,0:T(8,128)(2,1)S(1)}, bf16[64,768]{1,0:T(8,128)(2,1)S(1)}, u32[]{:S(2)}, u32[]{:S(2)}) collective-permute-start(bf16[64,768]{1,0:T(8,128)(2,1)S(1)} %get-tuple-element.37), channel_id=1, source_target_pairs={{0,24},{1,25},{2,26},{3,27},{4,28},{5,29},{6,30},{7,31},{8,16},{9,... | collective-permute-start | bytes 294920 | tf_op jit(solution)/shard_map/ppermute | solution.py:334
  53.2 5.5 %collective-permute-start.13 = (bf16[64,768]{1,0:T(8,128)(2,1)S(1)}, bf16[64,768]{1,0:T(8,128)(2,1)S(1)}, u32[]{:S(2)}, u32[]{:S(2)}) collective-permute-start(bf16[64,768]{1,0:T(8,128)(2,1)S(1)} %get-tuple-element.38), channel_id=1, source_target_pairs={{0,24},{1,25},{2,26},{3,27},{4,28},{5,29},{6,30},{7,31},{8,16},{9,... | collective-permute-start | bytes 294920 | tf_op jit(solution)/shard_map/ppermute | solution.py:334
  58.9 8.7 %collective-permute-start.14 = (bf16[128,768]{1,0:T(8,128)(2,1)S(1)}, bf16[128,768]{1,0:T(8,128)(2,1)S(1)}, u32[]{:S(2)}, u32[]{:S(2)}) collective-permute-start(bf16[128,768]{1,0:T(8,128)(2,1)S(1)} %get-tuple-element.39), channel_id=1, source_target_pairs={{0,6},{1,7},{2,4},{3,5},{4,2},{5,3},{6,0},{7,1},{8,14},{9,15},{10,... | collective-permute-start | bytes 589832 | tf_op jit(solution)/shard_map/ppermute | solution.py:334
  61.4 13.6 %collective-permute-start.15 = (bf16[128,768]{1,0:T(8,128)(2,1)S(1)}, bf16[128,768]{1,0:T(8,128)(2,1)S(1)}, u32[]{:S(2)}, u32[]{:S(2)}) collective-permute-start(bf16[128,768]{1,0:T(8,128)(2,1)S(1)} %get-tuple-element.40), channel_id=1, source_target_pairs={{0,4},{1,5},{2,6},{3,7},{4,0},{5,1},{6,2},{7,3},{8,12},{9,13},{10,... | collective-permute-start | bytes 589832 | tf_op jit(solution)/shard_map/ppermute | solution.py:334
  61.6 13.4 %collective-permute-start.16 = (bf16[128,768]{1,0:T(8,128)(2,1)S(1)}, bf16[128,768]{1,0:T(8,128)(2,1)S(1)}, u32[]{:S(2)}, u32[]{:S(2)}) collective-permute-start(bf16[128,768]{1,0:T(8,128)(2,1)S(1)} %get-tuple-element.41), channel_id=1, source_target_pairs={{0,2},{1,3},{2,0},{3,1},{4,6},{5,7},{6,4},{7,5},{8,10},{9,11},{10,... | collective-permute-start | bytes 589832 | tf_op jit(solution)/shard_map/ppermute | solution.py:334
  75.1 1.8 %collective-permute-start.17 = (bf16[1,128,1536]{2,1,0:T(8,128)(2,1)S(1)}, bf16[1,128,1536]{2,1,0:T(8,128)(2,1)S(1)}, u32[]{:S(2)}, u32[]{:S(2)}) collective-permute-start(bf16[1,128,1536]{2,1,0:T(8,128)(2,1)S(1)} %last.1), channel_id=1, source_target_pairs={{0,1},{1,0},{2,3},{3,2},{4,5},{5,4},{6,7},{7,6},{8,9},{9,8},{10,11... | collective-permute-start | bytes 1179656 | tf_op jit(solution)/shard_map/ppermute | solution.py:334

commit v7 on v6

--- a/solution.py
+++ b/solution.py
@@ -364,7 +364,6 @@
 
     own_send = project((upper, lower), 1)
     own = merge(whole, (project((upper, lower), 0), partner(own_send)))
-    upper, lower = hold((upper, lower), (own_send,))
     lower_1, upper_2 = swapped(lower, 1), swapped(upper, 2)
     held = hold((upper_1, lower_2), (lower_1, upper_2, *own))
     beside = (upper_1, lower_1, upper_2, lower_2)
@@ -374,10 +373,13 @@
         (beside_keep, partner(beside_send)),
     )
     across = (swapped(held[0], 2), swapped(held[1], 1))
-    across_sum = (project(across, 0), partner(project(across, 1, (beside_keep,))))
-    across = merge((((0, 0),), ((0, 1),)), across_sum, beside[:1])
     blocks = [*own, *(swapped(block, k + 1) for k, block in enumerate(beside))]
-    blocks += [swapped(block, 3) for block in across]
+    sent, done = beside_keep, beside[0]
+    for piece in across:
+        send = project((piece,), 1, (sent,))
+        (done,) = merge((((0, 0),),), (project((piece,), 0), partner(send)), (done,))
+        blocks.append(swapped(done, 3))
+        sent = send
     picked = call(pick_kernel, (single,) * n_head, "pick")(*blocks)
     arrived = [moved(picked[m], lambda i, j, s, m=m: (i, j ^ m, s)) for m in (3, 2, 1)]
     out = jax.ShapeDtypeStruct((1, rows, columns), jnp.bfloat16)

time: 77.8 us -> 76.7 us (0.986)
  waiting for transfers between devices: 37.9 us -> 36.2 us
  Pallas kernels: 12.2 us -> 13.7 us
  starting transfers between devices: 26.6 us -> 25.7 us
    ppermute x17 -> x18, waiting for transfers between devices: 31 us -> 29.2 us  [moved(): lax.ppermute(array, names, [(place[spot], place[target(*spot)]) for spot...]
    pallas_call x6 -> x8, Pallas kernels: 4.4 us -> 5.87 us  [project(): call(kernel, shape, 'project', in_specs=specs)(*picked, weight, *after)]
    ppermute x17 -> x18, starting transfers between devices: 21.7 us -> 20.8 us  [moved(): lax.ppermute(array, names, [(place[spot], place[target(*spot)]) for spot...]
  transfers between devices with their start and end apart: 18 -> 19, of which waited for: 13 -> 12; matrix products, arithmetic and copies ran while one was open for 0% -> 0% of each run, Pallas kernels for 10% -> 12%
where the time goes in v7:
time: 76.7 us; the launch traced here: 76.5 us
  waiting for transfers between devices  36.2 us (47%)
  starting transfers between devices  25.7 us (34%)
  Pallas kernels  13.7 us (18%)
    ppermute x18, waiting for transfers between devices, moved(): lax.ppermute(array, names, [(place[spot], place[target(*spot)]) for spot...  29.2 us
    ppermute x18, starting transfers between devices, moved(): lax.ppermute(array, names, [(place[spot], place[target(*spot)]) for spot...  20.8 us
    ppermute x1, waiting for transfers between devices, from_before(): return lax.ppermute(array, 'ctx', [(i, i + by) for i in range(n_ctx - by)])  6.98 us
    pallas_call x8, Pallas kernels, project(): call(kernel, shape, 'project', in_specs=specs)(*picked, weight, *after)  5.87 us
    ppermute x1, starting transfers between devices, from_before(): return lax.ppermute(array, 'ctx', [(i, i + by) for i in range(n_ctx - by)])  4.87 us
    pallas_call x1, Pallas kernels, on_device(): call(inside_kernel, (pltpu.VMEM((rows, width), jnp.float32), pltpu.VMEM((...  4.24 us
    pallas_call x1, Pallas kernels, on_device(): call(state_kernel, state_shape, 'shard_state', in_specs=[HBM] * 4, scratc...  2.58 us
  transfers between devices with their start and end apart: 19, of which 12 were waited for; matrix products, arithmetic and copies ran while one was open for 0% of the time, Pallas kernels for 12%

profile of v7, /device:TPU:0, one launch (start us, length us, event | category | flops | bytes accessed | tf_op | source)
XLA Modules:
  0.0 76.5 jit_solution(16564146741681077263)
XLA Ops:
  0.0 2.6 %shard_state.1 = bf16[2064,128]{1,0:T(8,128)(2,1)S(1)} custom-call(bf16[1,128,2048]{2,1,0:T(8,128)(2,1)} %key_hbm.3, bf16[1,128,2048]{2,1,0:T(8,128)(2,1)} %value_hbm.3, f32[1,16,128]{2,1,0:T(8,128)} %bitcast.1, s32[1,128]{1,0:T(1,128)} %doc_hbm.3), custom_call_target="tpu_custom_call" | custom-call | flops 1 | bytes 1 | tf_op jit(solution)/shard_map/shard_state/pallas_call | solution.py:258
  2.6 4.9 %collective-permute-start = (bf16[2064,128]{1,0:T(8,128)(2,1)S(1)}, bf16[2064,128]{1,0:T(8,128)(2,1)S(1)}, u32[]{:S(2)}, u32[]{:S(2)}) collective-permute-start(bf16[2064,128]{1,0:T(8,128)(2,1)S(1)} %shard_state.1), channel_id=1, source_target_pairs={{0,8},{8,16},{16,24},{1,9},{9,17},{17,25},{2,10},{10,18},{18,26},{... | collective-permute-start | bytes 1585160 | tf_op jit(solution)/shard_map/ppermute | solution.py:254
  7.5 4.2 %inside.1 = (f32[128,2048]{1,0:T(8,128)S(1)}, f32[128,2048]{1,0:T(8,128)S(1)}, f32[128,128]{1,0:T(8,128)S(1)}, bf16[128,2048]{1,0:T(8,128)(2,1)S(1)}, bf16[2048,1536]{1,0:T(8,128)(2,1)S(1)}) custom-call(bf16[1,128,2048]{2,1,0:T(8,128)(2,1)} %query_hbm.1, bf16[1,128,2048]{2,1,0:T(8,128)(2,1)} %key_hbm.3, bf16[1,128,2048]{2,1,0:T(8,128)(2,1)} %value_hbm.3, ...), custom_call_target="tpu_custom_call" | custom-call | flops 1 | bytes 1 | tf_op jit(solution)/shard_map/inside/pallas_call | solution.py:290
  11.7 7.0 %collective-permute-done.state_ref = bf16[2064,128]{1,0:T(8,128)(2,1)S(1)} collective-permute-done((bf16[2064,128]{1,0:T(8,128)(2,1)S(1)}, bf16[2064,128]{1,0:T(8,128)(2,1)S(1)}, u32[]{:S(2)}, u32[]{:S(2)}) %collective-permute-start) | collective-permute-done | bytes 528416 | tf_op jit(solution)/shard_map/ppermute | solution.py:254
  19.3 3.5 %collective-permute-start.4 = (bf16[64,2048]{1,0:T(8,128)(2,1)S(1)}, bf16[64,2048]{1,0:T(8,128)(2,1)S(1)}, u32[]{:S(2)}, u32[]{:S(2)}) collective-permute-start(bf16[64,2048]{1,0:T(8,128)(2,1)S(1)} %get-tuple-element.24.refs_0_), channel_id=1, source_target_pairs={{0,16},{1,17},{2,18},{3,19},{4,20},{5,21},{6,22},{7,23},{8,24},{9,... | collective-permute-start | bytes 786440 | tf_op jit(solution)/shard_map/ppermute | solution.py:334
  23.8 1.0 %collective-permute-start.3 = (bf16[64,2048]{1,0:T(8,128)(2,1)S(1)}, bf16[64,2048]{1,0:T(8,128)(2,1)S(1)}, u32[]{:S(2)}, u32[]{:S(2)}) collective-permute-start(bf16[64,2048]{1,0:T(8,128)(2,1)S(1)} %get-tuple-element.25.refs_1_), channel_id=1, source_target_pairs={{0,8},{1,9},{2,10},{3,11},{4,12},{5,13},{6,14},{7,15},{8,0},{9,1},... | collective-permute-start | bytes 786440 | tf_op jit(solution)/shard_map/ppermute | solution.py:334
  25.5 1.6 %collective-permute-start.1 = (bf16[2,64,768]{2,1,0:T(8,128)(2,1)S(1)}, bf16[2,64,768]{2,1,0:T(8,128)(2,1)S(1)}, u32[]{:S(2)}, u32[]{:S(2)}) collective-permute-start(bf16[2,64,768]{2,1,0:T(8,128)(2,1)S(1)} %project.9), channel_id=1, source_target_pairs={{0,2},{1,3},{2,0},{3,1},{4,6},{5,7},{6,4},{7,5},{8,10},{9,11},{10,... | collective-permute-start | bytes 589832 | tf_op jit(solution)/shard_map/ppermute | solution.py:334
  27.7 3.5 %collective-permute-done.1.refs_1_ = bf16[2,64,768]{2,1,0:T(8,128)(2,1)S(1)} collective-permute-done((bf16[2,64,768]{2,1,0:T(8,128)(2,1)S(1)}, bf16[2,64,768]{2,1,0:T(8,128)(2,1)S(1)}, u32[]{:S(2)}, u32[]{:S(2)}) %collective-permute-start.1) | collective-permute-done | bytes 196640 | tf_op jit(solution)/shard_map/ppermute | solution.py:334
  32.0 1.8 %collective-permute-done.5.refs_3_.lower_ref = bf16[64,2048]{1,0:T(8,128)(2,1)S(1)} collective-permute-done((bf16[64,2048]{1,0:T(8,128)(2,1)S(1)}, bf16[64,2048]{1,0:T(8,128)(2,1)S(1)}, u32[]{:S(2)}, u32[]{:S(2)}) %collective-permute-start.5) | collective-permute-done | bytes 262176 | tf_op jit(solution)/shard_map/ppermute | solution.py:334
  33.8 1.5 %collective-permute-done.3.refs_1_.refs_0_ = bf16[64,2048]{1,0:T(8,128)(2,1)S(1)} collective-permute-done((bf16[64,2048]{1,0:T(8,128)(2,1)S(1)}, bf16[64,2048]{1,0:T(8,128)(2,1)S(1)}, u32[]{:S(2)}, u32[]{:S(2)}) %collective-permute-start.3) | collective-permute-done | bytes 262176 | tf_op jit(solution)/shard_map/ppermute | solution.py:334
  35.2 1.0 %project.11 = bf16[4,64,768]{2,1,0:T(8,128)(2,1)S(1)} custom-call(bf16[64,2048]{1,0:T(8,128)(2,1)S(1)} %collective-permute-done.2.refs_0_.upper_ref, bf16[64,2048]{1,0:T(8,128)(2,1)S(1)} %collective-permute-done.3.refs_1_.refs_0_, bf16[64,2048]{1,0:T(8,128)(2,1)S(1)} %collective-permute-done.4.refs_2_.refs_1_, ...), custom_call_target="tpu_custom_call" | custom-call | flops 1 | bytes 1 | tf_op jit(solution)/shard_map/project/pallas_call | solution.py:345
  36.3 1.6 %collective-permute-start.6 = (bf16[4,64,768]{2,1,0:T(8,128)(2,1)S(1)}, bf16[4,64,768]{2,1,0:T(8,128)(2,1)S(1)}, u32[]{:S(2)}, u32[]{:S(2)}) collective-permute-start(bf16[4,64,768]{2,1,0:T(8,128)(2,1)S(1)} %project.11), channel_id=1, source_target_pairs={{0,2},{1,3},{2,0},{3,1},{4,6},{5,7},{6,4},{7,5},{8,10},{9,11},{10,... | collective-permute-start | bytes 1179656 | tf_op jit(solution)/shard_map/ppermute | solution.py:334
  39.1 1.0 %project.10.refs_0_.refs_2_ = bf16[4,64,768]{2,1,0:T(8,128)(2,1)S(1)} custom-call(bf16[64,2048]{1,0:T(8,128)(2,1)S(1)} %collective-permute-done.2.refs_0_.upper_ref, bf16[64,2048]{1,0:T(8,128)(2,1)S(1)} %collective-permute-done.3.refs_1_.refs_0_, bf16[64,2048]{1,0:T(8,128)(2,1)S(1)} %collective-permute-done.4.refs_2_.refs_1_, ...), custom_call_target="tpu_custom_call" | custom-call | flops 1 | bytes 1 | tf_op jit(solution)/shard_map/project/pallas_call | solution.py:345
  40.1 4.3 %collective-permute-done.9.refs_0_ = bf16[64,2048]{1,0:T(8,128)(2,1)S(1)} collective-permute-done((bf16[64,2048]{1,0:T(8,128)(2,1)S(1)}, bf16[64,2048]{1,0:T(8,128)(2,1)S(1)}, u32[]{:S(2)}, u32[]{:S(2)}) %collective-permute-start.9) | collective-permute-done | bytes 262176 | tf_op jit(solution)/shard_map/ppermute | solution.py:334
  46.2 1.6 %collective-permute-start.13 = (bf16[1,64,768]{2,1,0:T(8,128)(2,1)S(1)}, bf16[1,64,768]{2,1,0:T(8,128)(2,1)S(1)}, u32[]{:S(2)}, u32[]{:S(2)}) collective-permute-start(bf16[1,64,768]{2,1,0:T(8,128)(2,1)S(1)} %project.15), channel_id=1, source_target_pairs={{0,2},{1,3},{2,0},{3,1},{4,6},{5,7},{6,4},{7,5},{8,10},{9,11},{10,... | collective-permute-start | bytes 294920 | tf_op jit(solution)/shard_map/ppermute | solution.py:334
  51.0 2.1 %collective-permute-start.14 = (bf16[64,768]{1,0:T(8,128)(2,1)S(1)}, bf16[64,768]{1,0:T(8,128)(2,1)S(1)}, u32[]{:S(2)}, u32[]{:S(2)}) collective-permute-start(bf16[64,768]{1,0:T(8,128)(2,1)S(1)} %merge.7), channel_id=1, source_target_pairs={{0,24},{1,25},{2,26},{3,27},{4,28},{5,29},{6,30},{7,31},{8,16},{9,... | collective-permute-start | bytes 294920 | tf_op jit(solution)/shard_map/ppermute | solution.py:334
  53.0 0.9 %collective-permute-start.11 = (bf16[64,768]{1,0:T(8,128)(2,1)S(1)}, bf16[64,768]{1,0:T(8,128)(2,1)S(1)}, u32[]{:S(2)}, u32[]{:S(2)}) collective-permute-start(bf16[64,768]{1,0:T(8,128)(2,1)S(1)} %merge.6.refs_2_), channel_id=1, source_target_pairs={{0,24},{1,25},{2,26},{3,27},{4,28},{5,29},{6,30},{7,31},{8,16},{9,... | collective-permute-start | bytes 294920 | tf_op jit(solution)/shard_map/ppermute | solution.py:334
  53.9 2.6 %collective-permute-done.14.refs_4_ = bf16[64,768]{1,0:T(8,128)(2,1)S(1)} collective-permute-done((bf16[64,768]{1,0:T(8,128)(2,1)S(1)}, bf16[64,768]{1,0:T(8,128)(2,1)S(1)}, u32[]{:S(2)}, u32[]{:S(2)}) %collective-permute-start.14) | collective-permute-done | bytes 98336 | tf_op jit(solution)/shard_map/ppermute | solution.py:334
  56.5 2.0 %collective-permute-done.11.refs_3_ = bf16[64,768]{1,0:T(8,128)(2,1)S(1)} collective-permute-done((bf16[64,768]{1,0:T(8,128)(2,1)S(1)}, bf16[64,768]{1,0:T(8,128)(2,1)S(1)}, u32[]{:S(2)}, u32[]{:S(2)}) %collective-permute-start.11) | collective-permute-done | bytes 98336 | tf_op jit(solution)/shard_map/ppermute | solution.py:334
  58.7 2.8 %collective-permute-start.15 = (bf16[128,768]{1,0:T(8,128)(2,1)S(1)}, bf16[128,768]{1,0:T(8,128)(2,1)S(1)}, u32[]{:S(2)}, u32[]{:S(2)}) collective-permute-start(bf16[128,768]{1,0:T(8,128)(2,1)S(1)} %get-tuple-element.31), channel_id=1, source_target_pairs={{0,6},{1,7},{2,4},{3,5},{4,2},{5,3},{6,0},{7,1},{8,14},{9,15},{10,... | collective-permute-start | bytes 589832 | tf_op jit(solution)/shard_map/ppermute | solution.py:334
  61.5 1.7 %collective-permute-start.17 = (bf16[128,768]{1,0:T(8,128)(2,1)S(1)}, bf16[128,768]{1,0:T(8,128)(2,1)S(1)}, u32[]{:S(2)}, u32[]{:S(2)}) collective-permute-start(bf16[128,768]{1,0:T(8,128)(2,1)S(1)} %get-tuple-element.33), channel_id=1, source_target_pairs={{0,2},{1,3},{2,0},{3,1},{4,6},{5,7},{6,4},{7,5},{8,10},{9,11},{10,... | collective-permute-start | bytes 589832 | tf_op jit(solution)/shard_map/ppermute | solution.py:334
  63.1 3.4 %collective-permute-done.15.refs_0_ = bf16[128,768]{1,0:T(8,128)(2,1)S(1)} collective-permute-done((bf16[128,768]{1,0:T(8,128)(2,1)S(1)}, bf16[128,768]{1,0:T(8,128)(2,1)S(1)}, u32[]{:S(2)}, u32[]{:S(2)}) %collective-permute-start.15) | collective-permute-done | bytes 196640 | tf_op jit(solution)/shard_map/ppermute | solution.py:334
  66.5 7.3 %collective-permute-done.16.refs_1_ = bf16[128,768]{1,0:T(8,128)(2,1)S(1)} collective-permute-done((bf16[128,768]{1,0:T(8,128)(2,1)S(1)}, bf16[128,768]{1,0:T(8,128)(2,1)S(1)}, u32[]{:S(2)}, u32[]{:S(2)}) %collective-permute-start.16) | collective-permute-done | bytes 196640 | tf_op jit(solution)/shard_map/ppermute | solution.py:334
  74.0 1.7 %collective-permute-done.18 = bf16[1,128,1536]{2,1,0:T(8,128)(2,1)S(1)} collective-permute-done((bf16[1,128,1536]{2,1,0:T(8,128)(2,1)S(1)}, bf16[1,128,1536]{2,1,0:T(8,128)(2,1)S(1)}, u32[]{:S(2)}, u32[]{:S(2)}) %collective-permute-start.18) | collective-permute-done | bytes 393248 | tf_op jit(solution)/shard_map/ppermute | solution.py:334
  (33 shorter events, 10.8 us)
Async XLA Ops:
  2.6 16.1 %collective-permute-start = (bf16[2064,128]{1,0:T(8,128)(2,1)S(1)}, bf16[2064,128]{1,0:T(8,128)(2,1)S(1)}, u32[]{:S(2)}, u32[]{:S(2)}) collective-permute-start(bf16[2064,128]{1,0:T(8,128)(2,1)S(1)} %shard_state.1), channel_id=1, source_target_pairs={{0,8},{8,16},{16,24},{1,9},{9,17},{17,25},{2,10},{10,18},{18,26},{... | collective-permute-start | bytes 1585160 | tf_op jit(solution)/shard_map/ppermute | solution.py:254
  19.3 12.0 %collective-permute-start.4 = (bf16[64,2048]{1,0:T(8,128)(2,1)S(1)}, bf16[64,2048]{1,0:T(8,128)(2,1)S(1)}, u32[]{:S(2)}, u32[]{:S(2)}) collective-permute-start(bf16[64,2048]{1,0:T(8,128)(2,1)S(1)} %get-tuple-element.24.refs_0_), channel_id=1, source_target_pairs={{0,16},{1,17},{2,18},{3,19},{4,20},{5,21},{6,22},{7,23},{8,24},{9,... | collective-permute-start | bytes 786440 | tf_op jit(solution)/shard_map/ppermute | solution.py:334
  22.7 9.2 %collective-permute-start.2 = (bf16[64,2048]{1,0:T(8,128)(2,1)S(1)}, bf16[64,2048]{1,0:T(8,128)(2,1)S(1)}, u32[]{:S(2)}, u32[]{:S(2)}) collective-permute-start(bf16[64,2048]{1,0:T(8,128)(2,1)S(1)} %get-tuple-element.24.refs_0_), channel_id=1, source_target_pairs={{0,8},{1,9},{2,10},{3,11},{4,12},{5,13},{6,14},{7,15},{8,0},{9,1},... | collective-permute-start | bytes 786440 | tf_op jit(solution)/shard_map/ppermute | solution.py:334
  23.3 10.5 %collective-permute-start.5 = (bf16[64,2048]{1,0:T(8,128)(2,1)S(1)}, bf16[64,2048]{1,0:T(8,128)(2,1)S(1)}, u32[]{:S(2)}, u32[]{:S(2)}) collective-permute-start(bf16[64,2048]{1,0:T(8,128)(2,1)S(1)} %get-tuple-element.25.refs_1_), channel_id=1, source_target_pairs={{0,16},{1,17},{2,18},{3,19},{4,20},{5,21},{6,22},{7,23},{8,24},{9,... | collective-permute-start | bytes 786440 | tf_op jit(solution)/shard_map/ppermute | solution.py:334
  23.8 11.4 %collective-permute-start.3 = (bf16[64,2048]{1,0:T(8,128)(2,1)S(1)}, bf16[64,2048]{1,0:T(8,128)(2,1)S(1)}, u32[]{:S(2)}, u32[]{:S(2)}) collective-permute-start(bf16[64,2048]{1,0:T(8,128)(2,1)S(1)} %get-tuple-element.25.refs_1_), channel_id=1, source_target_pairs={{0,8},{1,9},{2,10},{3,11},{4,12},{5,13},{6,14},{7,15},{8,0},{9,1},... | collective-permute-start | bytes 786440 | tf_op jit(solution)/shard_map/ppermute | solution.py:334
  25.5 5.7 %collective-permute-start.1 = (bf16[2,64,768]{2,1,0:T(8,128)(2,1)S(1)}, bf16[2,64,768]{2,1,0:T(8,128)(2,1)S(1)}, u32[]{:S(2)}, u32[]{:S(2)}) collective-permute-start(bf16[2,64,768]{2,1,0:T(8,128)(2,1)S(1)} %project.9), channel_id=1, source_target_pairs={{0,2},{1,3},{2,0},{3,1},{4,6},{5,7},{6,4},{7,5},{8,10},{9,11},{10,... | collective-permute-start | bytes 589832 | tf_op jit(solution)/shard_map/ppermute | solution.py:334
  36.3 11.6 %collective-permute-start.6 = (bf16[4,64,768]{2,1,0:T(8,128)(2,1)S(1)}, bf16[4,64,768]{2,1,0:T(8,128)(2,1)S(1)}, u32[]{:S(2)}, u32[]{:S(2)}) collective-permute-start(bf16[4,64,768]{2,1,0:T(8,128)(2,1)S(1)} %project.11), channel_id=1, source_target_pairs={{0,2},{1,3},{2,0},{3,1},{4,6},{5,7},{6,4},{7,5},{8,10},{9,11},{10,... | collective-permute-start | bytes 1179656 | tf_op jit(solution)/shard_map/ppermute | solution.py:334
  37.9 6.4 %collective-permute-start.9 = (bf16[64,2048]{1,0:T(8,128)(2,1)S(1)}, bf16[64,2048]{1,0:T(8,128)(2,1)S(1)}, u32[]{:S(2)}, u32[]{:S(2)}) collective-permute-start(bf16[64,2048]{1,0:T(8,128)(2,1)S(1)} %get-tuple-element.29), channel_id=1, source_target_pairs={{0,16},{1,17},{2,18},{3,19},{4,20},{5,21},{6,22},{7,23},{8,24},{9,... | collective-permute-start | bytes 786440 | tf_op jit(solution)/shard_map/ppermute | solution.py:334
  38.4 7.2 %collective-permute-start.12 = (bf16[64,2048]{1,0:T(8,128)(2,1)S(1)}, bf16[64,2048]{1,0:T(8,128)(2,1)S(1)}, u32[]{:S(2)}, u32[]{:S(2)}) collective-permute-start(bf16[64,2048]{1,0:T(8,128)(2,1)S(1)} %get-tuple-element.30), channel_id=1, source_target_pairs={{0,8},{1,9},{2,10},{3,11},{4,12},{5,13},{6,14},{7,15},{8,0},{9,1},... | collective-permute-start | bytes 786440 | tf_op jit(solution)/shard_map/ppermute | solution.py:334
  45.0 5.4 %collective-permute-start.10 = (bf16[1,64,768]{2,1,0:T(8,128)(2,1)S(1)}, bf16[1,64,768]{2,1,0:T(8,128)(2,1)S(1)}, u32[]{:S(2)}, u32[]{:S(2)}) collective-permute-start(bf16[1,64,768]{2,1,0:T(8,128)(2,1)S(1)} %project.13.refs_2_), channel_id=1, source_target_pairs={{0,2},{1,3},{2,0},{3,1},{4,6},{5,7},{6,4},{7,5},{8,10},{9,11},{10,... | collective-permute-start | bytes 294920 | tf_op jit(solution)/shard_map/ppermute | solution.py:334
  46.2 4.7 %collective-permute-start.13 = (bf16[1,64,768]{2,1,0:T(8,128)(2,1)S(1)}, bf16[1,64,768]{2,1,0:T(8,128)(2,1)S(1)}, u32[]{:S(2)}, u32[]{:S(2)}) collective-permute-start(bf16[1,64,768]{2,1,0:T(8,128)(2,1)S(1)} %project.15), channel_id=1, source_target_pairs={{0,2},{1,3},{2,0},{3,1},{4,6},{5,7},{6,4},{7,5},{8,10},{9,11},{10,... | collective-permute-start | bytes 294920 | tf_op jit(solution)/shard_map/ppermute | solution.py:334
  48.0 10.6 %collective-permute-start.8 = (bf16[128,768]{1,0:T(8,128)(2,1)S(1)}, bf16[128,768]{1,0:T(8,128)(2,1)S(1)}, u32[]{:S(2)}, u32[]{:S(2)}) collective-permute-start(bf16[128,768]{1,0:T(8,128)(2,1)S(1)} %get-tuple-element.28), channel_id=1, source_target_pairs={{0,16},{1,17},{2,18},{3,19},{4,20},{5,21},{6,22},{7,23},{8,24},{9,... | collective-permute-start | bytes 589832 | tf_op jit(solution)/shard_map/ppermute | solution.py:334
  48.4 10.2 %collective-permute-start.7 = (bf16[128,768]{1,0:T(8,128)(2,1)S(1)}, bf16[128,768]{1,0:T(8,128)(2,1)S(1)}, u32[]{:S(2)}, u32[]{:S(2)}) collective-permute-start(bf16[128,768]{1,0:T(8,128)(2,1)S(1)} %get-tuple-element.27.refs_2_), channel_id=1, source_target_pairs={{0,8},{1,9},{2,10},{3,11},{4,12},{5,13},{6,14},{7,15},{8,0},{9,1},... | collective-permute-start | bytes 589832 | tf_op jit(solution)/shard_map/ppermute | solution.py:334
  51.0 5.6 %collective-permute-start.14 = (bf16[64,768]{1,0:T(8,128)(2,1)S(1)}, bf16[64,768]{1,0:T(8,128)(2,1)S(1)}, u32[]{:S(2)}, u32[]{:S(2)}) collective-permute-start(bf16[64,768]{1,0:T(8,128)(2,1)S(1)} %merge.7), channel_id=1, source_target_pairs={{0,24},{1,25},{2,26},{3,27},{4,28},{5,29},{6,30},{7,31},{8,16},{9,... | collective-permute-start | bytes 294920 | tf_op jit(solution)/shard_map/ppermute | solution.py:334
  53.0 5.5 %collective-permute-start.11 = (bf16[64,768]{1,0:T(8,128)(2,1)S(1)}, bf16[64,768]{1,0:T(8,128)(2,1)S(1)}, u32[]{:S(2)}, u32[]{:S(2)}) collective-permute-start(bf16[64,768]{1,0:T(8,128)(2,1)S(1)} %merge.6.refs_2_), channel_id=1, source_target_pairs={{0,24},{1,25},{2,26},{3,27},{4,28},{5,29},{6,30},{7,31},{8,16},{9,... | collective-permute-start | bytes 294920 | tf_op jit(solution)/shard_map/ppermute | solution.py:334
  58.7 7.8 %collective-permute-start.15 = (bf16[128,768]{1,0:T(8,128)(2,1)S(1)}, bf16[128,768]{1,0:T(8,128)(2,1)S(1)}, u32[]{:S(2)}, u32[]{:S(2)}) collective-permute-start(bf16[128,768]{1,0:T(8,128)(2,1)S(1)} %get-tuple-element.31), channel_id=1, source_target_pairs={{0,6},{1,7},{2,4},{3,5},{4,2},{5,3},{6,0},{7,1},{8,14},{9,15},{10,... | collective-permute-start | bytes 589832 | tf_op jit(solution)/shard_map/ppermute | solution.py:334
  61.5 12.4 %collective-permute-start.16 = (bf16[128,768]{1,0:T(8,128)(2,1)S(1)}, bf16[128,768]{1,0:T(8,128)(2,1)S(1)}, u32[]{:S(2)}, u32[]{:S(2)}) collective-permute-start(bf16[128,768]{1,0:T(8,128)(2,1)S(1)} %get-tuple-element.32), channel_id=1, source_target_pairs={{0,4},{1,5},{2,6},{3,7},{4,0},{5,1},{6,2},{7,3},{8,12},{9,13},{10,... | collective-permute-start | bytes 589832 | tf_op jit(solution)/shard_map/ppermute | solution.py:334
  61.5 12.4 %collective-permute-start.17 = (bf16[128,768]{1,0:T(8,128)(2,1)S(1)}, bf16[128,768]{1,0:T(8,128)(2,1)S(1)}, u32[]{:S(2)}, u32[]{:S(2)}) collective-permute-start(bf16[128,768]{1,0:T(8,128)(2,1)S(1)} %get-tuple-element.33), channel_id=1, source_target_pairs={{0,2},{1,3},{2,0},{3,1},{4,6},{5,7},{6,4},{7,5},{8,10},{9,11},{10,... | collective-permute-start | bytes 589832 | tf_op jit(solution)/shard_map/ppermute | solution.py:334
  73.9 1.8 %collective-permute-start.18 = (bf16[1,128,1536]{2,1,0:T(8,128)(2,1)S(1)}, bf16[1,128,1536]{2,1,0:T(8,128)(2,1)S(1)}, u32[]{:S(2)}, u32[]{:S(2)}) collective-permute-start(bf16[1,128,1536]{2,1,0:T(8,128)(2,1)S(1)} %last.1), channel_id=1, source_target_pairs={{0,1},{1,0},{2,3},{3,2},{4,5},{5,4},{6,7},{7,6},{8,9},{9,8},{10,11... | collective-permute-start | bytes 1179656 | tf_op jit(solution)/shard_map/ppermute | solution.py:334

commit v8 on v6

--- a/solution.py
+++ b/solution.py
@@ -364,7 +364,6 @@
 
     own_send = project((upper, lower), 1)
     own = merge(whole, (project((upper, lower), 0), partner(own_send)))
-    upper, lower = hold((upper, lower), (own_send,))
     lower_1, upper_2 = swapped(lower, 1), swapped(upper, 2)
     held = hold((upper_1, lower_2), (lower_1, upper_2, *own))
     beside = (upper_1, lower_1, upper_2, lower_2)
@@ -375,9 +374,8 @@
     )
     across = (swapped(held[0], 2), swapped(held[1], 1))
     across_sum = (project(across, 0), partner(project(across, 1, (beside_keep,))))
-    across = merge((((0, 0),), ((0, 1),)), across_sum, beside[:1])
-    blocks = [*own, *(swapped(block, k + 1) for k, block in enumerate(beside))]
-    blocks += [swapped(block, 3) for block in across]
+    across = merge(whole, across_sum, beside[:1])
+    blocks = [swapped(block, k) if k else block for k, block in enumerate((*own, *beside, *across))]
     picked = call(pick_kernel, (single,) * n_head, "pick")(*blocks)
     arrived = [moved(picked[m], lambda i, j, s, m=m: (i, j ^ m, s)) for m in (3, 2, 1)]
     out = jax.ShapeDtypeStruct((1, rows, columns), jnp.bfloat16)

time: 77.8 us -> 75.4 us (0.969)
  starting transfers between devices: 26.6 us -> 25.4 us
  waiting for transfers between devices: 37.9 us -> 36.7 us
    ppermute x17 -> x16, waiting for transfers between devices: 31 us -> 29.7 us  [moved(): lax.ppermute(array, names, [(place[spot], place[target(*spot)]) for spot...]
    ppermute x17 -> x16, starting transfers between devices: 21.7 us -> 20.6 us  [moved(): lax.ppermute(array, names, [(place[spot], place[target(*spot)]) for spot...]
  transfers between devices with their start and end apart: 18 -> 17, of which waited for: 13 -> 14; matrix products, arithmetic and copies ran while one was open for 0% -> 0% of each run, Pallas kernels for 10% -> 12%
where the time goes in v8:
time: 75.4 us; the launch traced here: 75.2 us
  waiting for transfers between devices  36.7 us (49%)
  starting transfers between devices  25.4 us (34%)
  Pallas kernels  12.2 us (16%)
    ppermute x16, waiting for transfers between devices, moved(): lax.ppermute(array, names, [(place[spot], place[target(*spot)]) for spot...  29.7 us
    ppermute x16, starting transfers between devices, moved(): lax.ppermute(array, names, [(place[spot], place[target(*spot)]) for spot...  20.6 us
    ppermute x1, waiting for transfers between devices, from_before(): return lax.ppermute(array, 'ctx', [(i, i + by) for i in range(n_ctx - by)])  6.98 us
    ppermute x1, starting transfers between devices, from_before(): return lax.ppermute(array, 'ctx', [(i, i + by) for i in range(n_ctx - by)])  4.87 us
    pallas_call x6, Pallas kernels, project(): call(kernel, shape, 'project', in_specs=specs)(*picked, weight, *after)  4.4 us
    pallas_call x1, Pallas kernels, on_device(): call(inside_kernel, (pltpu.VMEM((rows, width), jnp.float32), pltpu.VMEM((...  4.24 us
    pallas_call x1, Pallas kernels, on_device(): call(state_kernel, state_shape, 'shard_state', in_specs=[HBM] * 4, scratc...  2.58 us
  transfers between devices with their start and end apart: 17, of which 14 were waited for; matrix products, arithmetic and copies ran while one was open for 0% of the time, Pallas kernels for 12%

profile of v8, /device:TPU:0, one launch (start us, length us, event | category | flops | bytes accessed | tf_op | source)
XLA Modules:
  0.0 75.2 jit_solution(5379725552133974954)
XLA Ops:
  0.0 2.6 %shard_state.1 = bf16[2064,128]{1,0:T(8,128)(2,1)S(1)} custom-call(bf16[1,128,2048]{2,1,0:T(8,128)(2,1)} %key_hbm.3, bf16[1,128,2048]{2,1,0:T(8,128)(2,1)} %value_hbm.3, f32[1,16,128]{2,1,0:T(8,128)} %bitcast.1, s32[1,128]{1,0:T(1,128)} %doc_hbm.3), custom_call_target="tpu_custom_call" | custom-call | flops 1 | bytes 1 | tf_op jit(solution)/shard_map/shard_state/pallas_call | solution.py:258
  2.6 4.9 %collective-permute-start = (bf16[2064,128]{1,0:T(8,128)(2,1)S(1)}, bf16[2064,128]{1,0:T(8,128)(2,1)S(1)}, u32[]{:S(2)}, u32[]{:S(2)}) collective-permute-start(bf16[2064,128]{1,0:T(8,128)(2,1)S(1)} %shard_state.1), channel_id=1, source_target_pairs={{0,8},{8,16},{16,24},{1,9},{9,17},{17,25},{2,10},{10,18},{18,26},{... | collective-permute-start | bytes 1585160 | tf_op jit(solution)/shard_map/ppermute | solution.py:254
  7.5 4.2 %inside.1 = (f32[128,2048]{1,0:T(8,128)S(1)}, f32[128,2048]{1,0:T(8,128)S(1)}, f32[128,128]{1,0:T(8,128)S(1)}, bf16[128,2048]{1,0:T(8,128)(2,1)S(1)}, bf16[2048,1536]{1,0:T(8,128)(2,1)S(1)}) custom-call(bf16[1,128,2048]{2,1,0:T(8,128)(2,1)} %query_hbm.1, bf16[1,128,2048]{2,1,0:T(8,128)(2,1)} %key_hbm.3, bf16[1,128,2048]{2,1,0:T(8,128)(2,1)} %value_hbm.3, ...), custom_call_target="tpu_custom_call" | custom-call | flops 1 | bytes 1 | tf_op jit(solution)/shard_map/inside/pallas_call | solution.py:290
  11.7 7.0 %collective-permute-done.state_ref = bf16[2064,128]{1,0:T(8,128)(2,1)S(1)} collective-permute-done((bf16[2064,128]{1,0:T(8,128)(2,1)S(1)}, bf16[2064,128]{1,0:T(8,128)(2,1)S(1)}, u32[]{:S(2)}, u32[]{:S(2)}) %collective-permute-start) | collective-permute-done | bytes 528416 | tf_op jit(solution)/shard_map/ppermute | solution.py:254
  19.3 3.5 %collective-permute-start.4 = (bf16[64,2048]{1,0:T(8,128)(2,1)S(1)}, bf16[64,2048]{1,0:T(8,128)(2,1)S(1)}, u32[]{:S(2)}, u32[]{:S(2)}) collective-permute-start(bf16[64,2048]{1,0:T(8,128)(2,1)S(1)} %get-tuple-element.24.refs_0_), channel_id=1, source_target_pairs={{0,16},{1,17},{2,18},{3,19},{4,20},{5,21},{6,22},{7,23},{8,24},{9,... | collective-permute-start | bytes 786440 | tf_op jit(solution)/shard_map/ppermute | solution.py:334
  23.8 1.0 %collective-permute-start.3 = (bf16[64,2048]{1,0:T(8,128)(2,1)S(1)}, bf16[64,2048]{1,0:T(8,128)(2,1)S(1)}, u32[]{:S(2)}, u32[]{:S(2)}) collective-permute-start(bf16[64,2048]{1,0:T(8,128)(2,1)S(1)} %get-tuple-element.25.refs_1_), channel_id=1, source_target_pairs={{0,8},{1,9},{2,10},{3,11},{4,12},{5,13},{6,14},{7,15},{8,0},{9,1},... | collective-permute-start | bytes 786440 | tf_op jit(solution)/shard_map/ppermute | solution.py:334
  25.5 1.6 %collective-permute-start.1 = (bf16[2,64,768]{2,1,0:T(8,128)(2,1)S(1)}, bf16[2,64,768]{2,1,0:T(8,128)(2,1)S(1)}, u32[]{:S(2)}, u32[]{:S(2)}) collective-permute-start(bf16[2,64,768]{2,1,0:T(8,128)(2,1)S(1)} %project.7), channel_id=1, source_target_pairs={{0,2},{1,3},{2,0},{3,1},{4,6},{5,7},{6,4},{7,5},{8,10},{9,11},{10,... | collective-permute-start | bytes 589832 | tf_op jit(solution)/shard_map/ppermute | solution.py:334
  27.7 3.5 %collective-permute-done.1.refs_1_ = bf16[2,64,768]{2,1,0:T(8,128)(2,1)S(1)} collective-permute-done((bf16[2,64,768]{2,1,0:T(8,128)(2,1)S(1)}, bf16[2,64,768]{2,1,0:T(8,128)(2,1)S(1)}, u32[]{:S(2)}, u32[]{:S(2)}) %collective-permute-start.1) | collective-permute-done | bytes 196640 | tf_op jit(solution)/shard_map/ppermute | solution.py:334
  32.0 1.8 %collective-permute-done.5.refs_3_.lower_ref = bf16[64,2048]{1,0:T(8,128)(2,1)S(1)} collective-permute-done((bf16[64,2048]{1,0:T(8,128)(2,1)S(1)}, bf16[64,2048]{1,0:T(8,128)(2,1)S(1)}, u32[]{:S(2)}, u32[]{:S(2)}) %collective-permute-start.5) | collective-permute-done | bytes 262176 | tf_op jit(solution)/shard_map/ppermute | solution.py:334
  33.8 1.5 %collective-permute-done.3.refs_1_.refs_0_ = bf16[64,2048]{1,0:T(8,128)(2,1)S(1)} collective-permute-done((bf16[64,2048]{1,0:T(8,128)(2,1)S(1)}, bf16[64,2048]{1,0:T(8,128)(2,1)S(1)}, u32[]{:S(2)}, u32[]{:S(2)}) %collective-permute-start.3) | collective-permute-done | bytes 262176 | tf_op jit(solution)/shard_map/ppermute | solution.py:334
  37.5 1.6 %collective-permute-start.6 = (bf16[4,64,768]{2,1,0:T(8,128)(2,1)S(1)}, bf16[4,64,768]{2,1,0:T(8,128)(2,1)S(1)}, u32[]{:S(2)}, u32[]{:S(2)}) collective-permute-start(bf16[4,64,768]{2,1,0:T(8,128)(2,1)S(1)} %project.9), channel_id=1, source_target_pairs={{0,2},{1,3},{2,0},{3,1},{4,6},{5,7},{6,4},{7,5},{8,10},{9,11},{10,... | collective-permute-start | bytes 1179656 | tf_op jit(solution)/shard_map/ppermute | solution.py:334
  40.1 1.6 %collective-permute-done.9.refs_0_ = bf16[64,2048]{1,0:T(8,128)(2,1)S(1)} collective-permute-done((bf16[64,2048]{1,0:T(8,128)(2,1)S(1)}, bf16[64,2048]{1,0:T(8,128)(2,1)S(1)}, u32[]{:S(2)}, u32[]{:S(2)}) %collective-permute-start.9) | collective-permute-done | bytes 262176 | tf_op jit(solution)/shard_map/ppermute | solution.py:334
  42.7 1.6 %collective-permute-start.11 = (bf16[2,64,768]{2,1,0:T(8,128)(2,1)S(1)}, bf16[2,64,768]{2,1,0:T(8,128)(2,1)S(1)}, u32[]{:S(2)}, u32[]{:S(2)}) collective-permute-start(bf16[2,64,768]{2,1,0:T(8,128)(2,1)S(1)} %project.11), channel_id=1, source_target_pairs={{0,2},{1,3},{2,0},{3,1},{4,6},{5,7},{6,4},{7,5},{8,10},{9,11},{10,... | collective-permute-start | bytes 589832 | tf_op jit(solution)/shard_map/ppermute | solution.py:334
  44.9 3.0 %collective-permute-done.6.refs_1_ = bf16[4,64,768]{2,1,0:T(8,128)(2,1)S(1)} collective-permute-done((bf16[4,64,768]{2,1,0:T(8,128)(2,1)S(1)}, bf16[4,64,768]{2,1,0:T(8,128)(2,1)S(1)}, u32[]{:S(2)}, u32[]{:S(2)}) %collective-permute-start.6) | collective-permute-done | bytes 393248 | tf_op jit(solution)/shard_map/ppermute | solution.py:334
  48.0 1.5 %collective-permute-start.8 = (bf16[128,768]{1,0:T(8,128)(2,1)S(1)}, bf16[128,768]{1,0:T(8,128)(2,1)S(1)}, u32[]{:S(2)}, u32[]{:S(2)}) collective-permute-start(bf16[128,768]{1,0:T(8,128)(2,1)S(1)} %get-tuple-element.28), channel_id=1, source_target_pairs={{0,16},{1,17},{2,18},{3,19},{4,20},{5,21},{6,22},{7,23},{8,24},{9,... | collective-permute-start | bytes 589832 | tf_op jit(solution)/shard_map/ppermute | solution.py:334
  49.5 1.4 %collective-permute-start.7 = (bf16[128,768]{1,0:T(8,128)(2,1)S(1)}, bf16[128,768]{1,0:T(8,128)(2,1)S(1)}, u32[]{:S(2)}, u32[]{:S(2)}) collective-permute-start(bf16[128,768]{1,0:T(8,128)(2,1)S(1)} %get-tuple-element.27.refs_2_), channel_id=1, source_target_pairs={{0,8},{1,9},{2,10},{3,11},{4,12},{5,13},{6,14},{7,15},{8,0},{9,1},... | collective-permute-start | bytes 589832 | tf_op jit(solution)/shard_map/ppermute | solution.py:334
  51.0 1.4 %collective-permute-start.12 = (bf16[128,768]{1,0:T(8,128)(2,1)S(1)}, bf16[128,768]{1,0:T(8,128)(2,1)S(1)}, u32[]{:S(2)}, u32[]{:S(2)}) collective-permute-start(bf16[128,768]{1,0:T(8,128)(2,1)S(1)} %merge.5), channel_id=1, source_target_pairs={{0,24},{1,25},{2,26},{3,27},{4,28},{5,29},{6,30},{7,31},{8,16},{9,... | collective-permute-start | bytes 589832 | tf_op jit(solution)/shard_map/ppermute | solution.py:334
  52.5 1.7 %collective-permute-done.8.refs_2_ = bf16[128,768]{1,0:T(8,128)(2,1)S(1)} collective-permute-done((bf16[128,768]{1,0:T(8,128)(2,1)S(1)}, bf16[128,768]{1,0:T(8,128)(2,1)S(1)}, u32[]{:S(2)}, u32[]{:S(2)}) %collective-permute-start.8) | collective-permute-done | bytes 196640 | tf_op jit(solution)/shard_map/ppermute | solution.py:334
  54.2 1.0 %collective-permute-done.7.refs_1_ = bf16[128,768]{1,0:T(8,128)(2,1)S(1)} collective-permute-done((bf16[128,768]{1,0:T(8,128)(2,1)S(1)}, bf16[128,768]{1,0:T(8,128)(2,1)S(1)}, u32[]{:S(2)}, u32[]{:S(2)}) %collective-permute-start.7) | collective-permute-done | bytes 196640 | tf_op jit(solution)/shard_map/ppermute | solution.py:334
  55.2 2.4 %collective-permute-done.12.refs_3_ = bf16[128,768]{1,0:T(8,128)(2,1)S(1)} collective-permute-done((bf16[128,768]{1,0:T(8,128)(2,1)S(1)}, bf16[128,768]{1,0:T(8,128)(2,1)S(1)}, u32[]{:S(2)}, u32[]{:S(2)}) %collective-permute-start.12) | collective-permute-done | bytes 196640 | tf_op jit(solution)/shard_map/ppermute | solution.py:334
  57.8 3.6 %collective-permute-start.13 = (bf16[128,768]{1,0:T(8,128)(2,1)S(1)}, bf16[128,768]{1,0:T(8,128)(2,1)S(1)}, u32[]{:S(2)}, u32[]{:S(2)}) collective-permute-start(bf16[128,768]{1,0:T(8,128)(2,1)S(1)} %get-tuple-element.31), channel_id=1, source_target_pairs={{0,6},{1,7},{2,4},{3,5},{4,2},{5,3},{6,0},{7,1},{8,14},{9,15},{10,... | collective-permute-start | bytes 589832 | tf_op jit(solution)/shard_map/ppermute | solution.py:334
  62.2 3.2 %collective-permute-done.13.refs_0_ = bf16[128,768]{1,0:T(8,128)(2,1)S(1)} collective-permute-done((bf16[128,768]{1,0:T(8,128)(2,1)S(1)}, bf16[128,768]{1,0:T(8,128)(2,1)S(1)}, u32[]{:S(2)}, u32[]{:S(2)}) %collective-permute-start.13) | collective-permute-done | bytes 196640 | tf_op jit(solution)/shard_map/ppermute | solution.py:334
  65.5 7.1 %collective-permute-done.14.refs_1_ = bf16[128,768]{1,0:T(8,128)(2,1)S(1)} collective-permute-done((bf16[128,768]{1,0:T(8,128)(2,1)S(1)}, bf16[128,768]{1,0:T(8,128)(2,1)S(1)}, u32[]{:S(2)}, u32[]{:S(2)}) %collective-permute-start.14) | collective-permute-done | bytes 196640 | tf_op jit(solution)/shard_map/ppermute | solution.py:334
  72.7 1.7 %collective-permute-done.16 = bf16[1,128,1536]{2,1,0:T(8,128)(2,1)S(1)} collective-permute-done((bf16[1,128,1536]{2,1,0:T(8,128)(2,1)S(1)}, bf16[1,128,1536]{2,1,0:T(8,128)(2,1)S(1)}, u32[]{:S(2)}, u32[]{:S(2)}) %collective-permute-start.16) | collective-permute-done | bytes 393248 | tf_op jit(solution)/shard_map/ppermute | solution.py:334
  (26 shorter events, 10.4 us)
Async XLA Ops:
  2.6 16.1 %collective-permute-start = (bf16[2064,128]{1,0:T(8,128)(2,1)S(1)}, bf16[2064,128]{1,0:T(8,128)(2,1)S(1)}, u32[]{:S(2)}, u32[]{:S(2)}) collective-permute-start(bf16[2064,128]{1,0:T(8,128)(2,1)S(1)} %shard_state.1), channel_id=1, source_target_pairs={{0,8},{8,16},{16,24},{1,9},{9,17},{17,25},{2,10},{10,18},{18,26},{... | collective-permute-start | bytes 1585160 | tf_op jit(solution)/shard_map/ppermute | solution.py:254
  19.3 12.0 %collective-permute-start.4 = (bf16[64,2048]{1,0:T(8,128)(2,1)S(1)}, bf16[64,2048]{1,0:T(8,128)(2,1)S(1)}, u32[]{:S(2)}, u32[]{:S(2)}) collective-permute-start(bf16[64,2048]{1,0:T(8,128)(2,1)S(1)} %get-tuple-element.24.refs_0_), channel_id=1, source_target_pairs={{0,16},{1,17},{2,18},{3,19},{4,20},{5,21},{6,22},{7,23},{8,24},{9,... | collective-permute-start | bytes 786440 | tf_op jit(solution)/shard_map/ppermute | solution.py:334
  22.7 9.2 %collective-permute-start.2 = (bf16[64,2048]{1,0:T(8,128)(2,1)S(1)}, bf16[64,2048]{1,0:T(8,128)(2,1)S(1)}, u32[]{:S(2)}, u32[]{:S(2)}) collective-permute-start(bf16[64,2048]{1,0:T(8,128)(2,1)S(1)} %get-tuple-element.24.refs_0_), channel_id=1, source_target_pairs={{0,8},{1,9},{2,10},{3,11},{4,12},{5,13},{6,14},{7,15},{8,0},{9,1},... | collective-permute-start | bytes 786440 | tf_op jit(solution)/shard_map/ppermute | solution.py:334
  23.3 10.5 %collective-permute-start.5 = (bf16[64,2048]{1,0:T(8,128)(2,1)S(1)}, bf16[64,2048]{1,0:T(8,128)(2,1)S(1)}, u32[]{:S(2)}, u32[]{:S(2)}) collective-permute-start(bf16[64,2048]{1,0:T(8,128)(2,1)S(1)} %get-tuple-element.25.refs_1_), channel_id=1, source_target_pairs={{0,16},{1,17},{2,18},{3,19},{4,20},{5,21},{6,22},{7,23},{8,24},{9,... | collective-permute-start | bytes 786440 | tf_op jit(solution)/shard_map/ppermute | solution.py:334
  23.8 11.4 %collective-permute-start.3 = (bf16[64,2048]{1,0:T(8,128)(2,1)S(1)}, bf16[64,2048]{1,0:T(8,128)(2,1)S(1)}, u32[]{:S(2)}, u32[]{:S(2)}) collective-permute-start(bf16[64,2048]{1,0:T(8,128)(2,1)S(1)} %get-tuple-element.25.refs_1_), channel_id=1, source_target_pairs={{0,8},{1,9},{2,10},{3,11},{4,12},{5,13},{6,14},{7,15},{8,0},{9,1},... | collective-permute-start | bytes 786440 | tf_op jit(solution)/shard_map/ppermute | solution.py:334
  25.5 5.7 %collective-permute-start.1 = (bf16[2,64,768]{2,1,0:T(8,128)(2,1)S(1)}, bf16[2,64,768]{2,1,0:T(8,128)(2,1)S(1)}, u32[]{:S(2)}, u32[]{:S(2)}) collective-permute-start(bf16[2,64,768]{2,1,0:T(8,128)(2,1)S(1)} %project.7), channel_id=1, source_target_pairs={{0,2},{1,3},{2,0},{3,1},{4,6},{5,7},{6,4},{7,5},{8,10},{9,11},{10,... | collective-permute-start | bytes 589832 | tf_op jit(solution)/shard_map/ppermute | solution.py:334
  35.3 6.4 %collective-permute-start.9 = (bf16[64,2048]{1,0:T(8,128)(2,1)S(1)}, bf16[64,2048]{1,0:T(8,128)(2,1)S(1)}, u32[]{:S(2)}, u32[]{:S(2)}) collective-permute-start(bf16[64,2048]{1,0:T(8,128)(2,1)S(1)} %get-tuple-element.29), channel_id=1, source_target_pairs={{0,16},{1,17},{2,18},{3,19},{4,20},{5,21},{6,22},{7,23},{8,24},{9,... | collective-permute-start | bytes 786440 | tf_op jit(solution)/shard_map/ppermute | solution.py:334
  35.7 6.4 %collective-permute-start.10 = (bf16[64,2048]{1,0:T(8,128)(2,1)S(1)}, bf16[64,2048]{1,0:T(8,128)(2,1)S(1)}, u32[]{:S(2)}, u32[]{:S(2)}) collective-permute-start(bf16[64,2048]{1,0:T(8,128)(2,1)S(1)} %get-tuple-element.30), channel_id=1, source_target_pairs={{0,8},{1,9},{2,10},{3,11},{4,12},{5,13},{6,14},{7,15},{8,0},{9,1},... | collective-permute-start | bytes 786440 | tf_op jit(solution)/shard_map/ppermute | solution.py:334
  37.5 10.4 %collective-permute-start.6 = (bf16[4,64,768]{2,1,0:T(8,128)(2,1)S(1)}, bf16[4,64,768]{2,1,0:T(8,128)(2,1)S(1)}, u32[]{:S(2)}, u32[]{:S(2)}) collective-permute-start(bf16[4,64,768]{2,1,0:T(8,128)(2,1)S(1)} %project.9), channel_id=1, source_target_pairs={{0,2},{1,3},{2,0},{3,1},{4,6},{5,7},{6,4},{7,5},{8,10},{9,11},{10,... | collective-permute-start | bytes 1179656 | tf_op jit(solution)/shard_map/ppermute | solution.py:334
  42.7 8.3 %collective-permute-start.11 = (bf16[2,64,768]{2,1,0:T(8,128)(2,1)S(1)}, bf16[2,64,768]{2,1,0:T(8,128)(2,1)S(1)}, u32[]{:S(2)}, u32[]{:S(2)}) collective-permute-start(bf16[2,64,768]{2,1,0:T(8,128)(2,1)S(1)} %project.11), channel_id=1, source_target_pairs={{0,2},{1,3},{2,0},{3,1},{4,6},{5,7},{6,4},{7,5},{8,10},{9,11},{10,... | collective-permute-start | bytes 589832 | tf_op jit(solution)/shard_map/ppermute | solution.py:334
  48.0 6.2 %collective-permute-start.8 = (bf16[128,768]{1,0:T(8,128)(2,1)S(1)}, bf16[128,768]{1,0:T(8,128)(2,1)S(1)}, u32[]{:S(2)}, u32[]{:S(2)}) collective-permute-start(bf16[128,768]{1,0:T(8,128)(2,1)S(1)} %get-tuple-element.28), channel_id=1, source_target_pairs={{0,16},{1,17},{2,18},{3,19},{4,20},{5,21},{6,22},{7,23},{8,24},{9,... | collective-permute-start | bytes 589832 | tf_op jit(solution)/shard_map/ppermute | solution.py:334
  49.5 5.7 %collective-permute-start.7 = (bf16[128,768]{1,0:T(8,128)(2,1)S(1)}, bf16[128,768]{1,0:T(8,128)(2,1)S(1)}, u32[]{:S(2)}, u32[]{:S(2)}) collective-permute-start(bf16[128,768]{1,0:T(8,128)(2,1)S(1)} %get-tuple-element.27.refs_2_), channel_id=1, source_target_pairs={{0,8},{1,9},{2,10},{3,11},{4,12},{5,13},{6,14},{7,15},{8,0},{9,1},... | collective-permute-start | bytes 589832 | tf_op jit(solution)/shard_map/ppermute | solution.py:334
  51.0 6.6 %collective-permute-start.12 = (bf16[128,768]{1,0:T(8,128)(2,1)S(1)}, bf16[128,768]{1,0:T(8,128)(2,1)S(1)}, u32[]{:S(2)}, u32[]{:S(2)}) collective-permute-start(bf16[128,768]{1,0:T(8,128)(2,1)S(1)} %merge.5), channel_id=1, source_target_pairs={{0,24},{1,25},{2,26},{3,27},{4,28},{5,29},{6,30},{7,31},{8,16},{9,... | collective-permute-start | bytes 589832 | tf_op jit(solution)/shard_map/ppermute | solution.py:334
  57.8 7.7 %collective-permute-start.13 = (bf16[128,768]{1,0:T(8,128)(2,1)S(1)}, bf16[128,768]{1,0:T(8,128)(2,1)S(1)}, u32[]{:S(2)}, u32[]{:S(2)}) collective-permute-start(bf16[128,768]{1,0:T(8,128)(2,1)S(1)} %get-tuple-element.31), channel_id=1, source_target_pairs={{0,6},{1,7},{2,4},{3,5},{4,2},{5,3},{6,0},{7,1},{8,14},{9,15},{10,... | collective-permute-start | bytes 589832 | tf_op jit(solution)/shard_map/ppermute | solution.py:334
  61.4 11.1 %collective-permute-start.14 = (bf16[128,768]{1,0:T(8,128)(2,1)S(1)}, bf16[128,768]{1,0:T(8,128)(2,1)S(1)}, u32[]{:S(2)}, u32[]{:S(2)}) collective-permute-start(bf16[128,768]{1,0:T(8,128)(2,1)S(1)} %get-tuple-element.32), channel_id=1, source_target_pairs={{0,4},{1,5},{2,6},{3,7},{4,0},{5,1},{6,2},{7,3},{8,12},{9,13},{10,... | collective-permute-start | bytes 589832 | tf_op jit(solution)/shard_map/ppermute | solution.py:334
  61.4 11.1 %collective-permute-start.15 = (bf16[128,768]{1,0:T(8,128)(2,1)S(1)}, bf16[128,768]{1,0:T(8,128)(2,1)S(1)}, u32[]{:S(2)}, u32[]{:S(2)}) collective-permute-start(bf16[128,768]{1,0:T(8,128)(2,1)S(1)} %get-tuple-element.33), channel_id=1, source_target_pairs={{0,2},{1,3},{2,0},{3,1},{4,6},{5,7},{6,4},{7,5},{8,10},{9,11},{10,... | collective-permute-start | bytes 589832 | tf_op jit(solution)/shard_map/ppermute | solution.py:334
  72.7 1.8 %collective-permute-start.16 = (bf16[1,128,1536]{2,1,0:T(8,128)(2,1)S(1)}, bf16[1,128,1536]{2,1,0:T(8,128)(2,1)S(1)}, u32[]{:S(2)}, u32[]{:S(2)}) collective-permute-start(bf16[1,128,1536]{2,1,0:T(8,128)(2,1)S(1)} %last.1), channel_id=1, source_target_pairs={{0,1},{1,0},{2,3},{3,2},{4,5},{5,4},{6,7},{7,6},{8,9},{9,8},{10,11... | collective-permute-start | bytes 1179656 | tf_op jit(solution)/shard_map/ppermute | solution.py:334

commit v9 on v8

--- a/solution.py
+++ b/solution.py
@@ -52,7 +52,7 @@
         )
 
 
-def state_kernel(
+def state_work(
     key_hbm,
     value_hbm,
     rate_hbm,
@@ -90,6 +90,12 @@
         for copy in pieces[part]:
             copy.wait()
     own_fading(doc_ref[...], across, key_ref, value_ref, 0, out_ref)
+
+
+def state_kernel(*refs):
+    @pl.when(lax.axis_index("ctx") < lax.axis_size("ctx") - 1)
+    def _():
+        state_work(*refs)
 
 
 def inside_kernel(

time: 75.4 us -> 75.3 us (level)
  no operation moved by 1% of the time
where the time goes in v9:
time: 75.3 us; the launch traced here: 75.1 us
  waiting for transfers between devices  36.5 us (48%)
  starting transfers between devices  25.5 us (34%)
  Pallas kernels  12.2 us (16%)
    ppermute x16, waiting for transfers between devices, moved(): lax.ppermute(array, names, [(place[spot], place[target(*spot)]) for spot...  29.6 us
    ppermute x16, starting transfers between devices, moved(): lax.ppermute(array, names, [(place[spot], place[target(*spot)]) for spot...  20.6 us
    ppermute x1, waiting for transfers between devices, from_before(): return lax.ppermute(array, 'ctx', [(i, i + by) for i in range(n_ctx - by)])  6.98 us
    ppermute x1, starting transfers between devices, from_before(): return lax.ppermute(array, 'ctx', [(i, i + by) for i in range(n_ctx - by)])  4.87 us
    pallas_call x6, Pallas kernels, project(): call(kernel, shape, 'project', in_specs=specs)(*picked, weight, *after)  4.4 us
    pallas_call x1, Pallas kernels, on_device(): call(inside_kernel, (pltpu.VMEM((rows, width), jnp.float32), pltpu.VMEM((...  4.24 us
    pallas_call x1, Pallas kernels, on_device(): call(state_kernel, state_shape, 'shard_state', in_specs=[HBM] * 4, scratc...  2.58 us
  transfers between devices with their start and end apart: 17, of which 14 were waited for; matrix products, arithmetic and copies ran while one was open for 0% of the time, Pallas kernels for 12%

profile of v9, /device:TPU:0, one launch (start us, length us, event | category | flops | bytes accessed | tf_op | source)
XLA Modules:
  0.0 75.1 jit_solution(12488397540395827314)
XLA Ops:
  0.0 2.6 %shard_state.1 = bf16[2064,128]{1,0:T(8,128)(2,1)S(1)} custom-call(bf16[1,128,2048]{2,1,0:T(8,128)(2,1)} %refs_0_.1, bf16[1,128,2048]{2,1,0:T(8,128)(2,1)} %refs_1_.1, f32[1,16,128]{2,1,0:T(8,128)} %bitcast.1, s32[1,128]{1,0:T(1,128)} %refs_3_.1), custom_call_target="tpu_custom_call" | custom-call | flops 1 | bytes 1 | tf_op jit(solution)/shard_map/shard_state/pallas_call | solution.py:264
  2.6 4.9 %collective-permute-start = (bf16[2064,128]{1,0:T(8,128)(2,1)S(1)}, bf16[2064,128]{1,0:T(8,128)(2,1)S(1)}, u32[]{:S(2)}, u32[]{:S(2)}) collective-permute-start(bf16[2064,128]{1,0:T(8,128)(2,1)S(1)} %shard_state.1), channel_id=1, source_target_pairs={{0,8},{8,16},{16,24},{1,9},{9,17},{17,25},{2,10},{10,18},{18,26},{... | collective-permute-start | bytes 1585160 | tf_op jit(solution)/shard_map/ppermute | solution.py:260
  7.5 4.2 %inside.1 = (f32[128,2048]{1,0:T(8,128)S(1)}, f32[128,2048]{1,0:T(8,128)S(1)}, f32[128,128]{1,0:T(8,128)S(1)}, bf16[128,2048]{1,0:T(8,128)(2,1)S(1)}, bf16[2048,1536]{1,0:T(8,128)(2,1)S(1)}) custom-call(bf16[1,128,2048]{2,1,0:T(8,128)(2,1)} %query_hbm.1, bf16[1,128,2048]{2,1,0:T(8,128)(2,1)} %refs_0_.1, bf16[1,128,2048]{2,1,0:T(8,128)(2,1)} %refs_1_.1, ...), custom_call_target="tpu_custom_call" | custom-call | flops 1 | bytes 1 | tf_op jit(solution)/shard_map/inside/pallas_call | solution.py:296
  11.7 7.0 %collective-permute-done.state_ref = bf16[2064,128]{1,0:T(8,128)(2,1)S(1)} collective-permute-done((bf16[2064,128]{1,0:T(8,128)(2,1)S(1)}, bf16[2064,128]{1,0:T(8,128)(2,1)S(1)}, u32[]{:S(2)}, u32[]{:S(2)}) %collective-permute-start) | collective-permute-done | bytes 528416 | tf_op jit(solution)/shard_map/ppermute | solution.py:260
  19.3 3.5 %collective-permute-start.4 = (bf16[64,2048]{1,0:T(8,128)(2,1)S(1)}, bf16[64,2048]{1,0:T(8,128)(2,1)S(1)}, u32[]{:S(2)}, u32[]{:S(2)}) collective-permute-start(bf16[64,2048]{1,0:T(8,128)(2,1)S(1)} %get-tuple-element.24.refs_0_), channel_id=1, source_target_pairs={{0,16},{1,17},{2,18},{3,19},{4,20},{5,21},{6,22},{7,23},{8,24},{9,... | collective-permute-start | bytes 786440 | tf_op jit(solution)/shard_map/ppermute | solution.py:340
  22.7 1.1 %collective-permute-start.5 = (bf16[64,2048]{1,0:T(8,128)(2,1)S(1)}, bf16[64,2048]{1,0:T(8,128)(2,1)S(1)}, u32[]{:S(2)}, u32[]{:S(2)}) collective-permute-start(bf16[64,2048]{1,0:T(8,128)(2,1)S(1)} %get-tuple-element.25.refs_1_), channel_id=1, source_target_pairs={{0,16},{1,17},{2,18},{3,19},{4,20},{5,21},{6,22},{7,23},{8,24},{9,... | collective-permute-start | bytes 786440 | tf_op jit(solution)/shard_map/ppermute | solution.py:340
  25.5 1.6 %collective-permute-start.1 = (bf16[2,64,768]{2,1,0:T(8,128)(2,1)S(1)}, bf16[2,64,768]{2,1,0:T(8,128)(2,1)S(1)}, u32[]{:S(2)}, u32[]{:S(2)}) collective-permute-start(bf16[2,64,768]{2,1,0:T(8,128)(2,1)S(1)} %project.7), channel_id=1, source_target_pairs={{0,2},{1,3},{2,0},{3,1},{4,6},{5,7},{6,4},{7,5},{8,10},{9,11},{10,... | collective-permute-start | bytes 589832 | tf_op jit(solution)/shard_map/ppermute | solution.py:340
  27.7 3.5 %collective-permute-done.1.refs_1_ = bf16[2,64,768]{2,1,0:T(8,128)(2,1)S(1)} collective-permute-done((bf16[2,64,768]{2,1,0:T(8,128)(2,1)S(1)}, bf16[2,64,768]{2,1,0:T(8,128)(2,1)S(1)}, u32[]{:S(2)}, u32[]{:S(2)}) %collective-permute-start.1) | collective-permute-done | bytes 196640 | tf_op jit(solution)/shard_map/ppermute | solution.py:340
  32.0 1.8 %collective-permute-done.5.refs_3_.lower_ref = bf16[64,2048]{1,0:T(8,128)(2,1)S(1)} collective-permute-done((bf16[64,2048]{1,0:T(8,128)(2,1)S(1)}, bf16[64,2048]{1,0:T(8,128)(2,1)S(1)}, u32[]{:S(2)}, u32[]{:S(2)}) %collective-permute-start.5) | collective-permute-done | bytes 262176 | tf_op jit(solution)/shard_map/ppermute | solution.py:340
  33.8 1.5 %collective-permute-done.3.refs_1_.refs_0_ = bf16[64,2048]{1,0:T(8,128)(2,1)S(1)} collective-permute-done((bf16[64,2048]{1,0:T(8,128)(2,1)S(1)}, bf16[64,2048]{1,0:T(8,128)(2,1)S(1)}, u32[]{:S(2)}, u32[]{:S(2)}) %collective-permute-start.3) | collective-permute-done | bytes 262176 | tf_op jit(solution)/shard_map/ppermute | solution.py:340
  37.5 1.6 %collective-permute-start.6 = (bf16[4,64,768]{2,1,0:T(8,128)(2,1)S(1)}, bf16[4,64,768]{2,1,0:T(8,128)(2,1)S(1)}, u32[]{:S(2)}, u32[]{:S(2)}) collective-permute-start(bf16[4,64,768]{2,1,0:T(8,128)(2,1)S(1)} %project.9), channel_id=1, source_target_pairs={{0,2},{1,3},{2,0},{3,1},{4,6},{5,7},{6,4},{7,5},{8,10},{9,11},{10,... | collective-permute-start | bytes 1179656 | tf_op jit(solution)/shard_map/ppermute | solution.py:340
  40.1 1.6 %collective-permute-done.9.refs_0_ = bf16[64,2048]{1,0:T(8,128)(2,1)S(1)} collective-permute-done((bf16[64,2048]{1,0:T(8,128)(2,1)S(1)}, bf16[64,2048]{1,0:T(8,128)(2,1)S(1)}, u32[]{:S(2)}, u32[]{:S(2)}) %collective-permute-start.9) | collective-permute-done | bytes 262176 | tf_op jit(solution)/shard_map/ppermute | solution.py:340
  42.7 1.6 %collective-permute-start.11 = (bf16[2,64,768]{2,1,0:T(8,128)(2,1)S(1)}, bf16[2,64,768]{2,1,0:T(8,128)(2,1)S(1)}, u32[]{:S(2)}, u32[]{:S(2)}) collective-permute-start(bf16[2,64,768]{2,1,0:T(8,128)(2,1)S(1)} %project.11), channel_id=1, source_target_pairs={{0,2},{1,3},{2,0},{3,1},{4,6},{5,7},{6,4},{7,5},{8,10},{9,11},{10,... | collective-permute-start | bytes 589832 | tf_op jit(solution)/shard_map/ppermute | solution.py:340
  44.9 2.9 %collective-permute-done.6.refs_1_ = bf16[4,64,768]{2,1,0:T(8,128)(2,1)S(1)} collective-permute-done((bf16[4,64,768]{2,1,0:T(8,128)(2,1)S(1)}, bf16[4,64,768]{2,1,0:T(8,128)(2,1)S(1)}, u32[]{:S(2)}, u32[]{:S(2)}) %collective-permute-start.6) | collective-permute-done | bytes 393248 | tf_op jit(solution)/shard_map/ppermute | solution.py:340
  48.0 1.6 %collective-permute-start.8 = (bf16[128,768]{1,0:T(8,128)(2,1)S(1)}, bf16[128,768]{1,0:T(8,128)(2,1)S(1)}, u32[]{:S(2)}, u32[]{:S(2)}) collective-permute-start(bf16[128,768]{1,0:T(8,128)(2,1)S(1)} %get-tuple-element.28), channel_id=1, source_target_pairs={{0,16},{1,17},{2,18},{3,19},{4,20},{5,21},{6,22},{7,23},{8,24},{9,... | collective-permute-start | bytes 589832 | tf_op jit(solution)/shard_map/ppermute | solution.py:340
  49.5 1.5 %collective-permute-start.7 = (bf16[128,768]{1,0:T(8,128)(2,1)S(1)}, bf16[128,768]{1,0:T(8,128)(2,1)S(1)}, u32[]{:S(2)}, u32[]{:S(2)}) collective-permute-start(bf16[128,768]{1,0:T(8,128)(2,1)S(1)} %get-tuple-element.27.refs_2_), channel_id=1, source_target_pairs={{0,8},{1,9},{2,10},{3,11},{4,12},{5,13},{6,14},{7,15},{8,0},{9,1},... | collective-permute-start | bytes 589832 | tf_op jit(solution)/shard_map/ppermute | solution.py:340
  51.0 1.4 %collective-permute-start.12 = (bf16[128,768]{1,0:T(8,128)(2,1)S(1)}, bf16[128,768]{1,0:T(8,128)(2,1)S(1)}, u32[]{:S(2)}, u32[]{:S(2)}) collective-permute-start(bf16[128,768]{1,0:T(8,128)(2,1)S(1)} %merge.5), channel_id=1, source_target_pairs={{0,24},{1,25},{2,26},{3,27},{4,28},{5,29},{6,30},{7,31},{8,16},{9,... | collective-permute-start | bytes 589832 | tf_op jit(solution)/shard_map/ppermute | solution.py:340
  52.5 1.6 %collective-permute-done.8.refs_2_ = bf16[128,768]{1,0:T(8,128)(2,1)S(1)} collective-permute-done((bf16[128,768]{1,0:T(8,128)(2,1)S(1)}, bf16[128,768]{1,0:T(8,128)(2,1)S(1)}, u32[]{:S(2)}, u32[]{:S(2)}) %collective-permute-start.8) | collective-permute-done | bytes 196640 | tf_op jit(solution)/shard_map/ppermute | solution.py:340
  54.1 1.1 %collective-permute-done.7.refs_1_ = bf16[128,768]{1,0:T(8,128)(2,1)S(1)} collective-permute-done((bf16[128,768]{1,0:T(8,128)(2,1)S(1)}, bf16[128,768]{1,0:T(8,128)(2,1)S(1)}, u32[]{:S(2)}, u32[]{:S(2)}) %collective-permute-start.7) | collective-permute-done | bytes 196640 | tf_op jit(solution)/shard_map/ppermute | solution.py:340
  55.2 2.5 %collective-permute-done.12.refs_3_ = bf16[128,768]{1,0:T(8,128)(2,1)S(1)} collective-permute-done((bf16[128,768]{1,0:T(8,128)(2,1)S(1)}, bf16[128,768]{1,0:T(8,128)(2,1)S(1)}, u32[]{:S(2)}, u32[]{:S(2)}) %collective-permute-start.12) | collective-permute-done | bytes 196640 | tf_op jit(solution)/shard_map/ppermute | solution.py:340
  57.8 3.6 %collective-permute-start.13 = (bf16[128,768]{1,0:T(8,128)(2,1)S(1)}, bf16[128,768]{1,0:T(8,128)(2,1)S(1)}, u32[]{:S(2)}, u32[]{:S(2)}) collective-permute-start(bf16[128,768]{1,0:T(8,128)(2,1)S(1)} %get-tuple-element.31), channel_id=1, source_target_pairs={{0,6},{1,7},{2,4},{3,5},{4,2},{5,3},{6,0},{7,1},{8,14},{9,15},{10,... | collective-permute-start | bytes 589832 | tf_op jit(solution)/shard_map/ppermute | solution.py:340
  62.2 3.2 %collective-permute-done.13.refs_0_ = bf16[128,768]{1,0:T(8,128)(2,1)S(1)} collective-permute-done((bf16[128,768]{1,0:T(8,128)(2,1)S(1)}, bf16[128,768]{1,0:T(8,128)(2,1)S(1)}, u32[]{:S(2)}, u32[]{:S(2)}) %collective-permute-start.13) | collective-permute-done | bytes 196640 | tf_op jit(solution)/shard_map/ppermute | solution.py:340
  65.5 7.0 %collective-permute-done.14.refs_1_ = bf16[128,768]{1,0:T(8,128)(2,1)S(1)} collective-permute-done((bf16[128,768]{1,0:T(8,128)(2,1)S(1)}, bf16[128,768]{1,0:T(8,128)(2,1)S(1)}, u32[]{:S(2)}, u32[]{:S(2)}) %collective-permute-start.14) | collective-permute-done | bytes 196640 | tf_op jit(solution)/shard_map/ppermute | solution.py:340
  72.6 1.7 %collective-permute-done.16 = bf16[1,128,1536]{2,1,0:T(8,128)(2,1)S(1)} collective-permute-done((bf16[1,128,1536]{2,1,0:T(8,128)(2,1)S(1)}, bf16[1,128,1536]{2,1,0:T(8,128)(2,1)S(1)}, u32[]{:S(2)}, u32[]{:S(2)}) %collective-permute-start.16) | collective-permute-done | bytes 393248 | tf_op jit(solution)/shard_map/ppermute | solution.py:340
  (26 shorter events, 10.3 us)
Async XLA Ops:
  2.6 16.1 %collective-permute-start = (bf16[2064,128]{1,0:T(8,128)(2,1)S(1)}, bf16[2064,128]{1,0:T(8,128)(2,1)S(1)}, u32[]{:S(2)}, u32[]{:S(2)}) collective-permute-start(bf16[2064,128]{1,0:T(8,128)(2,1)S(1)} %shard_state.1), channel_id=1, source_target_pairs={{0,8},{8,16},{16,24},{1,9},{9,17},{17,25},{2,10},{10,18},{18,26},{... | collective-permute-start | bytes 1585160 | tf_op jit(solution)/shard_map/ppermute | solution.py:260
  19.3 12.0 %collective-permute-start.4 = (bf16[64,2048]{1,0:T(8,128)(2,1)S(1)}, bf16[64,2048]{1,0:T(8,128)(2,1)S(1)}, u32[]{:S(2)}, u32[]{:S(2)}) collective-permute-start(bf16[64,2048]{1,0:T(8,128)(2,1)S(1)} %get-tuple-element.24.refs_0_), channel_id=1, source_target_pairs={{0,16},{1,17},{2,18},{3,19},{4,20},{5,21},{6,22},{7,23},{8,24},{9,... | collective-permute-start | bytes 786440 | tf_op jit(solution)/shard_map/ppermute | solution.py:340
  22.7 9.2 %collective-permute-start.2 = (bf16[64,2048]{1,0:T(8,128)(2,1)S(1)}, bf16[64,2048]{1,0:T(8,128)(2,1)S(1)}, u32[]{:S(2)}, u32[]{:S(2)}) collective-permute-start(bf16[64,2048]{1,0:T(8,128)(2,1)S(1)} %get-tuple-element.24.refs_0_), channel_id=1, source_target_pairs={{0,8},{1,9},{2,10},{3,11},{4,12},{5,13},{6,14},{7,15},{8,0},{9,1},... | collective-permute-start | bytes 786440 | tf_op jit(solution)/shard_map/ppermute | solution.py:340
  22.7 11.0 %collective-permute-start.5 = (bf16[64,2048]{1,0:T(8,128)(2,1)S(1)}, bf16[64,2048]{1,0:T(8,128)(2,1)S(1)}, u32[]{:S(2)}, u32[]{:S(2)}) collective-permute-start(bf16[64,2048]{1,0:T(8,128)(2,1)S(1)} %get-tuple-element.25.refs_1_), channel_id=1, source_target_pairs={{0,16},{1,17},{2,18},{3,19},{4,20},{5,21},{6,22},{7,23},{8,24},{9,... | collective-permute-start | bytes 786440 | tf_op jit(solution)/shard_map/ppermute | solution.py:340
  23.8 11.4 %collective-permute-start.3 = (bf16[64,2048]{1,0:T(8,128)(2,1)S(1)}, bf16[64,2048]{1,0:T(8,128)(2,1)S(1)}, u32[]{:S(2)}, u32[]{:S(2)}) collective-permute-start(bf16[64,2048]{1,0:T(8,128)(2,1)S(1)} %get-tuple-element.25.refs_1_), channel_id=1, source_target_pairs={{0,8},{1,9},{2,10},{3,11},{4,12},{5,13},{6,14},{7,15},{8,0},{9,1},... | collective-permute-start | bytes 786440 | tf_op jit(solution)/shard_map/ppermute | solution.py:340
  25.5 5.7 %collective-permute-start.1 = (bf16[2,64,768]{2,1,0:T(8,128)(2,1)S(1)}, bf16[2,64,768]{2,1,0:T(8,128)(2,1)S(1)}, u32[]{:S(2)}, u32[]{:S(2)}) collective-permute-start(bf16[2,64,768]{2,1,0:T(8,128)(2,1)S(1)} %project.7), channel_id=1, source_target_pairs={{0,2},{1,3},{2,0},{3,1},{4,6},{5,7},{6,4},{7,5},{8,10},{9,11},{10,... | collective-permute-start | bytes 589832 | tf_op jit(solution)/shard_map/ppermute | solution.py:340
  35.3 6.4 %collective-permute-start.9 = (bf16[64,2048]{1,0:T(8,128)(2,1)S(1)}, bf16[64,2048]{1,0:T(8,128)(2,1)S(1)}, u32[]{:S(2)}, u32[]{:S(2)}) collective-permute-start(bf16[64,2048]{1,0:T(8,128)(2,1)S(1)} %get-tuple-element.29), channel_id=1, source_target_pairs={{0,16},{1,17},{2,18},{3,19},{4,20},{5,21},{6,22},{7,23},{8,24},{9,... | collective-permute-start | bytes 786440 | tf_op jit(solution)/shard_map/ppermute | solution.py:340
  35.7 6.4 %collective-permute-start.10 = (bf16[64,2048]{1,0:T(8,128)(2,1)S(1)}, bf16[64,2048]{1,0:T(8,128)(2,1)S(1)}, u32[]{:S(2)}, u32[]{:S(2)}) collective-permute-start(bf16[64,2048]{1,0:T(8,128)(2,1)S(1)} %get-tuple-element.30), channel_id=1, source_target_pairs={{0,8},{1,9},{2,10},{3,11},{4,12},{5,13},{6,14},{7,15},{8,0},{9,1},... | collective-permute-start | bytes 786440 | tf_op jit(solution)/shard_map/ppermute | solution.py:340
  37.5 10.4 %collective-permute-start.6 = (bf16[4,64,768]{2,1,0:T(8,128)(2,1)S(1)}, bf16[4,64,768]{2,1,0:T(8,128)(2,1)S(1)}, u32[]{:S(2)}, u32[]{:S(2)}) collective-permute-start(bf16[4,64,768]{2,1,0:T(8,128)(2,1)S(1)} %project.9), channel_id=1, source_target_pairs={{0,2},{1,3},{2,0},{3,1},{4,6},{5,7},{6,4},{7,5},{8,10},{9,11},{10,... | collective-permute-start | bytes 1179656 | tf_op jit(solution)/shard_map/ppermute | solution.py:340
  42.7 8.3 %collective-permute-start.11 = (bf16[2,64,768]{2,1,0:T(8,128)(2,1)S(1)}, bf16[2,64,768]{2,1,0:T(8,128)(2,1)S(1)}, u32[]{:S(2)}, u32[]{:S(2)}) collective-permute-start(bf16[2,64,768]{2,1,0:T(8,128)(2,1)S(1)} %project.11), channel_id=1, source_target_pairs={{0,2},{1,3},{2,0},{3,1},{4,6},{5,7},{6,4},{7,5},{8,10},{9,11},{10,... | collective-permute-start | bytes 589832 | tf_op jit(solution)/shard_map/ppermute | solution.py:340
  48.0 6.1 %collective-permute-start.8 = (bf16[128,768]{1,0:T(8,128)(2,1)S(1)}, bf16[128,768]{1,0:T(8,128)(2,1)S(1)}, u32[]{:S(2)}, u32[]{:S(2)}) collective-permute-start(bf16[128,768]{1,0:T(8,128)(2,1)S(1)} %get-tuple-element.28), channel_id=1, source_target_pairs={{0,16},{1,17},{2,18},{3,19},{4,20},{5,21},{6,22},{7,23},{8,24},{9,... | collective-permute-start | bytes 589832 | tf_op jit(solution)/shard_map/ppermute | solution.py:340
  49.5 5.7 %collective-permute-start.7 = (bf16[128,768]{1,0:T(8,128)(2,1)S(1)}, bf16[128,768]{1,0:T(8,128)(2,1)S(1)}, u32[]{:S(2)}, u32[]{:S(2)}) collective-permute-start(bf16[128,768]{1,0:T(8,128)(2,1)S(1)} %get-tuple-element.27.refs_2_), channel_id=1, source_target_pairs={{0,8},{1,9},{2,10},{3,11},{4,12},{5,13},{6,14},{7,15},{8,0},{9,1},... | collective-permute-start | bytes 589832 | tf_op jit(solution)/shard_map/ppermute | solution.py:340
  51.0 6.6 %collective-permute-start.12 = (bf16[128,768]{1,0:T(8,128)(2,1)S(1)}, bf16[128,768]{1,0:T(8,128)(2,1)S(1)}, u32[]{:S(2)}, u32[]{:S(2)}) collective-permute-start(bf16[128,768]{1,0:T(8,128)(2,1)S(1)} %merge.5), channel_id=1, source_target_pairs={{0,24},{1,25},{2,26},{3,27},{4,28},{5,29},{6,30},{7,31},{8,16},{9,... | collective-permute-start | bytes 589832 | tf_op jit(solution)/shard_map/ppermute | solution.py:340
  57.8 7.7 %collective-permute-start.13 = (bf16[128,768]{1,0:T(8,128)(2,1)S(1)}, bf16[128,768]{1,0:T(8,128)(2,1)S(1)}, u32[]{:S(2)}, u32[]{:S(2)}) collective-permute-start(bf16[128,768]{1,0:T(8,128)(2,1)S(1)} %get-tuple-element.31), channel_id=1, source_target_pairs={{0,6},{1,7},{2,4},{3,5},{4,2},{5,3},{6,0},{7,1},{8,14},{9,15},{10,... | collective-permute-start | bytes 589832 | tf_op jit(solution)/shard_map/ppermute | solution.py:340
  61.4 11.0 %collective-permute-start.14 = (bf16[128,768]{1,0:T(8,128)(2,1)S(1)}, bf16[128,768]{1,0:T(8,128)(2,1)S(1)}, u32[]{:S(2)}, u32[]{:S(2)}) collective-permute-start(bf16[128,768]{1,0:T(8,128)(2,1)S(1)} %get-tuple-element.32), channel_id=1, source_target_pairs={{0,4},{1,5},{2,6},{3,7},{4,0},{5,1},{6,2},{7,3},{8,12},{9,13},{10,... | collective-permute-start | bytes 589832 | tf_op jit(solution)/shard_map/ppermute | solution.py:340
  61.4 11.0 %collective-permute-start.15 = (bf16[128,768]{1,0:T(8,128)(2,1)S(1)}, bf16[128,768]{1,0:T(8,128)(2,1)S(1)}, u32[]{:S(2)}, u32[]{:S(2)}) collective-permute-start(bf16[128,768]{1,0:T(8,128)(2,1)S(1)} %get-tuple-element.33), channel_id=1, source_target_pairs={{0,2},{1,3},{2,0},{3,1},{4,6},{5,7},{6,4},{7,5},{8,10},{9,11},{10,... | collective-permute-start | bytes 589832 | tf_op jit(solution)/shard_map/ppermute | solution.py:340
  72.6 1.8 %collective-permute-start.16 = (bf16[1,128,1536]{2,1,0:T(8,128)(2,1)S(1)}, bf16[1,128,1536]{2,1,0:T(8,128)(2,1)S(1)}, u32[]{:S(2)}, u32[]{:S(2)}) collective-permute-start(bf16[1,128,1536]{2,1,0:T(8,128)(2,1)S(1)} %last.1), channel_id=1, source_target_pairs={{0,1},{1,0},{2,3},{3,2},{4,5},{5,4},{6,7},{7,6},{8,9},{9,8},{10,11... | collective-permute-start | bytes 1179656 | tf_op jit(solution)/shard_map/ppermute | solution.py:340

commit v10 on v9

--- a/solution.py
+++ b/solution.py
@@ -374,13 +374,13 @@
     held = hold((upper_1, lower_2), (lower_1, upper_2, *own))
     beside = (upper_1, lower_1, upper_2, lower_2)
     beside_send, beside_keep = project(beside, 1, own), project(beside, 0)
-    beside = merge(
-        (((0, 0), (0, 1)), ((0, 2), (0, 3))),
-        (beside_keep, partner(beside_send)),
-    )
+    beside_arrived = partner(beside_send)
     across = (swapped(held[0], 2), swapped(held[1], 1))
     across_sum = (project(across, 0), partner(project(across, 1, (beside_keep,))))
-    across = merge(whole, across_sum, beside[:1])
+    across = merge(whole, across_sum)
+    beside = merge(
+        (((0, 0), (0, 1)), ((0, 2), (0, 3))), (beside_keep, beside_arrived), across
+    )
     blocks = [swapped(block, k) if k else block for k, block in enumerate((*own, *beside, *across))]
     picked = call(pick_kernel, (single,) * n_head, "pick")(*blocks)
     arrived = [moved(picked[m], lambda i, j, s, m=m: (i, j ^ m, s)) for m in (3, 2, 1)]

time: 75.3 us -> 77.7 us (1.032)
  waiting for transfers between devices: 36.5 us -> 39.7 us
  starting transfers between devices: 25.5 us -> 24.7 us
    ppermute x16, waiting for transfers between devices: 29.6 us -> 32.7 us  [moved(): lax.ppermute(array, names, [(place[spot], place[target(*spot)]) for spot...]
    ppermute x16, starting transfers between devices: 20.6 us -> 19.8 us  [moved(): lax.ppermute(array, names, [(place[spot], place[target(*spot)]) for spot...]
  transfers between devices with their start and end apart: 17 -> 17, of which waited for: 14 -> 14; matrix products, arithmetic and copies ran while one was open for 0% -> 0% of each run, Pallas kernels for 12% -> 11%
where the time goes in v10:
time: 77.7 us; the launch traced here: 77.4 us
  waiting for transfers between devices  39.7 us (51%)
  starting transfers between devices  24.7 us (32%)
  Pallas kernels  12.2 us (16%)
    ppermute x16, waiting for transfers between devices, moved(): lax.ppermute(array, names, [(place[spot], place[target(*spot)]) for spot...  32.7 us
    ppermute x16, starting transfers between devices, moved(): lax.ppermute(array, names, [(place[spot], place[target(*spot)]) for spot...  19.8 us
    ppermute x1, waiting for transfers between devices, from_before(): return lax.ppermute(array, 'ctx', [(i, i + by) for i in range(n_ctx - by)])  6.98 us
    ppermute x1, starting transfers between devices, from_before(): return lax.ppermute(array, 'ctx', [(i, i + by) for i in range(n_ctx - by)])  4.87 us
    pallas_call x6, Pallas kernels, project(): call(kernel, shape, 'project', in_specs=specs)(*picked, weight, *after)  4.4 us
    pallas_call x1, Pallas kernels, on_device(): call(inside_kernel, (pltpu.VMEM((rows, width), jnp.float32), pltpu.VMEM((...  4.24 us
    pallas_call x1, Pallas kernels, on_device(): call(state_kernel, state_shape, 'shard_state', in_specs=[HBM] * 4, scratc...  2.58 us
  transfers between devices with their start and end apart: 17, of which 14 were waited for; matrix products, arithmetic and copies ran while one was open for 0% of the time, Pallas kernels for 11%

profile of v10, /device:TPU:0, one launch (start us, length us, event | category | flops | bytes accessed | tf_op | source)
XLA Modules:
  0.0 77.4 jit_solution(1045515592584099194)
XLA Ops:
  0.0 2.6 %shard_state.1 = bf16[2064,128]{1,0:T(8,128)(2,1)S(1)} custom-call(bf16[1,128,2048]{2,1,0:T(8,128)(2,1)} %refs_0_.1, bf16[1,128,2048]{2,1,0:T(8,128)(2,1)} %refs_1_.1, f32[1,16,128]{2,1,0:T(8,128)} %bitcast.1, s32[1,128]{1,0:T(1,128)} %refs_3_.1), custom_call_target="tpu_custom_call" | custom-call | flops 1 | bytes 1 | tf_op jit(solution)/shard_map/shard_state/pallas_call | solution.py:264
  2.6 4.9 %collective-permute-start = (bf16[2064,128]{1,0:T(8,128)(2,1)S(1)}, bf16[2064,128]{1,0:T(8,128)(2,1)S(1)}, u32[]{:S(2)}, u32[]{:S(2)}) collective-permute-start(bf16[2064,128]{1,0:T(8,128)(2,1)S(1)} %shard_state.1), channel_id=1, source_target_pairs={{0,8},{8,16},{16,24},{1,9},{9,17},{17,25},{2,10},{10,18},{18,26},{... | collective-permute-start | bytes 1585160 | tf_op jit(solution)/shard_map/ppermute | solution.py:260
  7.5 4.2 %inside.1 = (f32[128,2048]{1,0:T(8,128)S(1)}, f32[128,2048]{1,0:T(8,128)S(1)}, f32[128,128]{1,0:T(8,128)S(1)}, bf16[128,2048]{1,0:T(8,128)(2,1)S(1)}, bf16[2048,1536]{1,0:T(8,128)(2,1)S(1)}) custom-call(bf16[1,128,2048]{2,1,0:T(8,128)(2,1)} %query_hbm.1, bf16[1,128,2048]{2,1,0:T(8,128)(2,1)} %refs_0_.1, bf16[1,128,2048]{2,1,0:T(8,128)(2,1)} %refs_1_.1, ...), custom_call_target="tpu_custom_call" | custom-call | flops 1 | bytes 1 | tf_op jit(solution)/shard_map/inside/pallas_call | solution.py:296
  11.7 7.0 %collective-permute-done.state_ref = bf16[2064,128]{1,0:T(8,128)(2,1)S(1)} collective-permute-done((bf16[2064,128]{1,0:T(8,128)(2,1)S(1)}, bf16[2064,128]{1,0:T(8,128)(2,1)S(1)}, u32[]{:S(2)}, u32[]{:S(2)}) %collective-permute-start) | collective-permute-done | bytes 528416 | tf_op jit(solution)/shard_map/ppermute | solution.py:260
  19.3 3.5 %collective-permute-start.4 = (bf16[64,2048]{1,0:T(8,128)(2,1)S(1)}, bf16[64,2048]{1,0:T(8,128)(2,1)S(1)}, u32[]{:S(2)}, u32[]{:S(2)}) collective-permute-start(bf16[64,2048]{1,0:T(8,128)(2,1)S(1)} %get-tuple-element.24.refs_0_), channel_id=1, source_target_pairs={{0,16},{1,17},{2,18},{3,19},{4,20},{5,21},{6,22},{7,23},{8,24},{9,... | collective-permute-start | bytes 786440 | tf_op jit(solution)/shard_map/ppermute | solution.py:340
  22.7 1.1 %collective-permute-start.5 = (bf16[64,2048]{1,0:T(8,128)(2,1)S(1)}, bf16[64,2048]{1,0:T(8,128)(2,1)S(1)}, u32[]{:S(2)}, u32[]{:S(2)}) collective-permute-start(bf16[64,2048]{1,0:T(8,128)(2,1)S(1)} %get-tuple-element.25.refs_1_), channel_id=1, source_target_pairs={{0,16},{1,17},{2,18},{3,19},{4,20},{5,21},{6,22},{7,23},{8,24},{9,... | collective-permute-start | bytes 786440 | tf_op jit(solution)/shard_map/ppermute | solution.py:340
  23.8 1.0 %collective-permute-start.3 = (bf16[64,2048]{1,0:T(8,128)(2,1)S(1)}, bf16[64,2048]{1,0:T(8,128)(2,1)S(1)}, u32[]{:S(2)}, u32[]{:S(2)}) collective-permute-start(bf16[64,2048]{1,0:T(8,128)(2,1)S(1)} %get-tuple-element.25.refs_1_), channel_id=1, source_target_pairs={{0,8},{1,9},{2,10},{3,11},{4,12},{5,13},{6,14},{7,15},{8,0},{9,1},... | collective-permute-start | bytes 786440 | tf_op jit(solution)/shard_map/ppermute | solution.py:340
  25.5 1.6 %collective-permute-start.1 = (bf16[2,64,768]{2,1,0:T(8,128)(2,1)S(1)}, bf16[2,64,768]{2,1,0:T(8,128)(2,1)S(1)}, u32[]{:S(2)}, u32[]{:S(2)}) collective-permute-start(bf16[2,64,768]{2,1,0:T(8,128)(2,1)S(1)} %project.7), channel_id=1, source_target_pairs={{0,2},{1,3},{2,0},{3,1},{4,6},{5,7},{6,4},{7,5},{8,10},{9,11},{10,... | collective-permute-start | bytes 589832 | tf_op jit(solution)/shard_map/ppermute | solution.py:340
  27.7 3.5 %collective-permute-done.1.refs_1_ = bf16[2,64,768]{2,1,0:T(8,128)(2,1)S(1)} collective-permute-done((bf16[2,64,768]{2,1,0:T(8,128)(2,1)S(1)}, bf16[2,64,768]{2,1,0:T(8,128)(2,1)S(1)}, u32[]{:S(2)}, u32[]{:S(2)}) %collective-permute-start.1) | collective-permute-done | bytes 196640 | tf_op jit(solution)/shard_map/ppermute | solution.py:340
  32.0 1.8 %collective-permute-done.5.refs_3_.lower_ref = bf16[64,2048]{1,0:T(8,128)(2,1)S(1)} collective-permute-done((bf16[64,2048]{1,0:T(8,128)(2,1)S(1)}, bf16[64,2048]{1,0:T(8,128)(2,1)S(1)}, u32[]{:S(2)}, u32[]{:S(2)}) %collective-permute-start.5) | collective-permute-done | bytes 262176 | tf_op jit(solution)/shard_map/ppermute | solution.py:340
  33.8 1.5 %collective-permute-done.3.refs_1_.refs_0_ = bf16[64,2048]{1,0:T(8,128)(2,1)S(1)} collective-permute-done((bf16[64,2048]{1,0:T(8,128)(2,1)S(1)}, bf16[64,2048]{1,0:T(8,128)(2,1)S(1)}, u32[]{:S(2)}, u32[]{:S(2)}) %collective-permute-start.3) | collective-permute-done | bytes 262176 | tf_op jit(solution)/shard_map/ppermute | solution.py:340
  36.5 1.0 %project.9 = bf16[4,64,768]{2,1,0:T(8,128)(2,1)S(1)} custom-call(bf16[64,2048]{1,0:T(8,128)(2,1)S(1)} %collective-permute-done.2.refs_0_.upper_ref, bf16[64,2048]{1,0:T(8,128)(2,1)S(1)} %collective-permute-done.3.refs_1_.refs_0_, bf16[64,2048]{1,0:T(8,128)(2,1)S(1)} %collective-permute-done.4.refs_2_.refs_1_, ...), custom_call_target="tpu_custom_call" | custom-call | flops 1 | bytes 1 | tf_op jit(solution)/shard_map/project/pallas_call | solution.py:351
  37.5 1.6 %collective-permute-start.6 = (bf16[4,64,768]{2,1,0:T(8,128)(2,1)S(1)}, bf16[4,64,768]{2,1,0:T(8,128)(2,1)S(1)}, u32[]{:S(2)}, u32[]{:S(2)}) collective-permute-start(bf16[4,64,768]{2,1,0:T(8,128)(2,1)S(1)} %project.9), channel_id=1, source_target_pairs={{0,2},{1,3},{2,0},{3,1},{4,6},{5,7},{6,4},{7,5},{8,10},{9,11},{10,... | collective-permute-start | bytes 1179656 | tf_op jit(solution)/shard_map/ppermute | solution.py:340
  39.1 1.0 %project.8.refs_3_.refs_0_ = bf16[4,64,768]{2,1,0:T(8,128)(2,1)S(1)} custom-call(bf16[64,2048]{1,0:T(8,128)(2,1)S(1)} %collective-permute-done.2.refs_0_.upper_ref, bf16[64,2048]{1,0:T(8,128)(2,1)S(1)} %collective-permute-done.3.refs_1_.refs_0_, bf16[64,2048]{1,0:T(8,128)(2,1)S(1)} %collective-permute-done.4.refs_2_.refs_1_, ...), custom_call_target="tpu_custom_call" | custom-call | flops 1 | bytes 1 | tf_op jit(solution)/shard_map/project/pallas_call | solution.py:351
  40.1 1.6 %collective-permute-done.7.refs_0_ = bf16[64,2048]{1,0:T(8,128)(2,1)S(1)} collective-permute-done((bf16[64,2048]{1,0:T(8,128)(2,1)S(1)}, bf16[64,2048]{1,0:T(8,128)(2,1)S(1)}, u32[]{:S(2)}, u32[]{:S(2)}) %collective-permute-start.7) | collective-permute-done | bytes 262176 | tf_op jit(solution)/shard_map/ppermute | solution.py:340
  42.7 1.6 %collective-permute-start.9 = (bf16[2,64,768]{2,1,0:T(8,128)(2,1)S(1)}, bf16[2,64,768]{2,1,0:T(8,128)(2,1)S(1)}, u32[]{:S(2)}, u32[]{:S(2)}) collective-permute-start(bf16[2,64,768]{2,1,0:T(8,128)(2,1)S(1)} %project.11), channel_id=1, source_target_pairs={{0,2},{1,3},{2,0},{3,1},{4,6},{5,7},{6,4},{7,5},{8,10},{9,11},{10,... | collective-permute-start | bytes 589832 | tf_op jit(solution)/shard_map/ppermute | solution.py:340
  44.9 5.0 %collective-permute-done.9.refs_1_ = bf16[2,64,768]{2,1,0:T(8,128)(2,1)S(1)} collective-permute-done((bf16[2,64,768]{2,1,0:T(8,128)(2,1)S(1)}, bf16[2,64,768]{2,1,0:T(8,128)(2,1)S(1)}, u32[]{:S(2)}, u32[]{:S(2)}) %collective-permute-start.9) | collective-permute-done | bytes 196640 | tf_op jit(solution)/shard_map/ppermute | solution.py:340
  50.0 2.5 %collective-permute-start.12 = (bf16[128,768]{1,0:T(8,128)(2,1)S(1)}, bf16[128,768]{1,0:T(8,128)(2,1)S(1)}, u32[]{:S(2)}, u32[]{:S(2)}) collective-permute-start(bf16[128,768]{1,0:T(8,128)(2,1)S(1)} %merge.4.refs_2_), channel_id=1, source_target_pairs={{0,24},{1,25},{2,26},{3,27},{4,28},{5,29},{6,30},{7,31},{8,16},{9,... | collective-permute-start | bytes 589832 | tf_op jit(solution)/shard_map/ppermute | solution.py:340
  53.7 2.9 %collective-permute-done.12.refs_3_ = bf16[128,768]{1,0:T(8,128)(2,1)S(1)} collective-permute-done((bf16[128,768]{1,0:T(8,128)(2,1)S(1)}, bf16[128,768]{1,0:T(8,128)(2,1)S(1)}, u32[]{:S(2)}, u32[]{:S(2)}) %collective-permute-start.12) | collective-permute-done | bytes 196640 | tf_op jit(solution)/shard_map/ppermute | solution.py:340
  56.6 2.1 %collective-permute-done.10.refs_1_ = bf16[128,768]{1,0:T(8,128)(2,1)S(1)} collective-permute-done((bf16[128,768]{1,0:T(8,128)(2,1)S(1)}, bf16[128,768]{1,0:T(8,128)(2,1)S(1)}, u32[]{:S(2)}, u32[]{:S(2)}) %collective-permute-start.10) | collective-permute-done | bytes 196640 | tf_op jit(solution)/shard_map/ppermute | solution.py:340
  59.0 3.6 %collective-permute-start.13 = (bf16[128,768]{1,0:T(8,128)(2,1)S(1)}, bf16[128,768]{1,0:T(8,128)(2,1)S(1)}, u32[]{:S(2)}, u32[]{:S(2)}) collective-permute-start(bf16[128,768]{1,0:T(8,128)(2,1)S(1)} %get-tuple-element.31), channel_id=1, source_target_pairs={{0,6},{1,7},{2,4},{3,5},{4,2},{5,3},{6,0},{7,1},{8,14},{9,15},{10,... | collective-permute-start | bytes 589832 | tf_op jit(solution)/shard_map/ppermute | solution.py:340
  63.4 4.1 %collective-permute-done.13.refs_0_ = bf16[128,768]{1,0:T(8,128)(2,1)S(1)} collective-permute-done((bf16[128,768]{1,0:T(8,128)(2,1)S(1)}, bf16[128,768]{1,0:T(8,128)(2,1)S(1)}, u32[]{:S(2)}, u32[]{:S(2)}) %collective-permute-start.13) | collective-permute-done | bytes 196640 | tf_op jit(solution)/shard_map/ppermute | solution.py:340
  67.5 7.3 %collective-permute-done.14.refs_1_ = bf16[128,768]{1,0:T(8,128)(2,1)S(1)} collective-permute-done((bf16[128,768]{1,0:T(8,128)(2,1)S(1)}, bf16[128,768]{1,0:T(8,128)(2,1)S(1)}, u32[]{:S(2)}, u32[]{:S(2)}) %collective-permute-start.14) | collective-permute-done | bytes 196640 | tf_op jit(solution)/shard_map/ppermute | solution.py:340
  75.0 1.7 %collective-permute-done.16 = bf16[1,128,1536]{2,1,0:T(8,128)(2,1)S(1)} collective-permute-done((bf16[1,128,1536]{2,1,0:T(8,128)(2,1)S(1)}, bf16[1,128,1536]{2,1,0:T(8,128)(2,1)S(1)}, u32[]{:S(2)}, u32[]{:S(2)}) %collective-permute-start.16) | collective-permute-done | bytes 393248 | tf_op jit(solution)/shard_map/ppermute | solution.py:340
  (26 shorter events, 8.5 us)
Async XLA Ops:
  2.6 16.1 %collective-permute-start = (bf16[2064,128]{1,0:T(8,128)(2,1)S(1)}, bf16[2064,128]{1,0:T(8,128)(2,1)S(1)}, u32[]{:S(2)}, u32[]{:S(2)}) collective-permute-start(bf16[2064,128]{1,0:T(8,128)(2,1)S(1)} %shard_state.1), channel_id=1, source_target_pairs={{0,8},{8,16},{16,24},{1,9},{9,17},{17,25},{2,10},{10,18},{18,26},{... | collective-permute-start | bytes 1585160 | tf_op jit(solution)/shard_map/ppermute | solution.py:260
  19.3 12.0 %collective-permute-start.4 = (bf16[64,2048]{1,0:T(8,128)(2,1)S(1)}, bf16[64,2048]{1,0:T(8,128)(2,1)S(1)}, u32[]{:S(2)}, u32[]{:S(2)}) collective-permute-start(bf16[64,2048]{1,0:T(8,128)(2,1)S(1)} %get-tuple-element.24.refs_0_), channel_id=1, source_target_pairs={{0,16},{1,17},{2,18},{3,19},{4,20},{5,21},{6,22},{7,23},{8,24},{9,... | collective-permute-start | bytes 786440 | tf_op jit(solution)/shard_map/ppermute | solution.py:340
  22.7 9.2 %collective-permute-start.2 = (bf16[64,2048]{1,0:T(8,128)(2,1)S(1)}, bf16[64,2048]{1,0:T(8,128)(2,1)S(1)}, u32[]{:S(2)}, u32[]{:S(2)}) collective-permute-start(bf16[64,2048]{1,0:T(8,128)(2,1)S(1)} %get-tuple-element.24.refs_0_), channel_id=1, source_target_pairs={{0,8},{1,9},{2,10},{3,11},{4,12},{5,13},{6,14},{7,15},{8,0},{9,1},... | collective-permute-start | bytes 786440 | tf_op jit(solution)/shard_map/ppermute | solution.py:340
  22.7 11.0 %collective-permute-start.5 = (bf16[64,2048]{1,0:T(8,128)(2,1)S(1)}, bf16[64,2048]{1,0:T(8,128)(2,1)S(1)}, u32[]{:S(2)}, u32[]{:S(2)}) collective-permute-start(bf16[64,2048]{1,0:T(8,128)(2,1)S(1)} %get-tuple-element.25.refs_1_), channel_id=1, source_target_pairs={{0,16},{1,17},{2,18},{3,19},{4,20},{5,21},{6,22},{7,23},{8,24},{9,... | collective-permute-start | bytes 786440 | tf_op jit(solution)/shard_map/ppermute | solution.py:340
  23.8 11.4 %collective-permute-start.3 = (bf16[64,2048]{1,0:T(8,128)(2,1)S(1)}, bf16[64,2048]{1,0:T(8,128)(2,1)S(1)}, u32[]{:S(2)}, u32[]{:S(2)}) collective-permute-start(bf16[64,2048]{1,0:T(8,128)(2,1)S(1)} %get-tuple-element.25.refs_1_), channel_id=1, source_target_pairs={{0,8},{1,9},{2,10},{3,11},{4,12},{5,13},{6,14},{7,15},{8,0},{9,1},... | collective-permute-start | bytes 786440 | tf_op jit(solution)/shard_map/ppermute | solution.py:340
  25.5 5.7 %collective-permute-start.1 = (bf16[2,64,768]{2,1,0:T(8,128)(2,1)S(1)}, bf16[2,64,768]{2,1,0:T(8,128)(2,1)S(1)}, u32[]{:S(2)}, u32[]{:S(2)}) collective-permute-start(bf16[2,64,768]{2,1,0:T(8,128)(2,1)S(1)} %project.7), channel_id=1, source_target_pairs={{0,2},{1,3},{2,0},{3,1},{4,6},{5,7},{6,4},{7,5},{8,10},{9,11},{10,... | collective-permute-start | bytes 589832 | tf_op jit(solution)/shard_map/ppermute | solution.py:340
  35.3 6.4 %collective-permute-start.7 = (bf16[64,2048]{1,0:T(8,128)(2,1)S(1)}, bf16[64,2048]{1,0:T(8,128)(2,1)S(1)}, u32[]{:S(2)}, u32[]{:S(2)}) collective-permute-start(bf16[64,2048]{1,0:T(8,128)(2,1)S(1)} %get-tuple-element.27), channel_id=1, source_target_pairs={{0,16},{1,17},{2,18},{3,19},{4,20},{5,21},{6,22},{7,23},{8,24},{9,... | collective-permute-start | bytes 786440 | tf_op jit(solution)/shard_map/ppermute | solution.py:340
  35.7 6.4 %collective-permute-start.8 = (bf16[64,2048]{1,0:T(8,128)(2,1)S(1)}, bf16[64,2048]{1,0:T(8,128)(2,1)S(1)}, u32[]{:S(2)}, u32[]{:S(2)}) collective-permute-start(bf16[64,2048]{1,0:T(8,128)(2,1)S(1)} %get-tuple-element.28), channel_id=1, source_target_pairs={{0,8},{1,9},{2,10},{3,11},{4,12},{5,13},{6,14},{7,15},{8,0},{9,1},... | collective-permute-start | bytes 786440 | tf_op jit(solution)/shard_map/ppermute | solution.py:340
  37.5 15.0 %collective-permute-start.6 = (bf16[4,64,768]{2,1,0:T(8,128)(2,1)S(1)}, bf16[4,64,768]{2,1,0:T(8,128)(2,1)S(1)}, u32[]{:S(2)}, u32[]{:S(2)}) collective-permute-start(bf16[4,64,768]{2,1,0:T(8,128)(2,1)S(1)} %project.9), channel_id=1, source_target_pairs={{0,2},{1,3},{2,0},{3,1},{4,6},{5,7},{6,4},{7,5},{8,10},{9,11},{10,... | collective-permute-start | bytes 1179656 | tf_op jit(solution)/shard_map/ppermute | solution.py:340
  42.7 7.3 %collective-permute-start.9 = (bf16[2,64,768]{2,1,0:T(8,128)(2,1)S(1)}, bf16[2,64,768]{2,1,0:T(8,128)(2,1)S(1)}, u32[]{:S(2)}, u32[]{:S(2)}) collective-permute-start(bf16[2,64,768]{2,1,0:T(8,128)(2,1)S(1)} %project.11), channel_id=1, source_target_pairs={{0,2},{1,3},{2,0},{3,1},{4,6},{5,7},{6,4},{7,5},{8,10},{9,11},{10,... | collective-permute-start | bytes 589832 | tf_op jit(solution)/shard_map/ppermute | solution.py:340
  50.0 6.6 %collective-permute-start.12 = (bf16[128,768]{1,0:T(8,128)(2,1)S(1)}, bf16[128,768]{1,0:T(8,128)(2,1)S(1)}, u32[]{:S(2)}, u32[]{:S(2)}) collective-permute-start(bf16[128,768]{1,0:T(8,128)(2,1)S(1)} %merge.4.refs_2_), channel_id=1, source_target_pairs={{0,24},{1,25},{2,26},{3,27},{4,28},{5,29},{6,30},{7,31},{8,16},{9,... | collective-permute-start | bytes 589832 | tf_op jit(solution)/shard_map/ppermute | solution.py:340
  52.6 6.2 %collective-permute-start.10 = (bf16[128,768]{1,0:T(8,128)(2,1)S(1)}, bf16[128,768]{1,0:T(8,128)(2,1)S(1)}, u32[]{:S(2)}, u32[]{:S(2)}) collective-permute-start(bf16[128,768]{1,0:T(8,128)(2,1)S(1)} %get-tuple-element.29), channel_id=1, source_target_pairs={{0,8},{1,9},{2,10},{3,11},{4,12},{5,13},{6,14},{7,15},{8,0},{9,1},... | collective-permute-start | bytes 589832 | tf_op jit(solution)/shard_map/ppermute | solution.py:340
  53.2 5.7 %collective-permute-start.11 = (bf16[128,768]{1,0:T(8,128)(2,1)S(1)}, bf16[128,768]{1,0:T(8,128)(2,1)S(1)}, u32[]{:S(2)}, u32[]{:S(2)}) collective-permute-start(bf16[128,768]{1,0:T(8,128)(2,1)S(1)} %get-tuple-element.30), channel_id=1, source_target_pairs={{0,16},{1,17},{2,18},{3,19},{4,20},{5,21},{6,22},{7,23},{8,24},{9,... | collective-permute-start | bytes 589832 | tf_op jit(solution)/shard_map/ppermute | solution.py:340
  59.0 8.5 %collective-permute-start.13 = (bf16[128,768]{1,0:T(8,128)(2,1)S(1)}, bf16[128,768]{1,0:T(8,128)(2,1)S(1)}, u32[]{:S(2)}, u32[]{:S(2)}) collective-permute-start(bf16[128,768]{1,0:T(8,128)(2,1)S(1)} %get-tuple-element.31), channel_id=1, source_target_pairs={{0,6},{1,7},{2,4},{3,5},{4,2},{5,3},{6,0},{7,1},{8,14},{9,15},{10,... | collective-permute-start | bytes 589832 | tf_op jit(solution)/shard_map/ppermute | solution.py:340
  62.6 12.2 %collective-permute-start.14 = (bf16[128,768]{1,0:T(8,128)(2,1)S(1)}, bf16[128,768]{1,0:T(8,128)(2,1)S(1)}, u32[]{:S(2)}, u32[]{:S(2)}) collective-permute-start(bf16[128,768]{1,0:T(8,128)(2,1)S(1)} %get-tuple-element.32), channel_id=1, source_target_pairs={{0,4},{1,5},{2,6},{3,7},{4,0},{5,1},{6,2},{7,3},{8,12},{9,13},{10,... | collective-permute-start | bytes 589832 | tf_op jit(solution)/shard_map/ppermute | solution.py:340
  62.6 12.2 %collective-permute-start.15 = (bf16[128,768]{1,0:T(8,128)(2,1)S(1)}, bf16[128,768]{1,0:T(8,128)(2,1)S(1)}, u32[]{:S(2)}, u32[]{:S(2)}) collective-permute-start(bf16[128,768]{1,0:T(8,128)(2,1)S(1)} %get-tuple-element.33), channel_id=1, source_target_pairs={{0,2},{1,3},{2,0},{3,1},{4,6},{5,7},{6,4},{7,5},{8,10},{9,11},{10,... | collective-permute-start | bytes 589832 | tf_op jit(solution)/shard_map/ppermute | solution.py:340
  74.9 1.8 %collective-permute-start.16 = (bf16[1,128,1536]{2,1,0:T(8,128)(2,1)S(1)}, bf16[1,128,1536]{2,1,0:T(8,128)(2,1)S(1)}, u32[]{:S(2)}, u32[]{:S(2)}) collective-permute-start(bf16[1,128,1536]{2,1,0:T(8,128)(2,1)S(1)} %last.1), channel_id=1, source_target_pairs={{0,1},{1,0},{2,3},{3,2},{4,5},{5,4},{6,7},{7,6},{8,9},{9,8},{10,11... | collective-permute-start | bytes 1179656 | tf_op jit(solution)/shard_map/ppermute | solution.py:340

commit v11 on v9

--- a/solution.py
+++ b/solution.py
@@ -383,7 +383,7 @@
     across = merge(whole, across_sum, beside[:1])
     blocks = [swapped(block, k) if k else block for k, block in enumerate((*own, *beside, *across))]
     picked = call(pick_kernel, (single,) * n_head, "pick")(*blocks)
-    arrived = [moved(picked[m], lambda i, j, s, m=m: (i, j ^ m, s)) for m in (3, 2, 1)]
+    arrived = [moved(picked[m], lambda i, j, s, m=m: (i, j ^ m, s)) for m in (1, 2, 3)]
     out = jax.ShapeDtypeStruct((1, rows, columns), jnp.bfloat16)
     out = call(last_kernel, out, "last")(*arrived, picked[0])
     return moved(out, lambda i, j, s: (i, j, 1 - s))

time: 75.3 us -> 74.7 us (level)
  waiting for transfers between devices: 36.5 us -> 35.6 us
    ppermute x16, waiting for transfers between devices: 29.6 us -> 28.7 us  [moved(): lax.ppermute(array, names, [(place[spot], place[target(*spot)]) for spot...]
where the time goes in v11:
time: 74.7 us; the launch traced here: 74.2 us
  waiting for transfers between devices  35.6 us (48%)
  starting transfers between devices  25.5 us (34%)
  Pallas kernels  12.2 us (16%)
  local copies, waits for them, and re-layouts  0.75 us (1%)
    ppermute x16, waiting for transfers between devices, moved(): lax.ppermute(array, names, [(place[spot], place[target(*spot)]) for spot...  28.7 us
    ppermute x16, starting transfers between devices, moved(): lax.ppermute(array, names, [(place[spot], place[target(*spot)]) for spot...  20.6 us
    ppermute x1, waiting for transfers between devices, from_before(): return lax.ppermute(array, 'ctx', [(i, i + by) for i in range(n_ctx - by)])  6.98 us
    ppermute x1, starting transfers between devices, from_before(): return lax.ppermute(array, 'ctx', [(i, i + by) for i in range(n_ctx - by)])  4.87 us
    pallas_call x6, Pallas kernels, project(): call(kernel, shape, 'project', in_specs=specs)(*picked, weight, *after)  4.4 us
    pallas_call x1, Pallas kernels, on_device(): call(inside_kernel, (pltpu.VMEM((rows, width), jnp.float32), pltpu.VMEM((...  4.24 us
    pallas_call x1, Pallas kernels, on_device(): call(state_kernel, state_shape, 'shard_state', in_specs=[HBM] * 4, scratc...  2.58 us
  transfers between devices with their start and end apart: 17, of which 14 were waited for; matrix products, arithmetic and copies ran while one was open for 0% of the time, Pallas kernels for 12%

profile of v11, /device:TPU:0, one launch (start us, length us, event | category | flops | bytes accessed | tf_op | source)
XLA Modules:
  0.0 74.2 jit_solution(196242406434412814)
XLA Ops:
  0.0 2.6 %shard_state.1 = bf16[2064,128]{1,0:T(8,128)(2,1)S(1)} custom-call(bf16[1,128,2048]{2,1,0:T(8,128)(2,1)} %refs_0_.1, bf16[1,128,2048]{2,1,0:T(8,128)(2,1)} %refs_1_.1, f32[1,16,128]{2,1,0:T(8,128)} %bitcast.1, s32[1,128]{1,0:T(1,128)} %refs_3_.1), custom_call_target="tpu_custom_call" | custom-call | flops 1 | bytes 1 | tf_op jit(solution)/shard_map/shard_state/pallas_call | solution.py:264
  2.6 4.9 %collective-permute-start = (bf16[2064,128]{1,0:T(8,128)(2,1)S(1)}, bf16[2064,128]{1,0:T(8,128)(2,1)S(1)}, u32[]{:S(2)}, u32[]{:S(2)}) collective-permute-start(bf16[2064,128]{1,0:T(8,128)(2,1)S(1)} %shard_state.1), channel_id=1, source_target_pairs={{0,8},{8,16},{16,24},{1,9},{9,17},{17,25},{2,10},{10,18},{18,26},{... | collective-permute-start | bytes 1585160 | tf_op jit(solution)/shard_map/ppermute | solution.py:260
  7.5 4.2 %inside.1 = (f32[128,2048]{1,0:T(8,128)S(1)}, f32[128,2048]{1,0:T(8,128)S(1)}, f32[128,128]{1,0:T(8,128)S(1)}, bf16[128,2048]{1,0:T(8,128)(2,1)S(1)}, bf16[2048,1536]{1,0:T(8,128)(2,1)S(1)}) custom-call(bf16[1,128,2048]{2,1,0:T(8,128)(2,1)} %query_hbm.1, bf16[1,128,2048]{2,1,0:T(8,128)(2,1)} %refs_0_.1, bf16[1,128,2048]{2,1,0:T(8,128)(2,1)} %refs_1_.1, ...), custom_call_target="tpu_custom_call" | custom-call | flops 1 | bytes 1 | tf_op jit(solution)/shard_map/inside/pallas_call | solution.py:296
  11.7 7.0 %collective-permute-done.state_ref = bf16[2064,128]{1,0:T(8,128)(2,1)S(1)} collective-permute-done((bf16[2064,128]{1,0:T(8,128)(2,1)S(1)}, bf16[2064,128]{1,0:T(8,128)(2,1)S(1)}, u32[]{:S(2)}, u32[]{:S(2)}) %collective-permute-start) | collective-permute-done | bytes 528416 | tf_op jit(solution)/shard_map/ppermute | solution.py:260
  19.3 3.5 %collective-permute-start.4 = (bf16[64,2048]{1,0:T(8,128)(2,1)S(1)}, bf16[64,2048]{1,0:T(8,128)(2,1)S(1)}, u32[]{:S(2)}, u32[]{:S(2)}) collective-permute-start(bf16[64,2048]{1,0:T(8,128)(2,1)S(1)} %get-tuple-element.24.refs_0_), channel_id=1, source_target_pairs={{0,16},{1,17},{2,18},{3,19},{4,20},{5,21},{6,22},{7,23},{8,24},{9,... | collective-permute-start | bytes 786440 | tf_op jit(solution)/shard_map/ppermute | solution.py:340
  22.7 1.1 %collective-permute-start.5 = (bf16[64,2048]{1,0:T(8,128)(2,1)S(1)}, bf16[64,2048]{1,0:T(8,128)(2,1)S(1)}, u32[]{:S(2)}, u32[]{:S(2)}) collective-permute-start(bf16[64,2048]{1,0:T(8,128)(2,1)S(1)} %get-tuple-element.25.refs_1_), channel_id=1, source_target_pairs={{0,16},{1,17},{2,18},{3,19},{4,20},{5,21},{6,22},{7,23},{8,24},{9,... | collective-permute-start | bytes 786440 | tf_op jit(solution)/shard_map/ppermute | solution.py:340
  25.5 1.6 %collective-permute-start.1 = (bf16[2,64,768]{2,1,0:T(8,128)(2,1)S(1)}, bf16[2,64,768]{2,1,0:T(8,128)(2,1)S(1)}, u32[]{:S(2)}, u32[]{:S(2)}) collective-permute-start(bf16[2,64,768]{2,1,0:T(8,128)(2,1)S(1)} %project.7), channel_id=1, source_target_pairs={{0,2},{1,3},{2,0},{3,1},{4,6},{5,7},{6,4},{7,5},{8,10},{9,11},{10,... | collective-permute-start | bytes 589832 | tf_op jit(solution)/shard_map/ppermute | solution.py:340
  27.7 3.5 %collective-permute-done.1.refs_1_ = bf16[2,64,768]{2,1,0:T(8,128)(2,1)S(1)} collective-permute-done((bf16[2,64,768]{2,1,0:T(8,128)(2,1)S(1)}, bf16[2,64,768]{2,1,0:T(8,128)(2,1)S(1)}, u32[]{:S(2)}, u32[]{:S(2)}) %collective-permute-start.1) | collective-permute-done | bytes 196640 | tf_op jit(solution)/shard_map/ppermute | solution.py:340
  32.0 1.8 %collective-permute-done.5.refs_3_.lower_ref = bf16[64,2048]{1,0:T(8,128)(2,1)S(1)} collective-permute-done((bf16[64,2048]{1,0:T(8,128)(2,1)S(1)}, bf16[64,2048]{1,0:T(8,128)(2,1)S(1)}, u32[]{:S(2)}, u32[]{:S(2)}) %collective-permute-start.5) | collective-permute-done | bytes 262176 | tf_op jit(solution)/shard_map/ppermute | solution.py:340
  33.8 1.5 %collective-permute-done.3.refs_1_.refs_0_ = bf16[64,2048]{1,0:T(8,128)(2,1)S(1)} collective-permute-done((bf16[64,2048]{1,0:T(8,128)(2,1)S(1)}, bf16[64,2048]{1,0:T(8,128)(2,1)S(1)}, u32[]{:S(2)}, u32[]{:S(2)}) %collective-permute-start.3) | collective-permute-done | bytes 262176 | tf_op jit(solution)/shard_map/ppermute | solution.py:340
  37.5 1.6 %collective-permute-start.6 = (bf16[4,64,768]{2,1,0:T(8,128)(2,1)S(1)}, bf16[4,64,768]{2,1,0:T(8,128)(2,1)S(1)}, u32[]{:S(2)}, u32[]{:S(2)}) collective-permute-start(bf16[4,64,768]{2,1,0:T(8,128)(2,1)S(1)} %project.9), channel_id=1, source_target_pairs={{0,2},{1,3},{2,0},{3,1},{4,6},{5,7},{6,4},{7,5},{8,10},{9,11},{10,... | collective-permute-start | bytes 1179656 | tf_op jit(solution)/shard_map/ppermute | solution.py:340
  40.1 1.6 %collective-permute-done.9.refs_0_ = bf16[64,2048]{1,0:T(8,128)(2,1)S(1)} collective-permute-done((bf16[64,2048]{1,0:T(8,128)(2,1)S(1)}, bf16[64,2048]{1,0:T(8,128)(2,1)S(1)}, u32[]{:S(2)}, u32[]{:S(2)}) %collective-permute-start.9) | collective-permute-done | bytes 262176 | tf_op jit(solution)/shard_map/ppermute | solution.py:340
  42.7 1.6 %collective-permute-start.11 = (bf16[2,64,768]{2,1,0:T(8,128)(2,1)S(1)}, bf16[2,64,768]{2,1,0:T(8,128)(2,1)S(1)}, u32[]{:S(2)}, u32[]{:S(2)}) collective-permute-start(bf16[2,64,768]{2,1,0:T(8,128)(2,1)S(1)} %project.11), channel_id=1, source_target_pairs={{0,2},{1,3},{2,0},{3,1},{4,6},{5,7},{6,4},{7,5},{8,10},{9,11},{10,... | collective-permute-start | bytes 589832 | tf_op jit(solution)/shard_map/ppermute | solution.py:340
  44.9 2.9 %collective-permute-done.6.refs_1_ = bf16[4,64,768]{2,1,0:T(8,128)(2,1)S(1)} collective-permute-done((bf16[4,64,768]{2,1,0:T(8,128)(2,1)S(1)}, bf16[4,64,768]{2,1,0:T(8,128)(2,1)S(1)}, u32[]{:S(2)}, u32[]{:S(2)}) %collective-permute-start.6) | collective-permute-done | bytes 393248 | tf_op jit(solution)/shard_map/ppermute | solution.py:340
  48.0 1.6 %collective-permute-start.8 = (bf16[128,768]{1,0:T(8,128)(2,1)S(1)}, bf16[128,768]{1,0:T(8,128)(2,1)S(1)}, u32[]{:S(2)}, u32[]{:S(2)}) collective-permute-start(bf16[128,768]{1,0:T(8,128)(2,1)S(1)} %get-tuple-element.28), channel_id=1, source_target_pairs={{0,16},{1,17},{2,18},{3,19},{4,20},{5,21},{6,22},{7,23},{8,24},{9,... | collective-permute-start | bytes 589832 | tf_op jit(solution)/shard_map/ppermute | solution.py:340
  49.5 1.5 %collective-permute-start.7 = (bf16[128,768]{1,0:T(8,128)(2,1)S(1)}, bf16[128,768]{1,0:T(8,128)(2,1)S(1)}, u32[]{:S(2)}, u32[]{:S(2)}) collective-permute-start(bf16[128,768]{1,0:T(8,128)(2,1)S(1)} %get-tuple-element.27.refs_2_), channel_id=1, source_target_pairs={{0,8},{1,9},{2,10},{3,11},{4,12},{5,13},{6,14},{7,15},{8,0},{9,1},... | collective-permute-start | bytes 589832 | tf_op jit(solution)/shard_map/ppermute | solution.py:340
  51.0 1.4 %collective-permute-start.12 = (bf16[128,768]{1,0:T(8,128)(2,1)S(1)}, bf16[128,768]{1,0:T(8,128)(2,1)S(1)}, u32[]{:S(2)}, u32[]{:S(2)}) collective-permute-start(bf16[128,768]{1,0:T(8,128)(2,1)S(1)} %merge.5), channel_id=1, source_target_pairs={{0,24},{1,25},{2,26},{3,27},{4,28},{5,29},{6,30},{7,31},{8,16},{9,... | collective-permute-start | bytes 589832 | tf_op jit(solution)/shard_map/ppermute | solution.py:340
  52.5 1.6 %collective-permute-done.8.refs_2_ = bf16[128,768]{1,0:T(8,128)(2,1)S(1)} collective-permute-done((bf16[128,768]{1,0:T(8,128)(2,1)S(1)}, bf16[128,768]{1,0:T(8,128)(2,1)S(1)}, u32[]{:S(2)}, u32[]{:S(2)}) %collective-permute-start.8) | collective-permute-done | bytes 196640 | tf_op jit(solution)/shard_map/ppermute | solution.py:340
  55.2 2.5 %collective-permute-done.12.refs_3_ = bf16[128,768]{1,0:T(8,128)(2,1)S(1)} collective-permute-done((bf16[128,768]{1,0:T(8,128)(2,1)S(1)}, bf16[128,768]{1,0:T(8,128)(2,1)S(1)}, u32[]{:S(2)}, u32[]{:S(2)}) %collective-permute-start.12) | collective-permute-done | bytes 196640 | tf_op jit(solution)/shard_map/ppermute | solution.py:340
  57.8 1.6 %collective-permute-start.13 = (bf16[128,768]{1,0:T(8,128)(2,1)S(1)}, bf16[128,768]{1,0:T(8,128)(2,1)S(1)}, u32[]{:S(2)}, u32[]{:S(2)}) collective-permute-start(bf16[128,768]{1,0:T(8,128)(2,1)S(1)} %get-tuple-element.31), channel_id=1, source_target_pairs={{0,2},{1,3},{2,0},{3,1},{4,6},{5,7},{6,4},{7,5},{8,10},{9,11},{10,... | collective-permute-start | bytes 589832 | tf_op jit(solution)/shard_map/ppermute | solution.py:340
  59.4 2.6 %collective-permute-start.14 = (bf16[128,768]{1,0:T(8,128)(2,1)S(1)}, bf16[128,768]{1,0:T(8,128)(2,1)S(1)}, u32[]{:S(2)}, u32[]{:S(2)}) collective-permute-start(bf16[128,768]{1,0:T(8,128)(2,1)S(1)} %get-tuple-element.32), channel_id=1, source_target_pairs={{0,4},{1,5},{2,6},{3,7},{4,0},{5,1},{6,2},{7,3},{8,12},{9,13},{10,... | collective-permute-start | bytes 589832 | tf_op jit(solution)/shard_map/ppermute | solution.py:340
  62.2 3.8 %collective-permute-done.13.refs_0_ = bf16[128,768]{1,0:T(8,128)(2,1)S(1)} collective-permute-done((bf16[128,768]{1,0:T(8,128)(2,1)S(1)}, bf16[128,768]{1,0:T(8,128)(2,1)S(1)}, u32[]{:S(2)}, u32[]{:S(2)}) %collective-permute-start.13) | collective-permute-done | bytes 196640 | tf_op jit(solution)/shard_map/ppermute | solution.py:340
  66.1 5.5 %collective-permute-done.14.refs_1_ = bf16[128,768]{1,0:T(8,128)(2,1)S(1)} collective-permute-done((bf16[128,768]{1,0:T(8,128)(2,1)S(1)}, bf16[128,768]{1,0:T(8,128)(2,1)S(1)}, u32[]{:S(2)}, u32[]{:S(2)}) %collective-permute-start.14) | collective-permute-done | bytes 196640 | tf_op jit(solution)/shard_map/ppermute | solution.py:340
  71.7 1.7 %collective-permute-done.16 = bf16[1,128,1536]{2,1,0:T(8,128)(2,1)S(1)} collective-permute-done((bf16[1,128,1536]{2,1,0:T(8,128)(2,1)S(1)}, bf16[1,128,1536]{2,1,0:T(8,128)(2,1)S(1)}, u32[]{:S(2)}, u32[]{:S(2)}) %collective-permute-start.16) | collective-permute-done | bytes 393248 | tf_op jit(solution)/shard_map/ppermute | solution.py:340
  (26 shorter events, 10.8 us)
Async XLA Ops:
  2.6 16.1 %collective-permute-start = (bf16[2064,128]{1,0:T(8,128)(2,1)S(1)}, bf16[2064,128]{1,0:T(8,128)(2,1)S(1)}, u32[]{:S(2)}, u32[]{:S(2)}) collective-permute-start(bf16[2064,128]{1,0:T(8,128)(2,1)S(1)} %shard_state.1), channel_id=1, source_target_pairs={{0,8},{8,16},{16,24},{1,9},{9,17},{17,25},{2,10},{10,18},{18,26},{... | collective-permute-start | bytes 1585160 | tf_op jit(solution)/shard_map/ppermute | solution.py:260
  19.3 12.0 %collective-permute-start.4 = (bf16[64,2048]{1,0:T(8,128)(2,1)S(1)}, bf16[64,2048]{1,0:T(8,128)(2,1)S(1)}, u32[]{:S(2)}, u32[]{:S(2)}) collective-permute-start(bf16[64,2048]{1,0:T(8,128)(2,1)S(1)} %get-tuple-element.24.refs_0_), channel_id=1, source_target_pairs={{0,16},{1,17},{2,18},{3,19},{4,20},{5,21},{6,22},{7,23},{8,24},{9,... | collective-permute-start | bytes 786440 | tf_op jit(solution)/shard_map/ppermute | solution.py:340
  22.7 9.2 %collective-permute-start.2 = (bf16[64,2048]{1,0:T(8,128)(2,1)S(1)}, bf16[64,2048]{1,0:T(8,128)(2,1)S(1)}, u32[]{:S(2)}, u32[]{:S(2)}) collective-permute-start(bf16[64,2048]{1,0:T(8,128)(2,1)S(1)} %get-tuple-element.24.refs_0_), channel_id=1, source_target_pairs={{0,8},{1,9},{2,10},{3,11},{4,12},{5,13},{6,14},{7,15},{8,0},{9,1},... | collective-permute-start | bytes 786440 | tf_op jit(solution)/shard_map/ppermute | solution.py:340
  22.7 11.0 %collective-permute-start.5 = (bf16[64,2048]{1,0:T(8,128)(2,1)S(1)}, bf16[64,2048]{1,0:T(8,128)(2,1)S(1)}, u32[]{:S(2)}, u32[]{:S(2)}) collective-permute-start(bf16[64,2048]{1,0:T(8,128)(2,1)S(1)} %get-tuple-element.25.refs_1_), channel_id=1, source_target_pairs={{0,16},{1,17},{2,18},{3,19},{4,20},{5,21},{6,22},{7,23},{8,24},{9,... | collective-permute-start | bytes 786440 | tf_op jit(solution)/shard_map/ppermute | solution.py:340
  23.8 11.4 %collective-permute-start.3 = (bf16[64,2048]{1,0:T(8,128)(2,1)S(1)}, bf16[64,2048]{1,0:T(8,128)(2,1)S(1)}, u32[]{:S(2)}, u32[]{:S(2)}) collective-permute-start(bf16[64,2048]{1,0:T(8,128)(2,1)S(1)} %get-tuple-element.25.refs_1_), channel_id=1, source_target_pairs={{0,8},{1,9},{2,10},{3,11},{4,12},{5,13},{6,14},{7,15},{8,0},{9,1},... | collective-permute-start | bytes 786440 | tf_op jit(solution)/shard_map/ppermute | solution.py:340
  25.5 5.7 %collective-permute-start.1 = (bf16[2,64,768]{2,1,0:T(8,128)(2,1)S(1)}, bf16[2,64,768]{2,1,0:T(8,128)(2,1)S(1)}, u32[]{:S(2)}, u32[]{:S(2)}) collective-permute-start(bf16[2,64,768]{2,1,0:T(8,128)(2,1)S(1)} %project.7), channel_id=1, source_target_pairs={{0,2},{1,3},{2,0},{3,1},{4,6},{5,7},{6,4},{7,5},{8,10},{9,11},{10,... | collective-permute-start | bytes 589832 | tf_op jit(solution)/shard_map/ppermute | solution.py:340
  35.3 6.4 %collective-permute-start.9 = (bf16[64,2048]{1,0:T(8,128)(2,1)S(1)}, bf16[64,2048]{1,0:T(8,128)(2,1)S(1)}, u32[]{:S(2)}, u32[]{:S(2)}) collective-permute-start(bf16[64,2048]{1,0:T(8,128)(2,1)S(1)} %get-tuple-element.29), channel_id=1, source_target_pairs={{0,16},{1,17},{2,18},{3,19},{4,20},{5,21},{6,22},{7,23},{8,24},{9,... | collective-permute-start | bytes 786440 | tf_op jit(solution)/shard_map/ppermute | solution.py:340
  35.7 6.4 %collective-permute-start.10 = (bf16[64,2048]{1,0:T(8,128)(2,1)S(1)}, bf16[64,2048]{1,0:T(8,128)(2,1)S(1)}, u32[]{:S(2)}, u32[]{:S(2)}) collective-permute-start(bf16[64,2048]{1,0:T(8,128)(2,1)S(1)} %get-tuple-element.30), channel_id=1, source_target_pairs={{0,8},{1,9},{2,10},{3,11},{4,12},{5,13},{6,14},{7,15},{8,0},{9,1},... | collective-permute-start | bytes 786440 | tf_op jit(solution)/shard_map/ppermute | solution.py:340
  37.5 10.4 %collective-permute-start.6 = (bf16[4,64,768]{2,1,0:T(8,128)(2,1)S(1)}, bf16[4,64,768]{2,1,0:T(8,128)(2,1)S(1)}, u32[]{:S(2)}, u32[]{:S(2)}) collective-permute-start(bf16[4,64,768]{2,1,0:T(8,128)(2,1)S(1)} %project.9), channel_id=1, source_target_pairs={{0,2},{1,3},{2,0},{3,1},{4,6},{5,7},{6,4},{7,5},{8,10},{9,11},{10,... | collective-permute-start | bytes 1179656 | tf_op jit(solution)/shard_map/ppermute | solution.py:340
  42.7 8.3 %collective-permute-start.11 = (bf16[2,64,768]{2,1,0:T(8,128)(2,1)S(1)}, bf16[2,64,768]{2,1,0:T(8,128)(2,1)S(1)}, u32[]{:S(2)}, u32[]{:S(2)}) collective-permute-start(bf16[2,64,768]{2,1,0:T(8,128)(2,1)S(1)} %project.11), channel_id=1, source_target_pairs={{0,2},{1,3},{2,0},{3,1},{4,6},{5,7},{6,4},{7,5},{8,10},{9,11},{10,... | collective-permute-start | bytes 589832 | tf_op jit(solution)/shard_map/ppermute | solution.py:340
  48.0 6.1 %collective-permute-start.8 = (bf16[128,768]{1,0:T(8,128)(2,1)S(1)}, bf16[128,768]{1,0:T(8,128)(2,1)S(1)}, u32[]{:S(2)}, u32[]{:S(2)}) collective-permute-start(bf16[128,768]{1,0:T(8,128)(2,1)S(1)} %get-tuple-element.28), channel_id=1, source_target_pairs={{0,16},{1,17},{2,18},{3,19},{4,20},{5,21},{6,22},{7,23},{8,24},{9,... | collective-permute-start | bytes 589832 | tf_op jit(solution)/shard_map/ppermute | solution.py:340
  49.5 5.7 %collective-permute-start.7 = (bf16[128,768]{1,0:T(8,128)(2,1)S(1)}, bf16[128,768]{1,0:T(8,128)(2,1)S(1)}, u32[]{:S(2)}, u32[]{:S(2)}) collective-permute-start(bf16[128,768]{1,0:T(8,128)(2,1)S(1)} %get-tuple-element.27.refs_2_), channel_id=1, source_target_pairs={{0,8},{1,9},{2,10},{3,11},{4,12},{5,13},{6,14},{7,15},{8,0},{9,1},... | collective-permute-start | bytes 589832 | tf_op jit(solution)/shard_map/ppermute | solution.py:340
  51.0 6.6 %collective-permute-start.12 = (bf16[128,768]{1,0:T(8,128)(2,1)S(1)}, bf16[128,768]{1,0:T(8,128)(2,1)S(1)}, u32[]{:S(2)}, u32[]{:S(2)}) collective-permute-start(bf16[128,768]{1,0:T(8,128)(2,1)S(1)} %merge.5), channel_id=1, source_target_pairs={{0,24},{1,25},{2,26},{3,27},{4,28},{5,29},{6,30},{7,31},{8,16},{9,... | collective-permute-start | bytes 589832 | tf_op jit(solution)/shard_map/ppermute | solution.py:340
  57.8 8.3 %collective-permute-start.13 = (bf16[128,768]{1,0:T(8,128)(2,1)S(1)}, bf16[128,768]{1,0:T(8,128)(2,1)S(1)}, u32[]{:S(2)}, u32[]{:S(2)}) collective-permute-start(bf16[128,768]{1,0:T(8,128)(2,1)S(1)} %get-tuple-element.31), channel_id=1, source_target_pairs={{0,2},{1,3},{2,0},{3,1},{4,6},{5,7},{6,4},{7,5},{8,10},{9,11},{10,... | collective-permute-start | bytes 589832 | tf_op jit(solution)/shard_map/ppermute | solution.py:340
  59.4 12.2 %collective-permute-start.14 = (bf16[128,768]{1,0:T(8,128)(2,1)S(1)}, bf16[128,768]{1,0:T(8,128)(2,1)S(1)}, u32[]{:S(2)}, u32[]{:S(2)}) collective-permute-start(bf16[128,768]{1,0:T(8,128)(2,1)S(1)} %get-tuple-element.32), channel_id=1, source_target_pairs={{0,4},{1,5},{2,6},{3,7},{4,0},{5,1},{6,2},{7,3},{8,12},{9,13},{10,... | collective-permute-start | bytes 589832 | tf_op jit(solution)/shard_map/ppermute | solution.py:340
  62.0 9.6 %collective-permute-start.15 = (bf16[128,768]{1,0:T(8,128)(2,1)S(1)}, bf16[128,768]{1,0:T(8,128)(2,1)S(1)}, u32[]{:S(2)}, u32[]{:S(2)}) collective-permute-start(bf16[128,768]{1,0:T(8,128)(2,1)S(1)} %get-tuple-element.33), channel_id=1, source_target_pairs={{0,6},{1,7},{2,4},{3,5},{4,2},{5,3},{6,0},{7,1},{8,14},{9,15},{10,... | collective-permute-start | bytes 589832 | tf_op jit(solution)/shard_map/ppermute | solution.py:340
  71.7 1.8 %collective-permute-start.16 = (bf16[1,128,1536]{2,1,0:T(8,128)(2,1)S(1)}, bf16[1,128,1536]{2,1,0:T(8,128)(2,1)S(1)}, u32[]{:S(2)}, u32[]{:S(2)}) collective-permute-start(bf16[1,128,1536]{2,1,0:T(8,128)(2,1)S(1)} %last.1), channel_id=1, source_target_pairs={{0,1},{1,0},{2,3},{3,2},{4,5},{5,4},{6,7},{7,6},{8,9},{9,8},{10,11... | collective-permute-start | bytes 1179656 | tf_op jit(solution)/shard_map/ppermute | solution.py:340

commit v12 on v11

--- a/solution.py
+++ b/solution.py
@@ -219,13 +219,17 @@
                     out_ref[...] = jnp.concatenate([ref[...] for ref in block_refs[j:]], axis=0)
 
 
+def sum_kernel(one_ref, two_ref, out_ref):
+    total = one_ref[...].astype(jnp.float32) + two_ref[...].astype(jnp.float32)
+    out_ref[...] = total.astype(jnp.bfloat16)
+
+
 def last_kernel(*refs):
     out_ref = refs[-1]
     wide = refs[0].shape[1]
     for m in range(2):
-        total = refs[m][...].astype(jnp.float32) + refs[m + 2][...].astype(jnp.float32)
-        half = (lax.axis_index("head") & 1) ^ 1 ^ m
-        out_ref[0, :, pl.ds(pl.multiple_of(half * wide, wide), wide)] = total.astype(jnp.bfloat16)
+        half = (lax.axis_index("head") & 1) ^ m
+        out_ref[0, :, pl.ds(pl.multiple_of(half * wide, wide), wide)] = refs[m][...]
 
 
 def call(kernel, out_shape, name, limit=24, **more):
@@ -384,9 +388,11 @@
     blocks = [swapped(block, k) if k else block for k, block in enumerate((*own, *beside, *across))]
     picked = call(pick_kernel, (single,) * n_head, "pick")(*blocks)
     arrived = [moved(picked[m], lambda i, j, s, m=m: (i, j ^ m, s)) for m in (1, 2, 3)]
+    total = [call(sum_kernel, single, "sum")(picked[0], arrived[1])]
+    total.append(call(sum_kernel, single, "sum")(arrived[0], arrived[2]))
+    total = [moved(half, lambda i, j, s: (i, j, 1 - s)) for half in total]
     out = jax.ShapeDtypeStruct((1, rows, columns), jnp.bfloat16)
-    out = call(last_kernel, out, "last")(*arrived, picked[0])
-    return moved(out, lambda i, j, s: (i, j, 1 - s))
+    return call(last_kernel, out, "last")(*total)
 
 
 def solution(mesh):

time: 74.7 us -> 74.1 us (level)
  waiting for transfers between devices: 35.6 us -> 33.8 us
  Pallas kernels: 12.2 us -> 13 us
  local copies, waits for them, and re-layouts: 0.75 us -> 0 us
    ppermute x16 -> x17, waiting for transfers between devices: 28.7 us -> 26.8 us  [moved(): lax.ppermute(array, names, [(place[spot], place[target(*spot)]) for spot...]
    pallas_call x1 -> x3, Pallas kernels: 0.09 us -> 0.88 us  [the longest x1 0.79 us: on_device(): return call(last_kernel, out, 'last')(*total)]
    ppermute x16 -> x17, starting transfers between devices: 20.6 us -> 21.2 us  [moved(): lax.ppermute(array, names, [(place[spot], place[target(*spot)]) for spot...]
  transfers between devices with their start and end apart: 17 -> 18, of which waited for: 14 -> 14; matrix products, arithmetic and copies ran while one was open for 0% -> 0% of each run, Pallas kernels for 12% -> 12%
where the time goes in v12:
time: 74.1 us; the launch traced here: 72.9 us
  waiting for transfers between devices  33.8 us (46%)
  starting transfers between devices  26 us (35%)
  Pallas kernels  13 us (18%)
    ppermute x17, waiting for transfers between devices, moved(): lax.ppermute(array, names, [(place[spot], place[target(*spot)]) for spot...  26.8 us
    ppermute x17, starting transfers between devices, moved(): lax.ppermute(array, names, [(place[spot], place[target(*spot)]) for spot...  21.2 us
    ppermute x1, waiting for transfers between devices, from_before(): return lax.ppermute(array, 'ctx', [(i, i + by) for i in range(n_ctx - by)])  6.98 us
    ppermute x1, starting transfers between devices, from_before(): return lax.ppermute(array, 'ctx', [(i, i + by) for i in range(n_ctx - by)])  4.87 us
    pallas_call x6, Pallas kernels, project(): call(kernel, shape, 'project', in_specs=specs)(*picked, weight, *after)  4.4 us
    pallas_call x1, Pallas kernels, on_device(): call(inside_kernel, (pltpu.VMEM((rows, width), jnp.float32), pltpu.VMEM((...  4.24 us
    pallas_call x1, Pallas kernels, on_device(): call(state_kernel, state_shape, 'shard_state', in_specs=[HBM] * 4, scratc...  2.58 us
  transfers between devices with their start and end apart: 18, of which 14 were waited for; matrix products, arithmetic and copies ran while one was open for 0% of the time, Pallas kernels for 12%

profile of v12, /device:TPU:0, one launch (start us, length us, event | category | flops | bytes accessed | tf_op | source)
XLA Modules:
  0.0 72.9 jit_solution(12343860542983629160)
XLA Ops:
  0.0 2.6 %shard_state.1 = bf16[2064,128]{1,0:T(8,128)(2,1)S(1)} custom-call(bf16[1,128,2048]{2,1,0:T(8,128)(2,1)} %refs_0_.1, bf16[1,128,2048]{2,1,0:T(8,128)(2,1)} %refs_1_.1, f32[1,16,128]{2,1,0:T(8,128)} %bitcast.1, s32[1,128]{1,0:T(1,128)} %refs_3_.1), custom_call_target="tpu_custom_call" | custom-call | flops 1 | bytes 1 | tf_op jit(solution)/shard_map/shard_state/pallas_call | solution.py:268
  2.6 4.9 %collective-permute-start = (bf16[2064,128]{1,0:T(8,128)(2,1)S(1)}, bf16[2064,128]{1,0:T(8,128)(2,1)S(1)}, u32[]{:S(2)}, u32[]{:S(2)}) collective-permute-start(bf16[2064,128]{1,0:T(8,128)(2,1)S(1)} %shard_state.1), channel_id=1, source_target_pairs={{0,8},{8,16},{16,24},{1,9},{9,17},{17,25},{2,10},{10,18},{18,26},{... | collective-permute-start | bytes 1585160 | tf_op jit(solution)/shard_map/ppermute | solution.py:264
  7.5 4.2 %inside.1 = (f32[128,2048]{1,0:T(8,128)S(1)}, f32[128,2048]{1,0:T(8,128)S(1)}, f32[128,128]{1,0:T(8,128)S(1)}, bf16[128,2048]{1,0:T(8,128)(2,1)S(1)}, bf16[2048,1536]{1,0:T(8,128)(2,1)S(1)}) custom-call(bf16[1,128,2048]{2,1,0:T(8,128)(2,1)} %query_hbm.1, bf16[1,128,2048]{2,1,0:T(8,128)(2,1)} %refs_0_.1, bf16[1,128,2048]{2,1,0:T(8,128)(2,1)} %refs_1_.1, ...), custom_call_target="tpu_custom_call" | custom-call | flops 1 | bytes 1 | tf_op jit(solution)/shard_map/inside/pallas_call | solution.py:300
  11.7 7.0 %collective-permute-done.state_ref = bf16[2064,128]{1,0:T(8,128)(2,1)S(1)} collective-permute-done((bf16[2064,128]{1,0:T(8,128)(2,1)S(1)}, bf16[2064,128]{1,0:T(8,128)(2,1)S(1)}, u32[]{:S(2)}, u32[]{:S(2)}) %collective-permute-start) | collective-permute-done | bytes 528416 | tf_op jit(solution)/shard_map/ppermute | solution.py:264
  19.3 3.5 %collective-permute-start.4 = (bf16[64,2048]{1,0:T(8,128)(2,1)S(1)}, bf16[64,2048]{1,0:T(8,128)(2,1)S(1)}, u32[]{:S(2)}, u32[]{:S(2)}) collective-permute-start(bf16[64,2048]{1,0:T(8,128)(2,1)S(1)} %get-tuple-element.24.refs_0_), channel_id=1, source_target_pairs={{0,16},{1,17},{2,18},{3,19},{4,20},{5,21},{6,22},{7,23},{8,24},{9,... | collective-permute-start | bytes 786440 | tf_op jit(solution)/shard_map/ppermute | solution.py:344
  22.7 1.1 %collective-permute-start.5 = (bf16[64,2048]{1,0:T(8,128)(2,1)S(1)}, bf16[64,2048]{1,0:T(8,128)(2,1)S(1)}, u32[]{:S(2)}, u32[]{:S(2)}) collective-permute-start(bf16[64,2048]{1,0:T(8,128)(2,1)S(1)} %get-tuple-element.25.refs_1_), channel_id=1, source_target_pairs={{0,16},{1,17},{2,18},{3,19},{4,20},{5,21},{6,22},{7,23},{8,24},{9,... | collective-permute-start | bytes 786440 | tf_op jit(solution)/shard_map/ppermute | solution.py:344
  23.8 1.0 %collective-permute-start.3 = (bf16[64,2048]{1,0:T(8,128)(2,1)S(1)}, bf16[64,2048]{1,0:T(8,128)(2,1)S(1)}, u32[]{:S(2)}, u32[]{:S(2)}) collective-permute-start(bf16[64,2048]{1,0:T(8,128)(2,1)S(1)} %get-tuple-element.25.refs_1_), channel_id=1, source_target_pairs={{0,8},{1,9},{2,10},{3,11},{4,12},{5,13},{6,14},{7,15},{8,0},{9,1},... | collective-permute-start | bytes 786440 | tf_op jit(solution)/shard_map/ppermute | solution.py:344
  25.5 1.6 %collective-permute-start.1 = (bf16[2,64,768]{2,1,0:T(8,128)(2,1)S(1)}, bf16[2,64,768]{2,1,0:T(8,128)(2,1)S(1)}, u32[]{:S(2)}, u32[]{:S(2)}) collective-permute-start(bf16[2,64,768]{2,1,0:T(8,128)(2,1)S(1)} %project.7), channel_id=1, source_target_pairs={{0,2},{1,3},{2,0},{3,1},{4,6},{5,7},{6,4},{7,5},{8,10},{9,11},{10,... | collective-permute-start | bytes 589832 | tf_op jit(solution)/shard_map/ppermute | solution.py:344
  27.7 3.5 %collective-permute-done.1.refs_1_ = bf16[2,64,768]{2,1,0:T(8,128)(2,1)S(1)} collective-permute-done((bf16[2,64,768]{2,1,0:T(8,128)(2,1)S(1)}, bf16[2,64,768]{2,1,0:T(8,128)(2,1)S(1)}, u32[]{:S(2)}, u32[]{:S(2)}) %collective-permute-start.1) | collective-permute-done | bytes 196640 | tf_op jit(solution)/shard_map/ppermute | solution.py:344
  32.0 1.8 %collective-permute-done.5.refs_3_.lower_ref = bf16[64,2048]{1,0:T(8,128)(2,1)S(1)} collective-permute-done((bf16[64,2048]{1,0:T(8,128)(2,1)S(1)}, bf16[64,2048]{1,0:T(8,128)(2,1)S(1)}, u32[]{:S(2)}, u32[]{:S(2)}) %collective-permute-start.5) | collective-permute-done | bytes 262176 | tf_op jit(solution)/shard_map/ppermute | solution.py:344
  33.8 1.5 %collective-permute-done.3.refs_1_.refs_0_ = bf16[64,2048]{1,0:T(8,128)(2,1)S(1)} collective-permute-done((bf16[64,2048]{1,0:T(8,128)(2,1)S(1)}, bf16[64,2048]{1,0:T(8,128)(2,1)S(1)}, u32[]{:S(2)}, u32[]{:S(2)}) %collective-permute-start.3) | collective-permute-done | bytes 262176 | tf_op jit(solution)/shard_map/ppermute | solution.py:344
  37.5 1.6 %collective-permute-start.6 = (bf16[4,64,768]{2,1,0:T(8,128)(2,1)S(1)}, bf16[4,64,768]{2,1,0:T(8,128)(2,1)S(1)}, u32[]{:S(2)}, u32[]{:S(2)}) collective-permute-start(bf16[4,64,768]{2,1,0:T(8,128)(2,1)S(1)} %project.9), channel_id=1, source_target_pairs={{0,2},{1,3},{2,0},{3,1},{4,6},{5,7},{6,4},{7,5},{8,10},{9,11},{10,... | collective-permute-start | bytes 1179656 | tf_op jit(solution)/shard_map/ppermute | solution.py:344
  40.1 1.6 %collective-permute-done.9.refs_0_ = bf16[64,2048]{1,0:T(8,128)(2,1)S(1)} collective-permute-done((bf16[64,2048]{1,0:T(8,128)(2,1)S(1)}, bf16[64,2048]{1,0:T(8,128)(2,1)S(1)}, u32[]{:S(2)}, u32[]{:S(2)}) %collective-permute-start.9) | collective-permute-done | bytes 262176 | tf_op jit(solution)/shard_map/ppermute | solution.py:344
  42.7 1.6 %collective-permute-start.11 = (bf16[2,64,768]{2,1,0:T(8,128)(2,1)S(1)}, bf16[2,64,768]{2,1,0:T(8,128)(2,1)S(1)}, u32[]{:S(2)}, u32[]{:S(2)}) collective-permute-start(bf16[2,64,768]{2,1,0:T(8,128)(2,1)S(1)} %project.11), channel_id=1, source_target_pairs={{0,2},{1,3},{2,0},{3,1},{4,6},{5,7},{6,4},{7,5},{8,10},{9,11},{10,... | collective-permute-start | bytes 589832 | tf_op jit(solution)/shard_map/ppermute | solution.py:344
  44.9 2.9 %collective-permute-done.6.refs_1_ = bf16[4,64,768]{2,1,0:T(8,128)(2,1)S(1)} collective-permute-done((bf16[4,64,768]{2,1,0:T(8,128)(2,1)S(1)}, bf16[4,64,768]{2,1,0:T(8,128)(2,1)S(1)}, u32[]{:S(2)}, u32[]{:S(2)}) %collective-permute-start.6) | collective-permute-done | bytes 393248 | tf_op jit(solution)/shard_map/ppermute | solution.py:344
  48.0 1.6 %collective-permute-start.8 = (bf16[128,768]{1,0:T(8,128)(2,1)S(1)}, bf16[128,768]{1,0:T(8,128)(2,1)S(1)}, u32[]{:S(2)}, u32[]{:S(2)}) collective-permute-start(bf16[128,768]{1,0:T(8,128)(2,1)S(1)} %get-tuple-element.28), channel_id=1, source_target_pairs={{0,16},{1,17},{2,18},{3,19},{4,20},{5,21},{6,22},{7,23},{8,24},{9,... | collective-permute-start | bytes 589832 | tf_op jit(solution)/shard_map/ppermute | solution.py:344
  49.5 1.5 %collective-permute-start.7 = (bf16[128,768]{1,0:T(8,128)(2,1)S(1)}, bf16[128,768]{1,0:T(8,128)(2,1)S(1)}, u32[]{:S(2)}, u32[]{:S(2)}) collective-permute-start(bf16[128,768]{1,0:T(8,128)(2,1)S(1)} %get-tuple-element.27.refs_2_), channel_id=1, source_target_pairs={{0,8},{1,9},{2,10},{3,11},{4,12},{5,13},{6,14},{7,15},{8,0},{9,1},... | collective-permute-start | bytes 589832 | tf_op jit(solution)/shard_map/ppermute | solution.py:344
  51.0 1.4 %collective-permute-start.12 = (bf16[128,768]{1,0:T(8,128)(2,1)S(1)}, bf16[128,768]{1,0:T(8,128)(2,1)S(1)}, u32[]{:S(2)}, u32[]{:S(2)}) collective-permute-start(bf16[128,768]{1,0:T(8,128)(2,1)S(1)} %merge.5), channel_id=1, source_target_pairs={{0,24},{1,25},{2,26},{3,27},{4,28},{5,29},{6,30},{7,31},{8,16},{9,... | collective-permute-start | bytes 589832 | tf_op jit(solution)/shard_map/ppermute | solution.py:344
  52.5 1.6 %collective-permute-done.8.refs_2_ = bf16[128,768]{1,0:T(8,128)(2,1)S(1)} collective-permute-done((bf16[128,768]{1,0:T(8,128)(2,1)S(1)}, bf16[128,768]{1,0:T(8,128)(2,1)S(1)}, u32[]{:S(2)}, u32[]{:S(2)}) %collective-permute-start.8) | collective-permute-done | bytes 196640 | tf_op jit(solution)/shard_map/ppermute | solution.py:344
  54.1 1.1 %collective-permute-done.7.refs_1_ = bf16[128,768]{1,0:T(8,128)(2,1)S(1)} collective-permute-done((bf16[128,768]{1,0:T(8,128)(2,1)S(1)}, bf16[128,768]{1,0:T(8,128)(2,1)S(1)}, u32[]{:S(2)}, u32[]{:S(2)}) %collective-permute-start.7) | collective-permute-done | bytes 196640 | tf_op jit(solution)/shard_map/ppermute | solution.py:344
  55.2 2.5 %collective-permute-done.12.refs_3_ = bf16[128,768]{1,0:T(8,128)(2,1)S(1)} collective-permute-done((bf16[128,768]{1,0:T(8,128)(2,1)S(1)}, bf16[128,768]{1,0:T(8,128)(2,1)S(1)}, u32[]{:S(2)}, u32[]{:S(2)}) %collective-permute-start.12) | collective-permute-done | bytes 196640 | tf_op jit(solution)/shard_map/ppermute | solution.py:344
  57.8 2.7 %collective-permute-start.13 = (bf16[128,768]{1,0:T(8,128)(2,1)S(1)}, bf16[128,768]{1,0:T(8,128)(2,1)S(1)}, u32[]{:S(2)}, u32[]{:S(2)}) collective-permute-start(bf16[128,768]{1,0:T(8,128)(2,1)S(1)} %get-tuple-element.32), channel_id=1, source_target_pairs={{0,4},{1,5},{2,6},{3,7},{4,0},{5,1},{6,2},{7,3},{8,12},{9,13},{10,... | collective-permute-start | bytes 589832 | tf_op jit(solution)/shard_map/ppermute | solution.py:344
  60.4 1.6 %collective-permute-start.15 = (bf16[128,768]{1,0:T(8,128)(2,1)S(1)}, bf16[128,768]{1,0:T(8,128)(2,1)S(1)}, u32[]{:S(2)}, u32[]{:S(2)}) collective-permute-start(bf16[128,768]{1,0:T(8,128)(2,1)S(1)} %get-tuple-element.33), channel_id=1, source_target_pairs={{0,2},{1,3},{2,0},{3,1},{4,6},{5,7},{6,4},{7,5},{8,10},{9,11},{10,... | collective-permute-start | bytes 589832 | tf_op jit(solution)/shard_map/ppermute | solution.py:344
  62.2 8.1 %collective-permute-done.13.two_ref = bf16[128,768]{1,0:T(8,128)(2,1)S(1)} collective-permute-done((bf16[128,768]{1,0:T(8,128)(2,1)S(1)}, bf16[128,768]{1,0:T(8,128)(2,1)S(1)}, u32[]{:S(2)}, u32[]{:S(2)}) %collective-permute-start.13) | collective-permute-done | bytes 196640 | tf_op jit(solution)/shard_map/ppermute | solution.py:344
  (29 shorter events, 10.4 us)
Async XLA Ops:
  2.6 16.1 %collective-permute-start = (bf16[2064,128]{1,0:T(8,128)(2,1)S(1)}, bf16[2064,128]{1,0:T(8,128)(2,1)S(1)}, u32[]{:S(2)}, u32[]{:S(2)}) collective-permute-start(bf16[2064,128]{1,0:T(8,128)(2,1)S(1)} %shard_state.1), channel_id=1, source_target_pairs={{0,8},{8,16},{16,24},{1,9},{9,17},{17,25},{2,10},{10,18},{18,26},{... | collective-permute-start | bytes 1585160 | tf_op jit(solution)/shard_map/ppermute | solution.py:264
  19.3 12.0 %collective-permute-start.4 = (bf16[64,2048]{1,0:T(8,128)(2,1)S(1)}, bf16[64,2048]{1,0:T(8,128)(2,1)S(1)}, u32[]{:S(2)}, u32[]{:S(2)}) collective-permute-start(bf16[64,2048]{1,0:T(8,128)(2,1)S(1)} %get-tuple-element.24.refs_0_), channel_id=1, source_target_pairs={{0,16},{1,17},{2,18},{3,19},{4,20},{5,21},{6,22},{7,23},{8,24},{9,... | collective-permute-start | bytes 786440 | tf_op jit(solution)/shard_map/ppermute | solution.py:344
  22.7 9.2 %collective-permute-start.2 = (bf16[64,2048]{1,0:T(8,128)(2,1)S(1)}, bf16[64,2048]{1,0:T(8,128)(2,1)S(1)}, u32[]{:S(2)}, u32[]{:S(2)}) collective-permute-start(bf16[64,2048]{1,0:T(8,128)(2,1)S(1)} %get-tuple-element.24.refs_0_), channel_id=1, source_target_pairs={{0,8},{1,9},{2,10},{3,11},{4,12},{5,13},{6,14},{7,15},{8,0},{9,1},... | collective-permute-start | bytes 786440 | tf_op jit(solution)/shard_map/ppermute | solution.py:344
  22.7 11.0 %collective-permute-start.5 = (bf16[64,2048]{1,0:T(8,128)(2,1)S(1)}, bf16[64,2048]{1,0:T(8,128)(2,1)S(1)}, u32[]{:S(2)}, u32[]{:S(2)}) collective-permute-start(bf16[64,2048]{1,0:T(8,128)(2,1)S(1)} %get-tuple-element.25.refs_1_), channel_id=1, source_target_pairs={{0,16},{1,17},{2,18},{3,19},{4,20},{5,21},{6,22},{7,23},{8,24},{9,... | collective-permute-start | bytes 786440 | tf_op jit(solution)/shard_map/ppermute | solution.py:344
  23.8 11.4 %collective-permute-start.3 = (bf16[64,2048]{1,0:T(8,128)(2,1)S(1)}, bf16[64,2048]{1,0:T(8,128)(2,1)S(1)}, u32[]{:S(2)}, u32[]{:S(2)}) collective-permute-start(bf16[64,2048]{1,0:T(8,128)(2,1)S(1)} %get-tuple-element.25.refs_1_), channel_id=1, source_target_pairs={{0,8},{1,9},{2,10},{3,11},{4,12},{5,13},{6,14},{7,15},{8,0},{9,1},... | collective-permute-start | bytes 786440 | tf_op jit(solution)/shard_map/ppermute | solution.py:344
  25.5 5.7 %collective-permute-start.1 = (bf16[2,64,768]{2,1,0:T(8,128)(2,1)S(1)}, bf16[2,64,768]{2,1,0:T(8,128)(2,1)S(1)}, u32[]{:S(2)}, u32[]{:S(2)}) collective-permute-start(bf16[2,64,768]{2,1,0:T(8,128)(2,1)S(1)} %project.7), channel_id=1, source_target_pairs={{0,2},{1,3},{2,0},{3,1},{4,6},{5,7},{6,4},{7,5},{8,10},{9,11},{10,... | collective-permute-start | bytes 589832 | tf_op jit(solution)/shard_map/ppermute | solution.py:344
  35.3 6.4 %collective-permute-start.9 = (bf16[64,2048]{1,0:T(8,128)(2,1)S(1)}, bf16[64,2048]{1,0:T(8,128)(2,1)S(1)}, u32[]{:S(2)}, u32[]{:S(2)}) collective-permute-start(bf16[64,2048]{1,0:T(8,128)(2,1)S(1)} %get-tuple-element.29), channel_id=1, source_target_pairs={{0,16},{1,17},{2,18},{3,19},{4,20},{5,21},{6,22},{7,23},{8,24},{9,... | collective-permute-start | bytes 786440 | tf_op jit(solution)/shard_map/ppermute | solution.py:344
  35.7 6.4 %collective-permute-start.10 = (bf16[64,2048]{1,0:T(8,128)(2,1)S(1)}, bf16[64,2048]{1,0:T(8,128)(2,1)S(1)}, u32[]{:S(2)}, u32[]{:S(2)}) collective-permute-start(bf16[64,2048]{1,0:T(8,128)(2,1)S(1)} %get-tuple-element.30), channel_id=1, source_target_pairs={{0,8},{1,9},{2,10},{3,11},{4,12},{5,13},{6,14},{7,15},{8,0},{9,1},... | collective-permute-start | bytes 786440 | tf_op jit(solution)/shard_map/ppermute | solution.py:344
  37.5 10.4 %collective-permute-start.6 = (bf16[4,64,768]{2,1,0:T(8,128)(2,1)S(1)}, bf16[4,64,768]{2,1,0:T(8,128)(2,1)S(1)}, u32[]{:S(2)}, u32[]{:S(2)}) collective-permute-start(bf16[4,64,768]{2,1,0:T(8,128)(2,1)S(1)} %project.9), channel_id=1, source_target_pairs={{0,2},{1,3},{2,0},{3,1},{4,6},{5,7},{6,4},{7,5},{8,10},{9,11},{10,... | collective-permute-start | bytes 1179656 | tf_op jit(solution)/shard_map/ppermute | solution.py:344
  42.7 8.3 %collective-permute-start.11 = (bf16[2,64,768]{2,1,0:T(8,128)(2,1)S(1)}, bf16[2,64,768]{2,1,0:T(8,128)(2,1)S(1)}, u32[]{:S(2)}, u32[]{:S(2)}) collective-permute-start(bf16[2,64,768]{2,1,0:T(8,128)(2,1)S(1)} %project.11), channel_id=1, source_target_pairs={{0,2},{1,3},{2,0},{3,1},{4,6},{5,7},{6,4},{7,5},{8,10},{9,11},{10,... | collective-permute-start | bytes 589832 | tf_op jit(solution)/shard_map/ppermute | solution.py:344
  48.0 6.1 %collective-permute-start.8 = (bf16[128,768]{1,0:T(8,128)(2,1)S(1)}, bf16[128,768]{1,0:T(8,128)(2,1)S(1)}, u32[]{:S(2)}, u32[]{:S(2)}) collective-permute-start(bf16[128,768]{1,0:T(8,128)(2,1)S(1)} %get-tuple-element.28), channel_id=1, source_target_pairs={{0,16},{1,17},{2,18},{3,19},{4,20},{5,21},{6,22},{7,23},{8,24},{9,... | collective-permute-start | bytes 589832 | tf_op jit(solution)/shard_map/ppermute | solution.py:344
  49.5 5.7 %collective-permute-start.7 = (bf16[128,768]{1,0:T(8,128)(2,1)S(1)}, bf16[128,768]{1,0:T(8,128)(2,1)S(1)}, u32[]{:S(2)}, u32[]{:S(2)}) collective-permute-start(bf16[128,768]{1,0:T(8,128)(2,1)S(1)} %get-tuple-element.27.refs_2_), channel_id=1, source_target_pairs={{0,8},{1,9},{2,10},{3,11},{4,12},{5,13},{6,14},{7,15},{8,0},{9,1},... | collective-permute-start | bytes 589832 | tf_op jit(solution)/shard_map/ppermute | solution.py:344
  51.0 6.6 %collective-permute-start.12 = (bf16[128,768]{1,0:T(8,128)(2,1)S(1)}, bf16[128,768]{1,0:T(8,128)(2,1)S(1)}, u32[]{:S(2)}, u32[]{:S(2)}) collective-permute-start(bf16[128,768]{1,0:T(8,128)(2,1)S(1)} %merge.5), channel_id=1, source_target_pairs={{0,24},{1,25},{2,26},{3,27},{4,28},{5,29},{6,30},{7,31},{8,16},{9,... | collective-permute-start | bytes 589832 | tf_op jit(solution)/shard_map/ppermute | solution.py:344
  57.8 12.5 %collective-permute-start.13 = (bf16[128,768]{1,0:T(8,128)(2,1)S(1)}, bf16[128,768]{1,0:T(8,128)(2,1)S(1)}, u32[]{:S(2)}, u32[]{:S(2)}) collective-permute-start(bf16[128,768]{1,0:T(8,128)(2,1)S(1)} %get-tuple-element.32), channel_id=1, source_target_pairs={{0,4},{1,5},{2,6},{3,7},{4,0},{5,1},{6,2},{7,3},{8,12},{9,13},{10,... | collective-permute-start | bytes 589832 | tf_op jit(solution)/shard_map/ppermute | solution.py:344
  60.4 10.0 %collective-permute-start.15 = (bf16[128,768]{1,0:T(8,128)(2,1)S(1)}, bf16[128,768]{1,0:T(8,128)(2,1)S(1)}, u32[]{:S(2)}, u32[]{:S(2)}) collective-permute-start(bf16[128,768]{1,0:T(8,128)(2,1)S(1)} %get-tuple-element.33), channel_id=1, source_target_pairs={{0,2},{1,3},{2,0},{3,1},{4,6},{5,7},{6,4},{7,5},{8,10},{9,11},{10,... | collective-permute-start | bytes 589832 | tf_op jit(solution)/shard_map/ppermute | solution.py:344
  62.0 8.5 %collective-permute-start.16 = (bf16[128,768]{1,0:T(8,128)(2,1)S(1)}, bf16[128,768]{1,0:T(8,128)(2,1)S(1)}, u32[]{:S(2)}, u32[]{:S(2)}) collective-permute-start(bf16[128,768]{1,0:T(8,128)(2,1)S(1)} %get-tuple-element.34), channel_id=1, source_target_pairs={{0,6},{1,7},{2,4},{3,5},{4,2},{5,3},{6,0},{7,1},{8,14},{9,15},{10,... | collective-permute-start | bytes 589832 | tf_op jit(solution)/shard_map/ppermute | solution.py:344
  70.4 1.5 %collective-permute-start.14 = (bf16[128,768]{1,0:T(8,128)(2,1)S(1)}, bf16[128,768]{1,0:T(8,128)(2,1)S(1)}, u32[]{:S(2)}, u32[]{:S(2)}) collective-permute-start(bf16[128,768]{1,0:T(8,128)(2,1)S(1)} %sum.2), channel_id=1, source_target_pairs={{0,1},{1,0},{2,3},{3,2},{4,5},{5,4},{6,7},{7,6},{8,9},{9,8},{10,11... | collective-permute-start | bytes 589832 | tf_op jit(solution)/shard_map/ppermute | solution.py:344
  70.5 1.6 %collective-permute-start.17 = (bf16[128,768]{1,0:T(8,128)(2,1)S(1)}, bf16[128,768]{1,0:T(8,128)(2,1)S(1)}, u32[]{:S(2)}, u32[]{:S(2)}) collective-permute-start(bf16[128,768]{1,0:T(8,128)(2,1)S(1)} %sum.3), channel_id=1, source_target_pairs={{0,1},{1,0},{2,3},{3,2},{4,5},{5,4},{6,7},{7,6},{8,9},{9,8},{10,11... | collective-permute-start | bytes 589832 | tf_op jit(solution)/shard_map/ppermute | solution.py:344

commit v13 on v12

--- a/solution.py
+++ b/solution.py
@@ -375,15 +375,16 @@
     own_send = project((upper, lower), 1)
     own = merge(whole, (project((upper, lower), 0), partner(own_send)))
     lower_1, upper_2 = swapped(lower, 1), swapped(upper, 2)
-    held = hold((upper_1, lower_2), (lower_1, upper_2, *own))
-    beside = (upper_1, lower_1, upper_2, lower_2)
-    beside_send, beside_keep = project(beside, 1, own), project(beside, 0)
+    near, later = (upper_1, upper_2), (lower_1, lower_2)
+    near_send, near_keep = project(near, 1, own), project(near, 0)
+    held = hold((upper_1, lower_2), (lower_1, upper_2, *own, near_send, near_keep))
+    later_send, later_keep = project(later, 1), project(later, 0)
     beside = merge(
-        (((0, 0), (0, 1)), ((0, 2), (0, 3))),
-        (beside_keep, partner(beside_send)),
+        (((0, 0), (1, 0)), ((0, 1), (1, 1))),
+        (near_keep, partner(near_send), later_keep, partner(later_send)),
     )
     across = (swapped(held[0], 2), swapped(held[1], 1))
-    across_sum = (project(across, 0), partner(project(across, 1, (beside_keep,))))
+    across_sum = (project(across, 0), partner(project(across, 1, (later_keep,))))
     across = merge(whole, across_sum, beside[:1])
     blocks = [swapped(block, k) if k else block for k, block in enumerate((*own, *beside, *across))]
     picked = call(pick_kernel, (single,) * n_head, "pick")(*blocks)

time: 74.1 us -> 74.3 us (level)
    pallas_call x6 -> x8, Pallas kernels: 4.4 us -> 4.8 us  [project(): call(kernel, shape, 'project', in_specs=specs)(*picked, weight, *after)]
    ppermute x17 -> x18, starting transfers between devices: 21.2 us -> 21 us  [moved(): lax.ppermute(array, names, [(place[spot], place[target(*spot)]) for spot...]
    ppermute x17 -> x18, waiting for transfers between devices: 26.8 us -> 26.6 us  [moved(): lax.ppermute(array, names, [(place[spot], place[target(*spot)]) for spot...]
  transfers between devices with their start and end apart: 18 -> 19, of which waited for: 14 -> 14; matrix products, arithmetic and copies ran while one was open for 0% -> 0% of each run, Pallas kernels for 12% -> 13%
where the time goes in v13:
time: 74.3 us; the launch traced here: 73.1 us
  waiting for transfers between devices  33.6 us (45%)
  starting transfers between devices  25.9 us (35%)
  Pallas kernels  13.4 us (18%)
    ppermute x18, waiting for transfers between devices, moved(): lax.ppermute(array, names, [(place[spot], place[target(*spot)]) for spot...  26.6 us
    ppermute x18, starting transfers between devices, moved(): lax.ppermute(array, names, [(place[spot], place[target(*spot)]) for spot...  21 us
    ppermute x1, waiting for transfers between devices, from_before(): return lax.ppermute(array, 'ctx', [(i, i + by) for i in range(n_ctx - by)])  6.98 us
    ppermute x1, starting transfers between devices, from_before(): return lax.ppermute(array, 'ctx', [(i, i + by) for i in range(n_ctx - by)])  4.87 us
    pallas_call x8, Pallas kernels, project(): call(kernel, shape, 'project', in_specs=specs)(*picked, weight, *after)  4.8 us
    pallas_call x1, Pallas kernels, on_device(): call(inside_kernel, (pltpu.VMEM((rows, width), jnp.float32), pltpu.VMEM((...  4.24 us
    pallas_call x1, Pallas kernels, on_device(): call(state_kernel, state_shape, 'shard_state', in_specs=[HBM] * 4, scratc...  2.58 us
  transfers between devices with their start and end apart: 19, of which 14 were waited for; matrix products, arithmetic and copies ran while one was open for 0% of the time, Pallas kernels for 13%

profile of v13, /device:TPU:0, one launch (start us, length us, event | category | flops | bytes accessed | tf_op | source)
XLA Modules:
  0.0 73.1 jit_solution(10679232699830607521)
XLA Ops:
  0.0 2.6 %shard_state.1 = bf16[2064,128]{1,0:T(8,128)(2,1)S(1)} custom-call(bf16[1,128,2048]{2,1,0:T(8,128)(2,1)} %refs_0_.1, bf16[1,128,2048]{2,1,0:T(8,128)(2,1)} %refs_1_.1, f32[1,16,128]{2,1,0:T(8,128)} %bitcast.1, s32[1,128]{1,0:T(1,128)} %refs_3_.1), custom_call_target="tpu_custom_call" | custom-call | flops 1 | bytes 1 | tf_op jit(solution)/shard_map/shard_state/pallas_call | solution.py:268
  2.6 4.9 %collective-permute-start = (bf16[2064,128]{1,0:T(8,128)(2,1)S(1)}, bf16[2064,128]{1,0:T(8,128)(2,1)S(1)}, u32[]{:S(2)}, u32[]{:S(2)}) collective-permute-start(bf16[2064,128]{1,0:T(8,128)(2,1)S(1)} %shard_state.1), channel_id=1, source_target_pairs={{0,8},{8,16},{16,24},{1,9},{9,17},{17,25},{2,10},{10,18},{18,26},{... | collective-permute-start | bytes 1585160 | tf_op jit(solution)/shard_map/ppermute | solution.py:264
  7.5 4.2 %inside.1 = (f32[128,2048]{1,0:T(8,128)S(1)}, f32[128,2048]{1,0:T(8,128)S(1)}, f32[128,128]{1,0:T(8,128)S(1)}, bf16[128,2048]{1,0:T(8,128)(2,1)S(1)}, bf16[2048,1536]{1,0:T(8,128)(2,1)S(1)}) custom-call(bf16[1,128,2048]{2,1,0:T(8,128)(2,1)} %query_hbm.1, bf16[1,128,2048]{2,1,0:T(8,128)(2,1)} %refs_0_.1, bf16[1,128,2048]{2,1,0:T(8,128)(2,1)} %refs_1_.1, ...), custom_call_target="tpu_custom_call" | custom-call | flops 1 | bytes 1 | tf_op jit(solution)/shard_map/inside/pallas_call | solution.py:300
  11.7 7.0 %collective-permute-done.state_ref = bf16[2064,128]{1,0:T(8,128)(2,1)S(1)} collective-permute-done((bf16[2064,128]{1,0:T(8,128)(2,1)S(1)}, bf16[2064,128]{1,0:T(8,128)(2,1)S(1)}, u32[]{:S(2)}, u32[]{:S(2)}) %collective-permute-start) | collective-permute-done | bytes 528416 | tf_op jit(solution)/shard_map/ppermute | solution.py:264
  19.3 3.5 %collective-permute-start.3 = (bf16[64,2048]{1,0:T(8,128)(2,1)S(1)}, bf16[64,2048]{1,0:T(8,128)(2,1)S(1)}, u32[]{:S(2)}, u32[]{:S(2)}) collective-permute-start(bf16[64,2048]{1,0:T(8,128)(2,1)S(1)} %get-tuple-element.24.refs_0_), channel_id=1, source_target_pairs={{0,16},{1,17},{2,18},{3,19},{4,20},{5,21},{6,22},{7,23},{8,24},{9,... | collective-permute-start | bytes 786440 | tf_op jit(solution)/shard_map/ppermute | solution.py:344
  22.7 1.1 %collective-permute-start.6 = (bf16[64,2048]{1,0:T(8,128)(2,1)S(1)}, bf16[64,2048]{1,0:T(8,128)(2,1)S(1)}, u32[]{:S(2)}, u32[]{:S(2)}) collective-permute-start(bf16[64,2048]{1,0:T(8,128)(2,1)S(1)} %get-tuple-element.25.refs_1_), channel_id=1, source_target_pairs={{0,16},{1,17},{2,18},{3,19},{4,20},{5,21},{6,22},{7,23},{8,24},{9,... | collective-permute-start | bytes 786440 | tf_op jit(solution)/shard_map/ppermute | solution.py:344
  23.8 1.0 %collective-permute-start.5 = (bf16[64,2048]{1,0:T(8,128)(2,1)S(1)}, bf16[64,2048]{1,0:T(8,128)(2,1)S(1)}, u32[]{:S(2)}, u32[]{:S(2)}) collective-permute-start(bf16[64,2048]{1,0:T(8,128)(2,1)S(1)} %get-tuple-element.25.refs_1_), channel_id=1, source_target_pairs={{0,8},{1,9},{2,10},{3,11},{4,12},{5,13},{6,14},{7,15},{8,0},{9,1},... | collective-permute-start | bytes 786440 | tf_op jit(solution)/shard_map/ppermute | solution.py:344
  25.5 1.6 %collective-permute-start.1 = (bf16[2,64,768]{2,1,0:T(8,128)(2,1)S(1)}, bf16[2,64,768]{2,1,0:T(8,128)(2,1)S(1)}, u32[]{:S(2)}, u32[]{:S(2)}) collective-permute-start(bf16[2,64,768]{2,1,0:T(8,128)(2,1)S(1)} %project.9), channel_id=1, source_target_pairs={{0,2},{1,3},{2,0},{3,1},{4,6},{5,7},{6,4},{7,5},{8,10},{9,11},{10,... | collective-permute-start | bytes 589832 | tf_op jit(solution)/shard_map/ppermute | solution.py:344
  27.7 3.5 %collective-permute-done.1.refs_1_ = bf16[2,64,768]{2,1,0:T(8,128)(2,1)S(1)} collective-permute-done((bf16[2,64,768]{2,1,0:T(8,128)(2,1)S(1)}, bf16[2,64,768]{2,1,0:T(8,128)(2,1)S(1)}, u32[]{:S(2)}, u32[]{:S(2)}) %collective-permute-start.1) | collective-permute-done | bytes 196640 | tf_op jit(solution)/shard_map/ppermute | solution.py:344
  33.8 1.5 %collective-permute-done.5.refs_0_ = bf16[64,2048]{1,0:T(8,128)(2,1)S(1)} collective-permute-done((bf16[64,2048]{1,0:T(8,128)(2,1)S(1)}, bf16[64,2048]{1,0:T(8,128)(2,1)S(1)}, u32[]{:S(2)}, u32[]{:S(2)}) %collective-permute-start.5) | collective-permute-done | bytes 262176 | tf_op jit(solution)/shard_map/ppermute | solution.py:344
  36.5 1.6 %collective-permute-start.4 = (bf16[2,64,768]{2,1,0:T(8,128)(2,1)S(1)}, bf16[2,64,768]{2,1,0:T(8,128)(2,1)S(1)}, u32[]{:S(2)}, u32[]{:S(2)}) collective-permute-start(bf16[2,64,768]{2,1,0:T(8,128)(2,1)S(1)} %project.11.refs_3_), channel_id=1, source_target_pairs={{0,2},{1,3},{2,0},{3,1},{4,6},{5,7},{6,4},{7,5},{8,10},{9,11},{10,... | collective-permute-start | bytes 589832 | tf_op jit(solution)/shard_map/ppermute | solution.py:344
  39.8 2.0 %collective-permute-done.10.refs_0_ = bf16[64,2048]{1,0:T(8,128)(2,1)S(1)} collective-permute-done((bf16[64,2048]{1,0:T(8,128)(2,1)S(1)}, bf16[64,2048]{1,0:T(8,128)(2,1)S(1)}, u32[]{:S(2)}, u32[]{:S(2)}) %collective-permute-start.10) | collective-permute-done | bytes 262176 | tf_op jit(solution)/shard_map/ppermute | solution.py:344
  42.7 1.6 %collective-permute-start.12 = (bf16[2,64,768]{2,1,0:T(8,128)(2,1)S(1)}, bf16[2,64,768]{2,1,0:T(8,128)(2,1)S(1)}, u32[]{:S(2)}, u32[]{:S(2)}) collective-permute-start(bf16[2,64,768]{2,1,0:T(8,128)(2,1)S(1)} %project.15), channel_id=1, source_target_pairs={{0,2},{1,3},{2,0},{3,1},{4,6},{5,7},{6,4},{7,5},{8,10},{9,11},{10,... | collective-permute-start | bytes 589832 | tf_op jit(solution)/shard_map/ppermute | solution.py:344
  44.3 2.4 %collective-permute-done.7.refs_3_ = bf16[2,64,768]{2,1,0:T(8,128)(2,1)S(1)} collective-permute-done((bf16[2,64,768]{2,1,0:T(8,128)(2,1)S(1)}, bf16[2,64,768]{2,1,0:T(8,128)(2,1)S(1)}, u32[]{:S(2)}, u32[]{:S(2)}) %collective-permute-start.7) | collective-permute-done | bytes 196640 | tf_op jit(solution)/shard_map/ppermute | solution.py:344
  46.9 1.6 %collective-permute-start.9 = (bf16[128,768]{1,0:T(8,128)(2,1)S(1)}, bf16[128,768]{1,0:T(8,128)(2,1)S(1)}, u32[]{:S(2)}, u32[]{:S(2)}) collective-permute-start(bf16[128,768]{1,0:T(8,128)(2,1)S(1)} %get-tuple-element.28), channel_id=1, source_target_pairs={{0,16},{1,17},{2,18},{3,19},{4,20},{5,21},{6,22},{7,23},{8,24},{9,... | collective-permute-start | bytes 589832 | tf_op jit(solution)/shard_map/ppermute | solution.py:344
  48.4 1.5 %collective-permute-start.8 = (bf16[128,768]{1,0:T(8,128)(2,1)S(1)}, bf16[128,768]{1,0:T(8,128)(2,1)S(1)}, u32[]{:S(2)}, u32[]{:S(2)}) collective-permute-start(bf16[128,768]{1,0:T(8,128)(2,1)S(1)} %get-tuple-element.27.refs_2_), channel_id=1, source_target_pairs={{0,8},{1,9},{2,10},{3,11},{4,12},{5,13},{6,14},{7,15},{8,0},{9,1},... | collective-permute-start | bytes 589832 | tf_op jit(solution)/shard_map/ppermute | solution.py:344
  50.6 0.8 %collective-permute-start.13 = (bf16[128,768]{1,0:T(8,128)(2,1)S(1)}, bf16[128,768]{1,0:T(8,128)(2,1)S(1)}, u32[]{:S(2)}, u32[]{:S(2)}) collective-permute-start(bf16[128,768]{1,0:T(8,128)(2,1)S(1)} %merge.5), channel_id=1, source_target_pairs={{0,24},{1,25},{2,26},{3,27},{4,28},{5,29},{6,30},{7,31},{8,16},{9,... | collective-permute-start | bytes 589832 | tf_op jit(solution)/shard_map/ppermute | solution.py:344
  51.4 2.8 %collective-permute-done.9.refs_2_ = bf16[128,768]{1,0:T(8,128)(2,1)S(1)} collective-permute-done((bf16[128,768]{1,0:T(8,128)(2,1)S(1)}, bf16[128,768]{1,0:T(8,128)(2,1)S(1)}, u32[]{:S(2)}, u32[]{:S(2)}) %collective-permute-start.9) | collective-permute-done | bytes 196640 | tf_op jit(solution)/shard_map/ppermute | solution.py:344
  54.4 2.8 %collective-permute-done.13.refs_3_ = bf16[128,768]{1,0:T(8,128)(2,1)S(1)} collective-permute-done((bf16[128,768]{1,0:T(8,128)(2,1)S(1)}, bf16[128,768]{1,0:T(8,128)(2,1)S(1)}, u32[]{:S(2)}, u32[]{:S(2)}) %collective-permute-start.13) | collective-permute-done | bytes 196640 | tf_op jit(solution)/shard_map/ppermute | solution.py:344
  57.3 2.7 %collective-permute-start.14 = (bf16[128,768]{1,0:T(8,128)(2,1)S(1)}, bf16[128,768]{1,0:T(8,128)(2,1)S(1)}, u32[]{:S(2)}, u32[]{:S(2)}) collective-permute-start(bf16[128,768]{1,0:T(8,128)(2,1)S(1)} %get-tuple-element.32), channel_id=1, source_target_pairs={{0,4},{1,5},{2,6},{3,7},{4,0},{5,1},{6,2},{7,3},{8,12},{9,13},{10,... | collective-permute-start | bytes 589832 | tf_op jit(solution)/shard_map/ppermute | solution.py:344
  60.0 1.6 %collective-permute-start.16 = (bf16[128,768]{1,0:T(8,128)(2,1)S(1)}, bf16[128,768]{1,0:T(8,128)(2,1)S(1)}, u32[]{:S(2)}, u32[]{:S(2)}) collective-permute-start(bf16[128,768]{1,0:T(8,128)(2,1)S(1)} %get-tuple-element.33), channel_id=1, source_target_pairs={{0,2},{1,3},{2,0},{3,1},{4,6},{5,7},{6,4},{7,5},{8,10},{9,11},{10,... | collective-permute-start | bytes 589832 | tf_op jit(solution)/shard_map/ppermute | solution.py:344
  61.8 8.7 %collective-permute-done.14.two_ref = bf16[128,768]{1,0:T(8,128)(2,1)S(1)} collective-permute-done((bf16[128,768]{1,0:T(8,128)(2,1)S(1)}, bf16[128,768]{1,0:T(8,128)(2,1)S(1)}, u32[]{:S(2)}, u32[]{:S(2)}) %collective-permute-start.14) | collective-permute-done | bytes 196640 | tf_op jit(solution)/shard_map/ppermute | solution.py:344
  71.2 0.8 %collective-permute-done.15.refs_0_ = bf16[128,768]{1,0:T(8,128)(2,1)S(1)} collective-permute-done((bf16[128,768]{1,0:T(8,128)(2,1)S(1)}, bf16[128,768]{1,0:T(8,128)(2,1)S(1)}, u32[]{:S(2)}, u32[]{:S(2)}) %collective-permute-start.15) | collective-permute-done | bytes 196640 | tf_op jit(solution)/shard_map/ppermute | solution.py:344
  72.3 0.8 %last.1 = bf16[1,128,1536]{2,1,0:T(8,128)(2,1)} custom-call(bf16[128,768]{1,0:T(8,128)(2,1)S(1)} %collective-permute-done.15.refs_0_, bf16[128,768]{1,0:T(8,128)(2,1)S(1)} %collective-permute-done.18.refs_1_), custom_call_target="tpu_custom_call" | custom-call | flops 1 | bytes 1 | tf_op jit(solution)/shard_map/last/pallas_call | solution.py:396
  (33 shorter events, 10.5 us)
Async XLA Ops:
  2.6 16.1 %collective-permute-start = (bf16[2064,128]{1,0:T(8,128)(2,1)S(1)}, bf16[2064,128]{1,0:T(8,128)(2,1)S(1)}, u32[]{:S(2)}, u32[]{:S(2)}) collective-permute-start(bf16[2064,128]{1,0:T(8,128)(2,1)S(1)} %shard_state.1), channel_id=1, source_target_pairs={{0,8},{8,16},{16,24},{1,9},{9,17},{17,25},{2,10},{10,18},{18,26},{... | collective-permute-start | bytes 1585160 | tf_op jit(solution)/shard_map/ppermute | solution.py:264
  19.3 12.0 %collective-permute-start.3 = (bf16[64,2048]{1,0:T(8,128)(2,1)S(1)}, bf16[64,2048]{1,0:T(8,128)(2,1)S(1)}, u32[]{:S(2)}, u32[]{:S(2)}) collective-permute-start(bf16[64,2048]{1,0:T(8,128)(2,1)S(1)} %get-tuple-element.24.refs_0_), channel_id=1, source_target_pairs={{0,16},{1,17},{2,18},{3,19},{4,20},{5,21},{6,22},{7,23},{8,24},{9,... | collective-permute-start | bytes 786440 | tf_op jit(solution)/shard_map/ppermute | solution.py:344
  22.7 9.2 %collective-permute-start.2 = (bf16[64,2048]{1,0:T(8,128)(2,1)S(1)}, bf16[64,2048]{1,0:T(8,128)(2,1)S(1)}, u32[]{:S(2)}, u32[]{:S(2)}) collective-permute-start(bf16[64,2048]{1,0:T(8,128)(2,1)S(1)} %get-tuple-element.24.refs_0_), channel_id=1, source_target_pairs={{0,8},{1,9},{2,10},{3,11},{4,12},{5,13},{6,14},{7,15},{8,0},{9,1},... | collective-permute-start | bytes 786440 | tf_op jit(solution)/shard_map/ppermute | solution.py:344
  22.7 11.0 %collective-permute-start.6 = (bf16[64,2048]{1,0:T(8,128)(2,1)S(1)}, bf16[64,2048]{1,0:T(8,128)(2,1)S(1)}, u32[]{:S(2)}, u32[]{:S(2)}) collective-permute-start(bf16[64,2048]{1,0:T(8,128)(2,1)S(1)} %get-tuple-element.25.refs_1_), channel_id=1, source_target_pairs={{0,16},{1,17},{2,18},{3,19},{4,20},{5,21},{6,22},{7,23},{8,24},{9,... | collective-permute-start | bytes 786440 | tf_op jit(solution)/shard_map/ppermute | solution.py:344
  23.8 11.4 %collective-permute-start.5 = (bf16[64,2048]{1,0:T(8,128)(2,1)S(1)}, bf16[64,2048]{1,0:T(8,128)(2,1)S(1)}, u32[]{:S(2)}, u32[]{:S(2)}) collective-permute-start(bf16[64,2048]{1,0:T(8,128)(2,1)S(1)} %get-tuple-element.25.refs_1_), channel_id=1, source_target_pairs={{0,8},{1,9},{2,10},{3,11},{4,12},{5,13},{6,14},{7,15},{8,0},{9,1},... | collective-permute-start | bytes 786440 | tf_op jit(solution)/shard_map/ppermute | solution.py:344
  25.5 5.7 %collective-permute-start.1 = (bf16[2,64,768]{2,1,0:T(8,128)(2,1)S(1)}, bf16[2,64,768]{2,1,0:T(8,128)(2,1)S(1)}, u32[]{:S(2)}, u32[]{:S(2)}) collective-permute-start(bf16[2,64,768]{2,1,0:T(8,128)(2,1)S(1)} %project.9), channel_id=1, source_target_pairs={{0,2},{1,3},{2,0},{3,1},{4,6},{5,7},{6,4},{7,5},{8,10},{9,11},{10,... | collective-permute-start | bytes 589832 | tf_op jit(solution)/shard_map/ppermute | solution.py:344
  35.3 6.4 %collective-permute-start.10 = (bf16[64,2048]{1,0:T(8,128)(2,1)S(1)}, bf16[64,2048]{1,0:T(8,128)(2,1)S(1)}, u32[]{:S(2)}, u32[]{:S(2)}) collective-permute-start(bf16[64,2048]{1,0:T(8,128)(2,1)S(1)} %get-tuple-element.29), channel_id=1, source_target_pairs={{0,16},{1,17},{2,18},{3,19},{4,20},{5,21},{6,22},{7,23},{8,24},{9,... | collective-permute-start | bytes 786440 | tf_op jit(solution)/shard_map/ppermute | solution.py:344
  35.7 6.4 %collective-permute-start.11 = (bf16[64,2048]{1,0:T(8,128)(2,1)S(1)}, bf16[64,2048]{1,0:T(8,128)(2,1)S(1)}, u32[]{:S(2)}, u32[]{:S(2)}) collective-permute-start(bf16[64,2048]{1,0:T(8,128)(2,1)S(1)} %get-tuple-element.30), channel_id=1, source_target_pairs={{0,8},{1,9},{2,10},{3,11},{4,12},{5,13},{6,14},{7,15},{8,0},{9,1},... | collective-permute-start | bytes 786440 | tf_op jit(solution)/shard_map/ppermute | solution.py:344
  36.5 7.9 %collective-permute-start.4 = (bf16[2,64,768]{2,1,0:T(8,128)(2,1)S(1)}, bf16[2,64,768]{2,1,0:T(8,128)(2,1)S(1)}, u32[]{:S(2)}, u32[]{:S(2)}) collective-permute-start(bf16[2,64,768]{2,1,0:T(8,128)(2,1)S(1)} %project.11.refs_3_), channel_id=1, source_target_pairs={{0,2},{1,3},{2,0},{3,1},{4,6},{5,7},{6,4},{7,5},{8,10},{9,11},{10,... | collective-permute-start | bytes 589832 | tf_op jit(solution)/shard_map/ppermute | solution.py:344
  38.6 8.1 %collective-permute-start.7 = (bf16[2,64,768]{2,1,0:T(8,128)(2,1)S(1)}, bf16[2,64,768]{2,1,0:T(8,128)(2,1)S(1)}, u32[]{:S(2)}, u32[]{:S(2)}) collective-permute-start(bf16[2,64,768]{2,1,0:T(8,128)(2,1)S(1)} %project.13), channel_id=1, source_target_pairs={{0,2},{1,3},{2,0},{3,1},{4,6},{5,7},{6,4},{7,5},{8,10},{9,11},{10,... | collective-permute-start | bytes 589832 | tf_op jit(solution)/shard_map/ppermute | solution.py:344
  42.7 7.8 %collective-permute-start.12 = (bf16[2,64,768]{2,1,0:T(8,128)(2,1)S(1)}, bf16[2,64,768]{2,1,0:T(8,128)(2,1)S(1)}, u32[]{:S(2)}, u32[]{:S(2)}) collective-permute-start(bf16[2,64,768]{2,1,0:T(8,128)(2,1)S(1)} %project.15), channel_id=1, source_target_pairs={{0,2},{1,3},{2,0},{3,1},{4,6},{5,7},{6,4},{7,5},{8,10},{9,11},{10,... | collective-permute-start | bytes 589832 | tf_op jit(solution)/shard_map/ppermute | solution.py:344
  46.9 7.3 %collective-permute-start.9 = (bf16[128,768]{1,0:T(8,128)(2,1)S(1)}, bf16[128,768]{1,0:T(8,128)(2,1)S(1)}, u32[]{:S(2)}, u32[]{:S(2)}) collective-permute-start(bf16[128,768]{1,0:T(8,128)(2,1)S(1)} %get-tuple-element.28), channel_id=1, source_target_pairs={{0,16},{1,17},{2,18},{3,19},{4,20},{5,21},{6,22},{7,23},{8,24},{9,... | collective-permute-start | bytes 589832 | tf_op jit(solution)/shard_map/ppermute | solution.py:344
  48.4 6.0 %collective-permute-start.8 = (bf16[128,768]{1,0:T(8,128)(2,1)S(1)}, bf16[128,768]{1,0:T(8,128)(2,1)S(1)}, u32[]{:S(2)}, u32[]{:S(2)}) collective-permute-start(bf16[128,768]{1,0:T(8,128)(2,1)S(1)} %get-tuple-element.27.refs_2_), channel_id=1, source_target_pairs={{0,8},{1,9},{2,10},{3,11},{4,12},{5,13},{6,14},{7,15},{8,0},{9,1},... | collective-permute-start | bytes 589832 | tf_op jit(solution)/shard_map/ppermute | solution.py:344
  50.6 6.6 %collective-permute-start.13 = (bf16[128,768]{1,0:T(8,128)(2,1)S(1)}, bf16[128,768]{1,0:T(8,128)(2,1)S(1)}, u32[]{:S(2)}, u32[]{:S(2)}) collective-permute-start(bf16[128,768]{1,0:T(8,128)(2,1)S(1)} %merge.5), channel_id=1, source_target_pairs={{0,24},{1,25},{2,26},{3,27},{4,28},{5,29},{6,30},{7,31},{8,16},{9,... | collective-permute-start | bytes 589832 | tf_op jit(solution)/shard_map/ppermute | solution.py:344
  57.3 13.2 %collective-permute-start.14 = (bf16[128,768]{1,0:T(8,128)(2,1)S(1)}, bf16[128,768]{1,0:T(8,128)(2,1)S(1)}, u32[]{:S(2)}, u32[]{:S(2)}) collective-permute-start(bf16[128,768]{1,0:T(8,128)(2,1)S(1)} %get-tuple-element.32), channel_id=1, source_target_pairs={{0,4},{1,5},{2,6},{3,7},{4,0},{5,1},{6,2},{7,3},{8,12},{9,13},{10,... | collective-permute-start | bytes 589832 | tf_op jit(solution)/shard_map/ppermute | solution.py:344
  60.0 10.6 %collective-permute-start.16 = (bf16[128,768]{1,0:T(8,128)(2,1)S(1)}, bf16[128,768]{1,0:T(8,128)(2,1)S(1)}, u32[]{:S(2)}, u32[]{:S(2)}) collective-permute-start(bf16[128,768]{1,0:T(8,128)(2,1)S(1)} %get-tuple-element.33), channel_id=1, source_target_pairs={{0,2},{1,3},{2,0},{3,1},{4,6},{5,7},{6,4},{7,5},{8,10},{9,11},{10,... | collective-permute-start | bytes 589832 | tf_op jit(solution)/shard_map/ppermute | solution.py:344
  61.6 9.1 %collective-permute-start.17 = (bf16[128,768]{1,0:T(8,128)(2,1)S(1)}, bf16[128,768]{1,0:T(8,128)(2,1)S(1)}, u32[]{:S(2)}, u32[]{:S(2)}) collective-permute-start(bf16[128,768]{1,0:T(8,128)(2,1)S(1)} %get-tuple-element.34), channel_id=1, source_target_pairs={{0,6},{1,7},{2,4},{3,5},{4,2},{5,3},{6,0},{7,1},{8,14},{9,15},{10,... | collective-permute-start | bytes 589832 | tf_op jit(solution)/shard_map/ppermute | solution.py:344
  70.5 1.5 %collective-permute-start.15 = (bf16[128,768]{1,0:T(8,128)(2,1)S(1)}, bf16[128,768]{1,0:T(8,128)(2,1)S(1)}, u32[]{:S(2)}, u32[]{:S(2)}) collective-permute-start(bf16[128,768]{1,0:T(8,128)(2,1)S(1)} %sum.2), channel_id=1, source_target_pairs={{0,1},{1,0},{2,3},{3,2},{4,5},{5,4},{6,7},{7,6},{8,9},{9,8},{10,11... | collective-permute-start | bytes 589832 | tf_op jit(solution)/shard_map/ppermute | solution.py:344
  70.7 1.6 %collective-permute-start.18 = (bf16[128,768]{1,0:T(8,128)(2,1)S(1)}, bf16[128,768]{1,0:T(8,128)(2,1)S(1)}, u32[]{:S(2)}, u32[]{:S(2)}) collective-permute-start(bf16[128,768]{1,0:T(8,128)(2,1)S(1)} %sum.3), channel_id=1, source_target_pairs={{0,1},{1,0},{2,3},{3,2},{4,5},{5,4},{6,7},{7,6},{8,9},{9,8},{10,11... | collective-permute-start | bytes 589832 | tf_op jit(solution)/shard_map/ppermute | solution.py:344

commit v14 on v13

--- a/solution.py
+++ b/solution.py
@@ -390,7 +390,7 @@
     picked = call(pick_kernel, (single,) * n_head, "pick")(*blocks)
     arrived = [moved(picked[m], lambda i, j, s, m=m: (i, j ^ m, s)) for m in (1, 2, 3)]
     total = [call(sum_kernel, single, "sum")(picked[0], arrived[1])]
-    total.append(call(sum_kernel, single, "sum")(arrived[0], arrived[2]))
+    total.append(call(sum_kernel, single, "sum")(arrived[2], arrived[0]))
     total = [moved(half, lambda i, j, s: (i, j, 1 - s)) for half in total]
     out = jax.ShapeDtypeStruct((1, rows, columns), jnp.bfloat16)
     return call(last_kernel, out, "last")(*total)

time: 74.3 us -> 74.3 us (level)
  transfers between devices with their start and end apart: 19 -> 19, of which waited for: 14 -> 15; matrix products, arithmetic and copies ran while one was open for 0% -> 0% of each run, Pallas kernels for 13% -> 13%
where the time goes in v14:
time: 74.3 us; the launch traced here: 73 us
  waiting for transfers between devices  33.8 us (45%)
  starting transfers between devices  25.6 us (34%)
  Pallas kernels  13.4 us (18%)
    ppermute x18, waiting for transfers between devices, moved(): lax.ppermute(array, names, [(place[spot], place[target(*spot)]) for spot...  26.8 us
    ppermute x18, starting transfers between devices, moved(): lax.ppermute(array, names, [(place[spot], place[target(*spot)]) for spot...  20.8 us
    ppermute x1, waiting for transfers between devices, from_before(): return lax.ppermute(array, 'ctx', [(i, i + by) for i in range(n_ctx - by)])  6.98 us
    ppermute x1, starting transfers between devices, from_before(): return lax.ppermute(array, 'ctx', [(i, i + by) for i in range(n_ctx - by)])  4.87 us
    pallas_call x8, Pallas kernels, project(): call(kernel, shape, 'project', in_specs=specs)(*picked, weight, *after)  4.8 us
    pallas_call x1, Pallas kernels, on_device(): call(inside_kernel, (pltpu.VMEM((rows, width), jnp.float32), pltpu.VMEM((...  4.24 us
    pallas_call x1, Pallas kernels, on_device(): call(state_kernel, state_shape, 'shard_state', in_specs=[HBM] * 4, scratc...  2.58 us
  transfers between devices with their start and end apart: 19, of which 15 were waited for; matrix products, arithmetic and copies ran while one was open for 0% of the time, Pallas kernels for 13%

profile of v14, /device:TPU:0, one launch (start us, length us, event | category | flops | bytes accessed | tf_op | source)
XLA Modules:
  0.0 73.0 jit_solution(5537616734445633430)
XLA Ops:
  0.0 2.6 %shard_state.1 = bf16[2064,128]{1,0:T(8,128)(2,1)S(1)} custom-call(bf16[1,128,2048]{2,1,0:T(8,128)(2,1)} %refs_0_.1, bf16[1,128,2048]{2,1,0:T(8,128)(2,1)} %refs_1_.1, f32[1,16,128]{2,1,0:T(8,128)} %bitcast.1, s32[1,128]{1,0:T(1,128)} %refs_3_.1), custom_call_target="tpu_custom_call" | custom-call | flops 1 | bytes 1 | tf_op jit(solution)/shard_map/shard_state/pallas_call | solution.py:268
  2.6 4.9 %collective-permute-start = (bf16[2064,128]{1,0:T(8,128)(2,1)S(1)}, bf16[2064,128]{1,0:T(8,128)(2,1)S(1)}, u32[]{:S(2)}, u32[]{:S(2)}) collective-permute-start(bf16[2064,128]{1,0:T(8,128)(2,1)S(1)} %shard_state.1), channel_id=1, source_target_pairs={{0,8},{8,16},{16,24},{1,9},{9,17},{17,25},{2,10},{10,18},{18,26},{... | collective-permute-start | bytes 1585160 | tf_op jit(solution)/shard_map/ppermute | solution.py:264
  7.5 4.2 %inside.1 = (f32[128,2048]{1,0:T(8,128)S(1)}, f32[128,2048]{1,0:T(8,128)S(1)}, f32[128,128]{1,0:T(8,128)S(1)}, bf16[128,2048]{1,0:T(8,128)(2,1)S(1)}, bf16[2048,1536]{1,0:T(8,128)(2,1)S(1)}) custom-call(bf16[1,128,2048]{2,1,0:T(8,128)(2,1)} %query_hbm.1, bf16[1,128,2048]{2,1,0:T(8,128)(2,1)} %refs_0_.1, bf16[1,128,2048]{2,1,0:T(8,128)(2,1)} %refs_1_.1, ...), custom_call_target="tpu_custom_call" | custom-call | flops 1 | bytes 1 | tf_op jit(solution)/shard_map/inside/pallas_call | solution.py:300
  11.7 7.0 %collective-permute-done.state_ref = bf16[2064,128]{1,0:T(8,128)(2,1)S(1)} collective-permute-done((bf16[2064,128]{1,0:T(8,128)(2,1)S(1)}, bf16[2064,128]{1,0:T(8,128)(2,1)S(1)}, u32[]{:S(2)}, u32[]{:S(2)}) %collective-permute-start) | collective-permute-done | bytes 528416 | tf_op jit(solution)/shard_map/ppermute | solution.py:264
  19.3 3.5 %collective-permute-start.3 = (bf16[64,2048]{1,0:T(8,128)(2,1)S(1)}, bf16[64,2048]{1,0:T(8,128)(2,1)S(1)}, u32[]{:S(2)}, u32[]{:S(2)}) collective-permute-start(bf16[64,2048]{1,0:T(8,128)(2,1)S(1)} %get-tuple-element.24.refs_0_), channel_id=1, source_target_pairs={{0,16},{1,17},{2,18},{3,19},{4,20},{5,21},{6,22},{7,23},{8,24},{9,... | collective-permute-start | bytes 786440 | tf_op jit(solution)/shard_map/ppermute | solution.py:344
  22.7 1.1 %collective-permute-start.6 = (bf16[64,2048]{1,0:T(8,128)(2,1)S(1)}, bf16[64,2048]{1,0:T(8,128)(2,1)S(1)}, u32[]{:S(2)}, u32[]{:S(2)}) collective-permute-start(bf16[64,2048]{1,0:T(8,128)(2,1)S(1)} %get-tuple-element.25.refs_1_), channel_id=1, source_target_pairs={{0,16},{1,17},{2,18},{3,19},{4,20},{5,21},{6,22},{7,23},{8,24},{9,... | collective-permute-start | bytes 786440 | tf_op jit(solution)/shard_map/ppermute | solution.py:344
  23.8 1.0 %collective-permute-start.5 = (bf16[64,2048]{1,0:T(8,128)(2,1)S(1)}, bf16[64,2048]{1,0:T(8,128)(2,1)S(1)}, u32[]{:S(2)}, u32[]{:S(2)}) collective-permute-start(bf16[64,2048]{1,0:T(8,128)(2,1)S(1)} %get-tuple-element.25.refs_1_), channel_id=1, source_target_pairs={{0,8},{1,9},{2,10},{3,11},{4,12},{5,13},{6,14},{7,15},{8,0},{9,1},... | collective-permute-start | bytes 786440 | tf_op jit(solution)/shard_map/ppermute | solution.py:344
  25.5 1.6 %collective-permute-start.1 = (bf16[2,64,768]{2,1,0:T(8,128)(2,1)S(1)}, bf16[2,64,768]{2,1,0:T(8,128)(2,1)S(1)}, u32[]{:S(2)}, u32[]{:S(2)}) collective-permute-start(bf16[2,64,768]{2,1,0:T(8,128)(2,1)S(1)} %project.9), channel_id=1, source_target_pairs={{0,2},{1,3},{2,0},{3,1},{4,6},{5,7},{6,4},{7,5},{8,10},{9,11},{10,... | collective-permute-start | bytes 589832 | tf_op jit(solution)/shard_map/ppermute | solution.py:344
  27.7 3.5 %collective-permute-done.1.refs_1_ = bf16[2,64,768]{2,1,0:T(8,128)(2,1)S(1)} collective-permute-done((bf16[2,64,768]{2,1,0:T(8,128)(2,1)S(1)}, bf16[2,64,768]{2,1,0:T(8,128)(2,1)S(1)}, u32[]{:S(2)}, u32[]{:S(2)}) %collective-permute-start.1) | collective-permute-done | bytes 196640 | tf_op jit(solution)/shard_map/ppermute | solution.py:344
  33.8 1.5 %collective-permute-done.5.refs_0_ = bf16[64,2048]{1,0:T(8,128)(2,1)S(1)} collective-permute-done((bf16[64,2048]{1,0:T(8,128)(2,1)S(1)}, bf16[64,2048]{1,0:T(8,128)(2,1)S(1)}, u32[]{:S(2)}, u32[]{:S(2)}) %collective-permute-start.5) | collective-permute-done | bytes 262176 | tf_op jit(solution)/shard_map/ppermute | solution.py:344
  36.5 1.6 %collective-permute-start.4 = (bf16[2,64,768]{2,1,0:T(8,128)(2,1)S(1)}, bf16[2,64,768]{2,1,0:T(8,128)(2,1)S(1)}, u32[]{:S(2)}, u32[]{:S(2)}) collective-permute-start(bf16[2,64,768]{2,1,0:T(8,128)(2,1)S(1)} %project.11.refs_3_), channel_id=1, source_target_pairs={{0,2},{1,3},{2,0},{3,1},{4,6},{5,7},{6,4},{7,5},{8,10},{9,11},{10,... | collective-permute-start | bytes 589832 | tf_op jit(solution)/shard_map/ppermute | solution.py:344
  39.8 2.0 %collective-permute-done.10.refs_0_ = bf16[64,2048]{1,0:T(8,128)(2,1)S(1)} collective-permute-done((bf16[64,2048]{1,0:T(8,128)(2,1)S(1)}, bf16[64,2048]{1,0:T(8,128)(2,1)S(1)}, u32[]{:S(2)}, u32[]{:S(2)}) %collective-permute-start.10) | collective-permute-done | bytes 262176 | tf_op jit(solution)/shard_map/ppermute | solution.py:344
  42.7 1.6 %collective-permute-start.12 = (bf16[2,64,768]{2,1,0:T(8,128)(2,1)S(1)}, bf16[2,64,768]{2,1,0:T(8,128)(2,1)S(1)}, u32[]{:S(2)}, u32[]{:S(2)}) collective-permute-start(bf16[2,64,768]{2,1,0:T(8,128)(2,1)S(1)} %project.15), channel_id=1, source_target_pairs={{0,2},{1,3},{2,0},{3,1},{4,6},{5,7},{6,4},{7,5},{8,10},{9,11},{10,... | collective-permute-start | bytes 589832 | tf_op jit(solution)/shard_map/ppermute | solution.py:344
  44.3 2.4 %collective-permute-done.7.refs_3_ = bf16[2,64,768]{2,1,0:T(8,128)(2,1)S(1)} collective-permute-done((bf16[2,64,768]{2,1,0:T(8,128)(2,1)S(1)}, bf16[2,64,768]{2,1,0:T(8,128)(2,1)S(1)}, u32[]{:S(2)}, u32[]{:S(2)}) %collective-permute-start.7) | collective-permute-done | bytes 196640 | tf_op jit(solution)/shard_map/ppermute | solution.py:344
  46.9 1.6 %collective-permute-start.9 = (bf16[128,768]{1,0:T(8,128)(2,1)S(1)}, bf16[128,768]{1,0:T(8,128)(2,1)S(1)}, u32[]{:S(2)}, u32[]{:S(2)}) collective-permute-start(bf16[128,768]{1,0:T(8,128)(2,1)S(1)} %get-tuple-element.28), channel_id=1, source_target_pairs={{0,16},{1,17},{2,18},{3,19},{4,20},{5,21},{6,22},{7,23},{8,24},{9,... | collective-permute-start | bytes 589832 | tf_op jit(solution)/shard_map/ppermute | solution.py:344
  48.4 1.5 %collective-permute-start.8 = (bf16[128,768]{1,0:T(8,128)(2,1)S(1)}, bf16[128,768]{1,0:T(8,128)(2,1)S(1)}, u32[]{:S(2)}, u32[]{:S(2)}) collective-permute-start(bf16[128,768]{1,0:T(8,128)(2,1)S(1)} %get-tuple-element.27.refs_2_), channel_id=1, source_target_pairs={{0,8},{1,9},{2,10},{3,11},{4,12},{5,13},{6,14},{7,15},{8,0},{9,1},... | collective-permute-start | bytes 589832 | tf_op jit(solution)/shard_map/ppermute | solution.py:344
  50.6 0.8 %collective-permute-start.13 = (bf16[128,768]{1,0:T(8,128)(2,1)S(1)}, bf16[128,768]{1,0:T(8,128)(2,1)S(1)}, u32[]{:S(2)}, u32[]{:S(2)}) collective-permute-start(bf16[128,768]{1,0:T(8,128)(2,1)S(1)} %merge.5), channel_id=1, source_target_pairs={{0,24},{1,25},{2,26},{3,27},{4,28},{5,29},{6,30},{7,31},{8,16},{9,... | collective-permute-start | bytes 589832 | tf_op jit(solution)/shard_map/ppermute | solution.py:344
  51.4 2.8 %collective-permute-done.9.refs_2_ = bf16[128,768]{1,0:T(8,128)(2,1)S(1)} collective-permute-done((bf16[128,768]{1,0:T(8,128)(2,1)S(1)}, bf16[128,768]{1,0:T(8,128)(2,1)S(1)}, u32[]{:S(2)}, u32[]{:S(2)}) %collective-permute-start.9) | collective-permute-done | bytes 196640 | tf_op jit(solution)/shard_map/ppermute | solution.py:344
  54.4 2.8 %collective-permute-done.13.refs_3_ = bf16[128,768]{1,0:T(8,128)(2,1)S(1)} collective-permute-done((bf16[128,768]{1,0:T(8,128)(2,1)S(1)}, bf16[128,768]{1,0:T(8,128)(2,1)S(1)}, u32[]{:S(2)}, u32[]{:S(2)}) %collective-permute-start.13) | collective-permute-done | bytes 196640 | tf_op jit(solution)/shard_map/ppermute | solution.py:344
  57.3 2.7 %collective-permute-start.14 = (bf16[128,768]{1,0:T(8,128)(2,1)S(1)}, bf16[128,768]{1,0:T(8,128)(2,1)S(1)}, u32[]{:S(2)}, u32[]{:S(2)}) collective-permute-start(bf16[128,768]{1,0:T(8,128)(2,1)S(1)} %get-tuple-element.32), channel_id=1, source_target_pairs={{0,4},{1,5},{2,6},{3,7},{4,0},{5,1},{6,2},{7,3},{8,12},{9,13},{10,... | collective-permute-start | bytes 589832 | tf_op jit(solution)/shard_map/ppermute | solution.py:344
  60.0 1.4 %collective-permute-start.16 = (bf16[128,768]{1,0:T(8,128)(2,1)S(1)}, bf16[128,768]{1,0:T(8,128)(2,1)S(1)}, u32[]{:S(2)}, u32[]{:S(2)}) collective-permute-start(bf16[128,768]{1,0:T(8,128)(2,1)S(1)} %get-tuple-element.33), channel_id=1, source_target_pairs={{0,6},{1,7},{2,4},{3,5},{4,2},{5,3},{6,0},{7,1},{8,14},{9,15},{10,... | collective-permute-start | bytes 589832 | tf_op jit(solution)/shard_map/ppermute | solution.py:344
  61.6 8.8 %collective-permute-done.14.two_ref = bf16[128,768]{1,0:T(8,128)(2,1)S(1)} collective-permute-done((bf16[128,768]{1,0:T(8,128)(2,1)S(1)}, bf16[128,768]{1,0:T(8,128)(2,1)S(1)}, u32[]{:S(2)}, u32[]{:S(2)}) %collective-permute-start.14) | collective-permute-done | bytes 196640 | tf_op jit(solution)/shard_map/ppermute | solution.py:344
  71.1 0.8 %collective-permute-done.15.refs_0_ = bf16[128,768]{1,0:T(8,128)(2,1)S(1)} collective-permute-done((bf16[128,768]{1,0:T(8,128)(2,1)S(1)}, bf16[128,768]{1,0:T(8,128)(2,1)S(1)}, u32[]{:S(2)}, u32[]{:S(2)}) %collective-permute-start.15) | collective-permute-done | bytes 196640 | tf_op jit(solution)/shard_map/ppermute | solution.py:344
  72.2 0.8 %last.1 = bf16[1,128,1536]{2,1,0:T(8,128)(2,1)} custom-call(bf16[128,768]{1,0:T(8,128)(2,1)S(1)} %collective-permute-done.15.refs_0_, bf16[128,768]{1,0:T(8,128)(2,1)S(1)} %collective-permute-done.18.refs_1_), custom_call_target="tpu_custom_call" | custom-call | flops 1 | bytes 1 | tf_op jit(solution)/shard_map/last/pallas_call | solution.py:396
  (33 shorter events, 10.5 us)
Async XLA Ops:
  2.6 16.1 %collective-permute-start = (bf16[2064,128]{1,0:T(8,128)(2,1)S(1)}, bf16[2064,128]{1,0:T(8,128)(2,1)S(1)}, u32[]{:S(2)}, u32[]{:S(2)}) collective-permute-start(bf16[2064,128]{1,0:T(8,128)(2,1)S(1)} %shard_state.1), channel_id=1, source_target_pairs={{0,8},{8,16},{16,24},{1,9},{9,17},{17,25},{2,10},{10,18},{18,26},{... | collective-permute-start | bytes 1585160 | tf_op jit(solution)/shard_map/ppermute | solution.py:264
  19.3 12.0 %collective-permute-start.3 = (bf16[64,2048]{1,0:T(8,128)(2,1)S(1)}, bf16[64,2048]{1,0:T(8,128)(2,1)S(1)}, u32[]{:S(2)}, u32[]{:S(2)}) collective-permute-start(bf16[64,2048]{1,0:T(8,128)(2,1)S(1)} %get-tuple-element.24.refs_0_), channel_id=1, source_target_pairs={{0,16},{1,17},{2,18},{3,19},{4,20},{5,21},{6,22},{7,23},{8,24},{9,... | collective-permute-start | bytes 786440 | tf_op jit(solution)/shard_map/ppermute | solution.py:344
  22.7 9.2 %collective-permute-start.2 = (bf16[64,2048]{1,0:T(8,128)(2,1)S(1)}, bf16[64,2048]{1,0:T(8,128)(2,1)S(1)}, u32[]{:S(2)}, u32[]{:S(2)}) collective-permute-start(bf16[64,2048]{1,0:T(8,128)(2,1)S(1)} %get-tuple-element.24.refs_0_), channel_id=1, source_target_pairs={{0,8},{1,9},{2,10},{3,11},{4,12},{5,13},{6,14},{7,15},{8,0},{9,1},... | collective-permute-start | bytes 786440 | tf_op jit(solution)/shard_map/ppermute | solution.py:344
  22.7 11.0 %collective-permute-start.6 = (bf16[64,2048]{1,0:T(8,128)(2,1)S(1)}, bf16[64,2048]{1,0:T(8,128)(2,1)S(1)}, u32[]{:S(2)}, u32[]{:S(2)}) collective-permute-start(bf16[64,2048]{1,0:T(8,128)(2,1)S(1)} %get-tuple-element.25.refs_1_), channel_id=1, source_target_pairs={{0,16},{1,17},{2,18},{3,19},{4,20},{5,21},{6,22},{7,23},{8,24},{9,... | collective-permute-start | bytes 786440 | tf_op jit(solution)/shard_map/ppermute | solution.py:344
  23.8 11.4 %collective-permute-start.5 = (bf16[64,2048]{1,0:T(8,128)(2,1)S(1)}, bf16[64,2048]{1,0:T(8,128)(2,1)S(1)}, u32[]{:S(2)}, u32[]{:S(2)}) collective-permute-start(bf16[64,2048]{1,0:T(8,128)(2,1)S(1)} %get-tuple-element.25.refs_1_), channel_id=1, source_target_pairs={{0,8},{1,9},{2,10},{3,11},{4,12},{5,13},{6,14},{7,15},{8,0},{9,1},... | collective-permute-start | bytes 786440 | tf_op jit(solution)/shard_map/ppermute | solution.py:344
  25.5 5.7 %collective-permute-start.1 = (bf16[2,64,768]{2,1,0:T(8,128)(2,1)S(1)}, bf16[2,64,768]{2,1,0:T(8,128)(2,1)S(1)}, u32[]{:S(2)}, u32[]{:S(2)}) collective-permute-start(bf16[2,64,768]{2,1,0:T(8,128)(2,1)S(1)} %project.9), channel_id=1, source_target_pairs={{0,2},{1,3},{2,0},{3,1},{4,6},{5,7},{6,4},{7,5},{8,10},{9,11},{10,... | collective-permute-start | bytes 589832 | tf_op jit(solution)/shard_map/ppermute | solution.py:344
  35.3 6.4 %collective-permute-start.10 = (bf16[64,2048]{1,0:T(8,128)(2,1)S(1)}, bf16[64,2048]{1,0:T(8,128)(2,1)S(1)}, u32[]{:S(2)}, u32[]{:S(2)}) collective-permute-start(bf16[64,2048]{1,0:T(8,128)(2,1)S(1)} %get-tuple-element.29), channel_id=1, source_target_pairs={{0,16},{1,17},{2,18},{3,19},{4,20},{5,21},{6,22},{7,23},{8,24},{9,... | collective-permute-start | bytes 786440 | tf_op jit(solution)/shard_map/ppermute | solution.py:344
  35.7 6.4 %collective-permute-start.11 = (bf16[64,2048]{1,0:T(8,128)(2,1)S(1)}, bf16[64,2048]{1,0:T(8,128)(2,1)S(1)}, u32[]{:S(2)}, u32[]{:S(2)}) collective-permute-start(bf16[64,2048]{1,0:T(8,128)(2,1)S(1)} %get-tuple-element.30), channel_id=1, source_target_pairs={{0,8},{1,9},{2,10},{3,11},{4,12},{5,13},{6,14},{7,15},{8,0},{9,1},... | collective-permute-start | bytes 786440 | tf_op jit(solution)/shard_map/ppermute | solution.py:344
  36.5 7.9 %collective-permute-start.4 = (bf16[2,64,768]{2,1,0:T(8,128)(2,1)S(1)}, bf16[2,64,768]{2,1,0:T(8,128)(2,1)S(1)}, u32[]{:S(2)}, u32[]{:S(2)}) collective-permute-start(bf16[2,64,768]{2,1,0:T(8,128)(2,1)S(1)} %project.11.refs_3_), channel_id=1, source_target_pairs={{0,2},{1,3},{2,0},{3,1},{4,6},{5,7},{6,4},{7,5},{8,10},{9,11},{10,... | collective-permute-start | bytes 589832 | tf_op jit(solution)/shard_map/ppermute | solution.py:344
  38.6 8.1 %collective-permute-start.7 = (bf16[2,64,768]{2,1,0:T(8,128)(2,1)S(1)}, bf16[2,64,768]{2,1,0:T(8,128)(2,1)S(1)}, u32[]{:S(2)}, u32[]{:S(2)}) collective-permute-start(bf16[2,64,768]{2,1,0:T(8,128)(2,1)S(1)} %project.13), channel_id=1, source_target_pairs={{0,2},{1,3},{2,0},{3,1},{4,6},{5,7},{6,4},{7,5},{8,10},{9,11},{10,... | collective-permute-start | bytes 589832 | tf_op jit(solution)/shard_map/ppermute | solution.py:344
  42.7 7.8 %collective-permute-start.12 = (bf16[2,64,768]{2,1,0:T(8,128)(2,1)S(1)}, bf16[2,64,768]{2,1,0:T(8,128)(2,1)S(1)}, u32[]{:S(2)}, u32[]{:S(2)}) collective-permute-start(bf16[2,64,768]{2,1,0:T(8,128)(2,1)S(1)} %project.15), channel_id=1, source_target_pairs={{0,2},{1,3},{2,0},{3,1},{4,6},{5,7},{6,4},{7,5},{8,10},{9,11},{10,... | collective-permute-start | bytes 589832 | tf_op jit(solution)/shard_map/ppermute | solution.py:344
  46.9 7.3 %collective-permute-start.9 = (bf16[128,768]{1,0:T(8,128)(2,1)S(1)}, bf16[128,768]{1,0:T(8,128)(2,1)S(1)}, u32[]{:S(2)}, u32[]{:S(2)}) collective-permute-start(bf16[128,768]{1,0:T(8,128)(2,1)S(1)} %get-tuple-element.28), channel_id=1, source_target_pairs={{0,16},{1,17},{2,18},{3,19},{4,20},{5,21},{6,22},{7,23},{8,24},{9,... | collective-permute-start | bytes 589832 | tf_op jit(solution)/shard_map/ppermute | solution.py:344
  48.4 6.0 %collective-permute-start.8 = (bf16[128,768]{1,0:T(8,128)(2,1)S(1)}, bf16[128,768]{1,0:T(8,128)(2,1)S(1)}, u32[]{:S(2)}, u32[]{:S(2)}) collective-permute-start(bf16[128,768]{1,0:T(8,128)(2,1)S(1)} %get-tuple-element.27.refs_2_), channel_id=1, source_target_pairs={{0,8},{1,9},{2,10},{3,11},{4,12},{5,13},{6,14},{7,15},{8,0},{9,1},... | collective-permute-start | bytes 589832 | tf_op jit(solution)/shard_map/ppermute | solution.py:344
  50.6 6.6 %collective-permute-start.13 = (bf16[128,768]{1,0:T(8,128)(2,1)S(1)}, bf16[128,768]{1,0:T(8,128)(2,1)S(1)}, u32[]{:S(2)}, u32[]{:S(2)}) collective-permute-start(bf16[128,768]{1,0:T(8,128)(2,1)S(1)} %merge.5), channel_id=1, source_target_pairs={{0,24},{1,25},{2,26},{3,27},{4,28},{5,29},{6,30},{7,31},{8,16},{9,... | collective-permute-start | bytes 589832 | tf_op jit(solution)/shard_map/ppermute | solution.py:344
  57.3 13.1 %collective-permute-start.14 = (bf16[128,768]{1,0:T(8,128)(2,1)S(1)}, bf16[128,768]{1,0:T(8,128)(2,1)S(1)}, u32[]{:S(2)}, u32[]{:S(2)}) collective-permute-start(bf16[128,768]{1,0:T(8,128)(2,1)S(1)} %get-tuple-element.32), channel_id=1, source_target_pairs={{0,4},{1,5},{2,6},{3,7},{4,0},{5,1},{6,2},{7,3},{8,12},{9,13},{10,... | collective-permute-start | bytes 589832 | tf_op jit(solution)/shard_map/ppermute | solution.py:344
  60.0 10.5 %collective-permute-start.16 = (bf16[128,768]{1,0:T(8,128)(2,1)S(1)}, bf16[128,768]{1,0:T(8,128)(2,1)S(1)}, u32[]{:S(2)}, u32[]{:S(2)}) collective-permute-start(bf16[128,768]{1,0:T(8,128)(2,1)S(1)} %get-tuple-element.33), channel_id=1, source_target_pairs={{0,6},{1,7},{2,4},{3,5},{4,2},{5,3},{6,0},{7,1},{8,14},{9,15},{10,... | collective-permute-start | bytes 589832 | tf_op jit(solution)/shard_map/ppermute | solution.py:344
  61.3 9.2 %collective-permute-start.17 = (bf16[128,768]{1,0:T(8,128)(2,1)S(1)}, bf16[128,768]{1,0:T(8,128)(2,1)S(1)}, u32[]{:S(2)}, u32[]{:S(2)}) collective-permute-start(bf16[128,768]{1,0:T(8,128)(2,1)S(1)} %get-tuple-element.34), channel_id=1, source_target_pairs={{0,2},{1,3},{2,0},{3,1},{4,6},{5,7},{6,4},{7,5},{8,10},{9,11},{10,... | collective-permute-start | bytes 589832 | tf_op jit(solution)/shard_map/ppermute | solution.py:344
  70.4 1.5 %collective-permute-start.15 = (bf16[128,768]{1,0:T(8,128)(2,1)S(1)}, bf16[128,768]{1,0:T(8,128)(2,1)S(1)}, u32[]{:S(2)}, u32[]{:S(2)}) collective-permute-start(bf16[128,768]{1,0:T(8,128)(2,1)S(1)} %sum.2), channel_id=1, source_target_pairs={{0,1},{1,0},{2,3},{3,2},{4,5},{5,4},{6,7},{7,6},{8,9},{9,8},{10,11... | collective-permute-start | bytes 589832 | tf_op jit(solution)/shard_map/ppermute | solution.py:344
  70.6 1.6 %collective-permute-start.18 = (bf16[128,768]{1,0:T(8,128)(2,1)S(1)}, bf16[128,768]{1,0:T(8,128)(2,1)S(1)}, u32[]{:S(2)}, u32[]{:S(2)}) collective-permute-start(bf16[128,768]{1,0:T(8,128)(2,1)S(1)} %sum.3), channel_id=1, source_target_pairs={{0,1},{1,0},{2,3},{3,2},{4,5},{5,4},{6,7},{7,6},{8,9},{9,8},{10,11... | collective-permute-start | bytes 589832 | tf_op jit(solution)/shard_map/ppermute | solution.py:344

commit v15 on v12

--- a/solution.py
+++ b/solution.py
@@ -224,12 +224,17 @@
     out_ref[...] = total.astype(jnp.bfloat16)
 
 
-def last_kernel(*refs):
-    out_ref = refs[-1]
-    wide = refs[0].shape[1]
-    for m in range(2):
+def last_kernel(one_ref, two_ref, out_ref, sems):
+    wide = one_ref.shape[1]
+    copies = []
+    for m, half_ref in enumerate((one_ref, two_ref)):
         half = (lax.axis_index("head") & 1) ^ m
-        out_ref[0, :, pl.ds(pl.multiple_of(half * wide, wide), wide)] = refs[m][...]
+        span = pl.ds(pl.multiple_of(half * wide, wide), wide)
+        copies.append(pltpu.make_async_copy(half_ref, out_ref.at[0, :, span], sems.at[m]))
+    for copy in copies:
+        copy.start()
+    for copy in copies:
+        copy.wait()
 
 
 def call(kernel, out_shape, name, limit=24, **more):
@@ -392,7 +397,8 @@
     total.append(call(sum_kernel, single, "sum")(arrived[0], arrived[2]))
     total = [moved(half, lambda i, j, s: (i, j, 1 - s)) for half in total]
     out = jax.ShapeDtypeStruct((1, rows, columns), jnp.bfloat16)
-    return call(last_kernel, out, "last")(*total)
+    sems = [pltpu.SemaphoreType.DMA((2,))]
+    return call(last_kernel, out, "last", out_specs=ANY, scratch_shapes=sems)(*total)
 
 
 def solution(mesh):

time: 74.1 us -> 74.1 us (level)
  no operation moved by 1% of the time
where the time goes in v15:
time: 74.1 us; the launch traced here: 72.9 us
  waiting for transfers between devices  33.8 us (46%)
  starting transfers between devices  26 us (35%)
  Pallas kernels  13 us (18%)
    ppermute x17, waiting for transfers between devices, moved(): lax.ppermute(array, names, [(place[spot], place[target(*spot)]) for spot...  26.8 us
    ppermute x17, starting transfers between devices, moved(): lax.ppermute(array, names, [(place[spot], place[target(*spot)]) for spot...  21.2 us
    ppermute x1, waiting for transfers between devices, from_before(): return lax.ppermute(array, 'ctx', [(i, i + by) for i in range(n_ctx - by)])  6.98 us
    ppermute x1, starting transfers between devices, from_before(): return lax.ppermute(array, 'ctx', [(i, i + by) for i in range(n_ctx - by)])  4.87 us
    pallas_call x6, Pallas kernels, project(): call(kernel, shape, 'project', in_specs=specs)(*picked, weight, *after)  4.4 us
    pallas_call x1, Pallas kernels, on_device(): call(inside_kernel, (pltpu.VMEM((rows, width), jnp.float32), pltpu.VMEM((...  4.24 us
    pallas_call x1, Pallas kernels, on_device(): call(state_kernel, state_shape, 'shard_state', in_specs=[HBM] * 4, scratc...  2.58 us
  transfers between devices with their start and end apart: 18, of which 14 were waited for; matrix products, arithmetic and copies ran while one was open for 0% of the time, Pallas kernels for 12%

profile of v15, /device:TPU:0, one launch (start us, length us, event | category | flops | bytes accessed | tf_op | source)
XLA Modules:
  0.0 72.9 jit_solution(16040239276217064907)
XLA Ops:
  0.0 2.6 %shard_state.1 = bf16[2064,128]{1,0:T(8,128)(2,1)S(1)} custom-call(bf16[1,128,2048]{2,1,0:T(8,128)(2,1)} %refs_0_.1, bf16[1,128,2048]{2,1,0:T(8,128)(2,1)} %refs_1_.1, f32[1,16,128]{2,1,0:T(8,128)} %bitcast.1, s32[1,128]{1,0:T(1,128)} %refs_3_.1), custom_call_target="tpu_custom_call" | custom-call | flops 1 | bytes 1 | tf_op jit(solution)/shard_map/shard_state/pallas_call | solution.py:273
  2.6 4.9 %collective-permute-start = (bf16[2064,128]{1,0:T(8,128)(2,1)S(1)}, bf16[2064,128]{1,0:T(8,128)(2,1)S(1)}, u32[]{:S(2)}, u32[]{:S(2)}) collective-permute-start(bf16[2064,128]{1,0:T(8,128)(2,1)S(1)} %shard_state.1), channel_id=1, source_target_pairs={{0,8},{8,16},{16,24},{1,9},{9,17},{17,25},{2,10},{10,18},{18,26},{... | collective-permute-start | bytes 1585160 | tf_op jit(solution)/shard_map/ppermute | solution.py:269
  7.5 4.2 %inside.1 = (f32[128,2048]{1,0:T(8,128)S(1)}, f32[128,2048]{1,0:T(8,128)S(1)}, f32[128,128]{1,0:T(8,128)S(1)}, bf16[128,2048]{1,0:T(8,128)(2,1)S(1)}, bf16[2048,1536]{1,0:T(8,128)(2,1)S(1)}) custom-call(bf16[1,128,2048]{2,1,0:T(8,128)(2,1)} %query_hbm.1, bf16[1,128,2048]{2,1,0:T(8,128)(2,1)} %refs_0_.1, bf16[1,128,2048]{2,1,0:T(8,128)(2,1)} %refs_1_.1, ...), custom_call_target="tpu_custom_call" | custom-call | flops 1 | bytes 1 | tf_op jit(solution)/shard_map/inside/pallas_call | solution.py:305
  11.7 7.0 %collective-permute-done.state_ref = bf16[2064,128]{1,0:T(8,128)(2,1)S(1)} collective-permute-done((bf16[2064,128]{1,0:T(8,128)(2,1)S(1)}, bf16[2064,128]{1,0:T(8,128)(2,1)S(1)}, u32[]{:S(2)}, u32[]{:S(2)}) %collective-permute-start) | collective-permute-done | bytes 528416 | tf_op jit(solution)/shard_map/ppermute | solution.py:269
  19.3 3.5 %collective-permute-start.4 = (bf16[64,2048]{1,0:T(8,128)(2,1)S(1)}, bf16[64,2048]{1,0:T(8,128)(2,1)S(1)}, u32[]{:S(2)}, u32[]{:S(2)}) collective-permute-start(bf16[64,2048]{1,0:T(8,128)(2,1)S(1)} %get-tuple-element.24.refs_0_), channel_id=1, source_target_pairs={{0,16},{1,17},{2,18},{3,19},{4,20},{5,21},{6,22},{7,23},{8,24},{9,... | collective-permute-start | bytes 786440 | tf_op jit(solution)/shard_map/ppermute | solution.py:349
  22.7 1.1 %collective-permute-start.5 = (bf16[64,2048]{1,0:T(8,128)(2,1)S(1)}, bf16[64,2048]{1,0:T(8,128)(2,1)S(1)}, u32[]{:S(2)}, u32[]{:S(2)}) collective-permute-start(bf16[64,2048]{1,0:T(8,128)(2,1)S(1)} %get-tuple-element.25.refs_1_), channel_id=1, source_target_pairs={{0,16},{1,17},{2,18},{3,19},{4,20},{5,21},{6,22},{7,23},{8,24},{9,... | collective-permute-start | bytes 786440 | tf_op jit(solution)/shard_map/ppermute | solution.py:349
  23.8 1.0 %collective-permute-start.3 = (bf16[64,2048]{1,0:T(8,128)(2,1)S(1)}, bf16[64,2048]{1,0:T(8,128)(2,1)S(1)}, u32[]{:S(2)}, u32[]{:S(2)}) collective-permute-start(bf16[64,2048]{1,0:T(8,128)(2,1)S(1)} %get-tuple-element.25.refs_1_), channel_id=1, source_target_pairs={{0,8},{1,9},{2,10},{3,11},{4,12},{5,13},{6,14},{7,15},{8,0},{9,1},... | collective-permute-start | bytes 786440 | tf_op jit(solution)/shard_map/ppermute | solution.py:349
  25.5 1.6 %collective-permute-start.1 = (bf16[2,64,768]{2,1,0:T(8,128)(2,1)S(1)}, bf16[2,64,768]{2,1,0:T(8,128)(2,1)S(1)}, u32[]{:S(2)}, u32[]{:S(2)}) collective-permute-start(bf16[2,64,768]{2,1,0:T(8,128)(2,1)S(1)} %project.7), channel_id=1, source_target_pairs={{0,2},{1,3},{2,0},{3,1},{4,6},{5,7},{6,4},{7,5},{8,10},{9,11},{10,... | collective-permute-start | bytes 589832 | tf_op jit(solution)/shard_map/ppermute | solution.py:349
  27.7 3.5 %collective-permute-done.1.refs_1_ = bf16[2,64,768]{2,1,0:T(8,128)(2,1)S(1)} collective-permute-done((bf16[2,64,768]{2,1,0:T(8,128)(2,1)S(1)}, bf16[2,64,768]{2,1,0:T(8,128)(2,1)S(1)}, u32[]{:S(2)}, u32[]{:S(2)}) %collective-permute-start.1) | collective-permute-done | bytes 196640 | tf_op jit(solution)/shard_map/ppermute | solution.py:349
  32.0 1.8 %collective-permute-done.5.refs_3_.lower_ref = bf16[64,2048]{1,0:T(8,128)(2,1)S(1)} collective-permute-done((bf16[64,2048]{1,0:T(8,128)(2,1)S(1)}, bf16[64,2048]{1,0:T(8,128)(2,1)S(1)}, u32[]{:S(2)}, u32[]{:S(2)}) %collective-permute-start.5) | collective-permute-done | bytes 262176 | tf_op jit(solution)/shard_map/ppermute | solution.py:349
  33.8 1.5 %collective-permute-done.3.refs_1_.refs_0_ = bf16[64,2048]{1,0:T(8,128)(2,1)S(1)} collective-permute-done((bf16[64,2048]{1,0:T(8,128)(2,1)S(1)}, bf16[64,2048]{1,0:T(8,128)(2,1)S(1)}, u32[]{:S(2)}, u32[]{:S(2)}) %collective-permute-start.3) | collective-permute-done | bytes 262176 | tf_op jit(solution)/shard_map/ppermute | solution.py:349
  37.5 1.6 %collective-permute-start.6 = (bf16[4,64,768]{2,1,0:T(8,128)(2,1)S(1)}, bf16[4,64,768]{2,1,0:T(8,128)(2,1)S(1)}, u32[]{:S(2)}, u32[]{:S(2)}) collective-permute-start(bf16[4,64,768]{2,1,0:T(8,128)(2,1)S(1)} %project.9), channel_id=1, source_target_pairs={{0,2},{1,3},{2,0},{3,1},{4,6},{5,7},{6,4},{7,5},{8,10},{9,11},{10,... | collective-permute-start | bytes 1179656 | tf_op jit(solution)/shard_map/ppermute | solution.py:349
  40.1 1.6 %collective-permute-done.9.refs_0_ = bf16[64,2048]{1,0:T(8,128)(2,1)S(1)} collective-permute-done((bf16[64,2048]{1,0:T(8,128)(2,1)S(1)}, bf16[64,2048]{1,0:T(8,128)(2,1)S(1)}, u32[]{:S(2)}, u32[]{:S(2)}) %collective-permute-start.9) | collective-permute-done | bytes 262176 | tf_op jit(solution)/shard_map/ppermute | solution.py:349
  42.7 1.6 %collective-permute-start.11 = (bf16[2,64,768]{2,1,0:T(8,128)(2,1)S(1)}, bf16[2,64,768]{2,1,0:T(8,128)(2,1)S(1)}, u32[]{:S(2)}, u32[]{:S(2)}) collective-permute-start(bf16[2,64,768]{2,1,0:T(8,128)(2,1)S(1)} %project.11), channel_id=1, source_target_pairs={{0,2},{1,3},{2,0},{3,1},{4,6},{5,7},{6,4},{7,5},{8,10},{9,11},{10,... | collective-permute-start | bytes 589832 | tf_op jit(solution)/shard_map/ppermute | solution.py:349
  44.9 2.9 %collective-permute-done.6.refs_1_ = bf16[4,64,768]{2,1,0:T(8,128)(2,1)S(1)} collective-permute-done((bf16[4,64,768]{2,1,0:T(8,128)(2,1)S(1)}, bf16[4,64,768]{2,1,0:T(8,128)(2,1)S(1)}, u32[]{:S(2)}, u32[]{:S(2)}) %collective-permute-start.6) | collective-permute-done | bytes 393248 | tf_op jit(solution)/shard_map/ppermute | solution.py:349
  48.0 1.6 %collective-permute-start.8 = (bf16[128,768]{1,0:T(8,128)(2,1)S(1)}, bf16[128,768]{1,0:T(8,128)(2,1)S(1)}, u32[]{:S(2)}, u32[]{:S(2)}) collective-permute-start(bf16[128,768]{1,0:T(8,128)(2,1)S(1)} %get-tuple-element.28), channel_id=1, source_target_pairs={{0,16},{1,17},{2,18},{3,19},{4,20},{5,21},{6,22},{7,23},{8,24},{9,... | collective-permute-start | bytes 589832 | tf_op jit(solution)/shard_map/ppermute | solution.py:349
  49.5 1.5 %collective-permute-start.7 = (bf16[128,768]{1,0:T(8,128)(2,1)S(1)}, bf16[128,768]{1,0:T(8,128)(2,1)S(1)}, u32[]{:S(2)}, u32[]{:S(2)}) collective-permute-start(bf16[128,768]{1,0:T(8,128)(2,1)S(1)} %get-tuple-element.27.refs_2_), channel_id=1, source_target_pairs={{0,8},{1,9},{2,10},{3,11},{4,12},{5,13},{6,14},{7,15},{8,0},{9,1},... | collective-permute-start | bytes 589832 | tf_op jit(solution)/shard_map/ppermute | solution.py:349
  51.0 1.4 %collective-permute-start.12 = (bf16[128,768]{1,0:T(8,128)(2,1)S(1)}, bf16[128,768]{1,0:T(8,128)(2,1)S(1)}, u32[]{:S(2)}, u32[]{:S(2)}) collective-permute-start(bf16[128,768]{1,0:T(8,128)(2,1)S(1)} %merge.5), channel_id=1, source_target_pairs={{0,24},{1,25},{2,26},{3,27},{4,28},{5,29},{6,30},{7,31},{8,16},{9,... | collective-permute-start | bytes 589832 | tf_op jit(solution)/shard_map/ppermute | solution.py:349
  52.5 1.6 %collective-permute-done.8.refs_2_ = bf16[128,768]{1,0:T(8,128)(2,1)S(1)} collective-permute-done((bf16[128,768]{1,0:T(8,128)(2,1)S(1)}, bf16[128,768]{1,0:T(8,128)(2,1)S(1)}, u32[]{:S(2)}, u32[]{:S(2)}) %collective-permute-start.8) | collective-permute-done | bytes 196640 | tf_op jit(solution)/shard_map/ppermute | solution.py:349
  54.1 1.1 %collective-permute-done.7.refs_1_ = bf16[128,768]{1,0:T(8,128)(2,1)S(1)} collective-permute-done((bf16[128,768]{1,0:T(8,128)(2,1)S(1)}, bf16[128,768]{1,0:T(8,128)(2,1)S(1)}, u32[]{:S(2)}, u32[]{:S(2)}) %collective-permute-start.7) | collective-permute-done | bytes 196640 | tf_op jit(solution)/shard_map/ppermute | solution.py:349
  55.2 2.5 %collective-permute-done.12.refs_3_ = bf16[128,768]{1,0:T(8,128)(2,1)S(1)} collective-permute-done((bf16[128,768]{1,0:T(8,128)(2,1)S(1)}, bf16[128,768]{1,0:T(8,128)(2,1)S(1)}, u32[]{:S(2)}, u32[]{:S(2)}) %collective-permute-start.12) | collective-permute-done | bytes 196640 | tf_op jit(solution)/shard_map/ppermute | solution.py:349
  57.8 2.7 %collective-permute-start.13 = (bf16[128,768]{1,0:T(8,128)(2,1)S(1)}, bf16[128,768]{1,0:T(8,128)(2,1)S(1)}, u32[]{:S(2)}, u32[]{:S(2)}) collective-permute-start(bf16[128,768]{1,0:T(8,128)(2,1)S(1)} %get-tuple-element.32), channel_id=1, source_target_pairs={{0,4},{1,5},{2,6},{3,7},{4,0},{5,1},{6,2},{7,3},{8,12},{9,13},{10,... | collective-permute-start | bytes 589832 | tf_op jit(solution)/shard_map/ppermute | solution.py:349
  60.4 1.6 %collective-permute-start.15 = (bf16[128,768]{1,0:T(8,128)(2,1)S(1)}, bf16[128,768]{1,0:T(8,128)(2,1)S(1)}, u32[]{:S(2)}, u32[]{:S(2)}) collective-permute-start(bf16[128,768]{1,0:T(8,128)(2,1)S(1)} %get-tuple-element.33), channel_id=1, source_target_pairs={{0,2},{1,3},{2,0},{3,1},{4,6},{5,7},{6,4},{7,5},{8,10},{9,11},{10,... | collective-permute-start | bytes 589832 | tf_op jit(solution)/shard_map/ppermute | solution.py:349
  62.2 8.1 %collective-permute-done.13.two_ref = bf16[128,768]{1,0:T(8,128)(2,1)S(1)} collective-permute-done((bf16[128,768]{1,0:T(8,128)(2,1)S(1)}, bf16[128,768]{1,0:T(8,128)(2,1)S(1)}, u32[]{:S(2)}, u32[]{:S(2)}) %collective-permute-start.13) | collective-permute-done | bytes 196640 | tf_op jit(solution)/shard_map/ppermute | solution.py:349
  (29 shorter events, 10.4 us)
Async XLA Ops:
  2.6 16.1 %collective-permute-start = (bf16[2064,128]{1,0:T(8,128)(2,1)S(1)}, bf16[2064,128]{1,0:T(8,128)(2,1)S(1)}, u32[]{:S(2)}, u32[]{:S(2)}) collective-permute-start(bf16[2064,128]{1,0:T(8,128)(2,1)S(1)} %shard_state.1), channel_id=1, source_target_pairs={{0,8},{8,16},{16,24},{1,9},{9,17},{17,25},{2,10},{10,18},{18,26},{... | collective-permute-start | bytes 1585160 | tf_op jit(solution)/shard_map/ppermute | solution.py:269
  19.3 12.0 %collective-permute-start.4 = (bf16[64,2048]{1,0:T(8,128)(2,1)S(1)}, bf16[64,2048]{1,0:T(8,128)(2,1)S(1)}, u32[]{:S(2)}, u32[]{:S(2)}) collective-permute-start(bf16[64,2048]{1,0:T(8,128)(2,1)S(1)} %get-tuple-element.24.refs_0_), channel_id=1, source_target_pairs={{0,16},{1,17},{2,18},{3,19},{4,20},{5,21},{6,22},{7,23},{8,24},{9,... | collective-permute-start | bytes 786440 | tf_op jit(solution)/shard_map/ppermute | solution.py:349
  22.7 9.2 %collective-permute-start.2 = (bf16[64,2048]{1,0:T(8,128)(2,1)S(1)}, bf16[64,2048]{1,0:T(8,128)(2,1)S(1)}, u32[]{:S(2)}, u32[]{:S(2)}) collective-permute-start(bf16[64,2048]{1,0:T(8,128)(2,1)S(1)} %get-tuple-element.24.refs_0_), channel_id=1, source_target_pairs={{0,8},{1,9},{2,10},{3,11},{4,12},{5,13},{6,14},{7,15},{8,0},{9,1},... | collective-permute-start | bytes 786440 | tf_op jit(solution)/shard_map/ppermute | solution.py:349
  22.7 11.0 %collective-permute-start.5 = (bf16[64,2048]{1,0:T(8,128)(2,1)S(1)}, bf16[64,2048]{1,0:T(8,128)(2,1)S(1)}, u32[]{:S(2)}, u32[]{:S(2)}) collective-permute-start(bf16[64,2048]{1,0:T(8,128)(2,1)S(1)} %get-tuple-element.25.refs_1_), channel_id=1, source_target_pairs={{0,16},{1,17},{2,18},{3,19},{4,20},{5,21},{6,22},{7,23},{8,24},{9,... | collective-permute-start | bytes 786440 | tf_op jit(solution)/shard_map/ppermute | solution.py:349
  23.8 11.4 %collective-permute-start.3 = (bf16[64,2048]{1,0:T(8,128)(2,1)S(1)}, bf16[64,2048]{1,0:T(8,128)(2,1)S(1)}, u32[]{:S(2)}, u32[]{:S(2)}) collective-permute-start(bf16[64,2048]{1,0:T(8,128)(2,1)S(1)} %get-tuple-element.25.refs_1_), channel_id=1, source_target_pairs={{0,8},{1,9},{2,10},{3,11},{4,12},{5,13},{6,14},{7,15},{8,0},{9,1},... | collective-permute-start | bytes 786440 | tf_op jit(solution)/shard_map/ppermute | solution.py:349
  25.5 5.7 %collective-permute-start.1 = (bf16[2,64,768]{2,1,0:T(8,128)(2,1)S(1)}, bf16[2,64,768]{2,1,0:T(8,128)(2,1)S(1)}, u32[]{:S(2)}, u32[]{:S(2)}) collective-permute-start(bf16[2,64,768]{2,1,0:T(8,128)(2,1)S(1)} %project.7), channel_id=1, source_target_pairs={{0,2},{1,3},{2,0},{3,1},{4,6},{5,7},{6,4},{7,5},{8,10},{9,11},{10,... | collective-permute-start | bytes 589832 | tf_op jit(solution)/shard_map/ppermute | solution.py:349
  35.3 6.4 %collective-permute-start.9 = (bf16[64,2048]{1,0:T(8,128)(2,1)S(1)}, bf16[64,2048]{1,0:T(8,128)(2,1)S(1)}, u32[]{:S(2)}, u32[]{:S(2)}) collective-permute-start(bf16[64,2048]{1,0:T(8,128)(2,1)S(1)} %get-tuple-element.29), channel_id=1, source_target_pairs={{0,16},{1,17},{2,18},{3,19},{4,20},{5,21},{6,22},{7,23},{8,24},{9,... | collective-permute-start | bytes 786440 | tf_op jit(solution)/shard_map/ppermute | solution.py:349
  35.7 6.4 %collective-permute-start.10 = (bf16[64,2048]{1,0:T(8,128)(2,1)S(1)}, bf16[64,2048]{1,0:T(8,128)(2,1)S(1)}, u32[]{:S(2)}, u32[]{:S(2)}) collective-permute-start(bf16[64,2048]{1,0:T(8,128)(2,1)S(1)} %get-tuple-element.30), channel_id=1, source_target_pairs={{0,8},{1,9},{2,10},{3,11},{4,12},{5,13},{6,14},{7,15},{8,0},{9,1},... | collective-permute-start | bytes 786440 | tf_op jit(solution)/shard_map/ppermute | solution.py:349
  37.5 10.4 %collective-permute-start.6 = (bf16[4,64,768]{2,1,0:T(8,128)(2,1)S(1)}, bf16[4,64,768]{2,1,0:T(8,128)(2,1)S(1)}, u32[]{:S(2)}, u32[]{:S(2)}) collective-permute-start(bf16[4,64,768]{2,1,0:T(8,128)(2,1)S(1)} %project.9), channel_id=1, source_target_pairs={{0,2},{1,3},{2,0},{3,1},{4,6},{5,7},{6,4},{7,5},{8,10},{9,11},{10,... | collective-permute-start | bytes 1179656 | tf_op jit(solution)/shard_map/ppermute | solution.py:349
  42.7 8.3 %collective-permute-start.11 = (bf16[2,64,768]{2,1,0:T(8,128)(2,1)S(1)}, bf16[2,64,768]{2,1,0:T(8,128)(2,1)S(1)}, u32[]{:S(2)}, u32[]{:S(2)}) collective-permute-start(bf16[2,64,768]{2,1,0:T(8,128)(2,1)S(1)} %project.11), channel_id=1, source_target_pairs={{0,2},{1,3},{2,0},{3,1},{4,6},{5,7},{6,4},{7,5},{8,10},{9,11},{10,... | collective-permute-start | bytes 589832 | tf_op jit(solution)/shard_map/ppermute | solution.py:349
  48.0 6.1 %collective-permute-start.8 = (bf16[128,768]{1,0:T(8,128)(2,1)S(1)}, bf16[128,768]{1,0:T(8,128)(2,1)S(1)}, u32[]{:S(2)}, u32[]{:S(2)}) collective-permute-start(bf16[128,768]{1,0:T(8,128)(2,1)S(1)} %get-tuple-element.28), channel_id=1, source_target_pairs={{0,16},{1,17},{2,18},{3,19},{4,20},{5,21},{6,22},{7,23},{8,24},{9,... | collective-permute-start | bytes 589832 | tf_op jit(solution)/shard_map/ppermute | solution.py:349
  49.5 5.7 %collective-permute-start.7 = (bf16[128,768]{1,0:T(8,128)(2,1)S(1)}, bf16[128,768]{1,0:T(8,128)(2,1)S(1)}, u32[]{:S(2)}, u32[]{:S(2)}) collective-permute-start(bf16[128,768]{1,0:T(8,128)(2,1)S(1)} %get-tuple-element.27.refs_2_), channel_id=1, source_target_pairs={{0,8},{1,9},{2,10},{3,11},{4,12},{5,13},{6,14},{7,15},{8,0},{9,1},... | collective-permute-start | bytes 589832 | tf_op jit(solution)/shard_map/ppermute | solution.py:349
  51.0 6.6 %collective-permute-start.12 = (bf16[128,768]{1,0:T(8,128)(2,1)S(1)}, bf16[128,768]{1,0:T(8,128)(2,1)S(1)}, u32[]{:S(2)}, u32[]{:S(2)}) collective-permute-start(bf16[128,768]{1,0:T(8,128)(2,1)S(1)} %merge.5), channel_id=1, source_target_pairs={{0,24},{1,25},{2,26},{3,27},{4,28},{5,29},{6,30},{7,31},{8,16},{9,... | collective-permute-start | bytes 589832 | tf_op jit(solution)/shard_map/ppermute | solution.py:349
  57.8 12.5 %collective-permute-start.13 = (bf16[128,768]{1,0:T(8,128)(2,1)S(1)}, bf16[128,768]{1,0:T(8,128)(2,1)S(1)}, u32[]{:S(2)}, u32[]{:S(2)}) collective-permute-start(bf16[128,768]{1,0:T(8,128)(2,1)S(1)} %get-tuple-element.32), channel_id=1, source_target_pairs={{0,4},{1,5},{2,6},{3,7},{4,0},{5,1},{6,2},{7,3},{8,12},{9,13},{10,... | collective-permute-start | bytes 589832 | tf_op jit(solution)/shard_map/ppermute | solution.py:349
  60.4 10.0 %collective-permute-start.15 = (bf16[128,768]{1,0:T(8,128)(2,1)S(1)}, bf16[128,768]{1,0:T(8,128)(2,1)S(1)}, u32[]{:S(2)}, u32[]{:S(2)}) collective-permute-start(bf16[128,768]{1,0:T(8,128)(2,1)S(1)} %get-tuple-element.33), channel_id=1, source_target_pairs={{0,2},{1,3},{2,0},{3,1},{4,6},{5,7},{6,4},{7,5},{8,10},{9,11},{10,... | collective-permute-start | bytes 589832 | tf_op jit(solution)/shard_map/ppermute | solution.py:349
  62.0 8.5 %collective-permute-start.16 = (bf16[128,768]{1,0:T(8,128)(2,1)S(1)}, bf16[128,768]{1,0:T(8,128)(2,1)S(1)}, u32[]{:S(2)}, u32[]{:S(2)}) collective-permute-start(bf16[128,768]{1,0:T(8,128)(2,1)S(1)} %get-tuple-element.34), channel_id=1, source_target_pairs={{0,6},{1,7},{2,4},{3,5},{4,2},{5,3},{6,0},{7,1},{8,14},{9,15},{10,... | collective-permute-start | bytes 589832 | tf_op jit(solution)/shard_map/ppermute | solution.py:349
  70.4 1.5 %collective-permute-start.14 = (bf16[128,768]{1,0:T(8,128)(2,1)S(1)}, bf16[128,768]{1,0:T(8,128)(2,1)S(1)}, u32[]{:S(2)}, u32[]{:S(2)}) collective-permute-start(bf16[128,768]{1,0:T(8,128)(2,1)S(1)} %sum.2), channel_id=1, source_target_pairs={{0,1},{1,0},{2,3},{3,2},{4,5},{5,4},{6,7},{7,6},{8,9},{9,8},{10,11... | collective-permute-start | bytes 589832 | tf_op jit(solution)/shard_map/ppermute | solution.py:349
  70.5 1.6 %collective-permute-start.17 = (bf16[128,768]{1,0:T(8,128)(2,1)S(1)}, bf16[128,768]{1,0:T(8,128)(2,1)S(1)}, u32[]{:S(2)}, u32[]{:S(2)}) collective-permute-start(bf16[128,768]{1,0:T(8,128)(2,1)S(1)} %sum.3), channel_id=1, source_target_pairs={{0,1},{1,0},{2,3},{3,2},{4,5},{5,4},{6,7},{7,6},{8,9},{9,8},{10,11... | collective-permute-start | bytes 589832 | tf_op jit(solution)/shard_map/ppermute | solution.py:349
